TPU v7x, 128 devices: a whole 4x4x4 slice. The times are simulated.
128 devices in a mesh: leaf: 8 (over y, core), top: 16 (over x, z).
Axes of the slice: x: 4, y: 4, z: 4, core: 2. Of those that a mesh axis runs over, the one named last changes fastest.
Arguments:
- points: bfloat16 [1024, 64, 512], P(('leaf', 'top')), may hold values from -4 to 4
- right_sides: bfloat16 [1024, 64, 512], P(('leaf', 'top')), may hold values from -6 to 6
- leaf_basis: bfloat16 [1024, 512, 256], P(('leaf', 'top')), may hold values from -0.25 to 0.25
- transfer: bfloat16 [1024, 256, 256], P(('leaf', 'top')), may hold values from -0.125 to 0.125
- node_points: bfloat16 [8, 64, 256], P('leaf'), may hold values from -4 to 4
- neighbours: int32 [1024, 8], P(('leaf', 'top')), may hold values from -1 to 1023, as said below
- far_sources: int32 [1024, 16], P(('leaf', 'top')), may hold values from -1 to 1023, as said below
- skeleton: int32 [1024, 256], P(('leaf', 'top')), may hold values from 0 to 511, as said below
Outputs:
- product: bfloat16 [1024, 64, 512], P(('leaf', 'top'))
Inputs may be any that keep to these rules, and one draw needn't show every extreme that they name: `neighbours`: every entry is -1 or a leaf index that differs from its row's own leaf index by at most 8. `far_sources`: for row g, with d = g // 8 and r = d // 16, entry k is -1 or a leaf index in [(r * 16 + k) * 8, (r * 16 + k + 1) * 8). `skeleton`: each row holds 256 different indices.
All inputs are finite; a program needn't handle non-finite values.
Results may differ from a plain program's by a relative error of at most 0.015.
Values may be sent and summed in bfloat16 or wider, within the bound.
No kernel may reach another device: no remote copies, remote signals or barrier semaphores. Data moves between devices by JAX's collectives and lax.ppermute only.
A program may use at most 128 MiB of HBM per device.

v0:
```python
import jax
import jax.numpy as jnp
from jax import lax
from jax.sharding import PartitionSpec as P

F = 64


def extended(shard, sides, width):
    for axis, dim in sides:
        count, length = (lax.axis_size(axis), shard.shape[dim])
        up = [(i, (i + 1) % count) for i in range(count - 1)]
        down = [(j, i) for i, j in up]
        last = lax.slice_in_dim(shard, length - width, length, axis=dim)
        initial = lax.slice_in_dim(shard, 0, width, axis=dim)
        before = lax.ppermute(last, axis, up)
        after = lax.ppermute(initial, axis, down)
        shard = jnp.concatenate([before, shard, after], axis=dim)
    return shard


def kernel_block(source, target):
    crossed = jnp.einsum("nfa,nfb->nab", source, target, preferred_element_type=jnp.float32)
    source_norm = jnp.sum(jnp.square(source.astype(jnp.float32)), axis=1)
    target_norm = jnp.sum(jnp.square(target.astype(jnp.float32)), axis=1)
    distance = source_norm[:, :, None] + target_norm[:, None, :] - 2.0 * crossed
    return jnp.exp(distance * (-2.0 / F)).astype(jnp.bfloat16)


def on_device(
    points, right_sides, leaf_basis, transfer, node_points, neighbours, far_sources, skeleton
):
    leaf_count = points.shape[0]
    feature_count = points.shape[1]
    side_count = right_sides.shape[1]
    position = lax.axis_index(("leaf", "top"))
    first_leaf = position * leaf_count
    charges = jnp.einsum(
        "lrp,lps->lrs", right_sides, leaf_basis, preferred_element_type=jnp.float32
    ).astype(jnp.bfloat16)
    skel_points = jnp.take_along_axis(points, skeleton[:, None, :], axis=2)
    stacked = jnp.concatenate([points, right_sides], axis=1)
    window = extended(stacked, ((("leaf", "top"), 0),), leaf_count)
    near_sum = jnp.zeros((leaf_count, side_count, points.shape[2]), jnp.float32)
    for entry in range(neighbours.shape[1]):
        leaf_ids = neighbours[:, entry]
        present = leaf_ids >= 0
        local_ids = jnp.where(present, leaf_ids - first_leaf + leaf_count, 0)
        source = window[local_ids]
        kernel_tile = kernel_block(source[:, :feature_count], points)
        near_weights = source[:, feature_count:]
        near_weights = jnp.where(present[:, None, None], near_weights, jnp.zeros_like(near_weights))
        near_sum = near_sum + jnp.einsum(
            "lrp,lpq->lrq", near_weights, kernel_tile, preferred_element_type=jnp.float32
        )
    row_size = lax.axis_size("top")
    sources = jnp.concatenate([charges, skel_points], axis=1)
    row_first = lax.axis_index("leaf") * row_size * leaf_count
    far_present = far_sources >= 0
    owner_first = row_first + jnp.arange(row_size, dtype=jnp.int32)[None, :] * leaf_count
    wanted = jnp.where(far_present, far_sources - owner_first, 0)
    located = sources[lax.all_to_all(wanted.T, "top", split_axis=0, concat_axis=0, tiled=True)]
    fetched = lax.all_to_all(located, "top", split_axis=0, concat_axis=0, tiled=True)

    def far_step(running, element):
        fetched_piece, piece_present = element
        kernel_tile = kernel_block(fetched_piece[:, side_count:], skel_points)
        piece_charges = fetched_piece[:, :side_count]
        piece_charges = jnp.where(
            piece_present[:, None, None], piece_charges, jnp.zeros_like(piece_charges)
        )
        return (
            running
            + jnp.einsum(
                "lrs,lst->lrt", piece_charges, kernel_tile, preferred_element_type=jnp.float32
            ),
            None,
        )

    leaf_potential, unused = lax.scan(
        far_step,
        jnp.zeros((leaf_count, side_count, skeleton.shape[1]), jnp.float32),
        (fetched, far_present.T),
    )
    device_charge = jnp.einsum("lrs,lst->rt", charges, transfer, preferred_element_type=jnp.float32)
    node_total = lax.axis_size("leaf")
    node_sum = lax.psum(device_charge.astype(jnp.bfloat16), "top")
    node_all, node_all_points = (
        lax.all_gather(node_sum[None], "leaf", axis=0, tiled=True),
        lax.all_gather(node_points, "leaf", axis=0, tiled=True),
    )
    own_node = lax.axis_index("leaf")
    node_target = jnp.broadcast_to(node_points[0], node_all_points.shape)
    node_tiles = kernel_block(node_all_points, node_target)
    others = jnp.arange(node_total, dtype=jnp.int32) != own_node
    node_weights = jnp.where(others[:, None, None], node_all, jnp.zeros_like(node_all))
    top_potential = jnp.einsum(
        "mrs,mst->rt", node_weights, node_tiles, preferred_element_type=jnp.float32
    ).astype(jnp.bfloat16)
    potential = leaf_potential + jnp.einsum(
        "rt,lst->lrs", top_potential, transfer, preferred_element_type=jnp.float32
    )
    potential = potential.astype(jnp.bfloat16)
    far_out = jnp.einsum("lrs,lps->lrp", potential, leaf_basis, preferred_element_type=jnp.float32)
    return (near_sum + far_out).astype(jnp.bfloat16)


def solution(mesh):
    in_specs = (
        P(("leaf", "top"), None, None),
        P(("leaf", "top"), None, None),
        P(("leaf", "top"), None, None),
        P(("leaf", "top"), None, None),
        P("leaf", None, None),
        P(("leaf", "top"), None),
        P(("leaf", "top"), None),
        P(("leaf", "top"), None),
    )
    out_specs = P(("leaf", "top"), None, None)
    return jax.shard_map(
        on_device, mesh=mesh, in_specs=in_specs, out_specs=out_specs, check_vma=False
    )
```

profile of v0, /device:TPU:0, one launch (start us, length us, event | category | flops | bytes accessed | tf_op | source)
XLA Modules:
  0.0 464.2 jit_solution(12303333848603649348)
XLA Ops:
  1.5 8.0 %all-to-all-start = ((s32[16,1,8]{2,1,0:T(1,128)}), s32[16,1,8]{2,1,0:T(1,128)S(1)}, u32[]{:S(2)}, u32[]{:S(2)}) async-start(s32[16,1,8]{2,1,0:T(1,128)} %copy.20), calls=%async_computation | async-start | bytes 16384 | tf_op jit(solution)/shard_map/all_to_all | solution.py:62
  10.9 1.5 copy.17
  12.4 20.5 %gather_fusion.9 = bf16[2048,64]{1,0:T(8,128)(2,1)} fusion(bf16[8,64,512]{1,2,0:T(8,128)(2,1)S(1)} %copy.17, s32[2048]{0:T(1024)S(1)} %bitcast.75), kind=kCustom, calls=%fused_computation.9 | custom fusion | bytes 540672 | tf_op jit(solution)/shard_map/jit(take_along_axis)/gather | solution.py:41
  33.0 1.2 copy.19
  34.3 1.5 convolution_convert_fusion
  36.1 6.5 %gather_fusion.8 = bf16[128,128,256]{2,1,0:T(8,128)(2,1)} fusion(bf16[8,128,256]{2,1,0:T(8,128)(2,1)S(1)} %pad_maximum_fusion.1, s32[1024]{0:T(1024)S(1)} %pad_clamp_fusion), kind=kCustom, calls=%fused_computation.8 | custom fusion | bytes 16777728 | tf_op jit(solution)/shard_map/gather | solution.py:62
  42.6 7.4 %all-to-all-start.1 = ((bf16[16,8,128,256]{3,2,1,0:T(8,128)(2,1)}), bf16[16,8,128,256]{3,2,1,0:T(8,128)(2,1)}, u32[]{:S(2)}, u32[]{:S(2)}) async-start(bf16[16,8,128,256]{3,2,1,0:T(8,128)(2,1)} %bitcast.76), calls=%async_computation.1 | async-start | bytes 16777216 | tf_op jit(solution)/shard_map/all_to_all | solution.py:63
  50.9 1.9 constant_dynamic-update-slice_fusion
  52.8 1.3 collective-permute-start.1
  54.1 5.5 %collective-permute-start = (bf16[8,128,512]{2,1,0:T(8,128)(2,1)}, bf16[8,128,512]{2,1,0:T(8,128)(2,1)}, u32[]{:S(2)}, u32[]{:S(2)}) collective-permute-start(bf16[8,128,512]{2,1,0:T(8,128)(2,1)} %constant_dynamic-update-slice_fusion), channel_id=1, source_target_pairs={{0,1},{1,2},{2,3},{3,4},{4,5},{5,6},{6,7},{7,8},{8,9},{9,10},{10,1... | collective-permute-start | bytes 3145736 | tf_op jit(solution)/shard_map/ppermute | solution.py:16
  59.7 1.5 fusion.54
  61.3 220.8 %psum.7 = bf16[1,64,256]{2,1,0:T(8,128)(2,1)S(1)} all-reduce(bf16[1,64,256]{2,1,0:T(8,128)(2,1)S(1)} %fusion.54), channel_id=1, replica_groups=mesh['leaf'=8,'top'=16] {'top'}, use_global_device_ids=true, to_apply=%region_13.14 | all-reduce | flops 16384 | bytes 65536 | tf_op jit(solution)/shard_map/psum | solution.py:87
  283.7 12.8 %all_gather.7 = bf16[8,64,256]{2,1,0:T(8,128)(2,1)S(1)} all-gather(bf16[1,64,256]{2,1,0:T(8,128)(2,1)S(1)} %copy-done.3), channel_id=1, replica_groups=mesh['leaf'=8,'top'=16] {'leaf'}, dimensions={0}, use_global_device_ids=true | all-gather | bytes 294912 | tf_op jit(solution)/shard_map/all_gather | solution.py:90
  296.6 12.8 %all_gather.6 = bf16[8,64,256]{2,1,0:T(8,128)(2,1)S(1)} all-gather(bf16[1,64,256]{2,1,0:T(8,128)(2,1)S(1)} %psum.7), channel_id=1, replica_groups=mesh['leaf'=8,'top'=16] {'leaf'}, dimensions={0}, use_global_device_ids=true | all-gather | bytes 294912 | tf_op jit(solution)/shard_map/all_gather | solution.py:89
  309.6 1.5 fusion.53
  311.1 3.2 pad_maximum_fusion
  314.3 3.5 gather_fusion.7
  317.8 3.5 gather_fusion.6
  321.3 3.5 gather_fusion.5
  324.8 3.5 gather_fusion.4
  328.3 3.5 gather_fusion.3
  331.8 3.5 gather_fusion.2
  335.3 3.6 gather_fusion.1
  338.8 3.5 gather_fusion
  342.3 1.2 multiply_reduce_fusion.2
  343.5 1.2 multiply_reduce_fusion.3
  344.7 1.2 multiply_reduce_fusion.4
  345.9 1.2 multiply_reduce_fusion.5
  347.1 1.2 multiply_reduce_fusion.6
  348.2 1.2 multiply_reduce_fusion.7
  349.4 1.2 multiply_reduce_fusion.8
  350.6 1.2 multiply_reduce_fusion.10
  351.8 5.3 %fusion.20 = f32[8,64,512]{2,1,0:T(8,128)} fusion(f32[8,512]{1,0:T(8,128)S(1)} %multiply_reduce_fusion.2, f32[8,512]{1,0:T(8,128)S(1)} %multiply_reduce_fusion.9, bf16[8,64,512]{2,1,0:T(8,128)(2,1)S(1)} %copy-done.1, bf16[8,128,512]{2,1,0:T(8,128)(2,1)} %gather_fusion.7, pred[8]{0:T(512)(128)(4,1)S(1)} %copy-done.8), kind=kOutput, calls=%fused_computation.43 | convolution fusion | flops 547618816 | bytes 2654216 | tf_op jit(solution)/shard_map/lrp,lpq->lrq/dot_general | solution.py:53
  357.1 5.3 %fusion.19 = f32[8,64,512]{2,1,0:T(8,128)} fusion(f32[8,512]{1,0:T(8,128)S(1)} %multiply_reduce_fusion.3, f32[8,512]{1,0:T(8,128)S(1)} %multiply_reduce_fusion.9, bf16[8,64,512]{2,1,0:T(8,128)(2,1)S(1)} %copy-done.1, bf16[8,128,512]{2,1,0:T(8,128)(2,1)} %gather_fusion.6, pred[8]{0:T(512)(128)(4,1)S(1)} %copy-done.7), kind=kOutput, calls=%fused_computation.42 | convolution fusion | flops 547618816 | bytes 2654216 | tf_op jit(solution)/shard_map/lrp,lpq->lrq/dot_general | solution.py:53
  362.4 5.3 %fusion.18 = f32[8,64,512]{2,1,0:T(8,128)} fusion(f32[8,512]{1,0:T(8,128)S(1)} %multiply_reduce_fusion.4, f32[8,512]{1,0:T(8,128)S(1)} %multiply_reduce_fusion.9, bf16[8,64,512]{2,1,0:T(8,128)(2,1)S(1)} %copy-done.1, bf16[8,128,512]{2,1,0:T(8,128)(2,1)} %gather_fusion.5, pred[8]{0:T(512)(128)(4,1)S(1)} %copy-done.6), kind=kOutput, calls=%fused_computation.41 | convolution fusion | flops 547618816 | bytes 2654216 | tf_op jit(solution)/shard_map/lrp,lpq->lrq/dot_general | solution.py:53
  367.7 5.5 %fusion.17 = f32[8,64,512]{2,1,0:T(8,128)} fusion(f32[8,512]{1,0:T(8,128)S(1)} %multiply_reduce_fusion.5, f32[8,512]{1,0:T(8,128)S(1)} %multiply_reduce_fusion.9, bf16[8,64,512]{2,1,0:T(8,128)(2,1)S(1)} %copy-done.1, bf16[8,128,512]{2,1,0:T(8,128)(2,1)} %gather_fusion.4, pred[8]{0:T(512)(128)(4,1)S(1)} %copy-done.5), kind=kOutput, calls=%fused_computation.40 | convolution fusion | flops 547618816 | bytes 2654216 | tf_op jit(solution)/shard_map/lrp,lpq->lrq/dot_general | solution.py:53
  373.1 5.3 %fusion.16 = f32[8,64,512]{2,1,0:T(8,128)} fusion(f32[8,512]{1,0:T(8,128)S(1)} %multiply_reduce_fusion.6, f32[8,512]{1,0:T(8,128)S(1)} %multiply_reduce_fusion.9, bf16[8,64,512]{2,1,0:T(8,128)(2,1)S(1)} %copy-done.1, bf16[8,128,512]{2,1,0:T(8,128)(2,1)} %gather_fusion.3, pred[8]{0:T(512)(128)(4,1)S(1)} %get-tuple-element.106), kind=kOutput, calls=%fused_computation.39 | convolution fusion | flops 547618816 | bytes 2654216 | tf_op jit(solution)/shard_map/lrp,lpq->lrq/dot_general | solution.py:53
  378.4 5.3 %fusion.15 = f32[8,64,512]{2,1,0:T(8,128)} fusion(f32[8,512]{1,0:T(8,128)S(1)} %multiply_reduce_fusion.7, f32[8,512]{1,0:T(8,128)S(1)} %multiply_reduce_fusion.9, bf16[8,64,512]{2,1,0:T(8,128)(2,1)S(1)} %copy-done.1, bf16[8,128,512]{2,1,0:T(8,128)(2,1)} %gather_fusion.2, pred[8]{0:T(512)(128)(4,1)S(1)} %get-tuple-element.108), kind=kOutput, calls=%fused_computation.38 | convolution fusion | flops 547618816 | bytes 2654216 | tf_op jit(solution)/shard_map/lrp,lpq->lrq/dot_general | solution.py:53
  383.7 5.3 %fusion.14 = f32[8,64,512]{2,1,0:T(8,128)} fusion(f32[8,512]{1,0:T(8,128)S(1)} %multiply_reduce_fusion.8, f32[8,512]{1,0:T(8,128)S(1)} %multiply_reduce_fusion.9, bf16[8,64,512]{2,1,0:T(8,128)(2,1)S(1)} %copy-done.1, bf16[8,128,512]{2,1,0:T(8,128)(2,1)} %gather_fusion.1, pred[8]{0:T(512)(128)(4,1)S(1)} %get-tuple-element.110), kind=kOutput, calls=%fused_computation.37 | convolution fusion | flops 547618816 | bytes 2654216 | tf_op jit(solution)/shard_map/lrp,lpq->lrq/dot_general | solution.py:53
  389.0 64.0 %while.11 = (s32[]{:T(128)}, f32[8,64,256]{2,1,0:T(8,128)}, pred[16,8]{1,0:T(8,128)(4,1)S(1)}, bf16[16,8,128,256]{3,2,1,0:T(8,128)(2,1)}, bf16[8,64,256]{2,1,0:T(8,128)(2,1)S(1)}, /*index=5*/s32[]{:T(128)}, s32[]{:T(128)}) while((s32[]{:T(128)}, f32[8,64,256]{2,1,0:T(8,128)}, pred[16,8]{1,0:T(8,128)(4,1)S(1)}, ...), condition=%wide.region_12.13_spmd.clone, body=%wide.region_9.12_spmd.clone.sunk | while | flops 138014720 | bytes 3440767 | solution.py:80
  389.0 1.1 dynamic-slice_bitcast_fusion.4
  390.2 1.8 fusion.163
  392.0 1.1 dynamic-slice_bitcast_fusion.4
  393.2 2.8 fusion.163
  396.1 1.1 dynamic-slice_bitcast_fusion.4
  397.3 2.8 fusion.163
  400.1 1.1 dynamic-slice_bitcast_fusion.4
  401.4 2.8 fusion.163
  405.4 2.8 fusion.163
  409.5 2.8 fusion.163
  413.6 2.8 fusion.163
  417.7 2.8 fusion.163
  421.7 2.8 fusion.163
  425.8 2.8 fusion.163
  429.9 2.8 fusion.163
  433.9 2.8 fusion.163
  438.0 2.8 fusion.163
  442.1 2.8 fusion.163
  444.9 1.1 dynamic-slice_bitcast_fusion.4
  446.1 2.8 fusion.163
  448.9 1.1 dynamic-slice_bitcast_fusion.4
  450.2 2.8 fusion.163
  453.0 3.4 fusion.49
  456.4 7.8 %fusion.46 = bf16[8,64,512]{2,1,0:T(8,128)(2,1)} fusion(f32[8,64,512]{2,1,0:T(8,128)} %fusion.49, f32[8,64,512]{2,1,0:T(8,128)} %fusion.20, f32[8,64,512]{2,1,0:T(8,128)} %fusion.19, f32[8,64,512]{2,1,0:T(8,128)} %fusion.18, f32[8,64,512]{2,1,0:T(8,128)} %fusion.17, f32[8,64,512]{2,1,0:T(8,128)} %fusion.16, f32[8,64,512]{2,1,0:T(8,128)} %fusion.15, ...), kind=kOutput, calls=%fused_computation.63 | convolution fusion | flops 549978112 | bytes 10518536 | tf_op jit(solution)/shard_map/lrp,lpq->lrq/dot_general | solution.py:53
  (92 shorter events, 19.2 us)
Async XLA Ops:
  0.0 34.3 %copy-start = (bf16[8,512,256]{2,1,0:T(8,128)(2,1)S(1)}, bf16[8,512,256]{2,1,0:T(8,128)(2,1)}, u32[]{:S(2)}) copy-start(bf16[8,512,256]{2,1,0:T(8,128)(2,1)} %param.12) | copy-start | bytes 6291460
  1.5 34.3 %all-to-all-start = ((s32[16,1,8]{2,1,0:T(1,128)}), s32[16,1,8]{2,1,0:T(1,128)S(1)}, u32[]{:S(2)}, u32[]{:S(2)}) async-start(s32[16,1,8]{2,1,0:T(1,128)} %copy.20), calls=%async_computation | async-start | bytes 16384 | tf_op jit(solution)/shard_map/all_to_all | solution.py:62
  42.6 7.4 %copy-start.1 = (bf16[8,64,512]{2,1,0:T(8,128)(2,1)S(1)}, bf16[8,64,512]{2,1,0:T(8,128)(2,1)}, u32[]{:S(2)}) copy-start(bf16[8,64,512]{2,1,0:T(8,128)(2,1)} %param.10) | copy-start | bytes 1572868
  42.6 17.0 %copy-start.4 = (s32[8,16]{1,0:T(8,128)S(1)}, s32[8,16]{1,0:T(8,128)}, u32[]{:S(2)}) copy-start(s32[8,16]{1,0:T(8,128)} %param.16) | copy-start | bytes 1540
  42.6 239.4 %copy-start.2 = (s32[8,8]{1,0:T(8,128)S(1)}, s32[8,8]{1,0:T(8,128)}, u32[]{:S(2)}) copy-start(s32[8,8]{1,0:T(8,128)} %param.15) | copy-start | bytes 772
  42.6 241.1 %copy-start.3 = (bf16[1,64,256]{2,1,0:T(8,128)(2,1)S(1)}, bf16[1,64,256]{2,1,0:T(8,128)(2,1)}, u32[]{:S(2)}) copy-start(bf16[1,64,256]{2,1,0:T(8,128)(2,1)} %param.14) | copy-start | bytes 98308
  42.6 346.3 %all-to-all-start.1 = ((bf16[16,8,128,256]{3,2,1,0:T(8,128)(2,1)}), bf16[16,8,128,256]{3,2,1,0:T(8,128)(2,1)}, u32[]{:S(2)}, u32[]{:S(2)}) async-start(bf16[16,8,128,256]{3,2,1,0:T(8,128)(2,1)} %bitcast.76), calls=%async_computation.1 | async-start | bytes 16777216 | tf_op jit(solution)/shard_map/all_to_all | solution.py:63
  52.8 258.3 %collective-permute-start.1 = (bf16[8,128,512]{2,1,0:T(8,128)(2,1)}, bf16[8,128,512]{2,1,0:T(8,128)(2,1)}, u32[]{:S(2)}, u32[]{:S(2)}) collective-permute-start(bf16[8,128,512]{2,1,0:T(8,128)(2,1)} %constant_dynamic-update-slice_fusion), channel_id=1, source_target_pairs={{1,0},{2,1},{3,2},{4,3},{5,4},{6,5},{7,6},{8,7},{9,8},{10,9},{11,1... | collective-permute-start | bytes 3145736 | tf_op jit(solution)/shard_map/ppermute | solution.py:17
  54.1 257.0 %collective-permute-start = (bf16[8,128,512]{2,1,0:T(8,128)(2,1)}, bf16[8,128,512]{2,1,0:T(8,128)(2,1)}, u32[]{:S(2)}, u32[]{:S(2)}) collective-permute-start(bf16[8,128,512]{2,1,0:T(8,128)(2,1)} %constant_dynamic-update-slice_fusion), channel_id=1, source_target_pairs={{0,1},{1,2},{2,3},{3,4},{4,5},{5,6},{6,7},{7,8},{8,9},{9,10},{10,1... | collective-permute-start | bytes 3145736 | tf_op jit(solution)/shard_map/ppermute | solution.py:16
  321.3 30.5 %copy-start.8 = (pred[8]{0:T(512)(128)(4,1)S(1)}, pred[8]{0:T(512)(128)(4,1)}, u32[]{:S(2)}) copy-start(pred[8]{0:T(512)(128)(4,1)} %get-tuple-element.98) | copy-start | bytes 28
  343.5 13.6 %copy-start.7 = (pred[8]{0:T(512)(128)(4,1)S(1)}, pred[8]{0:T(512)(128)(4,1)}, u32[]{:S(2)}) copy-start(pred[8]{0:T(512)(128)(4,1)} %get-tuple-element.114) | copy-start | bytes 28
  357.1 5.3 %copy-start.6 = (pred[8]{0:T(512)(128)(4,1)S(1)}, pred[8]{0:T(512)(128)(4,1)}, u32[]{:S(2)}) copy-start(pred[8]{0:T(512)(128)(4,1)} %get-tuple-element.102) | copy-start | bytes 28
  362.4 5.3 %copy-start.5 = (pred[8]{0:T(512)(128)(4,1)S(1)}, pred[8]{0:T(512)(128)(4,1)}, u32[]{:S(2)}) copy-start(pred[8]{0:T(512)(128)(4,1)} %get-tuple-element.104) | copy-start | bytes 28
where the time goes:
time: 468 us; the launch traced here: 464 us
  blocking collectives  246 us (53%)
  matrix products  97 us (21%)
  local copies, waits for them, and re-layouts  79 us (17%)
  starting transfers between devices  22.2 us (5%)
  other arithmetic  19 us (4%)
    psum x1, blocking collectives, on_device(): node_sum = lax.psum(device_charge.astype(jnp.bfloat16), 'top')  221 us
    dot_general x8, matrix products, on_device(): jnp.einsum('lrp,lpq->lrq', near_weights, kernel_tile, preferred_element_t...  44.9 us
    dot_general x16, matrix products, far_step(): jnp.einsum('lrs,lst->lrt', piece_charges, kernel_tile, preferred_element_...  44.1 us
    gather x8, local copies, waits for them, and re-layouts, on_device(): source = window[local_ids]  28 us
    gather x2, local copies, waits for them, and re-layouts, on_device(): skel_points = jnp.take_along_axis(points, skeleton[:, None, :], axis=2)  21.8 us
    squeeze x16, local copies, waits for them, and re-layouts, on_device(): lax.scan(far_step, jnp.zeros((leaf_count, side_count, skeleton.shape[1]),...  17.2 us
    all_gather x1, blocking collectives, on_device(): lax.all_gather(node_points, 'leaf', axis=0, tiled=True)  12.8 us
    all_gather x1, blocking collectives, on_device(): lax.all_gather(node_sum[None], 'leaf', axis=0, tiled=True)  12.8 us
  transfers between devices with their start and end apart: 4, of which 0 were waited for; matrix products, arithmetic and copies ran while one was open for 24% of the time, Pallas kernels for 0%

commit v1 on v0

v1 whole, which is shorter than its diff:
```python
import functools

import jax
import jax.numpy as jnp
from jax import lax
from jax.experimental import pallas as pl
from jax.experimental.pallas import tpu as pltpu
from jax.sharding import PartitionSpec as P

BF = jnp.bfloat16
F32 = jnp.float32
F = 64
RHS = 64
LP = 512
SK = 256
LD = 8
SIDE = 4
AUG = 128
VM = pl.BlockSpec(memory_space=pltpu.VMEM)
SM = pl.BlockSpec(memory_space=pltpu.SMEM)


def params(mib=40):
    return pltpu.CompilerParams(vmem_limit_bytes=mib * 2**20)


def norm_rows(points, first):
    norm = jnp.sum(points * points, axis=0, keepdims=True) * (-2.0 / F)
    high = norm.astype(BF).astype(F32)
    mid = (norm - high).astype(BF).astype(F32)
    low = norm - high - mid
    row = lax.broadcasted_iota(jnp.int32, (16, points.shape[1]), 0)
    at = 0 if first else 3
    ones = jnp.where(row < 6, 1.0, 0.0).astype(F32)
    rows = jnp.where(row == at + 1, mid, jnp.where(row == at + 2, low, ones))
    return jnp.where(row == at, high, rows)


def source_side(points):
    points = points.astype(F32)
    zeros = jnp.zeros((AUG - F - 16, points.shape[1]), F32)
    full = jnp.concatenate([points, norm_rows(points, True), zeros], axis=0)
    return full.T.astype(BF)


def target_side(points):
    points = points.astype(F32)
    zeros = jnp.zeros((AUG - F - 16, points.shape[1]), F32)
    full = jnp.concatenate([points * (4.0 / F), norm_rows(points, False), zeros], axis=0)
    return full.astype(BF)


def prep_kernel(
    points, sides, basis, transfer, skeleton, far, near_msg, source_msg, target_msg, node, ids
):
    leaf = pl.program_id(0)
    near_msg[0, :F, :] = points[0]
    near_msg[0, F:, :] = sides[0]
    charge = jnp.dot(sides[0], basis[0], preferred_element_type=F32).astype(BF)
    position = lax.broadcasted_iota(jnp.int32, (LP, SK), 0)
    chosen = jnp.where(position == skeleton[0], 1.0, 0.0).astype(BF)
    skel = jnp.dot(points[0], chosen, preferred_element_type=F32).astype(BF)
    source_msg[pl.ds(pl.multiple_of(leaf * 2 * F, 2 * F), F), :] = charge
    source_msg[pl.ds(pl.multiple_of(leaf * 2 * F + F, F), F), :] = skel
    target_msg[pl.ds(pl.multiple_of(leaf * F, F), F), :] = skel
    part = jnp.dot(charge, transfer[0], preferred_element_type=F32)

    @pl.when(leaf == 0)
    def _():
        node[...] = part
        ids[...] = jnp.zeros_like(ids)
        named = far[...]
        ids[:LD, : SIDE * SIDE] = jnp.where(named >= 0, named & (LD - 1), -1).astype(F32)
        target_msg[LD * F :, :] = ids[...].astype(BF)

    @pl.when(leaf > 0)
    def _():
        node[...] += part

    @pl.when(leaf == LD - 1)
    def _():
        source_msg[LD * 2 * F :, :] = node[...].astype(BF)


def prep(points, sides, basis, transfer, skeleton, far):
    def block(*shape):
        return pl.BlockSpec((1, *shape), lambda i: (i, 0, 0))

    def whole(*shape):
        return pl.BlockSpec(shape, lambda i: (0,) * len(shape))

    source_rows, target_rows = LD * 2 * F + RHS, LD * F + 16
    return pl.pallas_call(
        prep_kernel,
        grid=(LD,),
        in_specs=[
            block(F, LP),
            block(RHS, LP),
            block(LP, SK),
            block(SK, SK),
            block(1, SK),
            whole(LD, SIDE * SIDE),
        ],
        out_specs=[block(2 * F, LP), whole(source_rows, SK), whole(target_rows, SK)],
        out_shape=[
            jax.ShapeDtypeStruct((LD, 2 * F, LP), BF),
            jax.ShapeDtypeStruct((source_rows, SK), BF),
            jax.ShapeDtypeStruct((target_rows, SK), BF),
        ],
        scratch_shapes=[pltpu.VMEM((RHS, SK), F32), pltpu.VMEM((16, SK), F32)],
        compiler_params=params(24),
        cost_estimate=pl.CostEstimate(
            flops=10**9, bytes_accessed=6 * 10**6, transcendentals=0
        ),
        name="prep",
    )(points, sides, basis, transfer, skeleton.reshape(LD, 1, SK), far)


def far_kernel(
    ids, place, s0, s1, s2, s3, t0, t1, t2, t3, nodes, own, r1, r2, r3, top, side, tile
):
    sources = (s0, s1, s2, s3)
    for d, source in enumerate(sources):

        @pl.loop(0, LD)
        def _(leaf, d=d, source=source):
            rows = pl.ds(pl.multiple_of(leaf * 2 * F + F, F), F)
            side[d * LD + leaf] = source_side(source[rows, :])

    x, z, self_node = place[0], place[1], place[2]
    shifts = (0, SIDE - 1, 1, 2)
    for b, (target, out) in enumerate(zip((t0, t1, t2, t3), (own, r1, r2, r3))):

        @pl.loop(0, LD)
        def _(leaf, b=b, target=target, out=out):
            rows = pl.ds(pl.multiple_of(leaf * F, F), F)
            points = target_side(target[rows, :])
            weights = []
            for d, source in enumerate(sources):
                column = lax.rem(x + shifts[d], SIDE) * SIDE + z
                named = ids[b * LD + leaf, column]
                at = jnp.maximum(named, 0)
                tile[d * SK : (d + 1) * SK, :] = jnp.exp(
                    jnp.dot(side[d * LD + at], points, preferred_element_type=F32)
                ).astype(BF)
                weight = source[pl.ds(pl.multiple_of(at * 2 * F, 2 * F), RHS), :]
                weights.append(jnp.where(named >= 0, weight, jnp.zeros_like(weight)))
            total = jnp.dot(
                jnp.concatenate(weights, axis=1), tile[...], preferred_element_type=F32
            )
            out[rows, :] = total.astype(out.dtype)

    points = target_side(nodes[self_node, RHS:, :])
    top[...] = jnp.zeros_like(top)
    total = jnp.zeros((RHS, SK), F32)
    for m in range(nodes.shape[0]):
        kernel = jnp.exp(
            jnp.dot(source_side(nodes[m, RHS:, :]), points, preferred_element_type=F32)
        ).astype(BF)
        weight = nodes[m, :RHS, :]
        weight = jnp.where(self_node == m, jnp.zeros_like(weight), weight)
        total += jnp.dot(weight, kernel, preferred_element_type=F32)
    top[...] = total
    for out in (r1, r2, r3):
        out[LD * F :, :] = total.astype(BF)


def far(ids, place, sources, targets, nodes):
    rows = LD * F
    return pl.pallas_call(
        far_kernel,
        in_specs=[SM, SM] + [VM] * 9,
        out_specs=[VM] * 5,
        out_shape=[jax.ShapeDtypeStruct((rows, SK), F32)]
        + [jax.ShapeDtypeStruct((rows + RHS, SK), BF)] * 3
        + [jax.ShapeDtypeStruct((RHS, SK), F32)],
        scratch_shapes=[
            pltpu.VMEM((SIDE * LD, SK, AUG), BF),
            pltpu.VMEM((SIDE * SK, SK), BF),
        ],
        compiler_params=params(),
        cost_estimate=pl.CostEstimate(
            flops=15 * 10**9, bytes_accessed=8 * 10**6, transcendentals=8 * 10**6
        ),
        name="far",
    )(ids, place, *sources, *targets, nodes)


def near_kernel(ids, first, own, before, after, out, side, rights, tile):
    for d, block in enumerate((before, own, after)):

        @pl.loop(0, LD)
        def _(leaf, d=d, block=block):
            side[d * LD + leaf] = source_side(block[leaf, :F, :])
            rights[d * LD + leaf] = block[leaf, F:, :]

    @pl.loop(0, LD)
    def _(leaf):
        points = target_side(own[leaf, :F, :])
        total = jnp.zeros((RHS, LP), F32)
        for group in range(2):
            weights = []
            for d in range(4):
                named = ids[leaf, group * 4 + d]
                at = jnp.clip(named - first[0], 0, 3 * LD - 1)
                tile[d * LP : (d + 1) * LP, :] = jnp.exp(
                    jnp.dot(side[at], points, preferred_element_type=F32)
                ).astype(BF)
                weight = rights[at]
                weights.append(jnp.where(named >= 0, weight, jnp.zeros_like(weight)))
            total += jnp.dot(
                jnp.concatenate(weights, axis=1), tile[...], preferred_element_type=F32
            )
        out[leaf] = total


def near(ids, first, own, before, after):
    return pl.pallas_call(
        near_kernel,
        in_specs=[SM, SM, VM, VM, VM],
        out_specs=VM,
        out_shape=jax.ShapeDtypeStruct((LD, RHS, LP), F32),
        scratch_shapes=[
            pltpu.VMEM((3 * LD, LP, AUG), BF),
            pltpu.VMEM((3 * LD, RHS, LP), BF),
            pltpu.VMEM((4 * LP, LP), BF),
        ],
        compiler_params=params(),
        cost_estimate=pl.CostEstimate(
            flops=30 * 10**9, bytes_accessed=4 * 10**6, transcendentals=16 * 10**6
        ),
        name="near",
    )(ids, first, own, before, after)


def final_kernel(near_sum, basis, transfer, own, r1, r2, r3, t0, q1, q2, q3, out):
    top = t0[...] + q1[...].astype(F32) + q2[...].astype(F32) + q3[...].astype(F32)
    potential = own[...] + r1[...].astype(F32) + r2[...].astype(F32) + r3[...].astype(F32)
    nt = (((1,), (1,)), ((), ()))
    potential += lax.dot_general(top.astype(BF), transfer[0], nt, preferred_element_type=F32)
    far_out = lax.dot_general(potential.astype(BF), basis[0], nt, preferred_element_type=F32)
    out[0] = (near_sum[0] + far_out).astype(BF)


def final(near_sum, basis, transfer, own, returned, top):
    def block(*shape):
        return pl.BlockSpec((1, *shape), lambda i: (i, 0, 0))

    row = pl.BlockSpec((RHS, SK), lambda i: (i, 0))
    zero = pl.BlockSpec((RHS, SK), lambda i: (0, 0))
    last = pl.BlockSpec((RHS, SK), lambda i: (LD, 0))
    return pl.pallas_call(
        final_kernel,
        grid=(LD,),
        in_specs=[block(RHS, LP), block(LP, SK), block(SK, SK)]
        + [row] * 4
        + [zero]
        + [last] * 3,
        out_specs=block(RHS, LP),
        out_shape=jax.ShapeDtypeStruct((LD, RHS, LP), BF),
        compiler_params=params(24),
        cost_estimate=pl.CostEstimate(
            flops=10**9, bytes_accessed=6 * 10**6, transcendentals=0
        ),
        name="final",
    )(near_sum, basis, transfer, own, *returned, top, *returned)


def shifted(value, dx, dz):
    pairs = []
    for x in range(SIDE):
        for z in range(SIDE):
            to = (x + dx) % SIDE * SIDE + (z + dz) % SIDE
            pairs.append((x * SIDE + z, to))
    return lax.ppermute(value, "top", pairs)


def on_device(
    points, right_sides, leaf_basis, transfer, node_points, neighbours, far_sources, skeleton
):
    node, at = lax.axis_index("leaf"), lax.axis_index("top")
    position = node * SIDE * SIDE + at
    near_msg, source_msg, target_msg = prep(
        points, right_sides, leaf_basis, transfer, skeleton, far_sources
    )
    sources = [source_msg]
    sources += [shifted(source_msg, dx, 0) for dx in (1, -1, 2)]
    targets = [target_msg]
    targets += [shifted(target_msg, 0, dz) for dz in (1, -1, 2)]
    count = lax.axis_size("leaf") * lax.axis_size("top")
    up = [(i, i + 1) for i in range(count - 1)]
    before = lax.ppermute(near_msg, ("leaf", "top"), up)
    after = lax.ppermute(near_msg, ("leaf", "top"), [(j, i) for i, j in up])
    row_charge = sum(s[LD * 2 * F :].astype(F32) for s in sources).astype(BF)
    nodes = lax.all_gather(
        jnp.concatenate([row_charge, node_points[0]], axis=0), "leaf", axis=0
    )
    ids = jnp.concatenate([t[LD * F : LD * F + LD, : SIDE * SIDE] for t in targets], axis=0)
    place = jnp.stack([at // SIDE, at % SIDE, node]).astype(jnp.int32)
    own, r1, r2, r3, top = far(ids.astype(jnp.int32), place, sources, targets, nodes)
    returned = [
        shifted(r, 0, dz) for r, dz in ((r1, -1), (r2, 1), (r3, 2))
    ]
    first = ((position - 1) * LD).astype(jnp.int32).reshape(1)
    near_sum = near(neighbours, first, near_msg, before, after)
    return final(near_sum, leaf_basis, transfer, own, returned, top)


def solution(mesh):
    leaves = P(("leaf", "top"), None, None)
    lists = P(("leaf", "top"), None)
    in_specs = (leaves, leaves, leaves, leaves, P("leaf", None, None), lists, lists, lists)
    return jax.shard_map(
        on_device, mesh=mesh, in_specs=in_specs, out_specs=leaves, check_vma=False
    )
```

time: 468 us -> 106 us (0.23)
  blocking collectives: 246 us -> 13.6 us
  matrix products: 97 us -> 0 us
  local copies, waits for them, and re-layouts: 79 us -> 7.31 us
  Pallas kernels: 0 us -> 47.3 us
  other arithmetic: 19 us -> 0.11 us
  waiting for transfers between devices: 0.01 us -> 15.7 us
    psum x1 -> x0, blocking collectives: 221 us -> none  [on_device(): node_sum = lax.psum(device_charge.astype(jnp.bfloat16), 'top')]
    dot_general x28 -> x0, matrix products: 97 us -> none  [the longest x8 44.9 us: on_device(): jnp.einsum('lrp,lpq->lrq', near_weights, kernel_tile, preferred_element_t...]
    gather x11 -> x0, local copies, waits for them, and re-layouts: 56.3 us -> none  [the longest x8 28 us: on_device(): source = window[local_ids]]
    pallas_call x0 -> x4, Pallas kernels: none -> 47.3 us  [the longest x1 21.2 us: far(): pl.pallas_call(far_kernel, in_specs=[SM, SM] + [VM] * 9, out_specs=[VM] *...]
    squeeze x16 -> x0, local copies, waits for them, and re-layouts: 17.2 us -> none  [on_device(): lax.scan(far_step, jnp.zeros((leaf_count, side_count, skeleton.shape[1]),...]
    ppermute x2 -> x11, waiting for transfers between devices: 0.01 us -> 15.7 us  [the longest x9 15.7 us: shifted(): return lax.ppermute(value, 'top', pairs)]
    all_to_all x2 -> x0, starting transfers between devices: 15.4 us -> none  [the longest x1 7.97 us: on_device(): lax.all_to_all(wanted.T, 'top', split_axis=0, concat_axis=0, tiled=True)]
    ppermute x2 -> x11, starting transfers between devices: 6.81 us -> 20.2 us  [the longest x9 16 us: shifted(): return lax.ppermute(value, 'top', pairs)]
  transfers between devices with their start and end apart: 4 -> 11, of which waited for: 0 -> 4; matrix products, arithmetic and copies ran while one was open for 24% -> 0% of each run, Pallas kernels for 0% -> 38%
where the time goes in v1:
time: 106 us; the launch traced here: 104 us
  Pallas kernels  47.3 us (45%)
  starting transfers between devices  20.2 us (19%)
  waiting for transfers between devices  15.7 us (15%)
  blocking collectives  13.6 us (13%)
  local copies, waits for them, and re-layouts  7.31 us (7%)
    pallas_call x1, Pallas kernels, far(): pl.pallas_call(far_kernel, in_specs=[SM, SM] + [VM] * 9, out_specs=[VM] *...  21.2 us
    pallas_call x1, Pallas kernels, near(): pl.pallas_call(near_kernel, in_specs=[SM, SM, VM, VM, VM], out_specs=VM,...  18.8 us
    ppermute x9, starting transfers between devices, shifted(): return lax.ppermute(value, 'top', pairs)  16 us
    ppermute x9, waiting for transfers between devices, shifted(): return lax.ppermute(value, 'top', pairs)  15.7 us
    all_gather x1, blocking collectives, on_device(): lax.all_gather(jnp.concatenate([row_charge, node_points[0]], axis=0), 'le...  13.6 us
    unnamed x22, local copies, waits for them, and re-layouts  6.59 us
    pallas_call x1, Pallas kernels, final(): pl.pallas_call(final_kernel, grid=(LD,), in_specs=[block(RHS, LP), block(...  4.54 us
    ppermute x1, starting transfers between devices, on_device(): before = lax.ppermute(near_msg, ('leaf', 'top'), up)  2.89 us
  transfers between devices with their start and end apart: 11, of which 4 were waited for; matrix products, arithmetic and copies ran while one was open for 0% of the time, Pallas kernels for 38%

profile of v1, /device:TPU:0, one launch (start us, length us, event | category | flops | bytes accessed | tf_op | source)
XLA Modules:
  0.0 104.5 jit_solution(6306355904359845146)
XLA Ops:
  0.0 0.7 reshape.7.skeleton
  0.7 0.0 copy-start
  0.7 1.6 %copy-done = bf16[8,512,256]{2,1,0:T(8,128)(2,1)S(1)} copy-done((bf16[8,512,256]{2,1,0:T(8,128)(2,1)S(1)}, bf16[8,512,256]{2,1,0:T(8,128)(2,1)}, u32[]{:S(2)}) %copy-start) | copy-done | bytes 2097176
  2.3 0.0 copy-start.2
  2.3 1.2 %copy-done.2 = bf16[8,256,256]{2,1,0:T(8,128)(2,1)S(1)} copy-done((bf16[8,256,256]{2,1,0:T(8,128)(2,1)S(1)}, bf16[8,256,256]{2,1,0:T(8,128)(2,1)}, u32[]{:S(2)}) %copy-start.2) | copy-done | bytes 1048600
  3.5 0.0 copy-start.4
  3.5 1.0 copy-done.4
  4.6 0.0 copy-start.5
  4.6 1.0 copy-done.5
  5.6 0.0 copy-start.6
  5.6 0.7 copy-done.6
  6.3 0.0 copy-start.10
  6.3 2.8 %prep.1 = (bf16[8,128,512]{2,1,0:T(8,128)(2,1)S(1)}, bf16[1088,256]{1,0:T(8,128)(2,1)S(1)}, bf16[528,256]{1,0:T(8,128)(2,1)S(1)}) custom-call(bf16[8,64,512]{2,1,0:T(8,128)(2,1)S(1)} %copy-done.4, bf16[8,64,512]{2,1,0:T(8,128)(2,1)S(1)} %copy-done.5, bf16[8,512,256]{2,1,0:T(8,128)(2,1)S(1)} %copy-done, bf16[8,256,256]{2,1,0:T(8,128)(2,1)S(1)} %copy-done.2, ...), custom_call_target="tpu_custom_call" | custom-call | flops 1000000000 | bytes 6000000 | tf_op jit(solution)/shard_map/prep/pallas_call | solution.py:93
  9.1 0.0 copy-start.7
  9.1 1.0 copy-done.7
  10.1 4.0 %collective-permute-start.4 = (bf16[528,256]{1,0:T(8,128)(2,1)S(1)}, bf16[528,256]{1,0:T(8,128)(2,1)S(1)}, u32[]{:S(2)}, u32[]{:S(2)}) collective-permute-start(bf16[528,256]{1,0:T(8,128)(2,1)S(1)} %get-tuple-element.14.t0), channel_id=1, source_target_pairs={{0,2},{1,3},{2,0},{3,1},{4,6},{5,7},{6,4},{7,5},{8,10},{9,11},{10,... | collective-permute-start | bytes 811016 | tf_op jit(solution)/shard_map/ppermute | solution.py:275
  14.0 1.5 %collective-permute-start.5 = (bf16[1088,256]{1,0:T(8,128)(2,1)S(1)}, bf16[1088,256]{1,0:T(8,128)(2,1)S(1)}, u32[]{:S(2)}, u32[]{:S(2)}) collective-permute-start(bf16[1088,256]{1,0:T(8,128)(2,1)S(1)} %get-tuple-element.15.s0), channel_id=1, source_target_pairs={{0,4},{1,5},{2,6},{3,7},{4,8},{5,9},{6,10},{7,11},{8,12},{9,13},{1... | collective-permute-start | bytes 1671176 | tf_op jit(solution)/shard_map/ppermute | solution.py:275
  15.5 1.7 %collective-permute-start.6 = (bf16[1088,256]{1,0:T(8,128)(2,1)S(1)}, bf16[1088,256]{1,0:T(8,128)(2,1)S(1)}, u32[]{:S(2)}, u32[]{:S(2)}) collective-permute-start(bf16[1088,256]{1,0:T(8,128)(2,1)S(1)} %get-tuple-element.15.s0), channel_id=1, source_target_pairs={{0,12},{1,13},{2,14},{3,15},{4,0},{5,1},{6,2},{7,3},{8,4},{9,5},{1... | collective-permute-start | bytes 1671176 | tf_op jit(solution)/shard_map/ppermute | solution.py:275
  17.3 1.8 %collective-permute-start.7 = (bf16[1088,256]{1,0:T(8,128)(2,1)S(1)}, bf16[1088,256]{1,0:T(8,128)(2,1)S(1)}, u32[]{:S(2)}, u32[]{:S(2)}) collective-permute-start(bf16[1088,256]{1,0:T(8,128)(2,1)S(1)} %get-tuple-element.15.s0), channel_id=1, source_target_pairs={{0,8},{1,9},{2,10},{3,11},{4,12},{5,13},{6,14},{7,15},{8,0},{9,1},... | collective-permute-start | bytes 1671176 | tf_op jit(solution)/shard_map/ppermute | solution.py:275
  19.1 0.7 collective-permute-start.3
  19.8 0.7 collective-permute-done.4.t3
  20.5 2.4 %collective-permute-start.2 = (bf16[528,256]{1,0:T(8,128)(2,1)S(1)}, bf16[528,256]{1,0:T(8,128)(2,1)S(1)}, u32[]{:S(2)}, u32[]{:S(2)}) collective-permute-start(bf16[528,256]{1,0:T(8,128)(2,1)S(1)} %get-tuple-element.14.t0), channel_id=1, source_target_pairs={{0,1},{1,2},{2,3},{3,0},{4,5},{5,6},{6,7},{7,4},{8,9},{9,10},{10,1... | collective-permute-start | bytes 811016 | tf_op jit(solution)/shard_map/ppermute | solution.py:275
  23.0 0.1 pad_add_fusion.place
  23.0 4.0 %collective-permute-done.3.t2 = bf16[528,256]{1,0:T(8,128)(2,1)S(1)} collective-permute-done((bf16[528,256]{1,0:T(8,128)(2,1)S(1)}, bf16[528,256]{1,0:T(8,128)(2,1)S(1)}, u32[]{:S(2)}, u32[]{:S(2)}) %collective-permute-start.3) | collective-permute-done | bytes 270368 | tf_op jit(solution)/shard_map/ppermute | solution.py:275
  27.0 2.9 %collective-permute-start = (bf16[8,128,512]{2,1,0:T(8,128)(2,1)}, bf16[8,128,512]{2,1,0:T(8,128)(2,1)S(1)}, u32[]{:S(2)}, u32[]{:S(2)}) collective-permute-start(bf16[8,128,512]{2,1,0:T(8,128)(2,1)} %copy-done.7), channel_id=1, source_target_pairs={{0,1},{1,2},{2,3},{3,4},{4,5},{5,6},{6,7},{7,8},{8,9},{9,10},{10,1... | collective-permute-start | bytes 3145736 | tf_op jit(solution)/shard_map/ppermute | solution.py:292
  30.0 0.0 collective-permute-done.2.t1
  30.0 1.3 %collective-permute-start.1 = (bf16[8,128,512]{2,1,0:T(8,128)(2,1)}, bf16[8,128,512]{2,1,0:T(8,128)(2,1)S(1)}, u32[]{:S(2)}, u32[]{:S(2)}) collective-permute-start(bf16[8,128,512]{2,1,0:T(8,128)(2,1)} %copy-done.7), channel_id=1, source_target_pairs={{1,0},{2,1},{3,2},{4,3},{5,4},{6,5},{7,6},{8,7},{9,8},{10,9},{11,1... | collective-permute-start | bytes 3145736 | tf_op jit(solution)/shard_map/ppermute | solution.py:293
  31.3 0.0 collective-permute-done.5.s1
  31.3 7.6 %collective-permute-done.6.s2 = bf16[1088,256]{1,0:T(8,128)(2,1)S(1)} collective-permute-done((bf16[1088,256]{1,0:T(8,128)(2,1)S(1)}, bf16[1088,256]{1,0:T(8,128)(2,1)S(1)}, u32[]{:S(2)}, u32[]{:S(2)}) %collective-permute-start.6) | collective-permute-done | bytes 557088 | tf_op jit(solution)/shard_map/ppermute | solution.py:275
  38.9 3.4 %collective-permute-done.7.s3 = bf16[1088,256]{1,0:T(8,128)(2,1)S(1)} collective-permute-done((bf16[1088,256]{1,0:T(8,128)(2,1)S(1)}, bf16[1088,256]{1,0:T(8,128)(2,1)S(1)}, u32[]{:S(2)}, u32[]{:S(2)}) %collective-permute-start.7) | collective-permute-done | bytes 557088 | tf_op jit(solution)/shard_map/ppermute | solution.py:275
  42.3 0.0 copy-done.10
  42.3 13.6 %all-gather = bf16[1024,256]{1,0:T(8,128)(2,1)S(1)} all-gather(bf16[128,256]{1,0:T(8,128)(2,1)S(1)} %pad_maximum_fusion), channel_id=2, replica_groups=mesh['leaf'=8,'top'=16] {'leaf'}, dimensions={0}, use_global_device_ids=true | all-gather | bytes 589824 | tf_op jit(solution)/shard_map/all_gather | solution.py:295
  55.9 0.0 copy-start.8
  55.9 0.0 copy-start.9
  55.9 21.2 %far.3 = (f32[512,256]{1,0:T(8,128)S(1)}, bf16[576,256]{1,0:T(8,128)(2,1)S(1)}, bf16[576,256]{1,0:T(8,128)(2,1)S(1)}, bf16[576,256]{1,0:T(8,128)(2,1)S(1)}, f32[64,256]{1,0:T(8,128)S(1)}) custom-call(s32[32,16]{1,0:T(8,128)S(1)} %maximum_convert_fusion.ids, s32[3]{0:T(128)S(1)} %pad_add_fusion.place, bf16[1088,256]{1,0:T(8,128)(2,1)S(1)} %get-tuple-element.15.s0, ...), custom_call_target="tpu_custom_call" | custom-call | flops 15000000512 | bytes 8000000 | tf_op jit(solution)/shard_map/far/pallas_call | solution.py:170
  77.1 2.3 %collective-permute-start.8 = (bf16[576,256]{1,0:T(8,128)(2,1)S(1)}, bf16[576,256]{1,0:T(8,128)(2,1)S(1)}, u32[]{:S(2)}, u32[]{:S(2)}) collective-permute-start(bf16[576,256]{1,0:T(8,128)(2,1)S(1)} %get-tuple-element.17), channel_id=1, source_target_pairs={{0,3},{1,0},{2,1},{3,2},{4,7},{5,4},{6,5},{7,6},{8,11},{9,8},{10,9... | collective-permute-start | bytes 884744 | tf_op jit(solution)/shard_map/ppermute | solution.py:275
  79.4 0.0 collective-permute-start.9
  79.4 1.5 %collective-permute-start.10 = (bf16[576,256]{1,0:T(8,128)(2,1)S(1)}, bf16[576,256]{1,0:T(8,128)(2,1)S(1)}, u32[]{:S(2)}, u32[]{:S(2)}) collective-permute-start(bf16[576,256]{1,0:T(8,128)(2,1)S(1)} %get-tuple-element.19), channel_id=1, source_target_pairs={{0,2},{1,3},{2,0},{3,1},{4,6},{5,7},{6,4},{7,5},{8,10},{9,11},{10,... | collective-permute-start | bytes 884744 | tf_op jit(solution)/shard_map/ppermute | solution.py:275
  81.0 0.0 collective-permute-done.before
  81.0 0.0 collective-permute-done.1.after
  81.0 0.0 copy-done.8
  81.0 0.0 copy-done.9
  81.0 0.0 copy-start.1
  81.0 0.0 copy-start.3
  81.0 18.8 %near.1.near_sum = f32[8,64,512]{2,1,0:T(8,128)S(1)} custom-call(s32[8,8]{1,0:T(8,128)S(1)} %copy-done.9, s32[1]{0:T(128)} %bitcast.first, bf16[8,128,512]{2,1,0:T(8,128)(2,1)S(1)} %copy-done.8, bf16[8,128,512]{2,1,0:T(8,128)(2,1)S(1)} %collective-permute-done.before, bf16[8,128,512]{2,1,0:T(8,128)(2,1)S(1)} %collective-permute-done.1.after), custom_call_target="tpu_custom_call" | custom-call | flops 30000001024 | bytes 4000000 | tf_op jit(solution)/shard_map/near/pallas_call | solution.py:218
  99.9 0.0 collective-permute-done.8.r1.q1
  99.9 0.0 collective-permute-done.9.r2.q2
  99.9 0.0 collective-permute-done.10.r3.q3
  99.9 0.0 copy-done.1
  99.9 0.0 copy-done.3
  99.9 4.5 %final.1 = bf16[8,64,512]{2,1,0:T(8,128)(2,1)} custom-call(f32[8,64,512]{2,1,0:T(8,128)S(1)} %near.1.near_sum, bf16[8,512,256]{2,1,0:T(8,128)(2,1)S(1)} %copy-done.1, bf16[8,256,256]{2,1,0:T(8,128)(2,1)S(1)} %copy-done.3, f32[512,256]{1,0:T(8,128)S(1)} %get-tuple-element.16.own, bf16[576,256]{1,0:T(8,128)(2,1)S(1)} %collective-permute-done.8.r1.q1, ...), custom_call_target="tpu_custom_call" | custom-call | flops 1000000000 | bytes 6000000 | tf_op jit(solution)/shard_map/final/pallas_call | solution.py:252
  (7 shorter events, 0.0 us)
Async XLA Ops:
  0.7 1.6 %copy-start = (bf16[8,512,256]{2,1,0:T(8,128)(2,1)S(1)}, bf16[8,512,256]{2,1,0:T(8,128)(2,1)}, u32[]{:S(2)}) copy-start(bf16[8,512,256]{2,1,0:T(8,128)(2,1)} %basis.3) | copy-start | bytes 6291460
  2.3 1.2 %copy-start.2 = (bf16[8,256,256]{2,1,0:T(8,128)(2,1)S(1)}, bf16[8,256,256]{2,1,0:T(8,128)(2,1)}, u32[]{:S(2)}) copy-start(bf16[8,256,256]{2,1,0:T(8,128)(2,1)} %transfer.3) | copy-start | bytes 3145732
  3.5 1.0 copy-start.4
  4.6 1.0 copy-start.5
  5.6 0.7 copy-start.6
  6.3 36.0 %copy-start.10 = (bf16[1,64,256]{2,1,0:T(8,128)(2,1)S(1)}, bf16[1,64,256]{2,1,0:T(8,128)(2,1)}, u32[]{:S(2)}) copy-start(bf16[1,64,256]{2,1,0:T(8,128)(2,1)} %param.12) | copy-start | bytes 98308
  9.1 1.0 copy-start.7
  10.1 10.4 %collective-permute-start.4 = (bf16[528,256]{1,0:T(8,128)(2,1)S(1)}, bf16[528,256]{1,0:T(8,128)(2,1)S(1)}, u32[]{:S(2)}, u32[]{:S(2)}) collective-permute-start(bf16[528,256]{1,0:T(8,128)(2,1)S(1)} %get-tuple-element.14.t0), channel_id=1, source_target_pairs={{0,2},{1,3},{2,0},{3,1},{4,6},{5,7},{6,4},{7,5},{8,10},{9,11},{10,... | collective-permute-start | bytes 811016 | tf_op jit(solution)/shard_map/ppermute | solution.py:275
  14.0 17.3 %collective-permute-start.5 = (bf16[1088,256]{1,0:T(8,128)(2,1)S(1)}, bf16[1088,256]{1,0:T(8,128)(2,1)S(1)}, u32[]{:S(2)}, u32[]{:S(2)}) collective-permute-start(bf16[1088,256]{1,0:T(8,128)(2,1)S(1)} %get-tuple-element.15.s0), channel_id=1, source_target_pairs={{0,4},{1,5},{2,6},{3,7},{4,8},{5,9},{6,10},{7,11},{8,12},{9,13},{1... | collective-permute-start | bytes 1671176 | tf_op jit(solution)/shard_map/ppermute | solution.py:275
  15.5 23.3 %collective-permute-start.6 = (bf16[1088,256]{1,0:T(8,128)(2,1)S(1)}, bf16[1088,256]{1,0:T(8,128)(2,1)S(1)}, u32[]{:S(2)}, u32[]{:S(2)}) collective-permute-start(bf16[1088,256]{1,0:T(8,128)(2,1)S(1)} %get-tuple-element.15.s0), channel_id=1, source_target_pairs={{0,12},{1,13},{2,14},{3,15},{4,0},{5,1},{6,2},{7,3},{8,4},{9,5},{1... | collective-permute-start | bytes 1671176 | tf_op jit(solution)/shard_map/ppermute | solution.py:275
  17.3 25.0 %collective-permute-start.7 = (bf16[1088,256]{1,0:T(8,128)(2,1)S(1)}, bf16[1088,256]{1,0:T(8,128)(2,1)S(1)}, u32[]{:S(2)}, u32[]{:S(2)}) collective-permute-start(bf16[1088,256]{1,0:T(8,128)(2,1)S(1)} %get-tuple-element.15.s0), channel_id=1, source_target_pairs={{0,8},{1,9},{2,10},{3,11},{4,12},{5,13},{6,14},{7,15},{8,0},{9,1},... | collective-permute-start | bytes 1671176 | tf_op jit(solution)/shard_map/ppermute | solution.py:275
  19.1 8.0 %collective-permute-start.3 = (bf16[528,256]{1,0:T(8,128)(2,1)S(1)}, bf16[528,256]{1,0:T(8,128)(2,1)S(1)}, u32[]{:S(2)}, u32[]{:S(2)}) collective-permute-start(bf16[528,256]{1,0:T(8,128)(2,1)S(1)} %get-tuple-element.14.t0), channel_id=1, source_target_pairs={{0,3},{1,0},{2,1},{3,2},{4,7},{5,4},{6,5},{7,6},{8,11},{9,8},{10,9... | collective-permute-start | bytes 811016 | tf_op jit(solution)/shard_map/ppermute | solution.py:275
  20.5 9.4 %collective-permute-start.2 = (bf16[528,256]{1,0:T(8,128)(2,1)S(1)}, bf16[528,256]{1,0:T(8,128)(2,1)S(1)}, u32[]{:S(2)}, u32[]{:S(2)}) collective-permute-start(bf16[528,256]{1,0:T(8,128)(2,1)S(1)} %get-tuple-element.14.t0), channel_id=1, source_target_pairs={{0,1},{1,2},{2,3},{3,0},{4,5},{5,6},{6,7},{7,4},{8,9},{9,10},{10,1... | collective-permute-start | bytes 811016 | tf_op jit(solution)/shard_map/ppermute | solution.py:275
  27.0 53.9 %collective-permute-start = (bf16[8,128,512]{2,1,0:T(8,128)(2,1)}, bf16[8,128,512]{2,1,0:T(8,128)(2,1)S(1)}, u32[]{:S(2)}, u32[]{:S(2)}) collective-permute-start(bf16[8,128,512]{2,1,0:T(8,128)(2,1)} %copy-done.7), channel_id=1, source_target_pairs={{0,1},{1,2},{2,3},{3,4},{4,5},{5,6},{6,7},{7,8},{8,9},{9,10},{10,1... | collective-permute-start | bytes 3145736 | tf_op jit(solution)/shard_map/ppermute | solution.py:292
  30.0 51.0 %collective-permute-start.1 = (bf16[8,128,512]{2,1,0:T(8,128)(2,1)}, bf16[8,128,512]{2,1,0:T(8,128)(2,1)S(1)}, u32[]{:S(2)}, u32[]{:S(2)}) collective-permute-start(bf16[8,128,512]{2,1,0:T(8,128)(2,1)} %copy-done.7), channel_id=1, source_target_pairs={{1,0},{2,1},{3,2},{4,3},{5,4},{6,5},{7,6},{8,7},{9,8},{10,9},{11,1... | collective-permute-start | bytes 3145736 | tf_op jit(solution)/shard_map/ppermute | solution.py:293
  55.9 25.1 %copy-start.8 = (bf16[8,128,512]{2,1,0:T(8,128)(2,1)S(1)}, bf16[8,128,512]{2,1,0:T(8,128)(2,1)}, u32[]{:S(2)}) copy-start(bf16[8,128,512]{2,1,0:T(8,128)(2,1)} %copy-done.7) | copy-start | bytes 3145732
  55.9 25.1 %copy-start.9 = (s32[8,8]{1,0:T(8,128)S(1)}, s32[8,8]{1,0:T(8,128)}, u32[]{:S(2)}) copy-start(s32[8,8]{1,0:T(8,128)} %ids.1) | copy-start | bytes 772
  77.1 22.7 %collective-permute-start.8 = (bf16[576,256]{1,0:T(8,128)(2,1)S(1)}, bf16[576,256]{1,0:T(8,128)(2,1)S(1)}, u32[]{:S(2)}, u32[]{:S(2)}) collective-permute-start(bf16[576,256]{1,0:T(8,128)(2,1)S(1)} %get-tuple-element.17), channel_id=1, source_target_pairs={{0,3},{1,0},{2,1},{3,2},{4,7},{5,4},{6,5},{7,6},{8,11},{9,8},{10,9... | collective-permute-start | bytes 884744 | tf_op jit(solution)/shard_map/ppermute | solution.py:275
  79.4 20.4 %collective-permute-start.9 = (bf16[576,256]{1,0:T(8,128)(2,1)S(1)}, bf16[576,256]{1,0:T(8,128)(2,1)S(1)}, u32[]{:S(2)}, u32[]{:S(2)}) collective-permute-start(bf16[576,256]{1,0:T(8,128)(2,1)S(1)} %get-tuple-element.18), channel_id=1, source_target_pairs={{0,1},{1,2},{2,3},{3,0},{4,5},{5,6},{6,7},{7,4},{8,9},{9,10},{10,1... | collective-permute-start | bytes 884744 | tf_op jit(solution)/shard_map/ppermute | solution.py:275
  79.4 20.4 %collective-permute-start.10 = (bf16[576,256]{1,0:T(8,128)(2,1)S(1)}, bf16[576,256]{1,0:T(8,128)(2,1)S(1)}, u32[]{:S(2)}, u32[]{:S(2)}) collective-permute-start(bf16[576,256]{1,0:T(8,128)(2,1)S(1)} %get-tuple-element.19), channel_id=1, source_target_pairs={{0,2},{1,3},{2,0},{3,1},{4,6},{5,7},{6,4},{7,5},{8,10},{9,11},{10,... | collective-permute-start | bytes 884744 | tf_op jit(solution)/shard_map/ppermute | solution.py:275
  81.0 18.9 %copy-start.1 = (bf16[8,512,256]{2,1,0:T(8,128)(2,1)S(1)}, bf16[8,512,256]{2,1,0:T(8,128)(2,1)}, u32[]{:S(2)}) copy-start(bf16[8,512,256]{2,1,0:T(8,128)(2,1)} %basis.3) | copy-start | bytes 6291460
  81.0 18.9 %copy-start.3 = (bf16[8,256,256]{2,1,0:T(8,128)(2,1)S(1)}, bf16[8,256,256]{2,1,0:T(8,128)(2,1)}, u32[]{:S(2)}) copy-start(bf16[8,256,256]{2,1,0:T(8,128)(2,1)} %transfer.3) | copy-start | bytes 3145732

commit v2 on v1

v2 whole, which is shorter than its diff:
```python
import functools

import jax
import jax.numpy as jnp
from jax import lax
from jax.experimental import pallas as pl
from jax.experimental.pallas import tpu as pltpu
from jax.sharding import PartitionSpec as P

BF = jnp.bfloat16
F32 = jnp.float32
F = 64
RHS = 64
LP = 512
SK = 256
LD = 8
SIDE = 4
AUG = 128
VM = pl.BlockSpec(memory_space=pltpu.VMEM)
SM = pl.BlockSpec(memory_space=pltpu.SMEM)


def params(mib=40):
    return pltpu.CompilerParams(vmem_limit_bytes=mib * 2**20)


def cost(us):
    return pl.CostEstimate(flops=us * 10**9, bytes_accessed=10**6, transcendentals=0)


def norm_rows(points, first):
    norm = jnp.sum(points * points, axis=0, keepdims=True) * (-2.0 / F)
    high = norm.astype(BF).astype(F32)
    mid = (norm - high).astype(BF).astype(F32)
    low = norm - high - mid
    row = lax.broadcasted_iota(jnp.int32, (16, points.shape[1]), 0)
    at = 0 if first else 3
    ones = jnp.where(row < 6, 1.0, 0.0).astype(F32)
    rows = jnp.where(row == at + 1, mid, jnp.where(row == at + 2, low, ones))
    return jnp.where(row == at, high, rows)


def source_side(points):
    points = points.astype(F32)
    zeros = jnp.zeros((AUG - F - 16, points.shape[1]), F32)
    full = jnp.concatenate([points, norm_rows(points, True), zeros], axis=0)
    return full.astype(BF).T


def target_side(points):
    points = points.astype(F32)
    zeros = jnp.zeros((AUG - F - 16, points.shape[1]), F32)
    full = jnp.concatenate([points * (4.0 / F), norm_rows(points, False), zeros], axis=0)
    return full.astype(BF)


def prep_kernel(
    points, sides, basis, transfer, skeleton, far, near_msg, source_msg, target_msg, node, ids
):
    leaf = pl.program_id(0)
    near_msg[0, :F, :] = points[0]
    near_msg[0, F:, :] = sides[0]
    charge = jnp.dot(sides[0], basis[0], preferred_element_type=F32).astype(BF)
    position = lax.broadcasted_iota(jnp.int32, (LP, SK), 0)
    chosen = jnp.where(position == skeleton[pl.ds(leaf, 1), :], 1.0, 0.0).astype(BF)
    skel = jnp.dot(points[0], chosen, preferred_element_type=F32).astype(BF)
    source_msg[pl.ds(pl.multiple_of(leaf * 2 * F, 2 * F), F), :] = charge
    source_msg[pl.ds(pl.multiple_of(leaf * 2 * F + F, F), F), :] = skel
    target_msg[pl.ds(pl.multiple_of(leaf * F, F), F), :] = skel
    part = jnp.dot(charge, transfer[0], preferred_element_type=F32)

    @pl.when(leaf == 0)
    def _():
        node[...] = part
        ids[...] = jnp.zeros_like(ids)
        named = far[...]
        ids[:LD, : SIDE * SIDE] = jnp.where(named >= 0, named & (LD - 1), -1).astype(F32)
        target_msg[LD * F :, :] = ids[...].astype(BF)

    @pl.when(leaf > 0)
    def _():
        node[...] += part

    @pl.when(leaf == LD - 1)
    def _():
        source_msg[LD * 2 * F :, :] = node[...].astype(BF)


def prep(points, sides, basis, transfer, skeleton, far):
    def block(*shape):
        return pl.BlockSpec((1, *shape), lambda i: (i, 0, 0))

    def whole(*shape):
        return pl.BlockSpec(shape, lambda i: (0,) * len(shape))

    source_rows, target_rows = LD * 2 * F + RHS, LD * F + 16
    return pl.pallas_call(
        prep_kernel,
        grid=(LD,),
        in_specs=[
            block(F, LP),
            block(RHS, LP),
            block(LP, SK),
            block(SK, SK),
            whole(LD, SK),
            whole(LD, SIDE * SIDE),
        ],
        out_specs=[block(2 * F, LP), whole(source_rows, SK), whole(target_rows, SK)],
        out_shape=[
            jax.ShapeDtypeStruct((LD, 2 * F, LP), BF),
            jax.ShapeDtypeStruct((source_rows, SK), BF),
            jax.ShapeDtypeStruct((target_rows, SK), BF),
        ],
        scratch_shapes=[pltpu.VMEM((RHS, SK), F32), pltpu.VMEM((16, SK), F32)],
        compiler_params=params(56),
        cost_estimate=cost(4),
        name="prep",
    )(points, sides, basis, transfer, skeleton, far)


def far_targets(ids, place, side, sources, target, out, b):
    x, z = place[0], place[1]
    shifts = (0, SIDE - 1, 1, 2)

    @pl.loop(0, LD, unroll=2)
    def _(leaf):
        rows = pl.ds(pl.multiple_of(leaf * F, F), F)
        points = target_side(target[rows, :])
        weights, tiles = [], []
        for d, source in enumerate(sources):
            column = lax.rem(x + shifts[d], SIDE) * SIDE + z
            named = ids[b * LD + leaf, column]
            at = jnp.maximum(named, 0)
            tiles.append(
                jnp.exp(
                    jnp.dot(side[d * LD + at], points, preferred_element_type=F32)
                ).astype(BF)
            )
            weight = source[pl.ds(pl.multiple_of(at * 2 * F, 2 * F), RHS), :]
            weights.append(jnp.where(named >= 0, weight, jnp.zeros_like(weight)))
        total = jnp.dot(
            jnp.concatenate(weights, axis=1),
            jnp.concatenate(tiles, axis=0),
            preferred_element_type=F32,
        )
        out[rows, :] = total.astype(out.dtype)


def far_own_kernel(ids, place, s0, s1, s2, s3, t0, out, side):
    sources = (s0, s1, s2, s3)
    for d, source in enumerate(sources):

        @pl.loop(0, LD)
        def _(leaf, d=d, source=source):
            rows = pl.ds(pl.multiple_of(leaf * 2 * F + F, F), F)
            side[d * LD + leaf] = source_side(source[rows, :])

    far_targets(ids, place, side, sources, t0, out, 0)


def far_own(ids, place, sources, target):
    return pl.pallas_call(
        far_own_kernel,
        in_specs=[SM, SM] + [VM] * 5,
        out_specs=[VM] * 2,
        out_shape=[
            jax.ShapeDtypeStruct((LD * F, SK), F32),
            jax.ShapeDtypeStruct((SIDE * LD, SK, AUG), BF),
        ],
        compiler_params=params(16),
        cost_estimate=cost(6),
        name="far_own",
    )(ids, place, *sources, target)


def far_rest_kernel(ids, place, side, s0, s1, s2, s3, gathered, r1, r2, r3):
    z = place[1]
    for b, out in enumerate((r1, r2, r3)):
        other = lax.rem(z + (SIDE - 1, 1, 2)[b], SIDE)
        far_targets(
            ids, place, side, (s0, s1, s2, s3), gathered.at[other], out, b + 1
        )


def far_rest(ids, place, side, sources, gathered):
    return pl.pallas_call(
        far_rest_kernel,
        in_specs=[SM, SM] + [VM] * 6,
        out_specs=[VM] * 3,
        out_shape=[jax.ShapeDtypeStruct((LD * F, SK), BF)] * 3,
        compiler_params=params(16),
        cost_estimate=cost(10),
        name="far_rest",
    )(ids, place, side, *sources, gathered)


def top_kernel(mine, pair, n1, n2, n3, a1, a2, a3, top, r1, r2, r3):
    points = target_side(mine[RHS:, :])
    total = jnp.zeros((RHS, SK), F32)
    rows = 2 * RHS
    others = [pair] + [n.at[i * rows : (i + 1) * rows] for n in (n1, n2, n3) for i in range(2)]
    for other in others:
        kernel = jnp.exp(
            jnp.dot(source_side(other[RHS:, :]), points, preferred_element_type=F32)
        ).astype(BF)
        total += jnp.dot(other[:RHS, :], kernel, preferred_element_type=F32)
    top[...] = total
    for given, out in ((a1, r1), (a2, r2), (a3, r3)):
        out[: LD * F, :] = given[...]
        out[LD * F :, :] = total.astype(BF)


def top_sum(mine, pair, others, parts):
    return pl.pallas_call(
        top_kernel,
        in_specs=[VM] * 8,
        out_specs=[VM] * 4,
        out_shape=[jax.ShapeDtypeStruct((RHS, SK), F32)]
        + [jax.ShapeDtypeStruct((LD * F + RHS, SK), BF)] * 3,
        compiler_params=params(16),
        cost_estimate=cost(2),
        name="top_sum",
    )(mine, pair, *others, *parts)


def near_groups(ids, first, leaf, low, high, points, side, rights, slots):
    count = jnp.int32(0)
    for d in range(ids.shape[1]):
        slots[d] = 0
    for d in range(ids.shape[1]):
        named = ids[leaf, d]
        at = named - first
        here = (named >= 0) & (at >= low) & (at < high)
        slots[count] = jnp.clip(at - low, 0, high - low - 1)
        count += here.astype(jnp.int32)
    size = 4

    def group(g, total):
        weights, tiles = [], []
        for d in range(size):
            k = g * size + d
            at = slots[k]
            tiles.append(
                jnp.exp(jnp.dot(side[at], points, preferred_element_type=F32)).astype(BF)
            )
            weight = rights(at)
            weights.append(jnp.where(k < count, weight, jnp.zeros_like(weight)))
        return total + jnp.dot(
            jnp.concatenate(weights, axis=1),
            jnp.concatenate(tiles, axis=0),
            preferred_element_type=F32,
        )

    return lax.fori_loop(
        0, lax.div(count + size - 1, size), group, jnp.zeros((RHS, LP), F32)
    )


def near_own_kernel(ids, first, own, out, side, slots):
    @pl.loop(0, LD)
    def _(leaf):
        side[leaf] = source_side(own[leaf, :F, :])

    @pl.loop(0, LD)
    def _(leaf):
        points = target_side(own[leaf, :F, :])
        out[leaf] = near_groups(
            ids, first[0], leaf, LD, 2 * LD, points, side, lambda at: own[at, F:, :], slots
        )


def near_own(ids, first, own):
    return pl.pallas_call(
        near_own_kernel,
        in_specs=[SM, SM, VM],
        out_specs=VM,
        out_shape=jax.ShapeDtypeStruct((LD, RHS, LP), F32),
        scratch_shapes=[pltpu.VMEM((LD, LP, AUG), BF), pltpu.SMEM((16,), jnp.int32)],
        compiler_params=params(16),
        cost_estimate=cost(9),
        name="near_own",
    )(ids, first, own)


def near_rest_kernel(ids, first, own, before, after, given, out, side, rights, slots):
    for d, block in enumerate((before, after)):

        @pl.loop(0, LD)
        def _(leaf, d=d, block=block):
            side[d * LD + leaf] = source_side(block[leaf, :F, :])
            rights[d * LD + leaf] = block[leaf, F:, :]

    @pl.loop(0, LD)
    def _(leaf):
        points = target_side(own[leaf, :F, :])
        total = given[leaf]
        for low in (0, 2 * LD):
            base = 0 if low == 0 else LD
            total += near_groups(
                ids, first[0], leaf, low, low + LD, points, side.at[base : base + LD],
                lambda at, base=base: rights[base + at], slots,
            )
        out[leaf] = total


def near_rest(ids, first, own, before, after, given):
    return pl.pallas_call(
        near_rest_kernel,
        in_specs=[SM, SM, VM, VM, VM, VM],
        out_specs=VM,
        out_shape=jax.ShapeDtypeStruct((LD, RHS, LP), F32),
        scratch_shapes=[
            pltpu.VMEM((2 * LD, LP, AUG), BF),
            pltpu.VMEM((2 * LD, RHS, LP), BF),
            pltpu.SMEM((16,), jnp.int32),
        ],
        compiler_params=params(24),
        cost_estimate=cost(11),
        name="near_rest",
    )(ids, first, own, before, after, given)


def final_kernel(near_sum, basis, transfer, own, r1, r2, r3, top, out):
    nt = (((1,), (1,)), ((), ()))
    last = LD * F
    total = top[...]
    for r in (r1, r2, r3):
        total += r[last:, :].astype(F32)
    total = total.astype(BF)

    @pl.loop(0, LD, unroll=2)
    def _(leaf):
        rows = pl.ds(pl.multiple_of(leaf * F, F), F)
        potential = own[rows, :]
        for r in (r1, r2, r3):
            potential += r[rows, :].astype(F32)
        potential += lax.dot_general(total, transfer[leaf], nt, preferred_element_type=F32)
        far_out = lax.dot_general(
            potential.astype(BF), basis[leaf], nt, preferred_element_type=F32
        )
        out[leaf] = (near_sum[leaf] + far_out).astype(BF)


def final(near_sum, basis, transfer, own, returned, top):
    return pl.pallas_call(
        final_kernel,
        in_specs=[VM] * 8,
        out_specs=VM,
        out_shape=jax.ShapeDtypeStruct((LD, RHS, LP), BF),
        compiler_params=params(16),
        cost_estimate=cost(3),
        name="final",
    )(near_sum, basis, transfer, own, *returned, top)


def shifted(value, dx, dz):
    pairs = []
    for x in range(SIDE):
        for z in range(SIDE):
            to = (x + dx) % SIDE * SIDE + (z + dz) % SIDE
            pairs.append((x * SIDE + z, to))
    return lax.ppermute(value, "top", pairs)


def leaf_shifted(value, dy):
    count = lax.axis_size("leaf")
    if dy == 0:
        return lax.ppermute(value, "leaf", [(i, i ^ 1) for i in range(count)])
    return lax.ppermute(value, "leaf", [(i, (i + 2 * dy) % count) for i in range(count)])


def on_device(
    points, right_sides, leaf_basis, transfer, node_points, neighbours, far_sources, skeleton
):
    node, at = lax.axis_index("leaf"), lax.axis_index("top")
    position = node * SIDE * SIDE + at
    near_msg, source_msg, target_msg = prep(
        points, right_sides, leaf_basis, transfer, skeleton, far_sources
    )
    sources = [source_msg]
    sources += [shifted(source_msg, dx, 0) for dx in (1, -1, 2)]
    lines = [[x * SIDE + z for z in range(SIDE)] for x in range(SIDE)]
    gathered = lax.all_gather(target_msg, "top", axis=0, axis_index_groups=lines)
    count = lax.axis_size("leaf") * lax.axis_size("top")
    up = [(i, i + 1) for i in range(count - 1)]
    before = lax.ppermute(near_msg, ("leaf", "top"), up)
    after = lax.ppermute(near_msg, ("leaf", "top"), [(j, i) for i, j in up])
    first = ((position - 1) * LD).astype(jnp.int32).reshape(1)
    near_sum = near_own(neighbours, first, near_msg)

    sources[1:], near_sum = lax.optimization_barrier((sources[1:], near_sum))
    row_charge = sum(s[LD * 2 * F :].astype(F32) for s in sources).astype(BF)
    mine = jnp.concatenate([row_charge, node_points[0]], axis=0)
    pair = leaf_shifted(mine, 0)
    place = jnp.stack([at // SIDE, at % SIDE]).astype(jnp.int32)
    own_ids = jnp.where(far_sources >= 0, far_sources & (LD - 1), -1)
    own, side = far_own(own_ids, place, sources, target_msg)
    both = jnp.concatenate([mine, pair], axis=0)
    others = [leaf_shifted(both, dy) for dy in (1, -1, 2)]
    ids = gathered[:, LD * F : LD * F + LD, : SIDE * SIDE].astype(jnp.int32)
    z = at % SIDE
    order = [z] + [lax.rem(z + d, SIDE) for d in (SIDE - 1, 1, 2)]
    ids = jnp.concatenate([lax.dynamic_index_in_dim(ids, o, keepdims=False) for o in order])
    parts = far_rest(ids, place, side, sources, gathered)
    top, *parts = top_sum(mine, pair, others, parts)
    returned = [shifted(r, 0, dz) for r, dz in zip(parts, (-1, 1, 2))]
    near_sum = near_rest(neighbours, first, near_msg, before, after, near_sum)
    return final(near_sum, leaf_basis, transfer, own, returned, top)


def solution(mesh):
    leaves = P(("leaf", "top"), None, None)
    lists = P(("leaf", "top"), None)
    in_specs = (leaves, leaves, leaves, leaves, P("leaf", None, None), lists, lists, lists)
    return jax.shard_map(
        on_device, mesh=mesh, in_specs=in_specs, out_specs=leaves, check_vma=False
    )
```

time: 106 us -> 134 us (1.26)
  the two profiles are of different devices: /device:TPU:0 before, /device:TPU:33 now
where the time goes in v2:
time: 134 us; the launch traced here: 132 us
  Pallas kernels  58.6 us (44%)
  starting transfers between devices  40.9 us (31%)
  between operations  13.7 us (10%)
  waiting for transfers between devices  9.79 us (7%)
  local copies, waits for them, and re-layouts  7.22 us (5%)
  other arithmetic  1.49 us (1%)
    ppermute x6, starting transfers between devices, shifted(): return lax.ppermute(value, 'top', pairs)  29 us
    pallas_call x1, Pallas kernels, near_rest(): pl.pallas_call(near_rest_kernel, in_specs=[SM, SM, VM, VM, VM, VM], out_s...  19.1 us
    pallas_call x1, Pallas kernels, near_own(): pl.pallas_call(near_own_kernel, in_specs=[SM, SM, VM], out_specs=VM, out_...  11 us
    pallas_call x1, Pallas kernels, far_rest(): pl.pallas_call(far_rest_kernel, in_specs=[SM, SM] + [VM] * 6, out_specs=[...  9.86 us
    ppermute x6, waiting for transfers between devices, shifted(): return lax.ppermute(value, 'top', pairs)  9.76 us
    pallas_call x1, Pallas kernels, prep(): pl.pallas_call(prep_kernel, grid=(LD,), in_specs=[block(F, LP), block(RHS...  7.3 us
    unnamed x32, local copies, waits for them, and re-layouts  7.21 us
    pallas_call x1, Pallas kernels, far_own(): pl.pallas_call(far_own_kernel, in_specs=[SM, SM] + [VM] * 5, out_specs=[V...  6.46 us
  transfers between devices with their start and end apart: 13, of which 1 were waited for; matrix products, arithmetic and copies ran while one was open for 1% of the time, Pallas kernels for 37%

profile of v2, /device:TPU:33, one launch (start us, length us, event | category | flops | bytes accessed | tf_op | source)
XLA Modules:
  0.0 131.7 jit_solution(10418108500598517278)
XLA Ops:
  6.5 0.0 copy-start.15
  6.5 0.0 copy-start.7
  6.5 0.0 all-gather.3.cloned.1.call-start
  6.5 7.3 %prep.1 = (bf16[8,128,512]{2,1,0:T(8,128)(2,1)}, bf16[1088,256]{1,0:T(8,128)(2,1)}, bf16[528,256]{1,0:T(8,128)(2,1)}) custom-call(bf16[8,64,512]{2,1,0:T(8,128)(2,1)} %points.1, bf16[8,64,512]{2,1,0:T(8,128)(2,1)} %sides.1, bf16[8,512,256]{2,1,0:T(8,128)(2,1)} %basis.3, bf16[8,256,256]{2,1,0:T(8,128)(2,1)} %transfer.3, s32[8,256]{1,0:T(8,128)} %skeleton.1, ...), custom_call_target="tpu_custom_call" | custom-call | flops 4000000000 | bytes 1000000 | tf_op jit(solution)/shard_map/prep/pallas_call | solution.py:97
  13.8 3.5 %collective-permute-start = (bf16[8,128,512]{2,1,0:T(8,128)(2,1)}, bf16[8,128,512]{2,1,0:T(8,128)(2,1)S(1)}, u32[]{:S(2)}, u32[]{:S(2)}) collective-permute-start(bf16[8,128,512]{2,1,0:T(8,128)(2,1)} %get-tuple-element.21.own), channel_id=1, source_target_pairs={{0,1},{1,2},{2,3},{3,4},{4,5},{5,6},{6,7},{7,8},{8,9},{9,10},{10,1... | collective-permute-start | bytes 3145736 | tf_op jit(solution)/shard_map/ppermute | solution.py:386
  17.4 1.9 %collective-permute-start.1 = (bf16[8,128,512]{2,1,0:T(8,128)(2,1)}, bf16[8,128,512]{2,1,0:T(8,128)(2,1)}, u32[]{:S(2)}, u32[]{:S(2)}) collective-permute-start(bf16[8,128,512]{2,1,0:T(8,128)(2,1)} %get-tuple-element.21.own), channel_id=1, source_target_pairs={{1,0},{2,1},{3,2},{4,3},{5,4},{6,5},{7,6},{8,7},{9,8},{10,9},{11,1... | collective-permute-start | bytes 3145736 | tf_op jit(solution)/shard_map/ppermute | solution.py:387
  19.3 1.3 collective-permute-start.2
  20.6 1.5 %collective-permute-start.3 = (bf16[1088,256]{1,0:T(8,128)(2,1)}, bf16[1088,256]{1,0:T(8,128)(2,1)S(1)}, u32[]{:S(2)}, u32[]{:S(2)}) collective-permute-start(bf16[1088,256]{1,0:T(8,128)(2,1)} %get-tuple-element.22.s0), channel_id=1, source_target_pairs={{0,12},{1,13},{2,14},{3,15},{4,0},{5,1},{6,2},{7,3},{8,4},{9,5},{1... | collective-permute-start | bytes 1671176 | tf_op jit(solution)/shard_map/ppermute | solution.py:362
  22.1 1.5 %collective-permute-start.4 = (bf16[1088,256]{1,0:T(8,128)(2,1)}, bf16[1088,256]{1,0:T(8,128)(2,1)S(1)}, u32[]{:S(2)}, u32[]{:S(2)}) collective-permute-start(bf16[1088,256]{1,0:T(8,128)(2,1)} %get-tuple-element.22.s0), channel_id=1, source_target_pairs={{0,8},{1,9},{2,10},{3,11},{4,12},{5,13},{6,14},{7,15},{8,0},{9,1},... | collective-permute-start | bytes 1671176 | tf_op jit(solution)/shard_map/ppermute | solution.py:362
  23.6 0.0 all-gather.3.cloned.1.call-update
  23.6 0.0 copy-done.15
  23.7 0.1 pad_add_fusion.1.place
  23.8 0.0 copy-done.7
  23.8 0.0 copy-start.5
  23.8 1.2 copy-done.5
  25.0 0.0 copy-start.1
  25.0 0.0 copy-start
  25.0 11.0 %near_own.1.given = f32[8,64,512]{2,1,0:T(8,128)S(1)} custom-call(s32[8,8]{1,0:T(8,128)S(1)} %copy-done.7, s32[1]{0:T(128)} %bitcast.first, bf16[8,128,512]{2,1,0:T(8,128)(2,1)S(1)} %copy-done.5), custom_call_target="tpu_custom_call" | custom-call | flops 8999999488 | bytes 1000000 | tf_op jit(solution)/shard_map/near_own/pallas_call | solution.py:273
  36.1 0.0 copy-start.12
  36.1 1.0 copy-done.12
  37.1 0.0 collective-permute-done.2.s1
  37.1 0.0 collective-permute-done.3.s2
  37.1 9.7 %collective-permute-done.4.s3 = bf16[1088,256]{1,0:T(8,128)(2,1)S(1)} collective-permute-done((bf16[1088,256]{1,0:T(8,128)(2,1)}, bf16[1088,256]{1,0:T(8,128)(2,1)S(1)}, u32[]{:S(2)}, u32[]{:S(2)}) %collective-permute-start.4) | collective-permute-done | bytes 557088 | tf_op jit(solution)/shard_map/ppermute | solution.py:362
  46.8 0.0 copy-done.1
  46.8 0.0 copy-done.14
  46.9 2.1 %collective-permute-start.5 = (bf16[128,256]{1,0:T(8,128)(2,1)S(1)}, bf16[128,256]{1,0:T(8,128)(2,1)S(1)}, u32[]{:S(2)}, u32[]{:S(2)}) collective-permute-start(bf16[128,256]{1,0:T(8,128)(2,1)S(1)} %pad_maximum_fusion.1.mine), channel_id=1, source_target_pairs={{0,16},{16,0},{32,48},{48,32},{64,80},{80,64},{96,112},{112,96},{1... | collective-permute-start | bytes 196616 | tf_op jit(solution)/shard_map/ppermute | solution.py:368
  48.9 0.0 copy-done
  48.9 6.5 %far_own.1 = (f32[512,256]{1,0:T(8,128)S(1)}, bf16[32,256,128]{2,1,0:T(8,128)(2,1)S(1)}) custom-call(s32[8,16]{1,0:T(8,128)S(1)} %and_select_fusion.ids, s32[2]{0:T(128)S(1)} %pad_add_fusion.1.place, bf16[1088,256]{1,0:T(8,128)(2,1)S(1)} %copy-done.1, bf16[1088,256]{1,0:T(8,128)(2,1)S(1)} %collective-permute-done.2.s1, ...), custom_call_target="tpu_custom_call" | custom-call | flops 6000000000 | bytes 1000000 | tf_op jit(solution)/shard_map/far_own/pallas_call | solution.py:162
  55.4 0.0 copy-start.8
  55.4 0.8 copy-done.8
  56.2 0.0 copy-start.10
  56.2 1.3 %copy-done.10 = bf16[32,256,128]{2,1,0:T(8,128)(2,1)} copy-done((bf16[32,256,128]{2,1,0:T(8,128)(2,1)}, bf16[32,256,128]{2,1,0:T(8,128)(2,1)S(1)}, u32[]{:S(2)}) %copy-start.10) | copy-done | bytes 2097176
  57.5 0.0 collective-permute-done.5.pair
  57.5 0.7 pad_maximum_fusion
  58.2 1.3 collective-permute-start.6
  59.5 1.4 %collective-permute-start.7 = (bf16[256,256]{1,0:T(8,128)(2,1)}, bf16[256,256]{1,0:T(8,128)(2,1)}, u32[]{:S(2)}, u32[]{:S(2)}) collective-permute-start(bf16[256,256]{1,0:T(8,128)(2,1)} %pad_maximum_fusion), channel_id=1, source_target_pairs={{0,96},{16,112},{32,0},{48,16},{64,32},{80,48},{96,64},{112,80},{1... | collective-permute-start | bytes 393224 | tf_op jit(solution)/shard_map/ppermute | solution.py:369
  60.9 1.6 %collective-permute-start.8 = (bf16[256,256]{1,0:T(8,128)(2,1)}, bf16[256,256]{1,0:T(8,128)(2,1)}, u32[]{:S(2)}, u32[]{:S(2)}) collective-permute-start(bf16[256,256]{1,0:T(8,128)(2,1)} %pad_maximum_fusion), channel_id=1, source_target_pairs={{0,64},{16,80},{32,96},{48,112},{64,0},{80,16},{96,32},{112,48},{1... | collective-permute-start | bytes 393224 | tf_op jit(solution)/shard_map/ppermute | solution.py:369
  62.6 0.0 all-gather.3.cloned.1.call-done
  62.6 0.7 slice_convert_fusion
  63.3 0.0 copy-start.2
  63.3 1.2 copy-done.2
  64.5 1.6 %copy-done.11 = bf16[32,256,128]{2,1,0:T(8,128)(2,1)S(1)} copy-done((bf16[32,256,128]{2,1,0:T(8,128)(2,1)S(1)}, bf16[32,256,128]{2,1,0:T(8,128)(2,1)}, u32[]{:S(2)}) %copy-start.11) | copy-done | bytes 2097176
  66.1 9.9 %far_rest.1 = (bf16[512,256]{1,0:T(8,128)(2,1)S(1)}, bf16[512,256]{1,0:T(8,128)(2,1)S(1)}, bf16[512,256]{1,0:T(8,128)(2,1)S(1)}) custom-call(s32[32,16]{1,0:T(8,128)S(1)} %pad_add_fusion.ids, s32[2]{0:T(128)S(1)} %pad_add_fusion.1.place, bf16[32,256,128]{2,1,0:T(8,128)(2,1)S(1)} %copy-done.11, bf16[1088,256]{1,0:T(8,128)(2,1)S(1)} %copy-done.1, ...), custom_call_target="tpu_custom_call" | custom-call | flops 10000000000 | bytes 1000000 | tf_op jit(solution)/shard_map/far_rest/pallas_call | solution.py:186
  76.0 0.0 collective-permute-done.6.n1
  76.0 0.0 collective-permute-done.7.n2
  76.0 0.0 collective-permute-done.8.n3
  76.0 0.0 copy-start.6
  76.0 0.0 copy-start.13
  76.0 2.0 %top_sum.1 = (f32[64,256]{1,0:T(8,128)S(1)}, bf16[576,256]{1,0:T(8,128)(2,1)S(1)}, bf16[576,256]{1,0:T(8,128)(2,1)S(1)}, bf16[576,256]{1,0:T(8,128)(2,1)S(1)}) custom-call(bf16[128,256]{1,0:T(8,128)(2,1)S(1)} %pad_maximum_fusion.1.mine, bf16[128,256]{1,0:T(8,128)(2,1)S(1)} %collective-permute-done.5.pair, bf16[256,256]{1,0:T(8,128)(2,1)S(1)} %collective-permute-done.6.n1, ...), custom_call_target="tpu_custom_call" | custom-call | flops 2000000000 | bytes 1000000 | tf_op jit(solution)/shard_map/top_sum/pallas_call | solution.py:214
  78.0 22.8 %collective-permute-start.9 = (bf16[576,256]{1,0:T(8,128)(2,1)S(1)}, bf16[576,256]{1,0:T(8,128)(2,1)S(1)}, u32[]{:S(2)}, u32[]{:S(2)}) collective-permute-start(bf16[576,256]{1,0:T(8,128)(2,1)S(1)} %get-tuple-element.33), channel_id=1, source_target_pairs={{0,3},{1,0},{2,1},{3,2},{4,7},{5,4},{6,5},{7,6},{8,11},{9,8},{10,9... | collective-permute-start | bytes 884744 | tf_op jit(solution)/shard_map/ppermute | solution.py:362
  100.9 0.0 collective-permute-start.10
  100.9 1.9 %collective-permute-start.11 = (bf16[576,256]{1,0:T(8,128)(2,1)S(1)}, bf16[576,256]{1,0:T(8,128)(2,1)S(1)}, u32[]{:S(2)}, u32[]{:S(2)}) collective-permute-start(bf16[576,256]{1,0:T(8,128)(2,1)S(1)} %get-tuple-element.35), channel_id=1, source_target_pairs={{0,2},{1,3},{2,0},{3,1},{4,6},{5,7},{6,4},{7,5},{8,10},{9,11},{10,... | collective-permute-start | bytes 884744 | tf_op jit(solution)/shard_map/ppermute | solution.py:362
  102.8 0.0 collective-permute-done.before
  102.8 0.0 collective-permute-done.1.after
  102.8 0.0 copy-done.6
  102.8 0.0 copy-done.13
  102.8 19.1 %near_rest.1.near_sum = f32[8,64,512]{2,1,0:T(8,128)S(1)} custom-call(s32[8,8]{1,0:T(8,128)S(1)} %copy-done.7, s32[1]{0:T(128)} %bitcast.first, bf16[8,128,512]{2,1,0:T(8,128)(2,1)S(1)} %copy-done.6, bf16[8,128,512]{2,1,0:T(8,128)(2,1)S(1)} %collective-permute-done.before, bf16[8,128,512]{2,1,0:T(8,128)(2,1)} %collective-permute-done.1.after, ...), custom_call_target="tpu_custom_call" | custom-call | flops 11000000512 | bytes 1000000 | tf_op jit(solution)/shard_map/near_rest/pallas_call | solution.py:307
  121.9 0.0 collective-permute-done.9.r1
  121.9 0.0 collective-permute-done.10.r2
  121.9 0.0 collective-permute-done.11.r3
  121.9 0.0 copy-done.3
  121.9 0.0 copy-done.4
  121.9 0.0 copy-done.9
  121.9 2.9 %final.1 = bf16[8,64,512]{2,1,0:T(8,128)(2,1)} custom-call(f32[8,64,512]{2,1,0:T(8,128)S(1)} %near_rest.1.near_sum, bf16[8,512,256]{2,1,0:T(8,128)(2,1)S(1)} %copy-done.3, bf16[8,256,256]{2,1,0:T(8,128)(2,1)S(1)} %copy-done.4, f32[512,256]{1,0:T(8,128)S(1)} %copy-done.9, bf16[576,256]{1,0:T(8,128)(2,1)S(1)} %collective-permute-done.9.r1, ...), custom_call_target="tpu_custom_call" | custom-call | flops 3000000000 | bytes 1000000 | tf_op jit(solution)/shard_map/final/pallas_call | solution.py:345
  (10 shorter events, 0.1 us)
Async XLA Ops:
  6.5 17.1 %copy-start.15 = (s32[8,16]{1,0:T(8,128)S(1)}, s32[8,16]{1,0:T(8,128)}, u32[]{:S(2)}) copy-start(s32[8,16]{1,0:T(8,128)} %far.1) | copy-start | bytes 1540
  6.5 17.3 %copy-start.7 = (s32[8,8]{1,0:T(8,128)S(1)}, s32[8,8]{1,0:T(8,128)}, u32[]{:S(2)}) copy-start(s32[8,8]{1,0:T(8,128)} %ids.3) | copy-start | bytes 772
  6.5 56.0 %all-gather.3.cloned.1.call-start = ((), (), s32[]{:S(2)}) async-start(), calls=%async_computation | async-start | bytes 1351680 | tf_op jit(solution)/shard_map/all_gather | solution.py:383
  13.8 88.9 %collective-permute-start = (bf16[8,128,512]{2,1,0:T(8,128)(2,1)}, bf16[8,128,512]{2,1,0:T(8,128)(2,1)S(1)}, u32[]{:S(2)}, u32[]{:S(2)}) collective-permute-start(bf16[8,128,512]{2,1,0:T(8,128)(2,1)} %get-tuple-element.21.own), channel_id=1, source_target_pairs={{0,1},{1,2},{2,3},{3,4},{4,5},{5,6},{6,7},{7,8},{8,9},{9,10},{10,1... | collective-permute-start | bytes 3145736 | tf_op jit(solution)/shard_map/ppermute | solution.py:386
  17.4 85.4 %collective-permute-start.1 = (bf16[8,128,512]{2,1,0:T(8,128)(2,1)}, bf16[8,128,512]{2,1,0:T(8,128)(2,1)}, u32[]{:S(2)}, u32[]{:S(2)}) collective-permute-start(bf16[8,128,512]{2,1,0:T(8,128)(2,1)} %get-tuple-element.21.own), channel_id=1, source_target_pairs={{1,0},{2,1},{3,2},{4,3},{5,4},{6,5},{7,6},{8,7},{9,8},{10,9},{11,1... | collective-permute-start | bytes 3145736 | tf_op jit(solution)/shard_map/ppermute | solution.py:387
  19.3 17.7 %collective-permute-start.2 = (bf16[1088,256]{1,0:T(8,128)(2,1)}, bf16[1088,256]{1,0:T(8,128)(2,1)S(1)}, u32[]{:S(2)}, u32[]{:S(2)}) collective-permute-start(bf16[1088,256]{1,0:T(8,128)(2,1)} %get-tuple-element.22.s0), channel_id=1, source_target_pairs={{0,4},{1,5},{2,6},{3,7},{4,8},{5,9},{6,10},{7,11},{8,12},{9,13},{1... | collective-permute-start | bytes 1671176 | tf_op jit(solution)/shard_map/ppermute | solution.py:362
  20.6 16.5 %collective-permute-start.3 = (bf16[1088,256]{1,0:T(8,128)(2,1)}, bf16[1088,256]{1,0:T(8,128)(2,1)S(1)}, u32[]{:S(2)}, u32[]{:S(2)}) collective-permute-start(bf16[1088,256]{1,0:T(8,128)(2,1)} %get-tuple-element.22.s0), channel_id=1, source_target_pairs={{0,12},{1,13},{2,14},{3,15},{4,0},{5,1},{6,2},{7,3},{8,4},{9,5},{1... | collective-permute-start | bytes 1671176 | tf_op jit(solution)/shard_map/ppermute | solution.py:362
  22.1 24.7 %collective-permute-start.4 = (bf16[1088,256]{1,0:T(8,128)(2,1)}, bf16[1088,256]{1,0:T(8,128)(2,1)S(1)}, u32[]{:S(2)}, u32[]{:S(2)}) collective-permute-start(bf16[1088,256]{1,0:T(8,128)(2,1)} %get-tuple-element.22.s0), channel_id=1, source_target_pairs={{0,8},{1,9},{2,10},{3,11},{4,12},{5,13},{6,14},{7,15},{8,0},{9,1},... | collective-permute-start | bytes 1671176 | tf_op jit(solution)/shard_map/ppermute | solution.py:362
  23.8 1.2 copy-start.5
  25.0 21.8 %copy-start.1 = (bf16[1088,256]{1,0:T(8,128)(2,1)S(1)}, bf16[1088,256]{1,0:T(8,128)(2,1)}, u32[]{:S(2)}) copy-start(bf16[1088,256]{1,0:T(8,128)(2,1)} %get-tuple-element.22.s0) | copy-start | bytes 1671172
  25.0 21.8 %copy-start.14 = (bf16[1,64,256]{2,1,0:T(8,128)(2,1)S(1)}, bf16[1,64,256]{2,1,0:T(8,128)(2,1)}, u32[]{:S(2)}) copy-start(bf16[1,64,256]{2,1,0:T(8,128)(2,1)} %param.12) | copy-start | bytes 98308
  25.0 23.9 %copy-start = (bf16[528,256]{1,0:T(8,128)(2,1)S(1)}, bf16[528,256]{1,0:T(8,128)(2,1)}, u32[]{:S(2)}) copy-start(bf16[528,256]{1,0:T(8,128)(2,1)} %get-tuple-element.27.t0) | copy-start | bytes 811012
  36.1 1.0 copy-start.12
  46.9 10.7 %collective-permute-start.5 = (bf16[128,256]{1,0:T(8,128)(2,1)S(1)}, bf16[128,256]{1,0:T(8,128)(2,1)S(1)}, u32[]{:S(2)}, u32[]{:S(2)}) collective-permute-start(bf16[128,256]{1,0:T(8,128)(2,1)S(1)} %pad_maximum_fusion.1.mine), channel_id=1, source_target_pairs={{0,16},{16,0},{32,48},{48,32},{64,80},{80,64},{96,112},{112,96},{1... | collective-permute-start | bytes 196616 | tf_op jit(solution)/shard_map/ppermute | solution.py:368
  55.4 0.8 copy-start.8
  56.2 1.3 %copy-start.10 = (bf16[32,256,128]{2,1,0:T(8,128)(2,1)}, bf16[32,256,128]{2,1,0:T(8,128)(2,1)S(1)}, u32[]{:S(2)}) copy-start(bf16[32,256,128]{2,1,0:T(8,128)(2,1)S(1)} %get-tuple-element.29.side) | copy-start | bytes 6291460
  58.2 17.8 %collective-permute-start.6 = (bf16[256,256]{1,0:T(8,128)(2,1)}, bf16[256,256]{1,0:T(8,128)(2,1)S(1)}, u32[]{:S(2)}, u32[]{:S(2)}) collective-permute-start(bf16[256,256]{1,0:T(8,128)(2,1)} %pad_maximum_fusion), channel_id=1, source_target_pairs={{0,32},{16,48},{32,64},{48,80},{64,96},{80,112},{96,0},{112,16},{1... | collective-permute-start | bytes 393224 | tf_op jit(solution)/shard_map/ppermute | solution.py:369
  59.5 16.5 %collective-permute-start.7 = (bf16[256,256]{1,0:T(8,128)(2,1)}, bf16[256,256]{1,0:T(8,128)(2,1)}, u32[]{:S(2)}, u32[]{:S(2)}) collective-permute-start(bf16[256,256]{1,0:T(8,128)(2,1)} %pad_maximum_fusion), channel_id=1, source_target_pairs={{0,96},{16,112},{32,0},{48,16},{64,32},{80,48},{96,64},{112,80},{1... | collective-permute-start | bytes 393224 | tf_op jit(solution)/shard_map/ppermute | solution.py:369
  60.9 15.1 %collective-permute-start.8 = (bf16[256,256]{1,0:T(8,128)(2,1)}, bf16[256,256]{1,0:T(8,128)(2,1)}, u32[]{:S(2)}, u32[]{:S(2)}) collective-permute-start(bf16[256,256]{1,0:T(8,128)(2,1)} %pad_maximum_fusion), channel_id=1, source_target_pairs={{0,64},{16,80},{32,96},{48,112},{64,0},{80,16},{96,32},{112,48},{1... | collective-permute-start | bytes 393224 | tf_op jit(solution)/shard_map/ppermute | solution.py:369
  63.3 1.2 copy-start.2
  64.5 1.6 %copy-start.11 = (bf16[32,256,128]{2,1,0:T(8,128)(2,1)S(1)}, bf16[32,256,128]{2,1,0:T(8,128)(2,1)}, u32[]{:S(2)}) copy-start(bf16[32,256,128]{2,1,0:T(8,128)(2,1)} %copy-done.10) | copy-start | bytes 6291460
  76.0 26.7 %copy-start.6 = (bf16[8,128,512]{2,1,0:T(8,128)(2,1)S(1)}, bf16[8,128,512]{2,1,0:T(8,128)(2,1)}, u32[]{:S(2)}) copy-start(bf16[8,128,512]{2,1,0:T(8,128)(2,1)} %get-tuple-element.21.own) | copy-start | bytes 3145732
  76.0 26.7 %copy-start.13 = (f32[8,64,512]{2,1,0:T(8,128)S(1)}, f32[8,64,512]{2,1,0:T(8,128)}, u32[]{:S(2)}) copy-start(f32[8,64,512]{2,1,0:T(8,128)} %copy-done.12) | copy-start | bytes 3145732
  78.0 43.8 %collective-permute-start.9 = (bf16[576,256]{1,0:T(8,128)(2,1)S(1)}, bf16[576,256]{1,0:T(8,128)(2,1)S(1)}, u32[]{:S(2)}, u32[]{:S(2)}) collective-permute-start(bf16[576,256]{1,0:T(8,128)(2,1)S(1)} %get-tuple-element.33), channel_id=1, source_target_pairs={{0,3},{1,0},{2,1},{3,2},{4,7},{5,4},{6,5},{7,6},{8,11},{9,8},{10,9... | collective-permute-start | bytes 884744 | tf_op jit(solution)/shard_map/ppermute | solution.py:362
  100.9 21.0 %collective-permute-start.10 = (bf16[576,256]{1,0:T(8,128)(2,1)S(1)}, bf16[576,256]{1,0:T(8,128)(2,1)S(1)}, u32[]{:S(2)}, u32[]{:S(2)}) collective-permute-start(bf16[576,256]{1,0:T(8,128)(2,1)S(1)} %get-tuple-element.34), channel_id=1, source_target_pairs={{0,1},{1,2},{2,3},{3,0},{4,5},{5,6},{6,7},{7,4},{8,9},{9,10},{10,1... | collective-permute-start | bytes 884744 | tf_op jit(solution)/shard_map/ppermute | solution.py:362
  100.9 21.0 %copy-start.3 = (bf16[8,512,256]{2,1,0:T(8,128)(2,1)S(1)}, bf16[8,512,256]{2,1,0:T(8,128)(2,1)}, u32[]{:S(2)}) copy-start(bf16[8,512,256]{2,1,0:T(8,128)(2,1)} %basis.3) | copy-start | bytes 6291460
  100.9 21.0 %copy-start.4 = (bf16[8,256,256]{2,1,0:T(8,128)(2,1)S(1)}, bf16[8,256,256]{2,1,0:T(8,128)(2,1)}, u32[]{:S(2)}) copy-start(bf16[8,256,256]{2,1,0:T(8,128)(2,1)} %transfer.3) | copy-start | bytes 3145732
  100.9 21.0 %copy-start.9 = (f32[512,256]{1,0:T(8,128)S(1)}, f32[512,256]{1,0:T(8,128)}, u32[]{:S(2)}) copy-start(f32[512,256]{1,0:T(8,128)} %copy-done.8) | copy-start | bytes 1572868
  100.9 21.0 %collective-permute-start.11 = (bf16[576,256]{1,0:T(8,128)(2,1)S(1)}, bf16[576,256]{1,0:T(8,128)(2,1)S(1)}, u32[]{:S(2)}, u32[]{:S(2)}) collective-permute-start(bf16[576,256]{1,0:T(8,128)(2,1)S(1)} %get-tuple-element.35), channel_id=1, source_target_pairs={{0,2},{1,3},{2,0},{3,1},{4,6},{5,7},{6,4},{7,5},{8,10},{9,11},{10,... | collective-permute-start | bytes 884744 | tf_op jit(solution)/shard_map/ppermute | solution.py:362
Sparse Core Ops, SparseCore 0:
  23.8 31.8 all-gather.2

commit v3 on v2

v3 whole, which is shorter than its diff:
```python
import functools

import jax
import jax.numpy as jnp
from jax import lax
from jax.experimental import pallas as pl
from jax.experimental.pallas import tpu as pltpu
from jax.sharding import PartitionSpec as P

BF = jnp.bfloat16
F32 = jnp.float32
F = 64
RHS = 64
LP = 512
SK = 256
LD = 8
SIDE = 4
AUG = 128
VM = pl.BlockSpec(memory_space=pltpu.VMEM)
SM = pl.BlockSpec(memory_space=pltpu.SMEM)


def params(mib=40):
    return pltpu.CompilerParams(vmem_limit_bytes=mib * 2**20)


def cost(us):
    return pl.CostEstimate(flops=us * 10**9, bytes_accessed=10**6, transcendentals=0)


def norm_rows(points, first):
    norm = jnp.sum(points * points, axis=0, keepdims=True) * (-2.0 / F)
    high = norm.astype(BF).astype(F32)
    mid = (norm - high).astype(BF).astype(F32)
    low = norm - high - mid
    row = lax.broadcasted_iota(jnp.int32, (16, points.shape[1]), 0)
    at = 0 if first else 3
    ones = jnp.where(row < 6, 1.0, 0.0).astype(F32)
    rows = jnp.where(row == at + 1, mid, jnp.where(row == at + 2, low, ones))
    return jnp.where(row == at, high, rows)


def source_side(points):
    points = points.astype(F32)
    zeros = jnp.zeros((AUG - F - 16, points.shape[1]), F32)
    full = jnp.concatenate([points, norm_rows(points, True), zeros], axis=0)
    return full.astype(BF).T


def target_side(points):
    points = points.astype(F32)
    zeros = jnp.zeros((AUG - F - 16, points.shape[1]), F32)
    full = jnp.concatenate([points * (4.0 / F), norm_rows(points, False), zeros], axis=0)
    return full.astype(BF)


def prep_kernel(
    points, sides, basis, transfer, skeleton, far, near_msg, source_msg, target_msg,
    own_points, own_sides, own_basis, own_transfer, node, ids, sems, out_sems,
):
    def fetch(leaf):
        pairs = (
            (points, own_points),
            (sides, own_sides),
            (basis, own_basis),
            (transfer, own_transfer),
        )
        return [
            pltpu.make_async_copy(src.at[leaf], dst.at[leaf], sems.at[k, leaf])
            for k, (src, dst) in enumerate(pairs)
        ]

    for leaf in range(LD):
        for copy in fetch(leaf):
            copy.start()
    stacked = [
        pltpu.make_async_copy(points, near_msg.at[:, :F, :], out_sems.at[0]),
        pltpu.make_async_copy(sides, near_msg.at[:, F:, :], out_sems.at[1]),
    ]
    for copy in stacked:
        copy.start()
    ids[...] = jnp.zeros_like(ids)
    named = far[...]
    ids[:LD, : SIDE * SIDE] = jnp.where(named >= 0, named & (LD - 1), -1).astype(F32)
    target_msg[LD * F :, :] = ids[...].astype(BF)
    node[...] = jnp.zeros_like(node)
    position = lax.broadcasted_iota(jnp.int32, (LP, SK), 0)
    for leaf in range(LD):
        for copy in fetch(leaf):
            copy.wait()
        charge = jnp.dot(
            own_sides[leaf], own_basis[leaf], preferred_element_type=F32
        ).astype(BF)
        chosen = jnp.where(position == skeleton[leaf : leaf + 1, :], 1.0, 0.0).astype(BF)
        skel = jnp.dot(own_points[leaf], chosen, preferred_element_type=F32).astype(BF)
        source_msg[leaf * 2 * F : leaf * 2 * F + F, :] = charge
        source_msg[leaf * 2 * F + F : (leaf + 1) * 2 * F, :] = skel
        target_msg[leaf * F : (leaf + 1) * F, :] = skel
        node[...] += jnp.dot(charge, own_transfer[leaf], preferred_element_type=F32)
    source_msg[LD * 2 * F :, :] = node[...].astype(BF)
    for copy in stacked:
        copy.wait()


def prep(points, sides, basis, transfer, skeleton, far):
    anywhere = pl.BlockSpec(memory_space=pl.ANY)
    return pl.pallas_call(
        prep_kernel,
        in_specs=[anywhere] * 4 + [VM] * 2,
        out_specs=[anywhere, VM, VM],
        out_shape=[
            jax.ShapeDtypeStruct((LD, 2 * F, LP), BF),
            jax.ShapeDtypeStruct((LD * 2 * F + RHS, SK), BF),
            jax.ShapeDtypeStruct((LD * F + 16, SK), BF),
        ],
        scratch_shapes=[
            pltpu.VMEM((LD, F, LP), BF),
            pltpu.VMEM((LD, RHS, LP), BF),
            pltpu.VMEM((LD, LP, SK), BF),
            pltpu.VMEM((LD, SK, SK), BF),
            pltpu.VMEM((RHS, SK), F32),
            pltpu.VMEM((16, SK), F32),
            pltpu.SemaphoreType.DMA((4, LD)),
            pltpu.SemaphoreType.DMA((2,)),
        ],
        compiler_params=params(56),
        cost_estimate=cost(4),
        name="prep",
    )(points, sides, basis, transfer, skeleton, far)


def far_total(ids, columns, row, target, side, weight_of):
    points = target_side(target)
    weights, tiles = [], []
    for d, column in enumerate(columns):
        named = ids[row, column]
        at = jnp.maximum(named, 0)
        tiles.append(
            jnp.exp(
                jnp.dot(side[d * LD + at], points, preferred_element_type=F32)
            ).astype(BF)
        )
        weight = weight_of(d, at)
        weights.append(jnp.where(named >= 0, weight, jnp.zeros_like(weight)))
    if len(weights) == 1:
        return jnp.dot(weights[0], tiles[0], preferred_element_type=F32)
    return jnp.dot(
        jnp.concatenate(weights, axis=1),
        jnp.concatenate(tiles, axis=0),
        preferred_element_type=F32,
    )


def rows_of(leaf):
    return pl.ds(pl.multiple_of(leaf * F, F), F)


def charges_at(source, leaf):
    return source[pl.ds(pl.multiple_of(leaf * 2 * F, 2 * F), RHS), :]


def skeleton_at(source, leaf):
    return source[pl.ds(pl.multiple_of(leaf * 2 * F + F, F), F), :]


def columns_of(place, shifts):
    x, z = place[0], place[1]
    return [x * SIDE + lax.rem(z + shift, SIDE) for shift in shifts]


def far_loop(ids, place, side, sources, targets, outs, base):
    columns = columns_of(place, (0, SIDE - 1, 1))
    for b, (target, out) in enumerate(zip(targets, outs)):

        @pl.loop(0, LD, unroll=2)
        def _(leaf, b=b, target=target, out=out):
            out[rows_of(leaf), :] = far_total(
                ids, columns, (base + b) * LD + leaf, target[rows_of(leaf), :], side,
                lambda d, at: charges_at(sources[d], at),
            )


def far_a_kernel(ids, place, s0, s1, s2, t0, t1, o0, o1, side):
    for d, source in enumerate((s0, s1, s2)):

        @pl.loop(0, LD, unroll=2)
        def _(leaf, d=d, source=source):
            side[d * LD + leaf] = source_side(skeleton_at(source, leaf))

    far_loop(ids, place, side, (s0, s1, s2), (t0, t1), (o0, o1), 0)


def far_a(ids, place, sources, targets):
    return pl.pallas_call(
        far_a_kernel,
        in_specs=[SM, SM] + [VM] * 5,
        out_specs=[VM] * 3,
        out_shape=[jax.ShapeDtypeStruct((LD * F, SK), F32)] * 2
        + [jax.ShapeDtypeStruct((3 * LD, SK, AUG), BF)],
        compiler_params=params(16),
        cost_estimate=cost(7),
        name="far_a",
    )(ids, place, *sources, *targets)


def far_b_kernel(ids, place, side, s0, s1, s2, t2, t3, o2, o3):
    far_loop(ids, place, side, (s0, s1, s2), (t2, t3), (o2, o3), 2)


def far_b(ids, place, side, sources, targets):
    return pl.pallas_call(
        far_b_kernel,
        in_specs=[SM, SM] + [VM] * 6,
        out_specs=[VM] * 2,
        out_shape=[jax.ShapeDtypeStruct((LD * F, SK), F32)] * 2,
        compiler_params=params(16),
        cost_estimate=cost(5),
        name="far_b",
    )(ids, place, side, *sources, *targets)


def far_c_kernel(
    ids, place, low, high, t0, t1, t2, t3, a0, a1, a2, a3, own, r1, r2, r3, side, weights
):
    half = LD // 2
    for d, source in enumerate((low, high)):

        @pl.loop(0, half, unroll=2)
        def _(leaf, d=d, source=source):
            side[d * half + leaf] = source_side(skeleton_at(source, leaf))
            weights[d * half + leaf] = charges_at(source, leaf)

    columns = columns_of(place, (2,))
    given = (a0, a1, a2, a3)
    for b, (target, out) in enumerate(zip((t0, t1, t2, t3), (own, r1, r2, r3))):

        @pl.loop(0, LD, unroll=4)
        def _(leaf, b=b, target=target, out=out):
            total = far_total(
                ids, columns, b * LD + leaf, target[rows_of(leaf), :], side,
                lambda d, at: weights[at],
            )
            out[rows_of(leaf), :] = (given[b][rows_of(leaf), :] + total).astype(out.dtype)


def far_c(ids, place, halves, targets, given):
    return pl.pallas_call(
        far_c_kernel,
        in_specs=[SM, SM] + [VM] * 10,
        out_specs=[VM] * 4,
        out_shape=[jax.ShapeDtypeStruct((LD * F, SK), F32)]
        + [jax.ShapeDtypeStruct((LD * F, SK), BF)] * 3,
        scratch_shapes=[
            pltpu.VMEM((LD, SK, AUG), BF),
            pltpu.VMEM((LD, RHS, SK), BF),
        ],
        compiler_params=params(16),
        cost_estimate=cost(5),
        name="far_c",
    )(ids, place, *halves, *targets, *given)


def top_kernel(mine, pair, n1, n2, n3, a1, a2, a3, top, r1, r2, r3):
    points = target_side(mine[RHS:, :])
    total = jnp.zeros((RHS, SK), F32)
    rows = 2 * RHS
    others = [pair] + [n.at[i * rows : (i + 1) * rows] for n in (n1, n2, n3) for i in range(2)]
    for other in others:
        kernel = jnp.exp(
            jnp.dot(source_side(other[RHS:, :]), points, preferred_element_type=F32)
        ).astype(BF)
        total += jnp.dot(other[:RHS, :], kernel, preferred_element_type=F32)
    top[...] = total
    for given, out in ((a1, r1), (a2, r2), (a3, r3)):
        out[: LD * F, :] = given[...]
        out[LD * F :, :] = total.astype(BF)


def top_sum(mine, pair, others, parts):
    return pl.pallas_call(
        top_kernel,
        in_specs=[VM] * 8,
        out_specs=[VM] * 4,
        out_shape=[jax.ShapeDtypeStruct((RHS, SK), F32)]
        + [jax.ShapeDtypeStruct((LD * F + RHS, SK), BF)] * 3,
        compiler_params=params(16),
        cost_estimate=cost(2),
        name="top_sum",
    )(mine, pair, *others, *parts)


def near_groups(ids, leaf, place_of, points, side, rights, slots):
    count = jnp.int32(0)
    for d in range(ids.shape[1]):
        slots[d] = 0
    for d in range(ids.shape[1]):
        here, at = place_of(ids[leaf, d])
        slots[count] = jnp.where(here, at, 0)
        count += here.astype(jnp.int32)
    size = 4

    def group(g, total):
        weights, tiles = [], []
        for d in range(size):
            k = g * size + d
            at = slots[k]
            tiles.append(
                jnp.exp(jnp.dot(side[at], points, preferred_element_type=F32)).astype(BF)
            )
            weight = rights(at)
            weights.append(jnp.where(k < count, weight, jnp.zeros_like(weight)))
        return total + jnp.dot(
            jnp.concatenate(weights, axis=1),
            jnp.concatenate(tiles, axis=0),
            preferred_element_type=F32,
        )

    return lax.fori_loop(
        0, lax.div(count + size - 1, size), group, jnp.zeros((RHS, LP), F32)
    )


def near_own_kernel(ids, first, own, out, side, slots):
    @pl.loop(0, LD, unroll=2)
    def _(leaf):
        side[leaf] = source_side(own[leaf, :F, :])

    def place_of(named):
        at = named - first[0]
        return (named >= 0) & (at >= 0) & (at < LD), at

    @pl.loop(0, LD)
    def _(leaf):
        points = target_side(own[leaf, :F, :])
        out[leaf] = near_groups(
            ids, leaf, place_of, points, side, lambda at: own[at, F:, :], slots
        )


def near_own(ids, first, own):
    return pl.pallas_call(
        near_own_kernel,
        in_specs=[SM, SM, VM],
        out_specs=VM,
        out_shape=jax.ShapeDtypeStruct((LD, RHS, LP), F32),
        scratch_shapes=[pltpu.VMEM((LD, LP, AUG), BF), pltpu.SMEM((16,), jnp.int32)],
        compiler_params=params(16),
        cost_estimate=cost(9),
        name="near_own",
    )(ids, first, own)


def near_rest_kernel(ids, first, own, before, after, given, out, side, rights, slots):
    for d, block in enumerate((before, after)):

        @pl.loop(0, LD, unroll=2)
        def _(leaf, d=d, block=block):
            side[d * LD + leaf] = source_side(block[leaf, :F, :])
            rights[d * LD + leaf] = block[leaf, F:, :]

    def place_of(named):
        at = named - first[0]
        below = (at >= -LD) & (at < 0)
        above = (at >= LD) & (at < 2 * LD)
        return (named >= 0) & (below | above), jnp.where(below, at + LD, at)

    @pl.loop(0, LD)
    def _(leaf):
        points = target_side(own[leaf, :F, :])
        out[leaf] = given[leaf] + near_groups(
            ids, leaf, place_of, points, side, lambda at: rights[at], slots
        )


def near_rest(ids, first, own, before, after, given):
    return pl.pallas_call(
        near_rest_kernel,
        in_specs=[SM, SM, VM, VM, VM, VM],
        out_specs=VM,
        out_shape=jax.ShapeDtypeStruct((LD, RHS, LP), F32),
        scratch_shapes=[
            pltpu.VMEM((2 * LD, LP, AUG), BF),
            pltpu.VMEM((2 * LD, RHS, LP), BF),
            pltpu.SMEM((16,), jnp.int32),
        ],
        compiler_params=params(24),
        cost_estimate=cost(11),
        name="near_rest",
    )(ids, first, own, before, after, given)


def final_kernel(near_sum, basis, transfer, own, r1, r2, r3, top, out):
    nt = (((1,), (1,)), ((), ()))
    last = LD * F
    total = top[...]
    for r in (r1, r2, r3):
        total += r[last:, :].astype(F32)
    total = total.astype(BF)

    @pl.loop(0, LD, unroll=2)
    def _(leaf):
        rows = pl.ds(pl.multiple_of(leaf * F, F), F)
        potential = own[rows, :]
        for r in (r1, r2, r3):
            potential += r[rows, :].astype(F32)
        potential += lax.dot_general(total, transfer[leaf], nt, preferred_element_type=F32)
        far_out = lax.dot_general(
            potential.astype(BF), basis[leaf], nt, preferred_element_type=F32
        )
        out[leaf] = (near_sum[leaf] + far_out).astype(BF)


def final(near_sum, basis, transfer, own, returned, top):
    return pl.pallas_call(
        final_kernel,
        in_specs=[VM] * 8,
        out_specs=VM,
        out_shape=jax.ShapeDtypeStruct((LD, RHS, LP), BF),
        compiler_params=params(16),
        cost_estimate=cost(3),
        name="final",
    )(near_sum, basis, transfer, own, *returned, top)


def shifted(value, dx, dz):
    pairs = []
    for x in range(SIDE):
        for z in range(SIDE):
            to = (x + dx) % SIDE * SIDE + (z + dz) % SIDE
            pairs.append((x * SIDE + z, to))
    return lax.ppermute(value, "top", pairs)


def leaf_shifted(value, dy):
    count = lax.axis_size("leaf")
    if dy == 0:
        return lax.ppermute(value, "leaf", [(i, i ^ 1) for i in range(count)])
    return lax.ppermute(value, "leaf", [(i, (i + 2 * dy) % count) for i in range(count)])


def on_device(
    points, right_sides, leaf_basis, transfer, node_points, neighbours, far_sources, skeleton
):
    node, at = lax.axis_index("leaf"), lax.axis_index("top")
    position = node * SIDE * SIDE + at
    near_msg, source_msg, target_msg = prep(
        points, right_sides, leaf_basis, transfer, skeleton, far_sources
    )
    sources = [source_msg] + [shifted(source_msg, 0, dz) for dz in (1, -1)]
    targets = [target_msg] + [shifted(target_msg, dx, 0) for dx in (1, -1, 2)]
    first = (position * LD).astype(jnp.int32).reshape(1)
    near_sum = near_own(neighbours, first, near_msg)

    sources, targets, near_msg, near_sum = lax.optimization_barrier(
        (sources, targets, near_msg, near_sum)
    )
    half = LD * F
    low = shifted(sources[1][:half], 0, 1)
    high = shifted(sources[2][half:], 0, -1)
    count = lax.axis_size("leaf") * lax.axis_size("top")
    up = [(i, i + 1) for i in range(count - 1)]
    before = lax.ppermute(near_msg, ("leaf", "top"), up)
    after = lax.ppermute(near_msg, ("leaf", "top"), [(j, i) for i, j in up])
    ids = jnp.concatenate([t[LD * F : LD * F + LD, : SIDE * SIDE] for t in targets])
    ids = ids.astype(jnp.int32)
    place = jnp.stack([at // SIDE, at % SIDE]).astype(jnp.int32)
    part0, part1, side = far_a(ids, place, sources, targets[:2])

    low, high, part0, part1, side = lax.optimization_barrier((low, high, part0, part1, side))
    line_charge = sum(s[2 * half :].astype(F32) for s in sources) + high[half:].astype(F32)
    mine = jnp.concatenate([line_charge.astype(BF), node_points[0]], axis=0)
    pair = leaf_shifted(mine, 0)
    part2, part3 = far_b(ids, place, side, sources, targets[2:])
    pair, part2, part3 = lax.optimization_barrier((pair, part2, part3))
    both = jnp.concatenate([mine, pair], axis=0)
    others = [leaf_shifted(both, dy) for dy in (1, -1, 2)]
    own, *parts = far_c(ids, place, (low, high), targets, (part0, part1, part2, part3))
    top, *parts = top_sum(mine, pair, others, parts)
    returned = [shifted(r, dx, 0) for r, dx in zip(parts, (-1, 1, 2))]
    near_sum = near_rest(neighbours, first, near_msg, before, after, near_sum)
    return final(near_sum, leaf_basis, transfer, own, returned, top)


def solution(mesh):
    leaves = P(("leaf", "top"), None, None)
    lists = P(("leaf", "top"), None)
    in_specs = (leaves, leaves, leaves, leaves, P("leaf", None, None), lists, lists, lists)
    return jax.shard_map(
        on_device, mesh=mesh, in_specs=in_specs, out_specs=leaves, check_vma=False
    )
```

time: 134 us -> 138 us (1.030)
  the two profiles are of different devices: /device:TPU:33 before, /device:TPU:0 now
where the time goes in v3:
time: 138 us; the launch traced here: 137 us
  Pallas kernels  81.9 us (59%)
  starting transfers between devices  26.9 us (19%)
  waiting for transfers between devices  26 us (19%)
  local copies, waits for them, and re-layouts  2.27 us (2%)
    pallas_call x1, Pallas kernels, prep(): pl.pallas_call(prep_kernel, in_specs=[anywhere] * 4 + [VM] * 2, out_specs...  34.8 us
    ppermute x10, waiting for transfers between devices, shifted(): return lax.ppermute(value, 'top', pairs)  26 us
    ppermute x10, starting transfers between devices, shifted(): return lax.ppermute(value, 'top', pairs)  17.4 us
    pallas_call x1, Pallas kernels, near_own(): pl.pallas_call(near_own_kernel, in_specs=[SM, SM, VM], out_specs=VM, out_...  11.7 us
    pallas_call x1, Pallas kernels, far_c(): pl.pallas_call(far_c_kernel, in_specs=[SM, SM] + [VM] * 10, out_specs=[VM...  8.97 us
    pallas_call x1, Pallas kernels, near_rest(): pl.pallas_call(near_rest_kernel, in_specs=[SM, SM, VM, VM, VM, VM], out_s...  8.47 us
    pallas_call x1, Pallas kernels, far_a(): pl.pallas_call(far_a_kernel, in_specs=[SM, SM] + [VM] * 5, out_specs=[VM]...  7.75 us
    pallas_call x1, Pallas kernels, far_b(): pl.pallas_call(far_b_kernel, in_specs=[SM, SM] + [VM] * 6, out_specs=[VM]...  6.45 us
  transfers between devices with their start and end apart: 16, of which 4 were waited for; matrix products, arithmetic and copies ran while one was open for 0% of the time, Pallas kernels for 32%

profile of v3, /device:TPU:0, one launch (start us, length us, event | category | flops | bytes accessed | tf_op | source)
XLA Modules:
  0.0 137.4 jit_solution(7344350030059815697)
XLA Ops:
  0.0 0.0 copy-start.6
  0.0 34.8 %prep.1 = (bf16[8,128,512]{2,1,0:T(8,128)(2,1)}, bf16[1088,256]{1,0:T(8,128)(2,1)}, bf16[528,256]{1,0:T(8,128)(2,1)}) custom-call(bf16[8,64,512]{2,1,0:T(8,128)(2,1)} %points.1, bf16[8,64,512]{2,1,0:T(8,128)(2,1)} %sides.1, bf16[8,512,256]{2,1,0:T(8,128)(2,1)} %basis.3, bf16[8,256,256]{2,1,0:T(8,128)(2,1)} %transfer.3, s32[8,256]{1,0:T(8,128)} %skeleton.1, ...), custom_call_target="tpu_custom_call" | custom-call | flops 4000000000 | bytes 1000000 | tf_op jit(solution)/shard_map/prep/pallas_call | solution.py:107
  34.8 2.1 %collective-permute-start = (bf16[1088,256]{1,0:T(8,128)(2,1)}, bf16[1088,256]{1,0:T(8,128)(2,1)S(1)}, u32[]{:S(2)}, u32[]{:S(2)}) collective-permute-start(bf16[1088,256]{1,0:T(8,128)(2,1)} %get-tuple-element.49.s0), channel_id=1, source_target_pairs={{0,1},{1,2},{2,3},{3,0},{4,5},{5,6},{6,7},{7,4},{8,9},{9,10},{10,1... | collective-permute-start | bytes 1671176 | tf_op jit(solution)/shard_map/ppermute | solution.py:431
  36.9 2.2 %collective-permute-start.1 = (bf16[1088,256]{1,0:T(8,128)(2,1)}, bf16[1088,256]{1,0:T(8,128)(2,1)S(1)}, u32[]{:S(2)}, u32[]{:S(2)}) collective-permute-start(bf16[1088,256]{1,0:T(8,128)(2,1)} %get-tuple-element.49.s0), channel_id=1, source_target_pairs={{0,3},{1,0},{2,1},{3,2},{4,7},{5,4},{6,5},{7,6},{8,11},{9,8},{10,9... | collective-permute-start | bytes 1671176 | tf_op jit(solution)/shard_map/ppermute | solution.py:431
  39.1 1.5 %collective-permute-start.2 = (bf16[528,256]{1,0:T(8,128)(2,1)}, bf16[528,256]{1,0:T(8,128)(2,1)S(1)}, u32[]{:S(2)}, u32[]{:S(2)}) collective-permute-start(bf16[528,256]{1,0:T(8,128)(2,1)} %get-tuple-element.43.t0), channel_id=1, source_target_pairs={{0,4},{1,5},{2,6},{3,7},{4,8},{5,9},{6,10},{7,11},{8,12},{9,13},{1... | collective-permute-start | bytes 811016 | tf_op jit(solution)/shard_map/ppermute | solution.py:431
  40.6 1.7 %collective-permute-start.3 = (bf16[528,256]{1,0:T(8,128)(2,1)}, bf16[528,256]{1,0:T(8,128)(2,1)S(1)}, u32[]{:S(2)}, u32[]{:S(2)}) collective-permute-start(bf16[528,256]{1,0:T(8,128)(2,1)} %get-tuple-element.43.t0), channel_id=1, source_target_pairs={{0,12},{1,13},{2,14},{3,15},{4,0},{5,1},{6,2},{7,3},{8,4},{9,5},{1... | collective-permute-start | bytes 811016 | tf_op jit(solution)/shard_map/ppermute | solution.py:431
  42.3 1.8 %collective-permute-start.4 = (bf16[528,256]{1,0:T(8,128)(2,1)}, bf16[528,256]{1,0:T(8,128)(2,1)S(1)}, u32[]{:S(2)}, u32[]{:S(2)}) collective-permute-start(bf16[528,256]{1,0:T(8,128)(2,1)} %get-tuple-element.43.t0), channel_id=1, source_target_pairs={{0,8},{1,9},{2,10},{3,11},{4,12},{5,13},{6,14},{7,15},{8,0},{9,1},... | collective-permute-start | bytes 811016 | tf_op jit(solution)/shard_map/ppermute | solution.py:431
  44.1 0.0 copy-done.6
  44.1 0.0 copy-start.4
  44.1 1.2 copy-done.4
  45.4 0.0 copy-start.1
  45.4 0.0 copy-start
  45.4 11.7 %near_own.1.given = f32[8,64,512]{2,1,0:T(8,128)S(1)} custom-call(s32[8,8]{1,0:T(8,128)S(1)} %copy-done.6, s32[1]{0:T(128)} %bitcast.first, bf16[8,128,512]{2,1,0:T(8,128)(2,1)S(1)} %copy-done.4), custom_call_target="tpu_custom_call" | custom-call | flops 8999999488 | bytes 1000000 | tf_op jit(solution)/shard_map/near_own/pallas_call | solution.py:341
  57.1 0.0 copy-start.7
  57.1 1.0 copy-done.7
  58.0 0.1 pad_add_fusion.place
  58.1 0.0 collective-permute-done.2.t1
  58.1 0.0 collective-permute-done.3.t2
  58.1 0.0 collective-permute-done.4.t3
  58.1 0.0 collective-permute-done.s1
  58.1 0.0 collective-permute-done.1.s2
  58.1 2.8 %collective-permute-start.5 = (bf16[8,128,512]{2,1,0:T(8,128)(2,1)}, bf16[8,128,512]{2,1,0:T(8,128)(2,1)S(1)}, u32[]{:S(2)}, u32[]{:S(2)}) collective-permute-start(bf16[8,128,512]{2,1,0:T(8,128)(2,1)} %get-tuple-element.41.own), channel_id=1, source_target_pairs={{0,1},{1,2},{2,3},{3,4},{4,5},{5,6},{6,7},{7,8},{8,9},{9,10},{10,1... | collective-permute-start | bytes 3145736 | tf_op jit(solution)/shard_map/ppermute | solution.py:462
  61.0 1.3 collective-permute-start.6
  62.3 0.0 copy-done.1
  62.3 2.7 %collective-permute-start.7 = (bf16[512,256]{1,0:T(8,128)(2,1)S(1)}, bf16[512,256]{1,0:T(8,128)(2,1)S(1)}, u32[]{:S(2)}, u32[]{:S(2)}) collective-permute-start(bf16[512,256]{1,0:T(8,128)(2,1)S(1)} %slice.34), channel_id=1, source_target_pairs={{0,1},{1,2},{2,3},{3,0},{4,5},{5,6},{6,7},{7,4},{8,9},{9,10},{10,1... | collective-permute-start | bytes 786440 | tf_op jit(solution)/shard_map/ppermute | solution.py:431
  65.1 0.7 collective-permute-start.8
  65.7 0.0 copy-done
  65.7 0.0 copy-start.9
  65.8 7.8 %far_a.1 = (f32[512,256]{1,0:T(8,128)S(1)}, f32[512,256]{1,0:T(8,128)S(1)}, bf16[24,256,128]{2,1,0:T(8,128)(2,1)S(1)}) custom-call(s32[32,16]{1,0:T(8,128)S(1)} %maximum_convert_fusion.ids, s32[2]{0:T(128)S(1)} %pad_add_fusion.place, bf16[1088,256]{1,0:T(8,128)(2,1)S(1)} %copy-done, bf16[1088,256]{1,0:T(8,128)(2,1)S(1)} %collective-permute-done.s1, ...), custom_call_target="tpu_custom_call" | custom-call | flops 7000000000 | bytes 1000000 | tf_op jit(solution)/shard_map/far_a/pallas_call | solution.py:194
  73.5 13.4 %collective-permute-done.7.low = bf16[512,256]{1,0:T(8,128)(2,1)S(1)} collective-permute-done((bf16[512,256]{1,0:T(8,128)(2,1)S(1)}, bf16[512,256]{1,0:T(8,128)(2,1)S(1)}, u32[]{:S(2)}, u32[]{:S(2)}) %collective-permute-start.7) | collective-permute-done | bytes 262176 | tf_op jit(solution)/shard_map/ppermute | solution.py:431
  86.9 6.8 %collective-permute-done.8.high = bf16[576,256]{1,0:T(8,128)(2,1)S(1)} collective-permute-done((bf16[576,256]{1,0:T(8,128)(2,1)S(1)}, bf16[576,256]{1,0:T(8,128)(2,1)S(1)}, u32[]{:S(2)}, u32[]{:S(2)}) %collective-permute-start.8) | collective-permute-done | bytes 294944 | tf_op jit(solution)/shard_map/ppermute | solution.py:431
  93.8 0.0 copy-done.9
  93.8 0.1 collective-permute-start.9
  93.9 6.5 %far_b.1 = (f32[512,256]{1,0:T(8,128)S(1)}, f32[512,256]{1,0:T(8,128)S(1)}) custom-call(s32[32,16]{1,0:T(8,128)S(1)} %maximum_convert_fusion.ids, s32[2]{0:T(128)S(1)} %pad_add_fusion.place, bf16[24,256,128]{2,1,0:T(8,128)(2,1)S(1)} %get-tuple-element.57.side, bf16[1088,256]{1,0:T(8,128)(2,1)S(1)} %copy-done, bf16[1088,256]{1,0:T(8,128)(2,1)S(1)} %collective-permute-done.s1, ...), custom_call_target="tpu_custom_call" | custom-call | flops 5000000000 | bytes 1000000 | tf_op jit(solution)/shard_map/far_b/pallas_call | solution.py:211
  100.3 0.0 collective-permute-done.9.pair
  100.4 1.9 %collective-permute-start.10 = (bf16[256,256]{1,0:T(8,128)(2,1)S(1)}, bf16[256,256]{1,0:T(8,128)(2,1)S(1)}, u32[]{:S(2)}, u32[]{:S(2)}) collective-permute-start(bf16[256,256]{1,0:T(8,128)(2,1)S(1)} %pad_maximum_fusion), channel_id=1, source_target_pairs={{0,32},{16,48},{32,64},{48,80},{64,96},{80,112},{96,0},{112,16},{1... | collective-permute-start | bytes 393224 | tf_op jit(solution)/shard_map/ppermute | solution.py:438
  102.3 1.4 %collective-permute-start.11 = (bf16[256,256]{1,0:T(8,128)(2,1)S(1)}, bf16[256,256]{1,0:T(8,128)(2,1)S(1)}, u32[]{:S(2)}, u32[]{:S(2)}) collective-permute-start(bf16[256,256]{1,0:T(8,128)(2,1)S(1)} %pad_maximum_fusion), channel_id=1, source_target_pairs={{0,96},{16,112},{32,0},{48,16},{64,32},{80,48},{96,64},{112,80},{1... | collective-permute-start | bytes 393224 | tf_op jit(solution)/shard_map/ppermute | solution.py:438
  103.7 1.9 %collective-permute-start.12 = (bf16[256,256]{1,0:T(8,128)(2,1)S(1)}, bf16[256,256]{1,0:T(8,128)(2,1)S(1)}, u32[]{:S(2)}, u32[]{:S(2)}) collective-permute-start(bf16[256,256]{1,0:T(8,128)(2,1)S(1)} %pad_maximum_fusion), channel_id=1, source_target_pairs={{0,64},{16,80},{32,96},{48,112},{64,0},{80,16},{96,32},{112,48},{1... | collective-permute-start | bytes 393224 | tf_op jit(solution)/shard_map/ppermute | solution.py:438
  105.6 9.0 %far_c.1 = (f32[512,256]{1,0:T(8,128)S(1)}, bf16[512,256]{1,0:T(8,128)(2,1)S(1)}, bf16[512,256]{1,0:T(8,128)(2,1)S(1)}, bf16[512,256]{1,0:T(8,128)(2,1)S(1)}) custom-call(s32[32,16]{1,0:T(8,128)S(1)} %maximum_convert_fusion.ids, s32[2]{0:T(128)S(1)} %pad_add_fusion.place, bf16[512,256]{1,0:T(8,128)(2,1)S(1)} %collective-permute-done.7.low, ...), custom_call_target="tpu_custom_call" | custom-call | flops 5000000000 | bytes 1000000 | tf_op jit(solution)/shard_map/far_c/pallas_call | solution.py:247
  114.6 0.0 collective-permute-done.10.n1
  114.6 0.0 collective-permute-done.11.n2
  114.6 0.0 collective-permute-done.12.n3
  114.6 0.0 copy-start.5
  114.7 0.0 copy-start.8
  114.7 0.8 top_sum.1
  115.5 3.2 %collective-permute-start.13 = (bf16[576,256]{1,0:T(8,128)(2,1)S(1)}, bf16[576,256]{1,0:T(8,128)(2,1)S(1)}, u32[]{:S(2)}, u32[]{:S(2)}) collective-permute-start(bf16[576,256]{1,0:T(8,128)(2,1)S(1)} %get-tuple-element.67), channel_id=1, source_target_pairs={{0,12},{1,13},{2,14},{3,15},{4,0},{5,1},{6,2},{7,3},{8,4},{9,5},{1... | collective-permute-start | bytes 884744 | tf_op jit(solution)/shard_map/ppermute | solution.py:431
  118.7 0.0 collective-permute-start.14
  118.7 0.0 copy-start.2
  118.7 0.0 copy-start.3
  118.7 1.5 %collective-permute-start.15 = (bf16[576,256]{1,0:T(8,128)(2,1)S(1)}, bf16[576,256]{1,0:T(8,128)(2,1)S(1)}, u32[]{:S(2)}, u32[]{:S(2)}) collective-permute-start(bf16[576,256]{1,0:T(8,128)(2,1)S(1)} %get-tuple-element.69), channel_id=1, source_target_pairs={{0,8},{1,9},{2,10},{3,11},{4,12},{5,13},{6,14},{7,15},{8,0},{9,1},... | collective-permute-start | bytes 884744 | tf_op jit(solution)/shard_map/ppermute | solution.py:431
  120.3 0.0 collective-permute-done.5.before
  120.3 0.0 collective-permute-done.6.after
  120.3 0.0 copy-done.5
  120.3 0.0 copy-done.8
  120.3 8.5 %near_rest.1.near_sum = f32[8,64,512]{2,1,0:T(8,128)S(1)} custom-call(s32[8,8]{1,0:T(8,128)S(1)} %copy-done.6, s32[1]{0:T(128)} %bitcast.first, bf16[8,128,512]{2,1,0:T(8,128)(2,1)S(1)} %copy-done.5, bf16[8,128,512]{2,1,0:T(8,128)(2,1)S(1)} %collective-permute-done.5.before, bf16[8,128,512]{2,1,0:T(8,128)(2,1)S(1)} %collective-permute-done.6.after, ...), custom_call_target="tpu_custom_call" | custom-call | flops 11000000512 | bytes 1000000 | tf_op jit(solution)/shard_map/near_rest/pallas_call | solution.py:376
  128.8 2.3 %collective-permute-done.13.r1 = bf16[576,256]{1,0:T(8,128)(2,1)S(1)} collective-permute-done((bf16[576,256]{1,0:T(8,128)(2,1)S(1)}, bf16[576,256]{1,0:T(8,128)(2,1)S(1)}, u32[]{:S(2)}, u32[]{:S(2)}) %collective-permute-start.13) | collective-permute-done | bytes 294944 | tf_op jit(solution)/shard_map/ppermute | solution.py:431
  131.1 3.4 %collective-permute-done.14.r2 = bf16[576,256]{1,0:T(8,128)(2,1)S(1)} collective-permute-done((bf16[576,256]{1,0:T(8,128)(2,1)S(1)}, bf16[576,256]{1,0:T(8,128)(2,1)S(1)}, u32[]{:S(2)}, u32[]{:S(2)}) %collective-permute-start.14) | collective-permute-done | bytes 294944 | tf_op jit(solution)/shard_map/ppermute | solution.py:431
  134.5 0.0 collective-permute-done.15.r3
  134.5 0.0 copy-done.2
  134.5 0.0 copy-done.3
  134.5 2.9 %final.1 = bf16[8,64,512]{2,1,0:T(8,128)(2,1)} custom-call(f32[8,64,512]{2,1,0:T(8,128)S(1)} %near_rest.1.near_sum, bf16[8,512,256]{2,1,0:T(8,128)(2,1)S(1)} %copy-done.2, bf16[8,256,256]{2,1,0:T(8,128)(2,1)S(1)} %copy-done.3, f32[512,256]{1,0:T(8,128)S(1)} %get-tuple-element.62.own, bf16[576,256]{1,0:T(8,128)(2,1)S(1)} %collective-permute-done.13.r1, ...), custom_call_target="tpu_custom_call" | custom-call | flops 3000000000 | bytes 1000000 | tf_op jit(solution)/shard_map/final/pallas_call | solution.py:414
  (10 shorter events, 0.1 us)
Async XLA Ops:
  0.0 44.1 %copy-start.6 = (s32[8,8]{1,0:T(8,128)S(1)}, s32[8,8]{1,0:T(8,128)}, u32[]{:S(2)}) copy-start(s32[8,8]{1,0:T(8,128)} %ids.3) | copy-start | bytes 772
  34.8 23.3 %collective-permute-start = (bf16[1088,256]{1,0:T(8,128)(2,1)}, bf16[1088,256]{1,0:T(8,128)(2,1)S(1)}, u32[]{:S(2)}, u32[]{:S(2)}) collective-permute-start(bf16[1088,256]{1,0:T(8,128)(2,1)} %get-tuple-element.49.s0), channel_id=1, source_target_pairs={{0,1},{1,2},{2,3},{3,0},{4,5},{5,6},{6,7},{7,4},{8,9},{9,10},{10,1... | collective-permute-start | bytes 1671176 | tf_op jit(solution)/shard_map/ppermute | solution.py:431
  36.9 21.3 %collective-permute-start.1 = (bf16[1088,256]{1,0:T(8,128)(2,1)}, bf16[1088,256]{1,0:T(8,128)(2,1)S(1)}, u32[]{:S(2)}, u32[]{:S(2)}) collective-permute-start(bf16[1088,256]{1,0:T(8,128)(2,1)} %get-tuple-element.49.s0), channel_id=1, source_target_pairs={{0,3},{1,0},{2,1},{3,2},{4,7},{5,4},{6,5},{7,6},{8,11},{9,8},{10,9... | collective-permute-start | bytes 1671176 | tf_op jit(solution)/shard_map/ppermute | solution.py:431
  39.1 19.0 %collective-permute-start.2 = (bf16[528,256]{1,0:T(8,128)(2,1)}, bf16[528,256]{1,0:T(8,128)(2,1)S(1)}, u32[]{:S(2)}, u32[]{:S(2)}) collective-permute-start(bf16[528,256]{1,0:T(8,128)(2,1)} %get-tuple-element.43.t0), channel_id=1, source_target_pairs={{0,4},{1,5},{2,6},{3,7},{4,8},{5,9},{6,10},{7,11},{8,12},{9,13},{1... | collective-permute-start | bytes 811016 | tf_op jit(solution)/shard_map/ppermute | solution.py:431
  40.6 17.5 %collective-permute-start.3 = (bf16[528,256]{1,0:T(8,128)(2,1)}, bf16[528,256]{1,0:T(8,128)(2,1)S(1)}, u32[]{:S(2)}, u32[]{:S(2)}) collective-permute-start(bf16[528,256]{1,0:T(8,128)(2,1)} %get-tuple-element.43.t0), channel_id=1, source_target_pairs={{0,12},{1,13},{2,14},{3,15},{4,0},{5,1},{6,2},{7,3},{8,4},{9,5},{1... | collective-permute-start | bytes 811016 | tf_op jit(solution)/shard_map/ppermute | solution.py:431
  42.3 15.8 %collective-permute-start.4 = (bf16[528,256]{1,0:T(8,128)(2,1)}, bf16[528,256]{1,0:T(8,128)(2,1)S(1)}, u32[]{:S(2)}, u32[]{:S(2)}) collective-permute-start(bf16[528,256]{1,0:T(8,128)(2,1)} %get-tuple-element.43.t0), channel_id=1, source_target_pairs={{0,8},{1,9},{2,10},{3,11},{4,12},{5,13},{6,14},{7,15},{8,0},{9,1},... | collective-permute-start | bytes 811016 | tf_op jit(solution)/shard_map/ppermute | solution.py:431
  44.1 1.2 copy-start.4
  45.4 16.9 %copy-start.1 = (bf16[528,256]{1,0:T(8,128)(2,1)S(1)}, bf16[528,256]{1,0:T(8,128)(2,1)}, u32[]{:S(2)}) copy-start(bf16[528,256]{1,0:T(8,128)(2,1)} %get-tuple-element.43.t0) | copy-start | bytes 811012
  45.4 20.4 %copy-start = (bf16[1088,256]{1,0:T(8,128)(2,1)S(1)}, bf16[1088,256]{1,0:T(8,128)(2,1)}, u32[]{:S(2)}) copy-start(bf16[1088,256]{1,0:T(8,128)(2,1)} %get-tuple-element.49.s0) | copy-start | bytes 1671172
  57.1 1.0 copy-start.7
  58.1 62.1 %collective-permute-start.5 = (bf16[8,128,512]{2,1,0:T(8,128)(2,1)}, bf16[8,128,512]{2,1,0:T(8,128)(2,1)S(1)}, u32[]{:S(2)}, u32[]{:S(2)}) collective-permute-start(bf16[8,128,512]{2,1,0:T(8,128)(2,1)} %get-tuple-element.41.own), channel_id=1, source_target_pairs={{0,1},{1,2},{2,3},{3,4},{4,5},{5,6},{6,7},{7,8},{8,9},{9,10},{10,1... | collective-permute-start | bytes 3145736 | tf_op jit(solution)/shard_map/ppermute | solution.py:462
  61.0 59.3 %collective-permute-start.6 = (bf16[8,128,512]{2,1,0:T(8,128)(2,1)}, bf16[8,128,512]{2,1,0:T(8,128)(2,1)S(1)}, u32[]{:S(2)}, u32[]{:S(2)}) collective-permute-start(bf16[8,128,512]{2,1,0:T(8,128)(2,1)} %get-tuple-element.41.own), channel_id=1, source_target_pairs={{1,0},{2,1},{3,2},{4,3},{5,4},{6,5},{7,6},{8,7},{9,8},{10,9},{11,1... | collective-permute-start | bytes 3145736 | tf_op jit(solution)/shard_map/ppermute | solution.py:463
  62.3 24.6 %collective-permute-start.7 = (bf16[512,256]{1,0:T(8,128)(2,1)S(1)}, bf16[512,256]{1,0:T(8,128)(2,1)S(1)}, u32[]{:S(2)}, u32[]{:S(2)}) collective-permute-start(bf16[512,256]{1,0:T(8,128)(2,1)S(1)} %slice.34), channel_id=1, source_target_pairs={{0,1},{1,2},{2,3},{3,0},{4,5},{5,6},{6,7},{7,4},{8,9},{9,10},{10,1... | collective-permute-start | bytes 786440 | tf_op jit(solution)/shard_map/ppermute | solution.py:431
  65.1 28.7 %collective-permute-start.8 = (bf16[576,256]{1,0:T(8,128)(2,1)S(1)}, bf16[576,256]{1,0:T(8,128)(2,1)S(1)}, u32[]{:S(2)}, u32[]{:S(2)}) collective-permute-start(bf16[576,256]{1,0:T(8,128)(2,1)S(1)} %slice.35), channel_id=1, source_target_pairs={{0,3},{1,0},{2,1},{3,2},{4,7},{5,4},{6,5},{7,6},{8,11},{9,8},{10,9... | collective-permute-start | bytes 884744 | tf_op jit(solution)/shard_map/ppermute | solution.py:431
  65.7 28.0 %copy-start.9 = (bf16[1,64,256]{2,1,0:T(8,128)(2,1)S(1)}, bf16[1,64,256]{2,1,0:T(8,128)(2,1)}, u32[]{:S(2)}) copy-start(bf16[1,64,256]{2,1,0:T(8,128)(2,1)} %param.12) | copy-start | bytes 98308
  93.8 6.6 %collective-permute-start.9 = (bf16[128,256]{1,0:T(8,128)(2,1)S(1)}, bf16[128,256]{1,0:T(8,128)(2,1)S(1)}, u32[]{:S(2)}, u32[]{:S(2)}) collective-permute-start(bf16[128,256]{1,0:T(8,128)(2,1)S(1)} %pad_maximum_fusion.1.mine), channel_id=1, source_target_pairs={{0,16},{16,0},{32,48},{48,32},{64,80},{80,64},{96,112},{112,96},{1... | collective-permute-start | bytes 196616 | tf_op jit(solution)/shard_map/ppermute | solution.py:437
  100.4 14.2 %collective-permute-start.10 = (bf16[256,256]{1,0:T(8,128)(2,1)S(1)}, bf16[256,256]{1,0:T(8,128)(2,1)S(1)}, u32[]{:S(2)}, u32[]{:S(2)}) collective-permute-start(bf16[256,256]{1,0:T(8,128)(2,1)S(1)} %pad_maximum_fusion), channel_id=1, source_target_pairs={{0,32},{16,48},{32,64},{48,80},{64,96},{80,112},{96,0},{112,16},{1... | collective-permute-start | bytes 393224 | tf_op jit(solution)/shard_map/ppermute | solution.py:438
  102.3 12.4 %collective-permute-start.11 = (bf16[256,256]{1,0:T(8,128)(2,1)S(1)}, bf16[256,256]{1,0:T(8,128)(2,1)S(1)}, u32[]{:S(2)}, u32[]{:S(2)}) collective-permute-start(bf16[256,256]{1,0:T(8,128)(2,1)S(1)} %pad_maximum_fusion), channel_id=1, source_target_pairs={{0,96},{16,112},{32,0},{48,16},{64,32},{80,48},{96,64},{112,80},{1... | collective-permute-start | bytes 393224 | tf_op jit(solution)/shard_map/ppermute | solution.py:438
  103.7 10.9 %collective-permute-start.12 = (bf16[256,256]{1,0:T(8,128)(2,1)S(1)}, bf16[256,256]{1,0:T(8,128)(2,1)S(1)}, u32[]{:S(2)}, u32[]{:S(2)}) collective-permute-start(bf16[256,256]{1,0:T(8,128)(2,1)S(1)} %pad_maximum_fusion), channel_id=1, source_target_pairs={{0,64},{16,80},{32,96},{48,112},{64,0},{80,16},{96,32},{112,48},{1... | collective-permute-start | bytes 393224 | tf_op jit(solution)/shard_map/ppermute | solution.py:438
  114.6 5.6 %copy-start.5 = (bf16[8,128,512]{2,1,0:T(8,128)(2,1)S(1)}, bf16[8,128,512]{2,1,0:T(8,128)(2,1)}, u32[]{:S(2)}) copy-start(bf16[8,128,512]{2,1,0:T(8,128)(2,1)} %get-tuple-element.41.own) | copy-start | bytes 3145732
  114.7 5.6 %copy-start.8 = (f32[8,64,512]{2,1,0:T(8,128)S(1)}, f32[8,64,512]{2,1,0:T(8,128)}, u32[]{:S(2)}) copy-start(f32[8,64,512]{2,1,0:T(8,128)} %copy-done.7) | copy-start | bytes 3145732
  115.5 15.6 %collective-permute-start.13 = (bf16[576,256]{1,0:T(8,128)(2,1)S(1)}, bf16[576,256]{1,0:T(8,128)(2,1)S(1)}, u32[]{:S(2)}, u32[]{:S(2)}) collective-permute-start(bf16[576,256]{1,0:T(8,128)(2,1)S(1)} %get-tuple-element.67), channel_id=1, source_target_pairs={{0,12},{1,13},{2,14},{3,15},{4,0},{5,1},{6,2},{7,3},{8,4},{9,5},{1... | collective-permute-start | bytes 884744 | tf_op jit(solution)/shard_map/ppermute | solution.py:431
  118.7 15.8 %collective-permute-start.14 = (bf16[576,256]{1,0:T(8,128)(2,1)S(1)}, bf16[576,256]{1,0:T(8,128)(2,1)S(1)}, u32[]{:S(2)}, u32[]{:S(2)}) collective-permute-start(bf16[576,256]{1,0:T(8,128)(2,1)S(1)} %get-tuple-element.68), channel_id=1, source_target_pairs={{0,4},{1,5},{2,6},{3,7},{4,8},{5,9},{6,10},{7,11},{8,12},{9,13},{1... | collective-permute-start | bytes 884744 | tf_op jit(solution)/shard_map/ppermute | solution.py:431
  118.7 15.8 %copy-start.2 = (bf16[8,512,256]{2,1,0:T(8,128)(2,1)S(1)}, bf16[8,512,256]{2,1,0:T(8,128)(2,1)}, u32[]{:S(2)}) copy-start(bf16[8,512,256]{2,1,0:T(8,128)(2,1)} %basis.3) | copy-start | bytes 6291460
  118.7 15.8 %copy-start.3 = (bf16[8,256,256]{2,1,0:T(8,128)(2,1)S(1)}, bf16[8,256,256]{2,1,0:T(8,128)(2,1)}, u32[]{:S(2)}) copy-start(bf16[8,256,256]{2,1,0:T(8,128)(2,1)} %transfer.3) | copy-start | bytes 3145732
  118.7 15.8 %collective-permute-start.15 = (bf16[576,256]{1,0:T(8,128)(2,1)S(1)}, bf16[576,256]{1,0:T(8,128)(2,1)S(1)}, u32[]{:S(2)}, u32[]{:S(2)}) collective-permute-start(bf16[576,256]{1,0:T(8,128)(2,1)S(1)} %get-tuple-element.69), channel_id=1, source_target_pairs={{0,8},{1,9},{2,10},{3,11},{4,12},{5,13},{6,14},{7,15},{8,0},{9,1},... | collective-permute-start | bytes 884744 | tf_op jit(solution)/shard_map/ppermute | solution.py:431

commit v4 on v3

--- a/solution.py
+++ b/solution.py
@@ -16,6 +16,7 @@
 LD = 8
 SIDE = 4
 AUG = 128
+UNROLL = 2
 VM = pl.BlockSpec(memory_space=pltpu.VMEM)
 SM = pl.BlockSpec(memory_space=pltpu.SMEM)
 
@@ -56,50 +57,42 @@
 
 def prep_kernel(
     points, sides, basis, transfer, skeleton, far, near_msg, source_msg, target_msg,
-    own_points, own_sides, own_basis, own_transfer, node, ids, sems, out_sems,
+    own_basis, own_transfer, node, ids, sems,
 ):
     def fetch(leaf):
         pairs = (
-            (points, own_points),
-            (sides, own_sides),
-            (basis, own_basis),
-            (transfer, own_transfer),
+            (points, near_msg.at[leaf, :F, :]),
+            (sides, near_msg.at[leaf, F:, :]),
+            (basis, own_basis.at[leaf]),
+            (transfer, own_transfer.at[leaf]),
         )
         return [
-            pltpu.make_async_copy(src.at[leaf], dst.at[leaf], sems.at[k, leaf])
+            pltpu.make_async_copy(src.at[leaf], dst, sems.at[k, leaf])
             for k, (src, dst) in enumerate(pairs)
         ]
 
     for leaf in range(LD):
         for copy in fetch(leaf):
             copy.start()
-    stacked = [
-        pltpu.make_async_copy(points, near_msg.at[:, :F, :], out_sems.at[0]),
-        pltpu.make_async_copy(sides, near_msg.at[:, F:, :], out_sems.at[1]),
-    ]
-    for copy in stacked:
-        copy.start()
     ids[...] = jnp.zeros_like(ids)
     named = far[...]
     ids[:LD, : SIDE * SIDE] = jnp.where(named >= 0, named & (LD - 1), -1).astype(F32)
     target_msg[LD * F :, :] = ids[...].astype(BF)
+    position = lax.broadcasted_iota(jnp.int32, (LP, SK), 0)
     node[...] = jnp.zeros_like(node)
-    position = lax.broadcasted_iota(jnp.int32, (LP, SK), 0)
     for leaf in range(LD):
         for copy in fetch(leaf):
             copy.wait()
         charge = jnp.dot(
-            own_sides[leaf], own_basis[leaf], preferred_element_type=F32
+            near_msg[leaf, F:, :], own_basis[leaf], preferred_element_type=F32
         ).astype(BF)
         chosen = jnp.where(position == skeleton[leaf : leaf + 1, :], 1.0, 0.0).astype(BF)
-        skel = jnp.dot(own_points[leaf], chosen, preferred_element_type=F32).astype(BF)
+        skel = jnp.dot(near_msg[leaf, :F, :], chosen, preferred_element_type=F32).astype(BF)
         source_msg[leaf * 2 * F : leaf * 2 * F + F, :] = charge
         source_msg[leaf * 2 * F + F : (leaf + 1) * 2 * F, :] = skel
         target_msg[leaf * F : (leaf + 1) * F, :] = skel
         node[...] += jnp.dot(charge, own_transfer[leaf], preferred_element_type=F32)
     source_msg[LD * 2 * F :, :] = node[...].astype(BF)
-    for copy in stacked:
-        copy.wait()
 
 
 def prep(points, sides, basis, transfer, skeleton, far):
@@ -107,21 +100,18 @@
     return pl.pallas_call(
         prep_kernel,
         in_specs=[anywhere] * 4 + [VM] * 2,
-        out_specs=[anywhere, VM, VM],
+        out_specs=[VM] * 3,
         out_shape=[
             jax.ShapeDtypeStruct((LD, 2 * F, LP), BF),
             jax.ShapeDtypeStruct((LD * 2 * F + RHS, SK), BF),
             jax.ShapeDtypeStruct((LD * F + 16, SK), BF),
         ],
         scratch_shapes=[
-            pltpu.VMEM((LD, F, LP), BF),
-            pltpu.VMEM((LD, RHS, LP), BF),
             pltpu.VMEM((LD, LP, SK), BF),
             pltpu.VMEM((LD, SK, SK), BF),
             pltpu.VMEM((RHS, SK), F32),
             pltpu.VMEM((16, SK), F32),
             pltpu.SemaphoreType.DMA((4, LD)),
-            pltpu.SemaphoreType.DMA((2,)),
         ],
         compiler_params=params(56),
         cost_estimate=cost(4),
@@ -163,101 +153,63 @@
     return source[pl.ds(pl.multiple_of(leaf * 2 * F + F, F), F), :]
 
 
-def columns_of(place, shifts):
+def columns_of(place):
     x, z = place[0], place[1]
-    return [x * SIDE + lax.rem(z + shift, SIDE) for shift in shifts]
+    return [lax.rem(x + shift, SIDE) * SIDE + z for shift in (0, SIDE - 1, 1, 2)]
 
 
 def far_loop(ids, place, side, sources, targets, outs, base):
-    columns = columns_of(place, (0, SIDE - 1, 1))
+    columns = columns_of(place)
     for b, (target, out) in enumerate(zip(targets, outs)):
 
-        @pl.loop(0, LD, unroll=2)
+        @pl.loop(0, LD, unroll=UNROLL)
         def _(leaf, b=b, target=target, out=out):
             out[rows_of(leaf), :] = far_total(
                 ids, columns, (base + b) * LD + leaf, target[rows_of(leaf), :], side,
                 lambda d, at: charges_at(sources[d], at),
-            )
-
-
-def far_a_kernel(ids, place, s0, s1, s2, t0, t1, o0, o1, side):
-    for d, source in enumerate((s0, s1, s2)):
-
-        @pl.loop(0, LD, unroll=2)
+            ).astype(out.dtype)
+
+
+def far_a_kernel(ids, place, s0, s1, s2, s3, t0, t1, o0, o1, side):
+    for d, source in enumerate((s0, s1, s2, s3)):
+
+        @pl.loop(0, LD, unroll=UNROLL)
         def _(leaf, d=d, source=source):
             side[d * LD + leaf] = source_side(skeleton_at(source, leaf))
 
-    far_loop(ids, place, side, (s0, s1, s2), (t0, t1), (o0, o1), 0)
+    far_loop(ids, place, side, (s0, s1, s2, s3), (t0, t1), (o0, o1), 0)
 
 
 def far_a(ids, place, sources, targets):
     return pl.pallas_call(
         far_a_kernel,
-        in_specs=[SM, SM] + [VM] * 5,
+        in_specs=[SM, SM] + [VM] * 6,
         out_specs=[VM] * 3,
-        out_shape=[jax.ShapeDtypeStruct((LD * F, SK), F32)] * 2
-        + [jax.ShapeDtypeStruct((3 * LD, SK, AUG), BF)],
+        out_shape=[
+            jax.ShapeDtypeStruct((LD * F, SK), F32),
+            jax.ShapeDtypeStruct((LD * F, SK), BF),
+            jax.ShapeDtypeStruct((SIDE * LD, SK, AUG), BF),
+        ],
+        compiler_params=params(16),
+        cost_estimate=cost(9),
+        name="far_a",
+    )(ids, place, *sources, *targets)
+
+
+def far_b_kernel(ids, place, side, s0, s1, s2, s3, t2, t3, o2, o3):
+    far_loop(ids, place, side, (s0, s1, s2, s3), (t2, t3), (o2, o3), 2)
+
+
+def far_b(ids, place, side, sources, targets):
+    return pl.pallas_call(
+        far_b_kernel,
+        in_specs=[SM, SM] + [VM] * 7,
+        out_specs=[VM] * 2,
+        out_shape=[jax.ShapeDtypeStruct((LD * F, SK), BF)] * 2,
         compiler_params=params(16),
         cost_estimate=cost(7),
-        name="far_a",
-    )(ids, place, *sources, *targets)
-
-
-def far_b_kernel(ids, place, side, s0, s1, s2, t2, t3, o2, o3):
-    far_loop(ids, place, side, (s0, s1, s2), (t2, t3), (o2, o3), 2)
-
-
-def far_b(ids, place, side, sources, targets):
-    return pl.pallas_call(
-        far_b_kernel,
-        in_specs=[SM, SM] + [VM] * 6,
-        out_specs=[VM] * 2,
-        out_shape=[jax.ShapeDtypeStruct((LD * F, SK), F32)] * 2,
-        compiler_params=params(16),
-        cost_estimate=cost(5),
         name="far_b",
     )(ids, place, side, *sources, *targets)
-
-
-def far_c_kernel(
-    ids, place, low, high, t0, t1, t2, t3, a0, a1, a2, a3, own, r1, r2, r3, side, weights
-):
-    half = LD // 2
-    for d, source in enumerate((low, high)):
-
-        @pl.loop(0, half, unroll=2)
-        def _(leaf, d=d, source=source):
-            side[d * half + leaf] = source_side(skeleton_at(source, leaf))
-            weights[d * half + leaf] = charges_at(source, leaf)
-
-    columns = columns_of(place, (2,))
-    given = (a0, a1, a2, a3)
-    for b, (target, out) in enumerate(zip((t0, t1, t2, t3), (own, r1, r2, r3))):
-
-        @pl.loop(0, LD, unroll=4)
-        def _(leaf, b=b, target=target, out=out):
-            total = far_total(
-                ids, columns, b * LD + leaf, target[rows_of(leaf), :], side,
-                lambda d, at: weights[at],
-            )
-            out[rows_of(leaf), :] = (given[b][rows_of(leaf), :] + total).astype(out.dtype)
-
-
-def far_c(ids, place, halves, targets, given):
-    return pl.pallas_call(
-        far_c_kernel,
-        in_specs=[SM, SM] + [VM] * 10,
-        out_specs=[VM] * 4,
-        out_shape=[jax.ShapeDtypeStruct((LD * F, SK), F32)]
-        + [jax.ShapeDtypeStruct((LD * F, SK), BF)] * 3,
-        scratch_shapes=[
-            pltpu.VMEM((LD, SK, AUG), BF),
-            pltpu.VMEM((LD, RHS, SK), BF),
-        ],
-        compiler_params=params(16),
-        cost_estimate=cost(5),
-        name="far_c",
-    )(ids, place, *halves, *targets, *given)
 
 
 def top_kernel(mine, pair, n1, n2, n3, a1, a2, a3, top, r1, r2, r3):
@@ -446,37 +398,34 @@
     near_msg, source_msg, target_msg = prep(
         points, right_sides, leaf_basis, transfer, skeleton, far_sources
     )
-    sources = [source_msg] + [shifted(source_msg, 0, dz) for dz in (1, -1)]
-    targets = [target_msg] + [shifted(target_msg, dx, 0) for dx in (1, -1, 2)]
+    sources = [source_msg] + [shifted(source_msg, dx, 0) for dx in (1, -1, 2)]
+    targets = [target_msg] + [shifted(target_msg, 0, dz) for dz in (1, -1)]
     first = (position * LD).astype(jnp.int32).reshape(1)
     near_sum = near_own(neighbours, first, near_msg)
 
-    sources, targets, near_msg, near_sum = lax.optimization_barrier(
-        (sources, targets, near_msg, near_sum)
+    targets, target_msg, near_msg, near_sum = lax.optimization_barrier(
+        (targets, target_msg, near_msg, near_sum)
     )
-    half = LD * F
-    low = shifted(sources[1][:half], 0, 1)
-    high = shifted(sources[2][half:], 0, -1)
+    targets.append(shifted(target_msg, 0, 2))
     count = lax.axis_size("leaf") * lax.axis_size("top")
     up = [(i, i + 1) for i in range(count - 1)]
     before = lax.ppermute(near_msg, ("leaf", "top"), up)
     after = lax.ppermute(near_msg, ("leaf", "top"), [(j, i) for i, j in up])
+
+    sources, near_sum = lax.optimization_barrier((sources, near_sum))
+    line_charge = sum(s[2 * LD * F :].astype(F32) for s in sources)
+    mine = jnp.concatenate([line_charge.astype(BF), node_points[0]], axis=0)
+    pair = leaf_shifted(mine, 0)
     ids = jnp.concatenate([t[LD * F : LD * F + LD, : SIDE * SIDE] for t in targets])
     ids = ids.astype(jnp.int32)
     place = jnp.stack([at // SIDE, at % SIDE]).astype(jnp.int32)
-    part0, part1, side = far_a(ids, place, sources, targets[:2])
-
-    low, high, part0, part1, side = lax.optimization_barrier((low, high, part0, part1, side))
-    line_charge = sum(s[2 * half :].astype(F32) for s in sources) + high[half:].astype(F32)
-    mine = jnp.concatenate([line_charge.astype(BF), node_points[0]], axis=0)
-    pair = leaf_shifted(mine, 0)
-    part2, part3 = far_b(ids, place, side, sources, targets[2:])
-    pair, part2, part3 = lax.optimization_barrier((pair, part2, part3))
+    own, part1, side = far_a(ids, place, sources, targets[:2])
+    pair, own, side = lax.optimization_barrier((pair, own, side))
     both = jnp.concatenate([mine, pair], axis=0)
     others = [leaf_shifted(both, dy) for dy in (1, -1, 2)]
-    own, *parts = far_c(ids, place, (low, high), targets, (part0, part1, part2, part3))
+    parts = [part1] + list(far_b(ids, place, side, sources, targets[2:]))
     top, *parts = top_sum(mine, pair, others, parts)
-    returned = [shifted(r, dx, 0) for r, dx in zip(parts, (-1, 1, 2))]
+    returned = [shifted(r, 0, dz) for r, dz in zip(parts, (-1, 1, 2))]
     near_sum = near_rest(neighbours, first, near_msg, before, after, near_sum)
     return final(near_sum, leaf_basis, transfer, own, returned, top)
 

time: 138 us -> 87.9 us (0.64)
  Pallas kernels: 81.9 us -> 43.1 us
  waiting for transfers between devices: 26 us -> 11 us
  starting transfers between devices: 26.9 us -> 30.9 us
    pallas_call x1, Pallas kernels: 34.8 us -> 4.89 us  [prep(): pl.pallas_call(prep_kernel, in_specs=[anywhere] * 4 + [VM] * 2, out_specs...]
    ppermute x10 -> x9, waiting for transfers between devices: 26 us -> 11 us  [shifted(): return lax.ppermute(value, 'top', pairs)]
    pallas_call x3 -> x2, Pallas kernels: 23.2 us -> 15.4 us  [the longest x1 8.51 us: far_a(): pl.pallas_call(far_a_kernel, in_specs=[SM, SM] + [VM] * 6, out_specs=[VM]...]
    ppermute x1, starting transfers between devices: 0.09 us -> 2.81 us  [leaf_shifted(): return lax.ppermute(value, 'leaf', [(i, i ^ 1) for i in range(count)])]
    ppermute x1, starting transfers between devices: 2.8 us -> 4.99 us  [on_device(): before = lax.ppermute(near_msg, ('leaf', 'top'), up)]
    ppermute x10 -> x9, starting transfers between devices: 17.4 us -> 17.6 us  [shifted(): return lax.ppermute(value, 'top', pairs)]
  transfers between devices with their start and end apart: 16 -> 15, of which waited for: 4 -> 3; matrix products, arithmetic and copies ran while one was open for 0% -> 0% of each run, Pallas kernels for 32% -> 40%
where the time goes in v4:
time: 87.9 us; the launch traced here: 87.6 us
  Pallas kernels  43.1 us (49%)
  starting transfers between devices  30.9 us (35%)
  waiting for transfers between devices  11 us (13%)
  local copies, waits for them, and re-layouts  2.22 us (3%)
    ppermute x9, starting transfers between devices, shifted(): return lax.ppermute(value, 'top', pairs)  17.6 us
    ppermute x9, waiting for transfers between devices, shifted(): return lax.ppermute(value, 'top', pairs)  11 us
    pallas_call x1, Pallas kernels, near_own(): pl.pallas_call(near_own_kernel, in_specs=[SM, SM, VM], out_specs=VM, out_...  10.7 us
    pallas_call x1, Pallas kernels, far_a(): pl.pallas_call(far_a_kernel, in_specs=[SM, SM] + [VM] * 6, out_specs=[VM]...  8.51 us
    pallas_call x1, Pallas kernels, near_rest(): pl.pallas_call(near_rest_kernel, in_specs=[SM, SM, VM, VM, VM, VM], out_s...  8.44 us
    pallas_call x1, Pallas kernels, far_b(): pl.pallas_call(far_b_kernel, in_specs=[SM, SM] + [VM] * 7, out_specs=[VM]...  6.84 us
    ppermute x1, starting transfers between devices, on_device(): before = lax.ppermute(near_msg, ('leaf', 'top'), up)  4.99 us
    pallas_call x1, Pallas kernels, prep(): pl.pallas_call(prep_kernel, in_specs=[anywhere] * 4 + [VM] * 2, out_specs...  4.89 us
  transfers between devices with their start and end apart: 15, of which 3 were waited for; matrix products, arithmetic and copies ran while one was open for 0% of the time, Pallas kernels for 40%

profile of v4, /device:TPU:0, one launch (start us, length us, event | category | flops | bytes accessed | tf_op | source)
XLA Modules:
  0.0 87.6 jit_solution(14067200362618983374)
XLA Ops:
  0.0 0.0 copy-start.6
  0.0 4.9 %prep.1 = (bf16[8,128,512]{2,1,0:T(8,128)(2,1)}, bf16[1088,256]{1,0:T(8,128)(2,1)}, bf16[528,256]{1,0:T(8,128)(2,1)}) custom-call(bf16[8,64,512]{2,1,0:T(8,128)(2,1)} %points.1, bf16[8,64,512]{2,1,0:T(8,128)(2,1)} %sides.1, bf16[8,512,256]{2,1,0:T(8,128)(2,1)} %basis.3, bf16[8,256,256]{2,1,0:T(8,128)(2,1)} %transfer.3, s32[8,256]{1,0:T(8,128)} %skeleton.1, ...), custom_call_target="tpu_custom_call" | custom-call | flops 4000000000 | bytes 1000000 | tf_op jit(solution)/shard_map/prep/pallas_call | solution.py:100
  4.9 2.1 %collective-permute-start = (bf16[528,256]{1,0:T(8,128)(2,1)}, bf16[528,256]{1,0:T(8,128)(2,1)S(1)}, u32[]{:S(2)}, u32[]{:S(2)}) collective-permute-start(bf16[528,256]{1,0:T(8,128)(2,1)} %get-tuple-element.41.t0), channel_id=1, source_target_pairs={{0,1},{1,2},{2,3},{3,0},{4,5},{5,6},{6,7},{7,4},{8,9},{9,10},{10,1... | collective-permute-start | bytes 811016 | tf_op jit(solution)/shard_map/ppermute | solution.py:383
  7.0 2.2 %collective-permute-start.1 = (bf16[528,256]{1,0:T(8,128)(2,1)}, bf16[528,256]{1,0:T(8,128)(2,1)S(1)}, u32[]{:S(2)}, u32[]{:S(2)}) collective-permute-start(bf16[528,256]{1,0:T(8,128)(2,1)} %get-tuple-element.41.t0), channel_id=1, source_target_pairs={{0,3},{1,0},{2,1},{3,2},{4,7},{5,4},{6,5},{7,6},{8,11},{9,8},{10,9... | collective-permute-start | bytes 811016 | tf_op jit(solution)/shard_map/ppermute | solution.py:383
  9.2 1.5 %collective-permute-start.4 = (bf16[1088,256]{1,0:T(8,128)(2,1)}, bf16[1088,256]{1,0:T(8,128)(2,1)S(1)}, u32[]{:S(2)}, u32[]{:S(2)}) collective-permute-start(bf16[1088,256]{1,0:T(8,128)(2,1)} %get-tuple-element.37.s0), channel_id=1, source_target_pairs={{0,4},{1,5},{2,6},{3,7},{4,8},{5,9},{6,10},{7,11},{8,12},{9,13},{1... | collective-permute-start | bytes 1671176 | tf_op jit(solution)/shard_map/ppermute | solution.py:383
  10.7 1.7 %collective-permute-start.5 = (bf16[1088,256]{1,0:T(8,128)(2,1)}, bf16[1088,256]{1,0:T(8,128)(2,1)S(1)}, u32[]{:S(2)}, u32[]{:S(2)}) collective-permute-start(bf16[1088,256]{1,0:T(8,128)(2,1)} %get-tuple-element.37.s0), channel_id=1, source_target_pairs={{0,12},{1,13},{2,14},{3,15},{4,0},{5,1},{6,2},{7,3},{8,4},{9,5},{1... | collective-permute-start | bytes 1671176 | tf_op jit(solution)/shard_map/ppermute | solution.py:383
  12.4 1.8 %collective-permute-start.6 = (bf16[1088,256]{1,0:T(8,128)(2,1)}, bf16[1088,256]{1,0:T(8,128)(2,1)S(1)}, u32[]{:S(2)}, u32[]{:S(2)}) collective-permute-start(bf16[1088,256]{1,0:T(8,128)(2,1)} %get-tuple-element.37.s0), channel_id=1, source_target_pairs={{0,8},{1,9},{2,10},{3,11},{4,12},{5,13},{6,14},{7,15},{8,0},{9,1},... | collective-permute-start | bytes 1671176 | tf_op jit(solution)/shard_map/ppermute | solution.py:383
  14.2 0.0 copy-done.6
  14.2 0.0 copy-start.4
  14.2 1.2 %copy-done.4 = bf16[8,128,512]{2,1,0:T(8,128)(2,1)S(1)} copy-done((bf16[8,128,512]{2,1,0:T(8,128)(2,1)S(1)}, bf16[8,128,512]{2,1,0:T(8,128)(2,1)}, u32[]{:S(2)}) %copy-start.4) | copy-done | bytes 1048600
  15.5 0.0 copy-start.1
  15.5 0.0 copy-start
  15.5 0.0 copy-start.9
  15.5 10.7 %near_own.1.given = f32[8,64,512]{2,1,0:T(8,128)S(1)} custom-call(s32[8,8]{1,0:T(8,128)S(1)} %copy-done.6, s32[1]{0:T(128)} %bitcast.first, bf16[8,128,512]{2,1,0:T(8,128)(2,1)S(1)} %copy-done.4), custom_call_target="tpu_custom_call" | custom-call | flops 8999999488 | bytes 1000000 | tf_op jit(solution)/shard_map/near_own/pallas_call | solution.py:293
  26.2 0.0 copy-start.7
  26.2 0.9 %copy-done.7 = f32[8,64,512]{2,1,0:T(8,128)} copy-done((f32[8,64,512]{2,1,0:T(8,128)}, f32[8,64,512]{2,1,0:T(8,128)S(1)}, u32[]{:S(2)}) %copy-start.7) | copy-done | bytes 1048600
  27.1 0.0 collective-permute-done.t1
  27.1 0.0 collective-permute-done.1.t2
  27.1 0.0 copy-done.1
  27.1 0.9 collective-permute-start.8
  28.0 0.1 pad_add_fusion.place
  28.1 5.0 %collective-permute-start.2 = (bf16[8,128,512]{2,1,0:T(8,128)(2,1)}, bf16[8,128,512]{2,1,0:T(8,128)(2,1)S(1)}, u32[]{:S(2)}, u32[]{:S(2)}) collective-permute-start(bf16[8,128,512]{2,1,0:T(8,128)(2,1)} %get-tuple-element.33.own), channel_id=1, source_target_pairs={{0,1},{1,2},{2,3},{3,4},{4,5},{5,6},{6,7},{7,8},{8,9},{9,10},{10,1... | collective-permute-start | bytes 3145736 | tf_op jit(solution)/shard_map/ppermute | solution.py:412
  33.1 5.0 %collective-permute-done.8.t3 = bf16[528,256]{1,0:T(8,128)(2,1)S(1)} collective-permute-done((bf16[528,256]{1,0:T(8,128)(2,1)S(1)}, bf16[528,256]{1,0:T(8,128)(2,1)S(1)}, u32[]{:S(2)}, u32[]{:S(2)}) %collective-permute-start.8) | collective-permute-done | bytes 270368 | tf_op jit(solution)/shard_map/ppermute | solution.py:383
  38.1 1.3 %collective-permute-start.3 = (bf16[8,128,512]{2,1,0:T(8,128)(2,1)}, bf16[8,128,512]{2,1,0:T(8,128)(2,1)S(1)}, u32[]{:S(2)}, u32[]{:S(2)}) collective-permute-start(bf16[8,128,512]{2,1,0:T(8,128)(2,1)} %get-tuple-element.33.own), channel_id=1, source_target_pairs={{1,0},{2,1},{3,2},{4,3},{5,4},{6,5},{7,6},{8,7},{9,8},{10,9},{11,1... | collective-permute-start | bytes 3145736 | tf_op jit(solution)/shard_map/ppermute | solution.py:413
  39.4 0.0 collective-permute-done.4.s1
  39.4 0.0 collective-permute-done.5.s2
  39.4 0.0 collective-permute-done.6.s3
  39.4 0.0 copy-done
  39.4 0.0 copy-done.9
  39.5 2.8 %collective-permute-start.7 = (bf16[128,256]{1,0:T(8,128)(2,1)S(1)}, bf16[128,256]{1,0:T(8,128)(2,1)S(1)}, u32[]{:S(2)}, u32[]{:S(2)}) collective-permute-start(bf16[128,256]{1,0:T(8,128)(2,1)S(1)} %pad_maximum_fusion.1.mine), channel_id=1, source_target_pairs={{0,16},{16,0},{32,48},{48,32},{64,80},{80,64},{96,112},{112,96},{1... | collective-permute-start | bytes 196616 | tf_op jit(solution)/shard_map/ppermute | solution.py:389
  42.3 8.5 %far_a.1 = (f32[512,256]{1,0:T(8,128)S(1)}, bf16[512,256]{1,0:T(8,128)(2,1)S(1)}, bf16[32,256,128]{2,1,0:T(8,128)(2,1)S(1)}) custom-call(s32[32,16]{1,0:T(8,128)S(1)} %maximum_convert_fusion.ids, s32[2]{0:T(128)S(1)} %pad_add_fusion.place, bf16[1088,256]{1,0:T(8,128)(2,1)S(1)} %copy-done, bf16[1088,256]{1,0:T(8,128)(2,1)S(1)} %collective-permute-done.4.s1, ...), custom_call_target="tpu_custom_call" | custom-call | flops 8999999488 | bytes 1000000 | tf_op jit(solution)/shard_map/far_a/pallas_call | solution.py:184
  50.8 0.0 collective-permute-done.7.pair
  50.8 0.5 collective-permute-start.9
  51.3 2.8 %collective-permute-start.10 = (bf16[256,256]{1,0:T(8,128)(2,1)S(1)}, bf16[256,256]{1,0:T(8,128)(2,1)S(1)}, u32[]{:S(2)}, u32[]{:S(2)}) collective-permute-start(bf16[256,256]{1,0:T(8,128)(2,1)S(1)} %pad_maximum_fusion), channel_id=1, source_target_pairs={{0,96},{16,112},{32,0},{48,16},{64,32},{80,48},{96,64},{112,80},{1... | collective-permute-start | bytes 393224 | tf_op jit(solution)/shard_map/ppermute | solution.py:390
  54.1 0.9 %collective-permute-start.11 = (bf16[256,256]{1,0:T(8,128)(2,1)S(1)}, bf16[256,256]{1,0:T(8,128)(2,1)S(1)}, u32[]{:S(2)}, u32[]{:S(2)}) collective-permute-start(bf16[256,256]{1,0:T(8,128)(2,1)S(1)} %pad_maximum_fusion), channel_id=1, source_target_pairs={{0,64},{16,80},{32,96},{48,112},{64,0},{80,16},{96,32},{112,48},{1... | collective-permute-start | bytes 393224 | tf_op jit(solution)/shard_map/ppermute | solution.py:390
  55.1 6.8 %far_b.1 = (bf16[512,256]{1,0:T(8,128)(2,1)S(1)}, bf16[512,256]{1,0:T(8,128)(2,1)S(1)}) custom-call(s32[32,16]{1,0:T(8,128)S(1)} %maximum_convert_fusion.ids, s32[2]{0:T(128)S(1)} %pad_add_fusion.place, bf16[32,256,128]{2,1,0:T(8,128)(2,1)S(1)} %get-tuple-element.50.side, bf16[1088,256]{1,0:T(8,128)(2,1)S(1)} %copy-done, ...), custom_call_target="tpu_custom_call" | custom-call | flops 7000000000 | bytes 1000000 | tf_op jit(solution)/shard_map/far_b/pallas_call | solution.py:204
  61.9 0.0 collective-permute-done.9.n1
  61.9 0.0 collective-permute-done.10.n2
  62.0 0.0 collective-permute-done.11.n3
  62.0 0.0 copy-start.5
  62.0 0.0 copy-start.8
  62.0 0.8 top_sum.1
  62.8 5.9 %collective-permute-start.12 = (bf16[576,256]{1,0:T(8,128)(2,1)S(1)}, bf16[576,256]{1,0:T(8,128)(2,1)S(1)}, u32[]{:S(2)}, u32[]{:S(2)}) collective-permute-start(bf16[576,256]{1,0:T(8,128)(2,1)S(1)} %get-tuple-element.53), channel_id=1, source_target_pairs={{0,3},{1,0},{2,1},{3,2},{4,7},{5,4},{6,5},{7,6},{8,11},{9,8},{10,9... | collective-permute-start | bytes 884744 | tf_op jit(solution)/shard_map/ppermute | solution.py:383
  68.7 0.0 collective-permute-start.13
  68.7 0.0 copy-start.2
  68.7 0.0 copy-start.3
  68.7 1.5 %collective-permute-start.14 = (bf16[576,256]{1,0:T(8,128)(2,1)S(1)}, bf16[576,256]{1,0:T(8,128)(2,1)S(1)}, u32[]{:S(2)}, u32[]{:S(2)}) collective-permute-start(bf16[576,256]{1,0:T(8,128)(2,1)S(1)} %get-tuple-element.55), channel_id=1, source_target_pairs={{0,2},{1,3},{2,0},{3,1},{4,6},{5,7},{6,4},{7,5},{8,10},{9,11},{10,... | collective-permute-start | bytes 884744 | tf_op jit(solution)/shard_map/ppermute | solution.py:383
  70.3 0.0 collective-permute-done.2.before
  70.3 0.0 collective-permute-done.3.after
  70.3 0.0 copy-done.5
  70.3 0.0 copy-done.8
  70.3 8.4 %near_rest.1.near_sum = f32[8,64,512]{2,1,0:T(8,128)S(1)} custom-call(s32[8,8]{1,0:T(8,128)S(1)} %copy-done.6, s32[1]{0:T(128)} %bitcast.first, bf16[8,128,512]{2,1,0:T(8,128)(2,1)S(1)} %copy-done.5, bf16[8,128,512]{2,1,0:T(8,128)(2,1)S(1)} %collective-permute-done.2.before, bf16[8,128,512]{2,1,0:T(8,128)(2,1)S(1)} %collective-permute-done.3.after, ...), custom_call_target="tpu_custom_call" | custom-call | flops 11000000512 | bytes 1000000 | tf_op jit(solution)/shard_map/near_rest/pallas_call | solution.py:328
  78.7 2.6 %collective-permute-done.12.r1 = bf16[576,256]{1,0:T(8,128)(2,1)S(1)} collective-permute-done((bf16[576,256]{1,0:T(8,128)(2,1)S(1)}, bf16[576,256]{1,0:T(8,128)(2,1)S(1)}, u32[]{:S(2)}, u32[]{:S(2)}) %collective-permute-start.12) | collective-permute-done | bytes 294944 | tf_op jit(solution)/shard_map/ppermute | solution.py:383
  81.3 3.4 %collective-permute-done.13.r2 = bf16[576,256]{1,0:T(8,128)(2,1)S(1)} collective-permute-done((bf16[576,256]{1,0:T(8,128)(2,1)S(1)}, bf16[576,256]{1,0:T(8,128)(2,1)S(1)}, u32[]{:S(2)}, u32[]{:S(2)}) %collective-permute-start.13) | collective-permute-done | bytes 294944 | tf_op jit(solution)/shard_map/ppermute | solution.py:383
  84.7 0.0 collective-permute-done.14.r3
  84.7 0.0 copy-done.2
  84.7 0.0 copy-done.3
  84.7 2.9 %final.1 = bf16[8,64,512]{2,1,0:T(8,128)(2,1)} custom-call(f32[8,64,512]{2,1,0:T(8,128)S(1)} %near_rest.1.near_sum, bf16[8,512,256]{2,1,0:T(8,128)(2,1)S(1)} %copy-done.2, bf16[8,256,256]{2,1,0:T(8,128)(2,1)S(1)} %copy-done.3, f32[512,256]{1,0:T(8,128)S(1)} %get-tuple-element.47.own, bf16[576,256]{1,0:T(8,128)(2,1)S(1)} %collective-permute-done.12.r1, ...), custom_call_target="tpu_custom_call" | custom-call | flops 3000000000 | bytes 1000000 | tf_op jit(solution)/shard_map/final/pallas_call | solution.py:366
  (8 shorter events, 0.1 us)
Async XLA Ops:
  0.0 14.2 %copy-start.6 = (s32[8,8]{1,0:T(8,128)S(1)}, s32[8,8]{1,0:T(8,128)}, u32[]{:S(2)}) copy-start(s32[8,8]{1,0:T(8,128)} %ids.3) | copy-start | bytes 772
  4.9 22.2 %collective-permute-start = (bf16[528,256]{1,0:T(8,128)(2,1)}, bf16[528,256]{1,0:T(8,128)(2,1)S(1)}, u32[]{:S(2)}, u32[]{:S(2)}) collective-permute-start(bf16[528,256]{1,0:T(8,128)(2,1)} %get-tuple-element.41.t0), channel_id=1, source_target_pairs={{0,1},{1,2},{2,3},{3,0},{4,5},{5,6},{6,7},{7,4},{8,9},{9,10},{10,1... | collective-permute-start | bytes 811016 | tf_op jit(solution)/shard_map/ppermute | solution.py:383
  7.0 20.1 %collective-permute-start.1 = (bf16[528,256]{1,0:T(8,128)(2,1)}, bf16[528,256]{1,0:T(8,128)(2,1)S(1)}, u32[]{:S(2)}, u32[]{:S(2)}) collective-permute-start(bf16[528,256]{1,0:T(8,128)(2,1)} %get-tuple-element.41.t0), channel_id=1, source_target_pairs={{0,3},{1,0},{2,1},{3,2},{4,7},{5,4},{6,5},{7,6},{8,11},{9,8},{10,9... | collective-permute-start | bytes 811016 | tf_op jit(solution)/shard_map/ppermute | solution.py:383
  9.2 30.2 %collective-permute-start.4 = (bf16[1088,256]{1,0:T(8,128)(2,1)}, bf16[1088,256]{1,0:T(8,128)(2,1)S(1)}, u32[]{:S(2)}, u32[]{:S(2)}) collective-permute-start(bf16[1088,256]{1,0:T(8,128)(2,1)} %get-tuple-element.37.s0), channel_id=1, source_target_pairs={{0,4},{1,5},{2,6},{3,7},{4,8},{5,9},{6,10},{7,11},{8,12},{9,13},{1... | collective-permute-start | bytes 1671176 | tf_op jit(solution)/shard_map/ppermute | solution.py:383
  10.7 28.7 %collective-permute-start.5 = (bf16[1088,256]{1,0:T(8,128)(2,1)}, bf16[1088,256]{1,0:T(8,128)(2,1)S(1)}, u32[]{:S(2)}, u32[]{:S(2)}) collective-permute-start(bf16[1088,256]{1,0:T(8,128)(2,1)} %get-tuple-element.37.s0), channel_id=1, source_target_pairs={{0,12},{1,13},{2,14},{3,15},{4,0},{5,1},{6,2},{7,3},{8,4},{9,5},{1... | collective-permute-start | bytes 1671176 | tf_op jit(solution)/shard_map/ppermute | solution.py:383
  12.4 27.0 %collective-permute-start.6 = (bf16[1088,256]{1,0:T(8,128)(2,1)}, bf16[1088,256]{1,0:T(8,128)(2,1)S(1)}, u32[]{:S(2)}, u32[]{:S(2)}) collective-permute-start(bf16[1088,256]{1,0:T(8,128)(2,1)} %get-tuple-element.37.s0), channel_id=1, source_target_pairs={{0,8},{1,9},{2,10},{3,11},{4,12},{5,13},{6,14},{7,15},{8,0},{9,1},... | collective-permute-start | bytes 1671176 | tf_op jit(solution)/shard_map/ppermute | solution.py:383
  14.2 1.2 %copy-start.4 = (bf16[8,128,512]{2,1,0:T(8,128)(2,1)S(1)}, bf16[8,128,512]{2,1,0:T(8,128)(2,1)}, u32[]{:S(2)}) copy-start(bf16[8,128,512]{2,1,0:T(8,128)(2,1)} %get-tuple-element.33.own) | copy-start | bytes 3145732
  15.5 11.7 %copy-start.1 = (bf16[528,256]{1,0:T(8,128)(2,1)S(1)}, bf16[528,256]{1,0:T(8,128)(2,1)}, u32[]{:S(2)}) copy-start(bf16[528,256]{1,0:T(8,128)(2,1)} %get-tuple-element.41.t0) | copy-start | bytes 811012
  15.5 24.0 %copy-start = (bf16[1088,256]{1,0:T(8,128)(2,1)S(1)}, bf16[1088,256]{1,0:T(8,128)(2,1)}, u32[]{:S(2)}) copy-start(bf16[1088,256]{1,0:T(8,128)(2,1)} %get-tuple-element.37.s0) | copy-start | bytes 1671172
  15.5 24.0 %copy-start.9 = (bf16[1,64,256]{2,1,0:T(8,128)(2,1)S(1)}, bf16[1,64,256]{2,1,0:T(8,128)(2,1)}, u32[]{:S(2)}) copy-start(bf16[1,64,256]{2,1,0:T(8,128)(2,1)} %param.12) | copy-start | bytes 98308
  26.2 1.0 %copy-start.7 = (f32[8,64,512]{2,1,0:T(8,128)}, f32[8,64,512]{2,1,0:T(8,128)S(1)}, u32[]{:S(2)}) copy-start(f32[8,64,512]{2,1,0:T(8,128)S(1)} %near_own.1.given) | copy-start | bytes 3145732
  27.1 10.9 %collective-permute-start.8 = (bf16[528,256]{1,0:T(8,128)(2,1)S(1)}, bf16[528,256]{1,0:T(8,128)(2,1)S(1)}, u32[]{:S(2)}, u32[]{:S(2)}) collective-permute-start(bf16[528,256]{1,0:T(8,128)(2,1)S(1)} %copy-done.1), channel_id=1, source_target_pairs={{0,2},{1,3},{2,0},{3,1},{4,6},{5,7},{6,4},{7,5},{8,10},{9,11},{10,... | collective-permute-start | bytes 811016 | tf_op jit(solution)/shard_map/ppermute | solution.py:383
  28.1 42.2 %collective-permute-start.2 = (bf16[8,128,512]{2,1,0:T(8,128)(2,1)}, bf16[8,128,512]{2,1,0:T(8,128)(2,1)S(1)}, u32[]{:S(2)}, u32[]{:S(2)}) collective-permute-start(bf16[8,128,512]{2,1,0:T(8,128)(2,1)} %get-tuple-element.33.own), channel_id=1, source_target_pairs={{0,1},{1,2},{2,3},{3,4},{4,5},{5,6},{6,7},{7,8},{8,9},{9,10},{10,1... | collective-permute-start | bytes 3145736 | tf_op jit(solution)/shard_map/ppermute | solution.py:412
  38.1 32.2 %collective-permute-start.3 = (bf16[8,128,512]{2,1,0:T(8,128)(2,1)}, bf16[8,128,512]{2,1,0:T(8,128)(2,1)S(1)}, u32[]{:S(2)}, u32[]{:S(2)}) collective-permute-start(bf16[8,128,512]{2,1,0:T(8,128)(2,1)} %get-tuple-element.33.own), channel_id=1, source_target_pairs={{1,0},{2,1},{3,2},{4,3},{5,4},{6,5},{7,6},{8,7},{9,8},{10,9},{11,1... | collective-permute-start | bytes 3145736 | tf_op jit(solution)/shard_map/ppermute | solution.py:413
  39.5 11.3 %collective-permute-start.7 = (bf16[128,256]{1,0:T(8,128)(2,1)S(1)}, bf16[128,256]{1,0:T(8,128)(2,1)S(1)}, u32[]{:S(2)}, u32[]{:S(2)}) collective-permute-start(bf16[128,256]{1,0:T(8,128)(2,1)S(1)} %pad_maximum_fusion.1.mine), channel_id=1, source_target_pairs={{0,16},{16,0},{32,48},{48,32},{64,80},{80,64},{96,112},{112,96},{1... | collective-permute-start | bytes 196616 | tf_op jit(solution)/shard_map/ppermute | solution.py:389
  50.8 11.1 %collective-permute-start.9 = (bf16[256,256]{1,0:T(8,128)(2,1)S(1)}, bf16[256,256]{1,0:T(8,128)(2,1)S(1)}, u32[]{:S(2)}, u32[]{:S(2)}) collective-permute-start(bf16[256,256]{1,0:T(8,128)(2,1)S(1)} %pad_maximum_fusion), channel_id=1, source_target_pairs={{0,32},{16,48},{32,64},{48,80},{64,96},{80,112},{96,0},{112,16},{1... | collective-permute-start | bytes 393224 | tf_op jit(solution)/shard_map/ppermute | solution.py:390
  51.3 10.6 %collective-permute-start.10 = (bf16[256,256]{1,0:T(8,128)(2,1)S(1)}, bf16[256,256]{1,0:T(8,128)(2,1)S(1)}, u32[]{:S(2)}, u32[]{:S(2)}) collective-permute-start(bf16[256,256]{1,0:T(8,128)(2,1)S(1)} %pad_maximum_fusion), channel_id=1, source_target_pairs={{0,96},{16,112},{32,0},{48,16},{64,32},{80,48},{96,64},{112,80},{1... | collective-permute-start | bytes 393224 | tf_op jit(solution)/shard_map/ppermute | solution.py:390
  54.1 7.8 %collective-permute-start.11 = (bf16[256,256]{1,0:T(8,128)(2,1)S(1)}, bf16[256,256]{1,0:T(8,128)(2,1)S(1)}, u32[]{:S(2)}, u32[]{:S(2)}) collective-permute-start(bf16[256,256]{1,0:T(8,128)(2,1)S(1)} %pad_maximum_fusion), channel_id=1, source_target_pairs={{0,64},{16,80},{32,96},{48,112},{64,0},{80,16},{96,32},{112,48},{1... | collective-permute-start | bytes 393224 | tf_op jit(solution)/shard_map/ppermute | solution.py:390
  62.0 8.3 %copy-start.5 = (bf16[8,128,512]{2,1,0:T(8,128)(2,1)S(1)}, bf16[8,128,512]{2,1,0:T(8,128)(2,1)}, u32[]{:S(2)}) copy-start(bf16[8,128,512]{2,1,0:T(8,128)(2,1)} %get-tuple-element.33.own) | copy-start | bytes 3145732
  62.0 8.3 %copy-start.8 = (f32[8,64,512]{2,1,0:T(8,128)S(1)}, f32[8,64,512]{2,1,0:T(8,128)}, u32[]{:S(2)}) copy-start(f32[8,64,512]{2,1,0:T(8,128)} %copy-done.7) | copy-start | bytes 3145732
  62.8 18.5 %collective-permute-start.12 = (bf16[576,256]{1,0:T(8,128)(2,1)S(1)}, bf16[576,256]{1,0:T(8,128)(2,1)S(1)}, u32[]{:S(2)}, u32[]{:S(2)}) collective-permute-start(bf16[576,256]{1,0:T(8,128)(2,1)S(1)} %get-tuple-element.53), channel_id=1, source_target_pairs={{0,3},{1,0},{2,1},{3,2},{4,7},{5,4},{6,5},{7,6},{8,11},{9,8},{10,9... | collective-permute-start | bytes 884744 | tf_op jit(solution)/shard_map/ppermute | solution.py:383
  68.7 16.0 %collective-permute-start.13 = (bf16[576,256]{1,0:T(8,128)(2,1)S(1)}, bf16[576,256]{1,0:T(8,128)(2,1)S(1)}, u32[]{:S(2)}, u32[]{:S(2)}) collective-permute-start(bf16[576,256]{1,0:T(8,128)(2,1)S(1)} %get-tuple-element.54), channel_id=1, source_target_pairs={{0,1},{1,2},{2,3},{3,0},{4,5},{5,6},{6,7},{7,4},{8,9},{9,10},{10,1... | collective-permute-start | bytes 884744 | tf_op jit(solution)/shard_map/ppermute | solution.py:383
  68.7 16.0 %copy-start.2 = (bf16[8,512,256]{2,1,0:T(8,128)(2,1)S(1)}, bf16[8,512,256]{2,1,0:T(8,128)(2,1)}, u32[]{:S(2)}) copy-start(bf16[8,512,256]{2,1,0:T(8,128)(2,1)} %basis.3) | copy-start | bytes 6291460
  68.7 16.0 %copy-start.3 = (bf16[8,256,256]{2,1,0:T(8,128)(2,1)S(1)}, bf16[8,256,256]{2,1,0:T(8,128)(2,1)}, u32[]{:S(2)}) copy-start(bf16[8,256,256]{2,1,0:T(8,128)(2,1)} %transfer.3) | copy-start | bytes 3145732
  68.7 16.0 %collective-permute-start.14 = (bf16[576,256]{1,0:T(8,128)(2,1)S(1)}, bf16[576,256]{1,0:T(8,128)(2,1)S(1)}, u32[]{:S(2)}, u32[]{:S(2)}) collective-permute-start(bf16[576,256]{1,0:T(8,128)(2,1)S(1)} %get-tuple-element.55), channel_id=1, source_target_pairs={{0,2},{1,3},{2,0},{3,1},{4,6},{5,7},{6,4},{7,5},{8,10},{9,11},{10,... | collective-permute-start | bytes 884744 | tf_op jit(solution)/shard_map/ppermute | solution.py:383

commit v5 on v4

--- a/solution.py
+++ b/solution.py
@@ -16,7 +16,7 @@
 LD = 8
 SIDE = 4
 AUG = 128
-UNROLL = 2
+UNROLL = 8
 VM = pl.BlockSpec(memory_space=pltpu.VMEM)
 SM = pl.BlockSpec(memory_space=pltpu.SMEM)
 
@@ -158,58 +158,94 @@
     return [lax.rem(x + shift, SIDE) * SIDE + z for shift in (0, SIDE - 1, 1, 2)]
 
 
-def far_loop(ids, place, side, sources, targets, outs, base):
-    columns = columns_of(place)
-    for b, (target, out) in enumerate(zip(targets, outs)):
-
-        @pl.loop(0, LD, unroll=UNROLL)
-        def _(leaf, b=b, target=target, out=out):
-            out[rows_of(leaf), :] = far_total(
-                ids, columns, (base + b) * LD + leaf, target[rows_of(leaf), :], side,
-                lambda d, at: charges_at(sources[d], at),
-            ).astype(out.dtype)
-
-
-def far_a_kernel(ids, place, s0, s1, s2, s3, t0, t1, o0, o1, side):
-    for d, source in enumerate((s0, s1, s2, s3)):
+def near_sources(ids, columns, side, sources, target, out, base):
+    @pl.loop(0, LD, unroll=UNROLL)
+    def _(leaf):
+        out[rows_of(leaf), :] = far_total(
+            ids, columns, base * LD + leaf, target[rows_of(leaf), :], side,
+            lambda d, at: charges_at(sources[d], at),
+        ).astype(out.dtype)
+
+
+def far_a_kernel(ids, place, s0, s1, s2, t0, t1, t2, o0, o1, o2, side):
+    sources = (s0, s1, s2)
+    for d, source in enumerate(sources):
 
         @pl.loop(0, LD, unroll=UNROLL)
         def _(leaf, d=d, source=source):
             side[d * LD + leaf] = source_side(skeleton_at(source, leaf))
 
-    far_loop(ids, place, side, (s0, s1, s2, s3), (t0, t1), (o0, o1), 0)
+    columns = columns_of(place)[:3]
+    for b, (target, out) in enumerate(((t0, o0), (t1, o1), (t2, o2))):
+        near_sources(ids, columns, side, sources, target, out, b)
 
 
 def far_a(ids, place, sources, targets):
     return pl.pallas_call(
         far_a_kernel,
         in_specs=[SM, SM] + [VM] * 6,
-        out_specs=[VM] * 3,
-        out_shape=[
-            jax.ShapeDtypeStruct((LD * F, SK), F32),
-            jax.ShapeDtypeStruct((LD * F, SK), BF),
-            jax.ShapeDtypeStruct((SIDE * LD, SK, AUG), BF),
-        ],
+        out_specs=[VM] * 4,
+        out_shape=[jax.ShapeDtypeStruct((LD * F, SK), F32)] * 3
+        + [jax.ShapeDtypeStruct((3 * LD, SK, AUG), BF)],
         compiler_params=params(16),
         cost_estimate=cost(9),
         name="far_a",
     )(ids, place, *sources, *targets)
 
 
-def far_b_kernel(ids, place, side, s0, s1, s2, s3, t2, t3, o2, o3):
-    far_loop(ids, place, side, (s0, s1, s2, s3), (t2, t3), (o2, o3), 2)
-
-
-def far_b(ids, place, side, sources, targets):
+def far_b_kernel(ids, place, given, s0, s1, s2, s3, t3, o3, last, side):
+    sources = (s0, s1, s2, s3)
+
+    @pl.loop(0, LD, unroll=UNROLL)
+    def _(leaf):
+        value = source_side(skeleton_at(s3, leaf))
+        side[3 * LD + leaf] = value
+        last[leaf] = value
+
+    side[: 3 * LD] = given[...]
+    near_sources(ids, columns_of(place), side, sources, t3, o3, 3)
+
+
+def far_b(ids, place, side, sources, target):
     return pl.pallas_call(
         far_b_kernel,
-        in_specs=[SM, SM] + [VM] * 7,
+        in_specs=[SM, SM] + [VM] * 6,
         out_specs=[VM] * 2,
-        out_shape=[jax.ShapeDtypeStruct((LD * F, SK), BF)] * 2,
-        compiler_params=params(16),
-        cost_estimate=cost(7),
+        out_shape=[
+            jax.ShapeDtypeStruct((LD * F, SK), BF),
+            jax.ShapeDtypeStruct((LD, SK, AUG), BF),
+        ],
+        scratch_shapes=[pltpu.VMEM((SIDE * LD, SK, AUG), BF)],
+        compiler_params=params(16),
+        cost_estimate=cost(4),
         name="far_b",
-    )(ids, place, side, *sources, *targets)
+    )(ids, place, side, *sources, target)
+
+
+def far_c_kernel(ids, place, side, s3, t0, t1, t2, a0, a1, a2, own, r1, r2):
+    columns = columns_of(place)[3:]
+    for b, (target, given, out) in enumerate(((t0, a0, own), (t1, a1, r1), (t2, a2, r2))):
+
+        @pl.loop(0, LD, unroll=UNROLL)
+        def _(leaf, b=b, target=target, given=given, out=out):
+            total = far_total(
+                ids, columns, b * LD + leaf, target[rows_of(leaf), :], side,
+                lambda d, at: charges_at(s3, at),
+            )
+            out[rows_of(leaf), :] = (given[rows_of(leaf), :] + total).astype(out.dtype)
+
+
+def far_c(ids, place, side, source, targets, given):
+    return pl.pallas_call(
+        far_c_kernel,
+        in_specs=[SM, SM] + [VM] * 8,
+        out_specs=[VM] * 3,
+        out_shape=[jax.ShapeDtypeStruct((LD * F, SK), F32)]
+        + [jax.ShapeDtypeStruct((LD * F, SK), BF)] * 2,
+        compiler_params=params(16),
+        cost_estimate=cost(4),
+        name="far_c",
+    )(ids, place, side, source, *targets, *given)
 
 
 def top_kernel(mine, pair, n1, n2, n3, a1, a2, a3, top, r1, r2, r3):
@@ -241,7 +277,7 @@
     )(mine, pair, *others, *parts)
 
 
-def near_groups(ids, leaf, place_of, points, side, rights, slots):
+def near_groups(ids, leaf, place_of, points, side, rights, slots, out, given=None):
     count = jnp.int32(0)
     for d in range(ids.shape[1]):
         slots[d] = 0
@@ -251,29 +287,34 @@
         count += here.astype(jnp.int32)
     size = 4
 
-    def group(g, total):
-        weights, tiles = [], []
-        for d in range(size):
-            k = g * size + d
-            at = slots[k]
+    def group(start, used, total):
+        tiles, weights = [], []
+        for d in range(used):
+            at = slots[start + d]
             tiles.append(
                 jnp.exp(jnp.dot(side[at], points, preferred_element_type=F32)).astype(BF)
             )
-            weight = rights(at)
-            weights.append(jnp.where(k < count, weight, jnp.zeros_like(weight)))
+            weights.append(rights(at))
         return total + jnp.dot(
             jnp.concatenate(weights, axis=1),
             jnp.concatenate(tiles, axis=0),
             preferred_element_type=F32,
         )
 
-    return lax.fori_loop(
-        0, lax.div(count + size - 1, size), group, jnp.zeros((RHS, LP), F32)
-    )
+    full = lax.div(count, size)
+    total = lax.fori_loop(
+        0, full, lambda g, t: group(g * size, size, t), jnp.zeros((RHS, LP), F32)
+    )
+    out[...] = total if given is None else total + given[...]
+    for used in range(1, size):
+
+        @pl.when(count - full * size == used)
+        def _(used=used):
+            out[...] = group(full * size, used, out[...])
 
 
 def near_own_kernel(ids, first, own, out, side, slots):
-    @pl.loop(0, LD, unroll=2)
+    @pl.loop(0, LD, unroll=4)
     def _(leaf):
         side[leaf] = source_side(own[leaf, :F, :])
 
@@ -284,8 +325,8 @@
     @pl.loop(0, LD)
     def _(leaf):
         points = target_side(own[leaf, :F, :])
-        out[leaf] = near_groups(
-            ids, leaf, place_of, points, side, lambda at: own[at, F:, :], slots
+        near_groups(
+            ids, leaf, place_of, points, side, lambda at: own[at, F:, :], slots, out.at[leaf]
         )
 
 
@@ -305,7 +346,7 @@
 def near_rest_kernel(ids, first, own, before, after, given, out, side, rights, slots):
     for d, block in enumerate((before, after)):
 
-        @pl.loop(0, LD, unroll=2)
+        @pl.loop(0, LD, unroll=4)
         def _(leaf, d=d, block=block):
             side[d * LD + leaf] = source_side(block[leaf, :F, :])
             rights[d * LD + leaf] = block[leaf, F:, :]
@@ -319,8 +360,9 @@
     @pl.loop(0, LD)
     def _(leaf):
         points = target_side(own[leaf, :F, :])
-        out[leaf] = given[leaf] + near_groups(
-            ids, leaf, place_of, points, side, lambda at: rights[at], slots
+        near_groups(
+            ids, leaf, place_of, points, side, lambda at: rights[at], slots, out.at[leaf],
+            given.at[leaf],
         )
 
 
@@ -403,28 +445,34 @@
     first = (position * LD).astype(jnp.int32).reshape(1)
     near_sum = near_own(neighbours, first, near_msg)
 
-    targets, target_msg, near_msg, near_sum = lax.optimization_barrier(
-        (targets, target_msg, near_msg, near_sum)
-    )
-    targets.append(shifted(target_msg, 0, 2))
+    targets, sources[:3], near_msg, near_sum = lax.optimization_barrier(
+        (targets, sources[:3], near_msg, near_sum)
+    )
+    targets.append(shifted(targets[0], 0, 2))
     count = lax.axis_size("leaf") * lax.axis_size("top")
     up = [(i, i + 1) for i in range(count - 1)]
     before = lax.ppermute(near_msg, ("leaf", "top"), up)
     after = lax.ppermute(near_msg, ("leaf", "top"), [(j, i) for i, j in up])
 
-    sources, near_sum = lax.optimization_barrier((sources, near_sum))
+    def ids_of(which):
+        ids = jnp.concatenate([t[LD * F : LD * F + LD, : SIDE * SIDE] for t in which])
+        return ids.astype(jnp.int32)
+
+    place = jnp.stack([at // SIDE, at % SIDE]).astype(jnp.int32)
+    *given, side = far_a(ids_of(targets[:3]), place, sources[:3], targets[:3])
+    sources[3], given, side, targets[3] = lax.optimization_barrier(
+        (sources[3], given, side, targets[3])
+    )
     line_charge = sum(s[2 * LD * F :].astype(F32) for s in sources)
     mine = jnp.concatenate([line_charge.astype(BF), node_points[0]], axis=0)
     pair = leaf_shifted(mine, 0)
-    ids = jnp.concatenate([t[LD * F : LD * F + LD, : SIDE * SIDE] for t in targets])
-    ids = ids.astype(jnp.int32)
-    place = jnp.stack([at // SIDE, at % SIDE]).astype(jnp.int32)
-    own, part1, side = far_a(ids, place, sources, targets[:2])
-    pair, own, side = lax.optimization_barrier((pair, own, side))
+    ids = ids_of(targets)
+    r3, last = far_b(ids, place, side, sources, targets[3])
+    pair, r3, last = lax.optimization_barrier((pair, r3, last))
     both = jnp.concatenate([mine, pair], axis=0)
     others = [leaf_shifted(both, dy) for dy in (1, -1, 2)]
-    parts = [part1] + list(far_b(ids, place, side, sources, targets[2:]))
-    top, *parts = top_sum(mine, pair, others, parts)
+    own, r1, r2 = far_c(ids, place, last, sources[3], targets[:3], given)
+    top, *parts = top_sum(mine, pair, others, (r1, r2, r3))
     returned = [shifted(r, 0, dz) for r, dz in zip(parts, (-1, 1, 2))]
     near_sum = near_rest(neighbours, first, near_msg, before, after, near_sum)
     return final(near_sum, leaf_basis, transfer, own, returned, top)

time: 87.9 us -> 107 us (1.22)
  waiting for transfers between devices: 11 us -> 28.9 us
  starting transfers between devices: 30.9 us -> 35.6 us
  Pallas kernels: 43.1 us -> 39.9 us
    ppermute x9, waiting for transfers between devices: 11 us -> 28.4 us  [shifted(): return lax.ppermute(value, 'top', pairs)]
    ppermute x3, starting transfers between devices: 4.25 us -> 14.8 us  [leaf_shifted(): lax.ppermute(value, 'leaf', [(i, (i + 2 * dy) % count) for i in range(cou...]
    pallas_call x1, Pallas kernels: 8.44 us -> 5.37 us  [near_rest(): pl.pallas_call(near_rest_kernel, in_specs=[SM, SM, VM, VM, VM, VM], out_s...]
    pallas_call x1 -> x2, Pallas kernels: 6.84 us -> 9.39 us  [the longest x1 5.89 us: far_c(): pl.pallas_call(far_c_kernel, in_specs=[SM, SM] + [VM] * 8, out_specs=[VM]...]
    ppermute x1, starting transfers between devices: 2.81 us -> 0.27 us  [leaf_shifted(): return lax.ppermute(value, 'leaf', [(i, i ^ 1) for i in range(count)])]
    pallas_call x1, Pallas kernels: 8.51 us -> 6.72 us  [far_a(): pl.pallas_call(far_a_kernel, in_specs=[SM, SM] + [VM] * 6, out_specs=[VM]...]
    ppermute x9, starting transfers between devices: 17.6 us -> 15.9 us  [shifted(): return lax.ppermute(value, 'top', pairs)]
    ppermute x1, starting transfers between devices: 4.99 us -> 3.44 us  [on_device(): before = lax.ppermute(near_msg, ('leaf', 'top'), up)]
  transfers between devices with their start and end apart: 15 -> 15, of which waited for: 3 -> 5; matrix products, arithmetic and copies ran while one was open for 0% -> 0% of each run, Pallas kernels for 40% -> 30%
where the time goes in v5:
time: 107 us
  Pallas kernels  39.9 us (37%)
  starting transfers between devices  35.6 us (33%)
  waiting for transfers between devices  28.9 us (27%)
  local copies, waits for them, and re-layouts  2.21 us (2%)
    ppermute x9, waiting for transfers between devices, shifted(): return lax.ppermute(value, 'top', pairs)  28.4 us
    ppermute x9, starting transfers between devices, shifted(): return lax.ppermute(value, 'top', pairs)  15.9 us
    ppermute x3, starting transfers between devices, leaf_shifted(): lax.ppermute(value, 'leaf', [(i, (i + 2 * dy) % count) for i in range(cou...  14.8 us
    pallas_call x1, Pallas kernels, near_own(): pl.pallas_call(near_own_kernel, in_specs=[SM, SM, VM], out_specs=VM, out_...  9.76 us
    pallas_call x1, Pallas kernels, far_a(): pl.pallas_call(far_a_kernel, in_specs=[SM, SM] + [VM] * 6, out_specs=[VM]...  6.72 us
    pallas_call x1, Pallas kernels, far_c(): pl.pallas_call(far_c_kernel, in_specs=[SM, SM] + [VM] * 8, out_specs=[VM]...  5.89 us
    pallas_call x1, Pallas kernels, near_rest(): pl.pallas_call(near_rest_kernel, in_specs=[SM, SM, VM, VM, VM, VM], out_s...  5.37 us
    pallas_call x1, Pallas kernels, prep(): pl.pallas_call(prep_kernel, in_specs=[anywhere] * 4 + [VM] * 2, out_specs...  4.89 us
  transfers between devices with their start and end apart: 15, of which 5 were waited for; matrix products, arithmetic and copies ran while one was open for 0% of the time, Pallas kernels for 30%

profile of v5, /device:TPU:0, one launch (start us, length us, event | category | flops | bytes accessed | tf_op | source)
XLA Modules:
  0.0 107.0 jit_solution(5426233014449119778)
XLA Ops:
  0.0 0.0 copy-start.6
  0.0 4.9 %prep.1 = (bf16[8,128,512]{2,1,0:T(8,128)(2,1)}, bf16[1088,256]{1,0:T(8,128)(2,1)}, bf16[528,256]{1,0:T(8,128)(2,1)}) custom-call(bf16[8,64,512]{2,1,0:T(8,128)(2,1)} %points.1, bf16[8,64,512]{2,1,0:T(8,128)(2,1)} %sides.1, bf16[8,512,256]{2,1,0:T(8,128)(2,1)} %basis.3, bf16[8,256,256]{2,1,0:T(8,128)(2,1)} %transfer.3, s32[8,256]{1,0:T(8,128)} %skeleton.1, ...), custom_call_target="tpu_custom_call" | custom-call | flops 4000000000 | bytes 1000000 | tf_op jit(solution)/shard_map/prep/pallas_call | solution.py:100
  4.9 2.1 %collective-permute-start = (bf16[528,256]{1,0:T(8,128)(2,1)}, bf16[528,256]{1,0:T(8,128)(2,1)S(1)}, u32[]{:S(2)}, u32[]{:S(2)}) collective-permute-start(bf16[528,256]{1,0:T(8,128)(2,1)} %get-tuple-element.43.t0), channel_id=1, source_target_pairs={{0,1},{1,2},{2,3},{3,0},{4,5},{5,6},{6,7},{7,4},{8,9},{9,10},{10,1... | collective-permute-start | bytes 811016 | tf_op jit(solution)/shard_map/ppermute | solution.py:425
  7.0 2.2 %collective-permute-start.1 = (bf16[528,256]{1,0:T(8,128)(2,1)}, bf16[528,256]{1,0:T(8,128)(2,1)S(1)}, u32[]{:S(2)}, u32[]{:S(2)}) collective-permute-start(bf16[528,256]{1,0:T(8,128)(2,1)} %get-tuple-element.43.t0), channel_id=1, source_target_pairs={{0,3},{1,0},{2,1},{3,2},{4,7},{5,4},{6,5},{7,6},{8,11},{9,8},{10,9... | collective-permute-start | bytes 811016 | tf_op jit(solution)/shard_map/ppermute | solution.py:425
  9.2 1.5 %collective-permute-start.2 = (bf16[1088,256]{1,0:T(8,128)(2,1)}, bf16[1088,256]{1,0:T(8,128)(2,1)S(1)}, u32[]{:S(2)}, u32[]{:S(2)}) collective-permute-start(bf16[1088,256]{1,0:T(8,128)(2,1)} %get-tuple-element.46.s0), channel_id=1, source_target_pairs={{0,4},{1,5},{2,6},{3,7},{4,8},{5,9},{6,10},{7,11},{8,12},{9,13},{1... | collective-permute-start | bytes 1671176 | tf_op jit(solution)/shard_map/ppermute | solution.py:425
  10.7 1.7 %collective-permute-start.3 = (bf16[1088,256]{1,0:T(8,128)(2,1)}, bf16[1088,256]{1,0:T(8,128)(2,1)S(1)}, u32[]{:S(2)}, u32[]{:S(2)}) collective-permute-start(bf16[1088,256]{1,0:T(8,128)(2,1)} %get-tuple-element.46.s0), channel_id=1, source_target_pairs={{0,12},{1,13},{2,14},{3,15},{4,0},{5,1},{6,2},{7,3},{8,4},{9,5},{1... | collective-permute-start | bytes 1671176 | tf_op jit(solution)/shard_map/ppermute | solution.py:425
  12.4 1.8 %collective-permute-start.6 = (bf16[1088,256]{1,0:T(8,128)(2,1)}, bf16[1088,256]{1,0:T(8,128)(2,1)S(1)}, u32[]{:S(2)}, u32[]{:S(2)}) collective-permute-start(bf16[1088,256]{1,0:T(8,128)(2,1)} %get-tuple-element.46.s0), channel_id=1, source_target_pairs={{0,8},{1,9},{2,10},{3,11},{4,12},{5,13},{6,14},{7,15},{8,0},{9,1},... | collective-permute-start | bytes 1671176 | tf_op jit(solution)/shard_map/ppermute | solution.py:425
  14.2 0.0 copy-done.6
  14.2 0.0 copy-start.4
  14.2 1.2 %copy-done.4 = bf16[8,128,512]{2,1,0:T(8,128)(2,1)S(1)} copy-done((bf16[8,128,512]{2,1,0:T(8,128)(2,1)S(1)}, bf16[8,128,512]{2,1,0:T(8,128)(2,1)}, u32[]{:S(2)}) %copy-start.4) | copy-done | bytes 1048600
  15.5 0.0 copy-start.1
  15.5 0.0 copy-start
  15.5 9.8 %near_own.1.given = f32[8,64,512]{2,1,0:T(8,128)S(1)} custom-call(s32[8,8]{1,0:T(8,128)S(1)} %copy-done.6, s32[1]{0:T(128)} %bitcast.first, bf16[8,128,512]{2,1,0:T(8,128)(2,1)S(1)} %copy-done.4), custom_call_target="tpu_custom_call" | custom-call | flops 8999999488 | bytes 1000000 | tf_op jit(solution)/shard_map/near_own/pallas_call | solution.py:334
  25.2 0.0 copy-start.7
  25.2 0.9 copy-done.7
  26.2 0.1 pad_add_fusion.place
  26.3 0.0 collective-permute-done.t1
  26.3 0.0 collective-permute-done.1.t2
  26.3 0.0 collective-permute-done.2.s1
  26.3 8.0 %collective-permute-done.3.s2 = bf16[1088,256]{1,0:T(8,128)(2,1)S(1)} collective-permute-done((bf16[1088,256]{1,0:T(8,128)(2,1)}, bf16[1088,256]{1,0:T(8,128)(2,1)S(1)}, u32[]{:S(2)}, u32[]{:S(2)}) %collective-permute-start.3) | collective-permute-done | bytes 557088 | tf_op jit(solution)/shard_map/ppermute | solution.py:425
  34.3 3.4 %collective-permute-start.4 = (bf16[8,128,512]{2,1,0:T(8,128)(2,1)}, bf16[8,128,512]{2,1,0:T(8,128)(2,1)S(1)}, u32[]{:S(2)}, u32[]{:S(2)}) collective-permute-start(bf16[8,128,512]{2,1,0:T(8,128)(2,1)} %get-tuple-element.41.own), channel_id=1, source_target_pairs={{0,1},{1,2},{2,3},{3,4},{4,5},{5,6},{6,7},{7,8},{8,9},{9,10},{10,1... | collective-permute-start | bytes 3145736 | tf_op jit(solution)/shard_map/ppermute | solution.py:454
  37.7 1.3 %collective-permute-start.5 = (bf16[8,128,512]{2,1,0:T(8,128)(2,1)}, bf16[8,128,512]{2,1,0:T(8,128)(2,1)S(1)}, u32[]{:S(2)}, u32[]{:S(2)}) collective-permute-start(bf16[8,128,512]{2,1,0:T(8,128)(2,1)} %get-tuple-element.41.own), channel_id=1, source_target_pairs={{1,0},{2,1},{3,2},{4,3},{5,4},{6,5},{7,6},{8,7},{9,8},{10,9},{11,1... | collective-permute-start | bytes 3145736 | tf_op jit(solution)/shard_map/ppermute | solution.py:455
  39.0 0.0 copy-done.1
  39.0 4.4 %collective-permute-start.7 = (bf16[528,256]{1,0:T(8,128)(2,1)S(1)}, bf16[528,256]{1,0:T(8,128)(2,1)S(1)}, u32[]{:S(2)}, u32[]{:S(2)}) collective-permute-start(bf16[528,256]{1,0:T(8,128)(2,1)S(1)} %copy-done.1), channel_id=1, source_target_pairs={{0,2},{1,3},{2,0},{3,1},{4,6},{5,7},{6,4},{7,5},{8,10},{9,11},{10,... | collective-permute-start | bytes 811016 | tf_op jit(solution)/shard_map/ppermute | solution.py:425
  43.5 0.0 copy-done
  43.5 0.0 copy-start.9
  43.5 6.7 %far_a.1 = (f32[512,256]{1,0:T(8,128)S(1)}, f32[512,256]{1,0:T(8,128)S(1)}, f32[512,256]{1,0:T(8,128)S(1)}, bf16[24,256,128]{2,1,0:T(8,128)(2,1)S(1)}) custom-call(s32[24,16]{1,0:T(8,128)S(1)} %maximum_convert_fusion.1.ids, s32[2]{0:T(128)S(1)} %pad_add_fusion.place, bf16[1088,256]{1,0:T(8,128)(2,1)S(1)} %copy-done, ...), custom_call_target="tpu_custom_call" | custom-call | flops 8999999488 | bytes 1000000 | tf_op jit(solution)/shard_map/far_a/pallas_call | solution.py:184
  50.2 0.0 collective-permute-done.6.s3
  50.2 11.6 %collective-permute-done.7.t3 = bf16[528,256]{1,0:T(8,128)(2,1)S(1)} collective-permute-done((bf16[528,256]{1,0:T(8,128)(2,1)S(1)}, bf16[528,256]{1,0:T(8,128)(2,1)S(1)}, u32[]{:S(2)}, u32[]{:S(2)}) %collective-permute-start.7) | collective-permute-done | bytes 270368 | tf_op jit(solution)/shard_map/ppermute | solution.py:425
  61.9 0.0 copy-done.9
  61.9 0.3 collective-permute-start.8
  62.2 3.5 %far_b.1 = (bf16[512,256]{1,0:T(8,128)(2,1)S(1)}, bf16[8,256,128]{2,1,0:T(8,128)(2,1)S(1)}) custom-call(s32[32,16]{1,0:T(8,128)S(1)} %maximum_convert_fusion.ids, s32[2]{0:T(128)S(1)} %pad_add_fusion.place, bf16[24,256,128]{2,1,0:T(8,128)(2,1)S(1)} %get-tuple-element.55.given, bf16[1088,256]{1,0:T(8,128)(2,1)S(1)} %copy-done, ...), custom_call_target="tpu_custom_call" | custom-call | flops 4000000000 | bytes 1000000 | tf_op jit(solution)/shard_map/far_b/pallas_call | solution.py:210
  65.7 0.0 collective-permute-done.8.pair
  65.7 11.8 %collective-permute-start.9 = (bf16[256,256]{1,0:T(8,128)(2,1)S(1)}, bf16[256,256]{1,0:T(8,128)(2,1)S(1)}, u32[]{:S(2)}, u32[]{:S(2)}) collective-permute-start(bf16[256,256]{1,0:T(8,128)(2,1)S(1)} %pad_maximum_fusion), channel_id=1, source_target_pairs={{0,32},{16,48},{32,64},{48,80},{64,96},{80,112},{96,0},{112,16},{1... | collective-permute-start | bytes 393224 | tf_op jit(solution)/shard_map/ppermute | solution.py:432
  77.4 1.4 %collective-permute-start.10 = (bf16[256,256]{1,0:T(8,128)(2,1)S(1)}, bf16[256,256]{1,0:T(8,128)(2,1)S(1)}, u32[]{:S(2)}, u32[]{:S(2)}) collective-permute-start(bf16[256,256]{1,0:T(8,128)(2,1)S(1)} %pad_maximum_fusion), channel_id=1, source_target_pairs={{0,96},{16,112},{32,0},{48,16},{64,32},{80,48},{96,64},{112,80},{1... | collective-permute-start | bytes 393224 | tf_op jit(solution)/shard_map/ppermute | solution.py:432
  78.9 1.6 %collective-permute-start.11 = (bf16[256,256]{1,0:T(8,128)(2,1)S(1)}, bf16[256,256]{1,0:T(8,128)(2,1)S(1)}, u32[]{:S(2)}, u32[]{:S(2)}) collective-permute-start(bf16[256,256]{1,0:T(8,128)(2,1)S(1)} %pad_maximum_fusion), channel_id=1, source_target_pairs={{0,64},{16,80},{32,96},{48,112},{64,0},{80,16},{96,32},{112,48},{1... | collective-permute-start | bytes 393224 | tf_op jit(solution)/shard_map/ppermute | solution.py:432
  80.5 5.9 %far_c.1 = (f32[512,256]{1,0:T(8,128)S(1)}, bf16[512,256]{1,0:T(8,128)(2,1)S(1)}, bf16[512,256]{1,0:T(8,128)(2,1)S(1)}) custom-call(s32[32,16]{1,0:T(8,128)S(1)} %maximum_convert_fusion.ids, s32[2]{0:T(128)S(1)} %pad_add_fusion.place, bf16[8,256,128]{2,1,0:T(8,128)(2,1)S(1)} %get-tuple-element.58.side, bf16[1088,256]{1,0:T(8,128)(2,1)S(1)} %collective-permute-done.6.s3, ...), custom_call_target="tpu_custom_call" | custom-call | flops 4000000000 | bytes 1000000 | tf_op jit(solution)/shard_map/far_c/pallas_call | solution.py:239
  86.4 0.0 collective-permute-done.9.n1
  86.4 0.0 collective-permute-done.10.n2
  86.4 0.6 collective-permute-done.11.n3
  86.9 0.0 copy-start.5
  86.9 0.0 copy-start.8
  86.9 0.8 top_sum.1
  87.8 0.1 collective-permute-start.12
  87.9 2.0 %collective-permute-start.13 = (bf16[576,256]{1,0:T(8,128)(2,1)S(1)}, bf16[576,256]{1,0:T(8,128)(2,1)S(1)}, u32[]{:S(2)}, u32[]{:S(2)}) collective-permute-start(bf16[576,256]{1,0:T(8,128)(2,1)S(1)} %get-tuple-element.68), channel_id=1, source_target_pairs={{0,1},{1,2},{2,3},{3,0},{4,5},{5,6},{6,7},{7,4},{8,9},{9,10},{10,1... | collective-permute-start | bytes 884744 | tf_op jit(solution)/shard_map/ppermute | solution.py:425
  89.9 0.0 copy-start.2
  89.9 0.0 copy-start.3
  89.9 0.0 collective-permute-start.14
  89.9 0.0 collective-permute-done.4.before
  89.9 0.0 collective-permute-done.5.after
  89.9 0.0 copy-done.5
  89.9 0.0 copy-done.8
  89.9 5.4 %near_rest.1.near_sum = f32[8,64,512]{2,1,0:T(8,128)S(1)} custom-call(s32[8,8]{1,0:T(8,128)S(1)} %copy-done.6, s32[1]{0:T(128)} %bitcast.first, bf16[8,128,512]{2,1,0:T(8,128)(2,1)S(1)} %copy-done.5, bf16[8,128,512]{2,1,0:T(8,128)(2,1)S(1)} %collective-permute-done.4.before, bf16[8,128,512]{2,1,0:T(8,128)(2,1)S(1)} %collective-permute-done.5.after, ...), custom_call_target="tpu_custom_call" | custom-call | flops 11000000512 | bytes 1000000 | tf_op jit(solution)/shard_map/near_rest/pallas_call | solution.py:370
  95.3 2.5 %collective-permute-done.12.r1 = bf16[576,256]{1,0:T(8,128)(2,1)S(1)} collective-permute-done((bf16[576,256]{1,0:T(8,128)(2,1)S(1)}, bf16[576,256]{1,0:T(8,128)(2,1)S(1)}, u32[]{:S(2)}, u32[]{:S(2)}) %collective-permute-start.12) | collective-permute-done | bytes 294944 | tf_op jit(solution)/shard_map/ppermute | solution.py:425
  97.8 6.3 %collective-permute-done.13.r2 = bf16[576,256]{1,0:T(8,128)(2,1)S(1)} collective-permute-done((bf16[576,256]{1,0:T(8,128)(2,1)S(1)}, bf16[576,256]{1,0:T(8,128)(2,1)S(1)}, u32[]{:S(2)}, u32[]{:S(2)}) %collective-permute-start.13) | collective-permute-done | bytes 294944 | tf_op jit(solution)/shard_map/ppermute | solution.py:425
  104.1 0.0 collective-permute-done.14.r3
  104.1 0.0 copy-done.2
  104.1 0.0 copy-done.3
  104.1 2.9 %final.1 = bf16[8,64,512]{2,1,0:T(8,128)(2,1)} custom-call(f32[8,64,512]{2,1,0:T(8,128)S(1)} %near_rest.1.near_sum, bf16[8,512,256]{2,1,0:T(8,128)(2,1)S(1)} %copy-done.2, bf16[8,256,256]{2,1,0:T(8,128)(2,1)S(1)} %copy-done.3, f32[512,256]{1,0:T(8,128)S(1)} %get-tuple-element.62.own, bf16[576,256]{1,0:T(8,128)(2,1)S(1)} %collective-permute-done.12.r1, ...), custom_call_target="tpu_custom_call" | custom-call | flops 3000000000 | bytes 1000000 | tf_op jit(solution)/shard_map/final/pallas_call | solution.py:408
  (9 shorter events, 0.1 us)
Async XLA Ops:
  0.0 14.2 %copy-start.6 = (s32[8,8]{1,0:T(8,128)S(1)}, s32[8,8]{1,0:T(8,128)}, u32[]{:S(2)}) copy-start(s32[8,8]{1,0:T(8,128)} %ids.3) | copy-start | bytes 772
  4.9 21.4 %collective-permute-start = (bf16[528,256]{1,0:T(8,128)(2,1)}, bf16[528,256]{1,0:T(8,128)(2,1)S(1)}, u32[]{:S(2)}, u32[]{:S(2)}) collective-permute-start(bf16[528,256]{1,0:T(8,128)(2,1)} %get-tuple-element.43.t0), channel_id=1, source_target_pairs={{0,1},{1,2},{2,3},{3,0},{4,5},{5,6},{6,7},{7,4},{8,9},{9,10},{10,1... | collective-permute-start | bytes 811016 | tf_op jit(solution)/shard_map/ppermute | solution.py:425
  7.0 19.3 %collective-permute-start.1 = (bf16[528,256]{1,0:T(8,128)(2,1)}, bf16[528,256]{1,0:T(8,128)(2,1)S(1)}, u32[]{:S(2)}, u32[]{:S(2)}) collective-permute-start(bf16[528,256]{1,0:T(8,128)(2,1)} %get-tuple-element.43.t0), channel_id=1, source_target_pairs={{0,3},{1,0},{2,1},{3,2},{4,7},{5,4},{6,5},{7,6},{8,11},{9,8},{10,9... | collective-permute-start | bytes 811016 | tf_op jit(solution)/shard_map/ppermute | solution.py:425
  9.2 17.1 %collective-permute-start.2 = (bf16[1088,256]{1,0:T(8,128)(2,1)}, bf16[1088,256]{1,0:T(8,128)(2,1)S(1)}, u32[]{:S(2)}, u32[]{:S(2)}) collective-permute-start(bf16[1088,256]{1,0:T(8,128)(2,1)} %get-tuple-element.46.s0), channel_id=1, source_target_pairs={{0,4},{1,5},{2,6},{3,7},{4,8},{5,9},{6,10},{7,11},{8,12},{9,13},{1... | collective-permute-start | bytes 1671176 | tf_op jit(solution)/shard_map/ppermute | solution.py:425
  10.7 23.6 %collective-permute-start.3 = (bf16[1088,256]{1,0:T(8,128)(2,1)}, bf16[1088,256]{1,0:T(8,128)(2,1)S(1)}, u32[]{:S(2)}, u32[]{:S(2)}) collective-permute-start(bf16[1088,256]{1,0:T(8,128)(2,1)} %get-tuple-element.46.s0), channel_id=1, source_target_pairs={{0,12},{1,13},{2,14},{3,15},{4,0},{5,1},{6,2},{7,3},{8,4},{9,5},{1... | collective-permute-start | bytes 1671176 | tf_op jit(solution)/shard_map/ppermute | solution.py:425
  12.4 37.8 %collective-permute-start.6 = (bf16[1088,256]{1,0:T(8,128)(2,1)}, bf16[1088,256]{1,0:T(8,128)(2,1)S(1)}, u32[]{:S(2)}, u32[]{:S(2)}) collective-permute-start(bf16[1088,256]{1,0:T(8,128)(2,1)} %get-tuple-element.46.s0), channel_id=1, source_target_pairs={{0,8},{1,9},{2,10},{3,11},{4,12},{5,13},{6,14},{7,15},{8,0},{9,1},... | collective-permute-start | bytes 1671176 | tf_op jit(solution)/shard_map/ppermute | solution.py:425
  14.2 1.2 %copy-start.4 = (bf16[8,128,512]{2,1,0:T(8,128)(2,1)S(1)}, bf16[8,128,512]{2,1,0:T(8,128)(2,1)}, u32[]{:S(2)}) copy-start(bf16[8,128,512]{2,1,0:T(8,128)(2,1)} %get-tuple-element.41.own) | copy-start | bytes 3145732
  15.5 23.6 %copy-start.1 = (bf16[528,256]{1,0:T(8,128)(2,1)S(1)}, bf16[528,256]{1,0:T(8,128)(2,1)}, u32[]{:S(2)}) copy-start(bf16[528,256]{1,0:T(8,128)(2,1)} %get-tuple-element.43.t0) | copy-start | bytes 811012
  15.5 28.0 %copy-start = (bf16[1088,256]{1,0:T(8,128)(2,1)S(1)}, bf16[1088,256]{1,0:T(8,128)(2,1)}, u32[]{:S(2)}) copy-start(bf16[1088,256]{1,0:T(8,128)(2,1)} %get-tuple-element.46.s0) | copy-start | bytes 1671172
  25.2 1.0 copy-start.7
  34.3 55.6 %collective-permute-start.4 = (bf16[8,128,512]{2,1,0:T(8,128)(2,1)}, bf16[8,128,512]{2,1,0:T(8,128)(2,1)S(1)}, u32[]{:S(2)}, u32[]{:S(2)}) collective-permute-start(bf16[8,128,512]{2,1,0:T(8,128)(2,1)} %get-tuple-element.41.own), channel_id=1, source_target_pairs={{0,1},{1,2},{2,3},{3,4},{4,5},{5,6},{6,7},{7,8},{8,9},{9,10},{10,1... | collective-permute-start | bytes 3145736 | tf_op jit(solution)/shard_map/ppermute | solution.py:454
  37.7 52.2 %collective-permute-start.5 = (bf16[8,128,512]{2,1,0:T(8,128)(2,1)}, bf16[8,128,512]{2,1,0:T(8,128)(2,1)S(1)}, u32[]{:S(2)}, u32[]{:S(2)}) collective-permute-start(bf16[8,128,512]{2,1,0:T(8,128)(2,1)} %get-tuple-element.41.own), channel_id=1, source_target_pairs={{1,0},{2,1},{3,2},{4,3},{5,4},{6,5},{7,6},{8,7},{9,8},{10,9},{11,1... | collective-permute-start | bytes 3145736 | tf_op jit(solution)/shard_map/ppermute | solution.py:455
  39.0 22.8 %collective-permute-start.7 = (bf16[528,256]{1,0:T(8,128)(2,1)S(1)}, bf16[528,256]{1,0:T(8,128)(2,1)S(1)}, u32[]{:S(2)}, u32[]{:S(2)}) collective-permute-start(bf16[528,256]{1,0:T(8,128)(2,1)S(1)} %copy-done.1), channel_id=1, source_target_pairs={{0,2},{1,3},{2,0},{3,1},{4,6},{5,7},{6,4},{7,5},{8,10},{9,11},{10,... | collective-permute-start | bytes 811016 | tf_op jit(solution)/shard_map/ppermute | solution.py:425
  43.5 18.4 %copy-start.9 = (bf16[1,64,256]{2,1,0:T(8,128)(2,1)S(1)}, bf16[1,64,256]{2,1,0:T(8,128)(2,1)}, u32[]{:S(2)}) copy-start(bf16[1,64,256]{2,1,0:T(8,128)(2,1)} %param.12) | copy-start | bytes 98308
  61.9 3.8 %collective-permute-start.8 = (bf16[128,256]{1,0:T(8,128)(2,1)S(1)}, bf16[128,256]{1,0:T(8,128)(2,1)S(1)}, u32[]{:S(2)}, u32[]{:S(2)}) collective-permute-start(bf16[128,256]{1,0:T(8,128)(2,1)S(1)} %pad_maximum_fusion.1.mine), channel_id=1, source_target_pairs={{0,16},{16,0},{32,48},{48,32},{64,80},{80,64},{96,112},{112,96},{1... | collective-permute-start | bytes 196616 | tf_op jit(solution)/shard_map/ppermute | solution.py:431
  65.7 20.7 %collective-permute-start.9 = (bf16[256,256]{1,0:T(8,128)(2,1)S(1)}, bf16[256,256]{1,0:T(8,128)(2,1)S(1)}, u32[]{:S(2)}, u32[]{:S(2)}) collective-permute-start(bf16[256,256]{1,0:T(8,128)(2,1)S(1)} %pad_maximum_fusion), channel_id=1, source_target_pairs={{0,32},{16,48},{32,64},{48,80},{64,96},{80,112},{96,0},{112,16},{1... | collective-permute-start | bytes 393224 | tf_op jit(solution)/shard_map/ppermute | solution.py:432
  77.4 8.9 %collective-permute-start.10 = (bf16[256,256]{1,0:T(8,128)(2,1)S(1)}, bf16[256,256]{1,0:T(8,128)(2,1)S(1)}, u32[]{:S(2)}, u32[]{:S(2)}) collective-permute-start(bf16[256,256]{1,0:T(8,128)(2,1)S(1)} %pad_maximum_fusion), channel_id=1, source_target_pairs={{0,96},{16,112},{32,0},{48,16},{64,32},{80,48},{96,64},{112,80},{1... | collective-permute-start | bytes 393224 | tf_op jit(solution)/shard_map/ppermute | solution.py:432
  78.9 8.1 %collective-permute-start.11 = (bf16[256,256]{1,0:T(8,128)(2,1)S(1)}, bf16[256,256]{1,0:T(8,128)(2,1)S(1)}, u32[]{:S(2)}, u32[]{:S(2)}) collective-permute-start(bf16[256,256]{1,0:T(8,128)(2,1)S(1)} %pad_maximum_fusion), channel_id=1, source_target_pairs={{0,64},{16,80},{32,96},{48,112},{64,0},{80,16},{96,32},{112,48},{1... | collective-permute-start | bytes 393224 | tf_op jit(solution)/shard_map/ppermute | solution.py:432
  86.9 3.0 %copy-start.5 = (bf16[8,128,512]{2,1,0:T(8,128)(2,1)S(1)}, bf16[8,128,512]{2,1,0:T(8,128)(2,1)}, u32[]{:S(2)}) copy-start(bf16[8,128,512]{2,1,0:T(8,128)(2,1)} %get-tuple-element.41.own) | copy-start | bytes 3145732
  86.9 3.0 %copy-start.8 = (f32[8,64,512]{2,1,0:T(8,128)S(1)}, f32[8,64,512]{2,1,0:T(8,128)}, u32[]{:S(2)}) copy-start(f32[8,64,512]{2,1,0:T(8,128)} %copy-done.7) | copy-start | bytes 3145732
  87.8 10.0 %collective-permute-start.12 = (bf16[576,256]{1,0:T(8,128)(2,1)S(1)}, bf16[576,256]{1,0:T(8,128)(2,1)S(1)}, u32[]{:S(2)}, u32[]{:S(2)}) collective-permute-start(bf16[576,256]{1,0:T(8,128)(2,1)S(1)} %get-tuple-element.67), channel_id=1, source_target_pairs={{0,3},{1,0},{2,1},{3,2},{4,7},{5,4},{6,5},{7,6},{8,11},{9,8},{10,9... | collective-permute-start | bytes 884744 | tf_op jit(solution)/shard_map/ppermute | solution.py:425
  87.9 16.2 %collective-permute-start.13 = (bf16[576,256]{1,0:T(8,128)(2,1)S(1)}, bf16[576,256]{1,0:T(8,128)(2,1)S(1)}, u32[]{:S(2)}, u32[]{:S(2)}) collective-permute-start(bf16[576,256]{1,0:T(8,128)(2,1)S(1)} %get-tuple-element.68), channel_id=1, source_target_pairs={{0,1},{1,2},{2,3},{3,0},{4,5},{5,6},{6,7},{7,4},{8,9},{9,10},{10,1... | collective-permute-start | bytes 884744 | tf_op jit(solution)/shard_map/ppermute | solution.py:425
  89.9 14.2 %copy-start.2 = (bf16[8,512,256]{2,1,0:T(8,128)(2,1)S(1)}, bf16[8,512,256]{2,1,0:T(8,128)(2,1)}, u32[]{:S(2)}) copy-start(bf16[8,512,256]{2,1,0:T(8,128)(2,1)} %basis.3) | copy-start | bytes 6291460
  89.9 14.2 %copy-start.3 = (bf16[8,256,256]{2,1,0:T(8,128)(2,1)S(1)}, bf16[8,256,256]{2,1,0:T(8,128)(2,1)}, u32[]{:S(2)}) copy-start(bf16[8,256,256]{2,1,0:T(8,128)(2,1)} %transfer.3) | copy-start | bytes 3145732
  89.9 14.2 %collective-permute-start.14 = (bf16[576,256]{1,0:T(8,128)(2,1)S(1)}, bf16[576,256]{1,0:T(8,128)(2,1)S(1)}, u32[]{:S(2)}, u32[]{:S(2)}) collective-permute-start(bf16[576,256]{1,0:T(8,128)(2,1)S(1)} %get-tuple-element.69), channel_id=1, source_target_pairs={{0,2},{1,3},{2,0},{3,1},{4,6},{5,7},{6,4},{7,5},{8,10},{9,11},{10,... | collective-permute-start | bytes 884744 | tf_op jit(solution)/shard_map/ppermute | solution.py:425

commit v6 on v5

--- a/solution.py
+++ b/solution.py
@@ -26,7 +26,7 @@
 
 
 def cost(us):
-    return pl.CostEstimate(flops=us * 10**9, bytes_accessed=10**6, transcendentals=0)
+    return pl.CostEstimate(flops=int(us * 10**9), bytes_accessed=10**6, transcendentals=0)
 
 
 def norm_rows(points, first):
@@ -167,62 +167,87 @@
         ).astype(out.dtype)
 
 
-def far_a_kernel(ids, place, s0, s1, s2, t0, t1, t2, o0, o1, o2, side):
-    sources = (s0, s1, s2)
-    for d, source in enumerate(sources):
+def sides_kernel(s0, s1, s2, side):
+    for d, source in enumerate((s0, s1, s2)):
 
         @pl.loop(0, LD, unroll=UNROLL)
         def _(leaf, d=d, source=source):
             side[d * LD + leaf] = source_side(skeleton_at(source, leaf))
 
+
+def sides_of(sources):
+    return pl.pallas_call(
+        sides_kernel,
+        in_specs=[VM] * 3,
+        out_specs=VM,
+        out_shape=jax.ShapeDtypeStruct((3 * LD, SK, AUG), BF),
+        compiler_params=params(16),
+        cost_estimate=cost(0.01),
+        name="sides",
+    )(*sources)
+
+
+def far_a_kernel(ids, place, side, s0, s1, s2, t0, t1, t2, o0, o1, o2):
     columns = columns_of(place)[:3]
     for b, (target, out) in enumerate(((t0, o0), (t1, o1), (t2, o2))):
-        near_sources(ids, columns, side, sources, target, out, b)
-
-
-def far_a(ids, place, sources, targets):
+        near_sources(ids, columns, side, (s0, s1, s2), target, out, b)
+
+
+def far_a(ids, place, side, sources, targets):
     return pl.pallas_call(
         far_a_kernel,
-        in_specs=[SM, SM] + [VM] * 6,
-        out_specs=[VM] * 4,
-        out_shape=[jax.ShapeDtypeStruct((LD * F, SK), F32)] * 3
-        + [jax.ShapeDtypeStruct((3 * LD, SK, AUG), BF)],
-        compiler_params=params(16),
-        cost_estimate=cost(9),
+        in_specs=[SM, SM] + [VM] * 7,
+        out_specs=[VM] * 3,
+        out_shape=[jax.ShapeDtypeStruct((LD * F, SK), F32)] * 3,
+        compiler_params=params(16),
+        cost_estimate=cost(0.01),
         name="far_a",
-    )(ids, place, *sources, *targets)
-
-
-def far_b_kernel(ids, place, given, s0, s1, s2, s3, t3, o3, last, side):
-    sources = (s0, s1, s2, s3)
+    )(ids, place, side, *sources, *targets)
+
+
+def far_b_kernel(ids, place, given, s0, s1, s2, low, high, t3, o3, last, right, side):
+    half = LD // 2
+    for d, source in enumerate((low, high)):
+
+        @pl.loop(0, half, unroll=half)
+        def _(leaf, d=d, source=source):
+            value = source_side(skeleton_at(source, leaf))
+            side[3 * LD + d * half + leaf] = value
+            last[d * half + leaf] = value
+            right[d * half + leaf] = charges_at(source, leaf)
+
+    side[: 3 * LD] = given[...]
+    columns = columns_of(place)
+
+    def weight_of(d, at):
+        return right[at] if d == 3 else charges_at((s0, s1, s2)[d], at)
 
     @pl.loop(0, LD, unroll=UNROLL)
     def _(leaf):
-        value = source_side(skeleton_at(s3, leaf))
-        side[3 * LD + leaf] = value
-        last[leaf] = value
-
-    side[: 3 * LD] = given[...]
-    near_sources(ids, columns_of(place), side, sources, t3, o3, 3)
-
-
-def far_b(ids, place, side, sources, target):
+        out = far_total(
+            ids, columns, 3 * LD + leaf, t3[rows_of(leaf), :], side, weight_of
+        )
+        o3[rows_of(leaf), :] = out.astype(o3.dtype)
+
+
+def far_b(ids, place, side, sources, halves, target):
     return pl.pallas_call(
         far_b_kernel,
-        in_specs=[SM, SM] + [VM] * 6,
-        out_specs=[VM] * 2,
+        in_specs=[SM, SM] + [VM] * 7,
+        out_specs=[VM] * 3,
         out_shape=[
             jax.ShapeDtypeStruct((LD * F, SK), BF),
             jax.ShapeDtypeStruct((LD, SK, AUG), BF),
+            jax.ShapeDtypeStruct((LD, RHS, SK), BF),
         ],
         scratch_shapes=[pltpu.VMEM((SIDE * LD, SK, AUG), BF)],
         compiler_params=params(16),
         cost_estimate=cost(4),
         name="far_b",
-    )(ids, place, side, *sources, target)
-
-
-def far_c_kernel(ids, place, side, s3, t0, t1, t2, a0, a1, a2, own, r1, r2):
+    )(ids, place, side, *sources, *halves, target)
+
+
+def far_c_kernel(ids, place, side, right, t0, t1, t2, a0, a1, a2, own, r1, r2):
     columns = columns_of(place)[3:]
     for b, (target, given, out) in enumerate(((t0, a0, own), (t1, a1, r1), (t2, a2, r2))):
 
@@ -230,12 +255,12 @@
         def _(leaf, b=b, target=target, given=given, out=out):
             total = far_total(
                 ids, columns, b * LD + leaf, target[rows_of(leaf), :], side,
-                lambda d, at: charges_at(s3, at),
+                lambda d, at: right[at],
             )
             out[rows_of(leaf), :] = (given[rows_of(leaf), :] + total).astype(out.dtype)
 
 
-def far_c(ids, place, side, source, targets, given):
+def far_c(ids, place, side, right, targets, given):
     return pl.pallas_call(
         far_c_kernel,
         in_specs=[SM, SM] + [VM] * 8,
@@ -245,7 +270,7 @@
         compiler_params=params(16),
         cost_estimate=cost(4),
         name="far_c",
-    )(ids, place, side, source, *targets, *given)
+    )(ids, place, side, right, *targets, *given)
 
 
 def top_kernel(mine, pair, n1, n2, n3, a1, a2, a3, top, r1, r2, r3):
@@ -440,15 +465,18 @@
     near_msg, source_msg, target_msg = prep(
         points, right_sides, leaf_basis, transfer, skeleton, far_sources
     )
-    sources = [source_msg] + [shifted(source_msg, dx, 0) for dx in (1, -1, 2)]
-    targets = [target_msg] + [shifted(target_msg, 0, dz) for dz in (1, -1)]
+    sources = [source_msg] + [shifted(source_msg, dx, 0) for dx in (1, -1)]
+    targets = [target_msg] + [shifted(target_msg, 0, dz) for dz in (1, -1, 2)]
     first = (position * LD).astype(jnp.int32).reshape(1)
     near_sum = near_own(neighbours, first, near_msg)
 
-    targets, sources[:3], near_msg, near_sum = lax.optimization_barrier(
-        (targets, sources[:3], near_msg, near_sum)
+    targets[:3], sources, near_msg, near_sum = lax.optimization_barrier(
+        (targets[:3], sources, near_msg, near_sum)
     )
-    targets.append(shifted(targets[0], 0, 2))
+    half = LD * F
+    low, high = shifted(sources[1][:half], 1, 0), shifted(sources[2][half:], -1, 0)
+    side = sides_of(sources)
+    near_msg, side = lax.optimization_barrier((near_msg, side))
     count = lax.axis_size("leaf") * lax.axis_size("top")
     up = [(i, i + 1) for i in range(count - 1)]
     before = lax.ppermute(near_msg, ("leaf", "top"), up)
@@ -459,19 +487,17 @@
         return ids.astype(jnp.int32)
 
     place = jnp.stack([at // SIDE, at % SIDE]).astype(jnp.int32)
-    *given, side = far_a(ids_of(targets[:3]), place, sources[:3], targets[:3])
-    sources[3], given, side, targets[3] = lax.optimization_barrier(
-        (sources[3], given, side, targets[3])
-    )
-    line_charge = sum(s[2 * LD * F :].astype(F32) for s in sources)
+    given = far_a(ids_of(targets[:3]), place, side, sources, targets[:3])
+    low, high, given, targets[3] = lax.optimization_barrier((low, high, given, targets[3]))
+    line_charge = sum(s[2 * half :].astype(F32) for s in sources) + high[half:].astype(F32)
     mine = jnp.concatenate([line_charge.astype(BF), node_points[0]], axis=0)
     pair = leaf_shifted(mine, 0)
     ids = ids_of(targets)
-    r3, last = far_b(ids, place, side, sources, targets[3])
+    r3, last, right = far_b(ids, place, side, sources, (low, high), targets[3])
     pair, r3, last = lax.optimization_barrier((pair, r3, last))
     both = jnp.concatenate([mine, pair], axis=0)
     others = [leaf_shifted(both, dy) for dy in (1, -1, 2)]
-    own, r1, r2 = far_c(ids, place, last, sources[3], targets[:3], given)
+    own, r1, r2 = far_c(ids, place, last, right, targets[:3], given)
     top, *parts = top_sum(mine, pair, others, (r1, r2, r3))
     returned = [shifted(r, 0, dz) for r, dz in zip(parts, (-1, 1, 2))]
     near_sum = near_rest(neighbours, first, near_msg, before, after, near_sum)

time: 107 us -> 87.7 us (0.82); the launches traced: 107 us -> 86.6 us
  waiting for transfers between devices: 28.9 us -> 10.8 us
  starting transfers between devices: 35.6 us -> 32.6 us
  local copies, waits for them, and re-layouts: 2.21 us -> 4.32 us
  Pallas kernels: 39.9 us -> 38.6 us
    ppermute x9 -> x10, waiting for transfers between devices: 28.4 us -> 10.7 us  [shifted(): return lax.ppermute(value, 'top', pairs)]
    ppermute x3, starting transfers between devices: 14.8 us -> 7.58 us  [leaf_shifted(): lax.ppermute(value, 'leaf', [(i, (i + 2 * dy) % count) for i in range(cou...]
    ppermute x1, starting transfers between devices: 0.27 us -> 3.31 us  [leaf_shifted(): return lax.ppermute(value, 'leaf', [(i, i ^ 1) for i in range(count)])]
    pallas_call x1, Pallas kernels: 9.76 us -> 6.85 us  [near_own(): pl.pallas_call(near_own_kernel, in_specs=[SM, SM, VM], out_specs=VM, out_...]
    pallas_call x1, Pallas kernels: 5.37 us -> 6.92 us  [near_rest(): pl.pallas_call(near_rest_kernel, in_specs=[SM, SM, VM, VM, VM, VM], out_s...]
    slice x0 -> x2, local copies, waits for them, and re-layouts: none -> 1.47 us  [the longest x1 0.73 us: on_device(): sources[2][half:]]
    ppermute x9 -> x10, starting transfers between devices: 15.9 us -> 17.3 us  [shifted(): return lax.ppermute(value, 'top', pairs)]
    pallas_call x2 -> x3, Pallas kernels: 10.2 us -> 10.3 us  [the longest x1 6.27 us: far_a(): pl.pallas_call(far_a_kernel, in_specs=[SM, SM] + [VM] * 7, out_specs=[VM]...]
  transfers between devices with their start and end apart: 15 -> 16, of which waited for: 5 -> 3; matrix products, arithmetic and copies ran while one was open for 0% -> 1% of each run, Pallas kernels for 30% -> 36%
where the time goes in v6:
time: 87.7 us; the launch traced here: 86.6 us
  Pallas kernels  38.6 us (44%)
  starting transfers between devices  32.6 us (37%)
  waiting for transfers between devices  10.8 us (12%)
  local copies, waits for them, and re-layouts  4.32 us (5%)
    ppermute x10, starting transfers between devices, shifted(): return lax.ppermute(value, 'top', pairs)  17.3 us
    ppermute x10, waiting for transfers between devices, shifted(): return lax.ppermute(value, 'top', pairs)  10.7 us
    ppermute x3, starting transfers between devices, leaf_shifted(): lax.ppermute(value, 'leaf', [(i, (i + 2 * dy) % count) for i in range(cou...  7.58 us
    pallas_call x1, Pallas kernels, near_rest(): pl.pallas_call(near_rest_kernel, in_specs=[SM, SM, VM, VM, VM, VM], out_s...  6.92 us
    pallas_call x1, Pallas kernels, near_own(): pl.pallas_call(near_own_kernel, in_specs=[SM, SM, VM], out_specs=VM, out_...  6.85 us
    pallas_call x1, Pallas kernels, far_a(): pl.pallas_call(far_a_kernel, in_specs=[SM, SM] + [VM] * 7, out_specs=[VM]...  6.27 us
    pallas_call x1, Pallas kernels, far_c(): pl.pallas_call(far_c_kernel, in_specs=[SM, SM] + [VM] * 8, out_specs=[VM]...  5.89 us
    pallas_call x1, Pallas kernels, prep(): pl.pallas_call(prep_kernel, in_specs=[anywhere] * 4 + [VM] * 2, out_specs...  4.9 us
  transfers between devices with their start and end apart: 16, of which 3 were waited for; matrix products, arithmetic and copies ran while one was open for 1% of the time, Pallas kernels for 36%

profile of v6, /device:TPU:0, one launch (start us, length us, event | category | flops | bytes accessed | tf_op | source)
XLA Modules:
  0.0 86.6 jit_solution(16129581521859140562)
XLA Ops:
  0.0 0.0 copy-start.6
  0.0 4.9 %prep.1 = (bf16[8,128,512]{2,1,0:T(8,128)(2,1)}, bf16[1088,256]{1,0:T(8,128)(2,1)}, bf16[528,256]{1,0:T(8,128)(2,1)}) custom-call(bf16[8,64,512]{2,1,0:T(8,128)(2,1)} %points.1, bf16[8,64,512]{2,1,0:T(8,128)(2,1)} %sides.2, bf16[8,512,256]{2,1,0:T(8,128)(2,1)} %basis.3, bf16[8,256,256]{2,1,0:T(8,128)(2,1)} %transfer.3, s32[8,256]{1,0:T(8,128)} %skeleton.1, ...), custom_call_target="tpu_custom_call" | custom-call | flops 4000000000 | bytes 1000000 | tf_op jit(solution)/shard_map/prep/pallas_call | solution.py:100
  4.9 2.1 %collective-permute-start = (bf16[528,256]{1,0:T(8,128)(2,1)}, bf16[528,256]{1,0:T(8,128)(2,1)S(1)}, u32[]{:S(2)}, u32[]{:S(2)}) collective-permute-start(bf16[528,256]{1,0:T(8,128)(2,1)} %get-tuple-element.49.t0), channel_id=1, source_target_pairs={{0,1},{1,2},{2,3},{3,0},{4,5},{5,6},{6,7},{7,4},{8,9},{9,10},{10,1... | collective-permute-start | bytes 811016 | tf_op jit(solution)/shard_map/ppermute | solution.py:450
  7.0 2.2 %collective-permute-start.1 = (bf16[528,256]{1,0:T(8,128)(2,1)}, bf16[528,256]{1,0:T(8,128)(2,1)S(1)}, u32[]{:S(2)}, u32[]{:S(2)}) collective-permute-start(bf16[528,256]{1,0:T(8,128)(2,1)} %get-tuple-element.49.t0), channel_id=1, source_target_pairs={{0,3},{1,0},{2,1},{3,2},{4,7},{5,4},{6,5},{7,6},{8,11},{9,8},{10,9... | collective-permute-start | bytes 811016 | tf_op jit(solution)/shard_map/ppermute | solution.py:450
  9.2 1.5 %collective-permute-start.2 = (bf16[1088,256]{1,0:T(8,128)(2,1)}, bf16[1088,256]{1,0:T(8,128)(2,1)S(1)}, u32[]{:S(2)}, u32[]{:S(2)}) collective-permute-start(bf16[1088,256]{1,0:T(8,128)(2,1)} %get-tuple-element.44.s0), channel_id=1, source_target_pairs={{0,4},{1,5},{2,6},{3,7},{4,8},{5,9},{6,10},{7,11},{8,12},{9,13},{1... | collective-permute-start | bytes 1671176 | tf_op jit(solution)/shard_map/ppermute | solution.py:450
  10.7 1.7 %collective-permute-start.3 = (bf16[1088,256]{1,0:T(8,128)(2,1)}, bf16[1088,256]{1,0:T(8,128)(2,1)S(1)}, u32[]{:S(2)}, u32[]{:S(2)}) collective-permute-start(bf16[1088,256]{1,0:T(8,128)(2,1)} %get-tuple-element.44.s0), channel_id=1, source_target_pairs={{0,12},{1,13},{2,14},{3,15},{4,0},{5,1},{6,2},{7,3},{8,4},{9,5},{1... | collective-permute-start | bytes 1671176 | tf_op jit(solution)/shard_map/ppermute | solution.py:450
  12.4 0.0 copy-done.6
  12.4 0.0 copy-start.4
  12.4 1.2 %copy-done.4 = bf16[8,128,512]{2,1,0:T(8,128)(2,1)S(1)} copy-done((bf16[8,128,512]{2,1,0:T(8,128)(2,1)S(1)}, bf16[8,128,512]{2,1,0:T(8,128)(2,1)}, u32[]{:S(2)}) %copy-start.4) | copy-done | bytes 1048600
  13.6 0.0 copy-start.1
  13.6 0.0 copy-start
  13.7 6.8 %near_own.1.given = f32[8,64,512]{2,1,0:T(8,128)S(1)} custom-call(s32[8,8]{1,0:T(8,128)S(1)} %copy-done.6, s32[1]{0:T(128)} %bitcast.first, bf16[8,128,512]{2,1,0:T(8,128)(2,1)S(1)} %copy-done.4), custom_call_target="tpu_custom_call" | custom-call | flops 8999999488 | bytes 1000000 | tf_op jit(solution)/shard_map/near_own/pallas_call | solution.py:359
  20.5 0.0 copy-start.7
  20.5 1.0 %copy-done.7 = f32[8,64,512]{2,1,0:T(8,128)} copy-done((f32[8,64,512]{2,1,0:T(8,128)}, f32[8,64,512]{2,1,0:T(8,128)S(1)}, u32[]{:S(2)}) %copy-start.7) | copy-done | bytes 1048600
  21.5 0.0 collective-permute-done.t1
  21.5 0.0 collective-permute-done.1.t2
  21.5 3.2 %collective-permute-done.2.s1 = bf16[1088,256]{1,0:T(8,128)(2,1)S(1)} collective-permute-done((bf16[1088,256]{1,0:T(8,128)(2,1)}, bf16[1088,256]{1,0:T(8,128)(2,1)S(1)}, u32[]{:S(2)}, u32[]{:S(2)}) %collective-permute-start.2) | collective-permute-done | bytes 557088 | tf_op jit(solution)/shard_map/ppermute | solution.py:450
  24.7 0.0 collective-permute-done.3.s2
  24.7 0.7 slice.37
  25.4 3.0 %collective-permute-start.7 = (bf16[576,256]{1,0:T(8,128)(2,1)}, bf16[576,256]{1,0:T(8,128)(2,1)S(1)}, u32[]{:S(2)}, u32[]{:S(2)}) collective-permute-start(bf16[576,256]{1,0:T(8,128)(2,1)} %slice.37), channel_id=1, source_target_pairs={{0,12},{1,13},{2,14},{3,15},{4,0},{5,1},{6,2},{7,3},{8,4},{9,5},{1... | collective-permute-start | bytes 884744 | tf_op jit(solution)/shard_map/ppermute | solution.py:450
  28.4 0.0 copy-done.1
  28.4 1.5 %collective-permute-start.8 = (bf16[528,256]{1,0:T(8,128)(2,1)S(1)}, bf16[528,256]{1,0:T(8,128)(2,1)S(1)}, u32[]{:S(2)}, u32[]{:S(2)}) collective-permute-start(bf16[528,256]{1,0:T(8,128)(2,1)S(1)} %copy-done.1), channel_id=1, source_target_pairs={{0,2},{1,3},{2,0},{3,1},{4,6},{5,7},{6,4},{7,5},{8,10},{9,11},{10,... | collective-permute-start | bytes 811016 | tf_op jit(solution)/shard_map/ppermute | solution.py:450
  29.9 0.7 slice.36
  30.6 0.0 collective-permute-start.6
  30.6 0.0 copy-start.5
  30.6 0.1 pad_add_fusion.place
  30.7 0.0 copy-done
  30.7 0.5 sides.3.side.given
  31.2 0.6 copy-done.5
  31.9 3.0 %collective-permute-start.4 = (bf16[8,128,512]{2,1,0:T(8,128)(2,1)S(1)}, bf16[8,128,512]{2,1,0:T(8,128)(2,1)S(1)}, u32[]{:S(2)}, u32[]{:S(2)}) collective-permute-start(bf16[8,128,512]{2,1,0:T(8,128)(2,1)S(1)} %copy-done.5), channel_id=1, source_target_pairs={{0,1},{1,2},{2,3},{3,4},{4,5},{5,6},{6,7},{7,8},{8,9},{9,10},{10,1... | collective-permute-start | bytes 3145736 | tf_op jit(solution)/shard_map/ppermute | solution.py:482
  34.8 1.5 %collective-permute-start.5 = (bf16[8,128,512]{2,1,0:T(8,128)(2,1)S(1)}, bf16[8,128,512]{2,1,0:T(8,128)(2,1)S(1)}, u32[]{:S(2)}, u32[]{:S(2)}) collective-permute-start(bf16[8,128,512]{2,1,0:T(8,128)(2,1)S(1)} %copy-done.5), channel_id=1, source_target_pairs={{1,0},{2,1},{3,2},{4,3},{5,4},{6,5},{7,6},{8,7},{9,8},{10,9},{11,1... | collective-permute-start | bytes 3145736 | tf_op jit(solution)/shard_map/ppermute | solution.py:483
  36.4 0.0 copy-start.9
  36.4 6.3 %far_a.1 = (f32[512,256]{1,0:T(8,128)S(1)}, f32[512,256]{1,0:T(8,128)S(1)}, f32[512,256]{1,0:T(8,128)S(1)}) custom-call(s32[24,16]{1,0:T(8,128)S(1)} %maximum_convert_fusion.1.ids, s32[2]{0:T(128)S(1)} %pad_add_fusion.place, bf16[24,256,128]{2,1,0:T(8,128)(2,1)S(1)} %sides.3.side.given, bf16[1088,256]{1,0:T(8,128)(2,1)S(1)} %copy-done, ...), custom_call_target="tpu_custom_call" | custom-call | flops 10000000 | bytes 1000000 | tf_op jit(solution)/shard_map/far_a/pallas_call | solution.py:197
  42.7 0.0 collective-permute-done.8.t3
  42.7 0.0 collective-permute-done.6.low
  42.7 0.0 collective-permute-done.7.high
  42.7 0.0 copy-done.9
  42.8 3.3 %collective-permute-start.9 = (bf16[128,256]{1,0:T(8,128)(2,1)S(1)}, bf16[128,256]{1,0:T(8,128)(2,1)S(1)}, u32[]{:S(2)}, u32[]{:S(2)}) collective-permute-start(bf16[128,256]{1,0:T(8,128)(2,1)S(1)} %pad_maximum_fusion.1.mine), channel_id=1, source_target_pairs={{0,16},{16,0},{32,48},{48,32},{64,80},{80,64},{96,112},{112,96},{1... | collective-permute-start | bytes 196616 | tf_op jit(solution)/shard_map/ppermute | solution.py:456
  46.1 3.5 %far_b.1 = (bf16[512,256]{1,0:T(8,128)(2,1)S(1)}, bf16[8,256,128]{2,1,0:T(8,128)(2,1)S(1)}, bf16[8,64,256]{2,1,0:T(8,128)(2,1)S(1)}) custom-call(s32[32,16]{1,0:T(8,128)S(1)} %maximum_convert_fusion.ids, s32[2]{0:T(128)S(1)} %pad_add_fusion.place, bf16[24,256,128]{2,1,0:T(8,128)(2,1)S(1)} %sides.3.side.given, bf16[1088,256]{1,0:T(8,128)(2,1)S(1)} %copy-done, ...), custom_call_target="tpu_custom_call" | custom-call | flops 4000000000 | bytes 1000000 | tf_op jit(solution)/shard_map/far_b/pallas_call | solution.py:234
  49.6 0.0 collective-permute-done.9.pair
  49.6 3.9 %collective-permute-start.10 = (bf16[256,256]{1,0:T(8,128)(2,1)S(1)}, bf16[256,256]{1,0:T(8,128)(2,1)S(1)}, u32[]{:S(2)}, u32[]{:S(2)}) collective-permute-start(bf16[256,256]{1,0:T(8,128)(2,1)S(1)} %pad_maximum_fusion), channel_id=1, source_target_pairs={{0,32},{16,48},{32,64},{48,80},{64,96},{80,112},{96,0},{112,16},{1... | collective-permute-start | bytes 393224 | tf_op jit(solution)/shard_map/ppermute | solution.py:457
  53.5 1.5 %collective-permute-start.11 = (bf16[256,256]{1,0:T(8,128)(2,1)S(1)}, bf16[256,256]{1,0:T(8,128)(2,1)S(1)}, u32[]{:S(2)}, u32[]{:S(2)}) collective-permute-start(bf16[256,256]{1,0:T(8,128)(2,1)S(1)} %pad_maximum_fusion), channel_id=1, source_target_pairs={{0,96},{16,112},{32,0},{48,16},{64,32},{80,48},{96,64},{112,80},{1... | collective-permute-start | bytes 393224 | tf_op jit(solution)/shard_map/ppermute | solution.py:457
  55.0 2.1 %collective-permute-start.12 = (bf16[256,256]{1,0:T(8,128)(2,1)S(1)}, bf16[256,256]{1,0:T(8,128)(2,1)S(1)}, u32[]{:S(2)}, u32[]{:S(2)}) collective-permute-start(bf16[256,256]{1,0:T(8,128)(2,1)S(1)} %pad_maximum_fusion), channel_id=1, source_target_pairs={{0,64},{16,80},{32,96},{48,112},{64,0},{80,16},{96,32},{112,48},{1... | collective-permute-start | bytes 393224 | tf_op jit(solution)/shard_map/ppermute | solution.py:457
  57.2 5.9 %far_c.1 = (f32[512,256]{1,0:T(8,128)S(1)}, bf16[512,256]{1,0:T(8,128)(2,1)S(1)}, bf16[512,256]{1,0:T(8,128)(2,1)S(1)}) custom-call(s32[32,16]{1,0:T(8,128)S(1)} %maximum_convert_fusion.ids, s32[2]{0:T(128)S(1)} %pad_add_fusion.place, bf16[8,256,128]{2,1,0:T(8,128)(2,1)S(1)} %get-tuple-element.61.side, bf16[8,64,256]{2,1,0:T(8,128)(2,1)S(1)} %get-tuple-element.62.right, ...), custom_call_target="tpu_custom_call" | custom-call | flops 4000000000 | bytes 1000000 | tf_op jit(solution)/shard_map/far_c/pallas_call | solution.py:264
  63.1 0.0 collective-permute-done.10.n1
  63.1 0.0 collective-permute-done.11.n2
  63.1 0.0 collective-permute-done.12.n3
  63.1 0.0 copy-start.8
  63.1 0.8 top_sum.1
  64.0 3.7 %collective-permute-start.13 = (bf16[576,256]{1,0:T(8,128)(2,1)S(1)}, bf16[576,256]{1,0:T(8,128)(2,1)S(1)}, u32[]{:S(2)}, u32[]{:S(2)}) collective-permute-start(bf16[576,256]{1,0:T(8,128)(2,1)S(1)} %get-tuple-element.71), channel_id=1, source_target_pairs={{0,3},{1,0},{2,1},{3,2},{4,7},{5,4},{6,5},{7,6},{8,11},{9,8},{10,9... | collective-permute-start | bytes 884744 | tf_op jit(solution)/shard_map/ppermute | solution.py:450
  67.7 0.0 collective-permute-start.14
  67.7 0.0 copy-start.2
  67.7 0.0 copy-start.3
  67.7 1.5 %collective-permute-start.15 = (bf16[576,256]{1,0:T(8,128)(2,1)S(1)}, bf16[576,256]{1,0:T(8,128)(2,1)S(1)}, u32[]{:S(2)}, u32[]{:S(2)}) collective-permute-start(bf16[576,256]{1,0:T(8,128)(2,1)S(1)} %get-tuple-element.73), channel_id=1, source_target_pairs={{0,2},{1,3},{2,0},{3,1},{4,6},{5,7},{6,4},{7,5},{8,10},{9,11},{10,... | collective-permute-start | bytes 884744 | tf_op jit(solution)/shard_map/ppermute | solution.py:450
  69.3 0.0 collective-permute-done.4.before
  69.3 0.0 collective-permute-done.5.after
  69.3 0.0 copy-done.8
  69.3 6.9 %near_rest.1.near_sum = f32[8,64,512]{2,1,0:T(8,128)S(1)} custom-call(s32[8,8]{1,0:T(8,128)S(1)} %copy-done.6, s32[1]{0:T(128)} %bitcast.first, bf16[8,128,512]{2,1,0:T(8,128)(2,1)S(1)} %copy-done.5, bf16[8,128,512]{2,1,0:T(8,128)(2,1)S(1)} %collective-permute-done.4.before, bf16[8,128,512]{2,1,0:T(8,128)(2,1)S(1)} %collective-permute-done.5.after, ...), custom_call_target="tpu_custom_call" | custom-call | flops 11000000512 | bytes 1000000 | tf_op jit(solution)/shard_map/near_rest/pallas_call | solution.py:395
  76.2 4.1 %collective-permute-done.13.r1 = bf16[576,256]{1,0:T(8,128)(2,1)S(1)} collective-permute-done((bf16[576,256]{1,0:T(8,128)(2,1)S(1)}, bf16[576,256]{1,0:T(8,128)(2,1)S(1)}, u32[]{:S(2)}, u32[]{:S(2)}) %collective-permute-start.13) | collective-permute-done | bytes 294944 | tf_op jit(solution)/shard_map/ppermute | solution.py:450
  80.3 3.4 %collective-permute-done.14.r2 = bf16[576,256]{1,0:T(8,128)(2,1)S(1)} collective-permute-done((bf16[576,256]{1,0:T(8,128)(2,1)S(1)}, bf16[576,256]{1,0:T(8,128)(2,1)S(1)}, u32[]{:S(2)}, u32[]{:S(2)}) %collective-permute-start.14) | collective-permute-done | bytes 294944 | tf_op jit(solution)/shard_map/ppermute | solution.py:450
  83.7 0.0 collective-permute-done.15.r3
  83.7 0.0 copy-done.2
  83.7 0.0 copy-done.3
  83.7 2.9 %final.1 = bf16[8,64,512]{2,1,0:T(8,128)(2,1)} custom-call(f32[8,64,512]{2,1,0:T(8,128)S(1)} %near_rest.1.near_sum, bf16[8,512,256]{2,1,0:T(8,128)(2,1)S(1)} %copy-done.2, bf16[8,256,256]{2,1,0:T(8,128)(2,1)S(1)} %copy-done.3, f32[512,256]{1,0:T(8,128)S(1)} %get-tuple-element.66.own, bf16[576,256]{1,0:T(8,128)(2,1)S(1)} %collective-permute-done.13.r1, ...), custom_call_target="tpu_custom_call" | custom-call | flops 3000000000 | bytes 1000000 | tf_op jit(solution)/shard_map/final/pallas_call | solution.py:433
  (9 shorter events, 0.1 us)
Async XLA Ops:
  0.0 12.4 %copy-start.6 = (s32[8,8]{1,0:T(8,128)S(1)}, s32[8,8]{1,0:T(8,128)}, u32[]{:S(2)}) copy-start(s32[8,8]{1,0:T(8,128)} %ids.3) | copy-start | bytes 772
  4.9 16.6 %collective-permute-start = (bf16[528,256]{1,0:T(8,128)(2,1)}, bf16[528,256]{1,0:T(8,128)(2,1)S(1)}, u32[]{:S(2)}, u32[]{:S(2)}) collective-permute-start(bf16[528,256]{1,0:T(8,128)(2,1)} %get-tuple-element.49.t0), channel_id=1, source_target_pairs={{0,1},{1,2},{2,3},{3,0},{4,5},{5,6},{6,7},{7,4},{8,9},{9,10},{10,1... | collective-permute-start | bytes 811016 | tf_op jit(solution)/shard_map/ppermute | solution.py:450
  7.0 14.5 %collective-permute-start.1 = (bf16[528,256]{1,0:T(8,128)(2,1)}, bf16[528,256]{1,0:T(8,128)(2,1)S(1)}, u32[]{:S(2)}, u32[]{:S(2)}) collective-permute-start(bf16[528,256]{1,0:T(8,128)(2,1)} %get-tuple-element.49.t0), channel_id=1, source_target_pairs={{0,3},{1,0},{2,1},{3,2},{4,7},{5,4},{6,5},{7,6},{8,11},{9,8},{10,9... | collective-permute-start | bytes 811016 | tf_op jit(solution)/shard_map/ppermute | solution.py:450
  9.2 15.5 %collective-permute-start.2 = (bf16[1088,256]{1,0:T(8,128)(2,1)}, bf16[1088,256]{1,0:T(8,128)(2,1)S(1)}, u32[]{:S(2)}, u32[]{:S(2)}) collective-permute-start(bf16[1088,256]{1,0:T(8,128)(2,1)} %get-tuple-element.44.s0), channel_id=1, source_target_pairs={{0,4},{1,5},{2,6},{3,7},{4,8},{5,9},{6,10},{7,11},{8,12},{9,13},{1... | collective-permute-start | bytes 1671176 | tf_op jit(solution)/shard_map/ppermute | solution.py:450
  10.7 14.0 %collective-permute-start.3 = (bf16[1088,256]{1,0:T(8,128)(2,1)}, bf16[1088,256]{1,0:T(8,128)(2,1)S(1)}, u32[]{:S(2)}, u32[]{:S(2)}) collective-permute-start(bf16[1088,256]{1,0:T(8,128)(2,1)} %get-tuple-element.44.s0), channel_id=1, source_target_pairs={{0,12},{1,13},{2,14},{3,15},{4,0},{5,1},{6,2},{7,3},{8,4},{9,5},{1... | collective-permute-start | bytes 1671176 | tf_op jit(solution)/shard_map/ppermute | solution.py:450
  12.4 1.2 %copy-start.4 = (bf16[8,128,512]{2,1,0:T(8,128)(2,1)S(1)}, bf16[8,128,512]{2,1,0:T(8,128)(2,1)}, u32[]{:S(2)}) copy-start(bf16[8,128,512]{2,1,0:T(8,128)(2,1)} %get-tuple-element.47.own) | copy-start | bytes 3145732
  13.6 14.7 %copy-start.1 = (bf16[528,256]{1,0:T(8,128)(2,1)S(1)}, bf16[528,256]{1,0:T(8,128)(2,1)}, u32[]{:S(2)}) copy-start(bf16[528,256]{1,0:T(8,128)(2,1)} %get-tuple-element.49.t0) | copy-start | bytes 811012
  13.6 17.1 %copy-start = (bf16[1088,256]{1,0:T(8,128)(2,1)S(1)}, bf16[1088,256]{1,0:T(8,128)(2,1)}, u32[]{:S(2)}) copy-start(bf16[1088,256]{1,0:T(8,128)(2,1)} %get-tuple-element.44.s0) | copy-start | bytes 1671172
  20.5 1.0 %copy-start.7 = (f32[8,64,512]{2,1,0:T(8,128)}, f32[8,64,512]{2,1,0:T(8,128)S(1)}, u32[]{:S(2)}) copy-start(f32[8,64,512]{2,1,0:T(8,128)S(1)} %near_own.1.given) | copy-start | bytes 3145732
  25.4 17.3 %collective-permute-start.7 = (bf16[576,256]{1,0:T(8,128)(2,1)}, bf16[576,256]{1,0:T(8,128)(2,1)S(1)}, u32[]{:S(2)}, u32[]{:S(2)}) collective-permute-start(bf16[576,256]{1,0:T(8,128)(2,1)} %slice.37), channel_id=1, source_target_pairs={{0,12},{1,13},{2,14},{3,15},{4,0},{5,1},{6,2},{7,3},{8,4},{9,5},{1... | collective-permute-start | bytes 884744 | tf_op jit(solution)/shard_map/ppermute | solution.py:450
  28.4 14.3 %collective-permute-start.8 = (bf16[528,256]{1,0:T(8,128)(2,1)S(1)}, bf16[528,256]{1,0:T(8,128)(2,1)S(1)}, u32[]{:S(2)}, u32[]{:S(2)}) collective-permute-start(bf16[528,256]{1,0:T(8,128)(2,1)S(1)} %copy-done.1), channel_id=1, source_target_pairs={{0,2},{1,3},{2,0},{3,1},{4,6},{5,7},{6,4},{7,5},{8,10},{9,11},{10,... | collective-permute-start | bytes 811016 | tf_op jit(solution)/shard_map/ppermute | solution.py:450
  30.6 12.0 %collective-permute-start.6 = (bf16[512,256]{1,0:T(8,128)(2,1)}, bf16[512,256]{1,0:T(8,128)(2,1)S(1)}, u32[]{:S(2)}, u32[]{:S(2)}) collective-permute-start(bf16[512,256]{1,0:T(8,128)(2,1)} %slice.36), channel_id=1, source_target_pairs={{0,4},{1,5},{2,6},{3,7},{4,8},{5,9},{6,10},{7,11},{8,12},{9,13},{1... | collective-permute-start | bytes 786440 | tf_op jit(solution)/shard_map/ppermute | solution.py:450
  30.6 1.2 %copy-start.5 = (bf16[8,128,512]{2,1,0:T(8,128)(2,1)S(1)}, bf16[8,128,512]{2,1,0:T(8,128)(2,1)}, u32[]{:S(2)}) copy-start(bf16[8,128,512]{2,1,0:T(8,128)(2,1)} %get-tuple-element.47.own) | copy-start | bytes 3145732
  31.9 37.4 %collective-permute-start.4 = (bf16[8,128,512]{2,1,0:T(8,128)(2,1)S(1)}, bf16[8,128,512]{2,1,0:T(8,128)(2,1)S(1)}, u32[]{:S(2)}, u32[]{:S(2)}) collective-permute-start(bf16[8,128,512]{2,1,0:T(8,128)(2,1)S(1)} %copy-done.5), channel_id=1, source_target_pairs={{0,1},{1,2},{2,3},{3,4},{4,5},{5,6},{6,7},{7,8},{8,9},{9,10},{10,1... | collective-permute-start | bytes 3145736 | tf_op jit(solution)/shard_map/ppermute | solution.py:482
  34.8 34.4 %collective-permute-start.5 = (bf16[8,128,512]{2,1,0:T(8,128)(2,1)S(1)}, bf16[8,128,512]{2,1,0:T(8,128)(2,1)S(1)}, u32[]{:S(2)}, u32[]{:S(2)}) collective-permute-start(bf16[8,128,512]{2,1,0:T(8,128)(2,1)S(1)} %copy-done.5), channel_id=1, source_target_pairs={{1,0},{2,1},{3,2},{4,3},{5,4},{6,5},{7,6},{8,7},{9,8},{10,9},{11,1... | collective-permute-start | bytes 3145736 | tf_op jit(solution)/shard_map/ppermute | solution.py:483
  36.4 6.4 %copy-start.9 = (bf16[1,64,256]{2,1,0:T(8,128)(2,1)S(1)}, bf16[1,64,256]{2,1,0:T(8,128)(2,1)}, u32[]{:S(2)}) copy-start(bf16[1,64,256]{2,1,0:T(8,128)(2,1)} %param.12) | copy-start | bytes 98308
  42.8 6.8 %collective-permute-start.9 = (bf16[128,256]{1,0:T(8,128)(2,1)S(1)}, bf16[128,256]{1,0:T(8,128)(2,1)S(1)}, u32[]{:S(2)}, u32[]{:S(2)}) collective-permute-start(bf16[128,256]{1,0:T(8,128)(2,1)S(1)} %pad_maximum_fusion.1.mine), channel_id=1, source_target_pairs={{0,16},{16,0},{32,48},{48,32},{64,80},{80,64},{96,112},{112,96},{1... | collective-permute-start | bytes 196616 | tf_op jit(solution)/shard_map/ppermute | solution.py:456
  49.6 13.5 %collective-permute-start.10 = (bf16[256,256]{1,0:T(8,128)(2,1)S(1)}, bf16[256,256]{1,0:T(8,128)(2,1)S(1)}, u32[]{:S(2)}, u32[]{:S(2)}) collective-permute-start(bf16[256,256]{1,0:T(8,128)(2,1)S(1)} %pad_maximum_fusion), channel_id=1, source_target_pairs={{0,32},{16,48},{32,64},{48,80},{64,96},{80,112},{96,0},{112,16},{1... | collective-permute-start | bytes 393224 | tf_op jit(solution)/shard_map/ppermute | solution.py:457
  53.5 9.5 %collective-permute-start.11 = (bf16[256,256]{1,0:T(8,128)(2,1)S(1)}, bf16[256,256]{1,0:T(8,128)(2,1)S(1)}, u32[]{:S(2)}, u32[]{:S(2)}) collective-permute-start(bf16[256,256]{1,0:T(8,128)(2,1)S(1)} %pad_maximum_fusion), channel_id=1, source_target_pairs={{0,96},{16,112},{32,0},{48,16},{64,32},{80,48},{96,64},{112,80},{1... | collective-permute-start | bytes 393224 | tf_op jit(solution)/shard_map/ppermute | solution.py:457
  55.0 8.1 %collective-permute-start.12 = (bf16[256,256]{1,0:T(8,128)(2,1)S(1)}, bf16[256,256]{1,0:T(8,128)(2,1)S(1)}, u32[]{:S(2)}, u32[]{:S(2)}) collective-permute-start(bf16[256,256]{1,0:T(8,128)(2,1)S(1)} %pad_maximum_fusion), channel_id=1, source_target_pairs={{0,64},{16,80},{32,96},{48,112},{64,0},{80,16},{96,32},{112,48},{1... | collective-permute-start | bytes 393224 | tf_op jit(solution)/shard_map/ppermute | solution.py:457
  63.1 6.2 %copy-start.8 = (f32[8,64,512]{2,1,0:T(8,128)S(1)}, f32[8,64,512]{2,1,0:T(8,128)}, u32[]{:S(2)}) copy-start(f32[8,64,512]{2,1,0:T(8,128)} %copy-done.7) | copy-start | bytes 3145732
  64.0 16.3 %collective-permute-start.13 = (bf16[576,256]{1,0:T(8,128)(2,1)S(1)}, bf16[576,256]{1,0:T(8,128)(2,1)S(1)}, u32[]{:S(2)}, u32[]{:S(2)}) collective-permute-start(bf16[576,256]{1,0:T(8,128)(2,1)S(1)} %get-tuple-element.71), channel_id=1, source_target_pairs={{0,3},{1,0},{2,1},{3,2},{4,7},{5,4},{6,5},{7,6},{8,11},{9,8},{10,9... | collective-permute-start | bytes 884744 | tf_op jit(solution)/shard_map/ppermute | solution.py:450
  67.7 16.0 %collective-permute-start.14 = (bf16[576,256]{1,0:T(8,128)(2,1)S(1)}, bf16[576,256]{1,0:T(8,128)(2,1)S(1)}, u32[]{:S(2)}, u32[]{:S(2)}) collective-permute-start(bf16[576,256]{1,0:T(8,128)(2,1)S(1)} %get-tuple-element.72), channel_id=1, source_target_pairs={{0,1},{1,2},{2,3},{3,0},{4,5},{5,6},{6,7},{7,4},{8,9},{9,10},{10,1... | collective-permute-start | bytes 884744 | tf_op jit(solution)/shard_map/ppermute | solution.py:450
  67.7 16.0 %copy-start.2 = (bf16[8,512,256]{2,1,0:T(8,128)(2,1)S(1)}, bf16[8,512,256]{2,1,0:T(8,128)(2,1)}, u32[]{:S(2)}) copy-start(bf16[8,512,256]{2,1,0:T(8,128)(2,1)} %basis.3) | copy-start | bytes 6291460
  67.7 16.0 %copy-start.3 = (bf16[8,256,256]{2,1,0:T(8,128)(2,1)S(1)}, bf16[8,256,256]{2,1,0:T(8,128)(2,1)}, u32[]{:S(2)}) copy-start(bf16[8,256,256]{2,1,0:T(8,128)(2,1)} %transfer.3) | copy-start | bytes 3145732
  67.7 16.0 %collective-permute-start.15 = (bf16[576,256]{1,0:T(8,128)(2,1)S(1)}, bf16[576,256]{1,0:T(8,128)(2,1)S(1)}, u32[]{:S(2)}, u32[]{:S(2)}) collective-permute-start(bf16[576,256]{1,0:T(8,128)(2,1)S(1)} %get-tuple-element.73), channel_id=1, source_target_pairs={{0,2},{1,3},{2,0},{3,1},{4,6},{5,7},{6,4},{7,5},{8,10},{9,11},{10,... | collective-permute-start | bytes 884744 | tf_op jit(solution)/shard_map/ppermute | solution.py:450

commit v7 on v6

--- a/solution.py
+++ b/solution.py
@@ -17,6 +17,7 @@
 SIDE = 4
 AUG = 128
 UNROLL = 8
+BATCH = 2
 VM = pl.BlockSpec(memory_space=pltpu.VMEM)
 SM = pl.BlockSpec(memory_space=pltpu.SMEM)
 
@@ -119,26 +120,51 @@
     )(points, sides, basis, transfer, skeleton, far)
 
 
-def far_total(ids, columns, row, target, side, weight_of):
-    points = target_side(target)
-    weights, tiles = [], []
-    for d, column in enumerate(columns):
-        named = ids[row, column]
-        at = jnp.maximum(named, 0)
-        tiles.append(
-            jnp.exp(
-                jnp.dot(side[d * LD + at], points, preferred_element_type=F32)
+def far_run(ids, columns, jobs, side_of, weight_of, tile):
+    depth = len(columns)
+
+    def first(slot, job):
+        row, target, _ = job
+        points = target_side(target())
+        for d, column in enumerate(columns):
+            at = jnp.maximum(ids[row, column], 0)
+            tile[slot, d * SK : (d + 1) * SK, :] = jnp.exp(
+                jnp.dot(side_of(d, at), points, preferred_element_type=F32)
             ).astype(BF)
-        )
-        weight = weight_of(d, at)
-        weights.append(jnp.where(named >= 0, weight, jnp.zeros_like(weight)))
-    if len(weights) == 1:
-        return jnp.dot(weights[0], tiles[0], preferred_element_type=F32)
-    return jnp.dot(
-        jnp.concatenate(weights, axis=1),
-        jnp.concatenate(tiles, axis=0),
-        preferred_element_type=F32,
-    )
+
+    def second(slot, job):
+        row, _, store = job
+        weights = []
+        for d, column in enumerate(columns):
+            named = ids[row, column]
+            weight = weight_of(d, jnp.maximum(named, 0))
+            weights.append(jnp.where(named >= 0, weight, jnp.zeros_like(weight)))
+        weight = weights[0] if depth == 1 else jnp.concatenate(weights, axis=1)
+        store(jnp.dot(weight, tile[slot, : depth * SK, :], preferred_element_type=F32))
+
+    slots = 2 * BATCH
+    groups = [jobs[i : i + BATCH] for i in range(0, len(jobs), BATCH)]
+    for g in range(len(groups) + 1):
+        if g < len(groups):
+            for k, job in enumerate(groups[g]):
+                first((g * BATCH + k) % slots, job)
+        if g > 0:
+            for k, job in enumerate(groups[g - 1]):
+                second(((g - 1) * BATCH + k) % slots, job)
+
+
+def target_jobs(base, target, out, given=None):
+    def job(leaf):
+        rows = slice(leaf * F, leaf * F + F)
+
+        def store(total):
+            if given is not None:
+                total = total + given[rows, :]
+            out[rows, :] = total.astype(out.dtype)
+
+        return base * LD + leaf, lambda: target[rows, :], store
+
+    return [job(leaf) for leaf in range(LD)]
 
 
 def rows_of(leaf):
@@ -156,15 +182,6 @@
 def columns_of(place):
     x, z = place[0], place[1]
     return [lax.rem(x + shift, SIDE) * SIDE + z for shift in (0, SIDE - 1, 1, 2)]
-
-
-def near_sources(ids, columns, side, sources, target, out, base):
-    @pl.loop(0, LD, unroll=UNROLL)
-    def _(leaf):
-        out[rows_of(leaf), :] = far_total(
-            ids, columns, base * LD + leaf, target[rows_of(leaf), :], side,
-            lambda d, at: charges_at(sources[d], at),
-        ).astype(out.dtype)
 
 
 def sides_kernel(s0, s1, s2, side):
@@ -187,10 +204,14 @@
     )(*sources)
 
 
-def far_a_kernel(ids, place, side, s0, s1, s2, t0, t1, t2, o0, o1, o2):
-    columns = columns_of(place)[:3]
+def far_a_kernel(ids, place, side, s0, s1, s2, t0, t1, t2, o0, o1, o2, tile):
+    jobs = []
     for b, (target, out) in enumerate(((t0, o0), (t1, o1), (t2, o2))):
-        near_sources(ids, columns, side, (s0, s1, s2), target, out, b)
+        jobs += target_jobs(b, target, out)
+    far_run(
+        ids, columns_of(place)[:3], jobs, lambda d, at: side[d * LD + at],
+        lambda d, at: charges_at((s0, s1, s2)[d], at), tile,
+    )
 
 
 def far_a(ids, place, side, sources, targets):
@@ -199,78 +220,63 @@
         in_specs=[SM, SM] + [VM] * 7,
         out_specs=[VM] * 3,
         out_shape=[jax.ShapeDtypeStruct((LD * F, SK), F32)] * 3,
+        scratch_shapes=[pltpu.VMEM((2 * BATCH, 3 * SK, SK), BF)],
         compiler_params=params(16),
         cost_estimate=cost(0.01),
         name="far_a",
     )(ids, place, side, *sources, *targets)
 
 
-def far_b_kernel(ids, place, given, s0, s1, s2, low, high, t3, o3, last, right, side):
-    half = LD // 2
-    for d, source in enumerate((low, high)):
-
-        @pl.loop(0, half, unroll=half)
-        def _(leaf, d=d, source=source):
-            value = source_side(skeleton_at(source, leaf))
-            side[3 * LD + d * half + leaf] = value
-            last[d * half + leaf] = value
-            right[d * half + leaf] = charges_at(source, leaf)
-
-    side[: 3 * LD] = given[...]
-    columns = columns_of(place)
-
-    def weight_of(d, at):
-        return right[at] if d == 3 else charges_at((s0, s1, s2)[d], at)
-
+def far_b_kernel(ids, place, side, s0, s1, s2, s3, t3, o3, last, tile):
     @pl.loop(0, LD, unroll=UNROLL)
     def _(leaf):
-        out = far_total(
-            ids, columns, 3 * LD + leaf, t3[rows_of(leaf), :], side, weight_of
-        )
-        o3[rows_of(leaf), :] = out.astype(o3.dtype)
-
-
-def far_b(ids, place, side, sources, halves, target):
+        last[leaf] = source_side(skeleton_at(s3, leaf))
+
+    far_run(
+        ids, columns_of(place), target_jobs(3, t3, o3),
+        lambda d, at: last[at] if d == 3 else side[d * LD + at],
+        lambda d, at: charges_at((s0, s1, s2, s3)[d], at), tile,
+    )
+
+
+def far_b(ids, place, side, sources, target):
     return pl.pallas_call(
         far_b_kernel,
-        in_specs=[SM, SM] + [VM] * 7,
-        out_specs=[VM] * 3,
+        in_specs=[SM, SM] + [VM] * 6,
+        out_specs=[VM] * 2,
         out_shape=[
             jax.ShapeDtypeStruct((LD * F, SK), BF),
             jax.ShapeDtypeStruct((LD, SK, AUG), BF),
-            jax.ShapeDtypeStruct((LD, RHS, SK), BF),
         ],
-        scratch_shapes=[pltpu.VMEM((SIDE * LD, SK, AUG), BF)],
-        compiler_params=params(16),
-        cost_estimate=cost(4),
+        scratch_shapes=[pltpu.VMEM((2 * BATCH, SIDE * SK, SK), BF)],
+        compiler_params=params(16),
+        cost_estimate=cost(3),
         name="far_b",
-    )(ids, place, side, *sources, *halves, target)
-
-
-def far_c_kernel(ids, place, side, right, t0, t1, t2, a0, a1, a2, own, r1, r2):
-    columns = columns_of(place)[3:]
+    )(ids, place, side, *sources, target)
+
+
+def far_c_kernel(ids, place, side, s3, t0, t1, t2, a0, a1, a2, own, r1, r2, tile):
+    jobs = []
     for b, (target, given, out) in enumerate(((t0, a0, own), (t1, a1, r1), (t2, a2, r2))):
-
-        @pl.loop(0, LD, unroll=UNROLL)
-        def _(leaf, b=b, target=target, given=given, out=out):
-            total = far_total(
-                ids, columns, b * LD + leaf, target[rows_of(leaf), :], side,
-                lambda d, at: right[at],
-            )
-            out[rows_of(leaf), :] = (given[rows_of(leaf), :] + total).astype(out.dtype)
-
-
-def far_c(ids, place, side, right, targets, given):
+        jobs += target_jobs(b, target, out, given)
+    far_run(
+        ids, columns_of(place)[3:], jobs, lambda d, at: side[at],
+        lambda d, at: charges_at(s3, at), tile,
+    )
+
+
+def far_c(ids, place, side, source, targets, given):
     return pl.pallas_call(
         far_c_kernel,
         in_specs=[SM, SM] + [VM] * 8,
         out_specs=[VM] * 3,
         out_shape=[jax.ShapeDtypeStruct((LD * F, SK), F32)]
         + [jax.ShapeDtypeStruct((LD * F, SK), BF)] * 2,
+        scratch_shapes=[pltpu.VMEM((2 * BATCH, SK, SK), BF)],
         compiler_params=params(16),
         cost_estimate=cost(4),
         name="far_c",
-    )(ids, place, side, right, *targets, *given)
+    )(ids, place, side, source, *targets, *given)
 
 
 def top_kernel(mine, pair, n1, n2, n3, a1, a2, a3, top, r1, r2, r3):
@@ -416,7 +422,7 @@
         total += r[last:, :].astype(F32)
     total = total.astype(BF)
 
-    @pl.loop(0, LD, unroll=2)
+    @pl.loop(0, LD, unroll=UNROLL)
     def _(leaf):
         rows = pl.ds(pl.multiple_of(leaf * F, F), F)
         potential = own[rows, :]
@@ -473,8 +479,7 @@
     targets[:3], sources, near_msg, near_sum = lax.optimization_barrier(
         (targets[:3], sources, near_msg, near_sum)
     )
-    half = LD * F
-    low, high = shifted(sources[1][:half], 1, 0), shifted(sources[2][half:], -1, 0)
+    opposite = shifted(sources[1], 1, 0)
     side = sides_of(sources)
     near_msg, side = lax.optimization_barrier((near_msg, side))
     count = lax.axis_size("leaf") * lax.axis_size("top")
@@ -488,16 +493,17 @@
 
     place = jnp.stack([at // SIDE, at % SIDE]).astype(jnp.int32)
     given = far_a(ids_of(targets[:3]), place, side, sources, targets[:3])
-    low, high, given, targets[3] = lax.optimization_barrier((low, high, given, targets[3]))
-    line_charge = sum(s[2 * half :].astype(F32) for s in sources) + high[half:].astype(F32)
+    opposite, given, targets[3] = lax.optimization_barrier((opposite, given, targets[3]))
+    sources.append(opposite)
+    line_charge = sum(s[2 * LD * F :].astype(F32) for s in sources)
     mine = jnp.concatenate([line_charge.astype(BF), node_points[0]], axis=0)
     pair = leaf_shifted(mine, 0)
     ids = ids_of(targets)
-    r3, last, right = far_b(ids, place, side, sources, (low, high), targets[3])
+    r3, last = far_b(ids, place, side, sources, targets[3])
     pair, r3, last = lax.optimization_barrier((pair, r3, last))
     both = jnp.concatenate([mine, pair], axis=0)
     others = [leaf_shifted(both, dy) for dy in (1, -1, 2)]
-    own, r1, r2 = far_c(ids, place, last, right, targets[:3], given)
+    own, r1, r2 = far_c(ids, place, last, opposite, targets[:3], given)
     top, *parts = top_sum(mine, pair, others, (r1, r2, r3))
     returned = [shifted(r, 0, dz) for r, dz in zip(parts, (-1, 1, 2))]
     near_sum = near_rest(neighbours, first, near_msg, before, after, near_sum)

time: 87.7 us -> 82.7 us (0.943)
  the two profiles are of different devices: /device:TPU:0 before, /device:TPU:14 now
where the time goes in v7:
time: 82.7 us; the launch traced here: 82.4 us
  Pallas kernels  36.1 us (44%)
  starting transfers between devices  22.7 us (27%)
  waiting for transfers between devices  20.4 us (25%)
  local copies, waits for them, and re-layouts  2.84 us (3%)
    ppermute x3, waiting for transfers between devices, leaf_shifted(): lax.ppermute(value, 'leaf', [(i, (i + 2 * dy) % count) for i in range(cou...  11.7 us
    ppermute x9, starting transfers between devices, shifted(): return lax.ppermute(value, 'top', pairs)  10.1 us
    pallas_call x1, Pallas kernels, near_rest(): pl.pallas_call(near_rest_kernel, in_specs=[SM, SM, VM, VM, VM, VM], out_s...  9.16 us
    ppermute x9, waiting for transfers between devices, shifted(): return lax.ppermute(value, 'top', pairs)  8.72 us
    pallas_call x1, Pallas kernels, near_own(): pl.pallas_call(near_own_kernel, in_specs=[SM, SM, VM], out_specs=VM, out_...  7.81 us
    ppermute x1, starting transfers between devices, on_device(): after = lax.ppermute(near_msg, ('leaf', 'top'), [(j, i) for i, j in up])  5.03 us
    pallas_call x1, Pallas kernels, far_a(): pl.pallas_call(far_a_kernel, in_specs=[SM, SM] + [VM] * 7, out_specs=[VM]...  4.96 us
    pallas_call x1, Pallas kernels, prep(): pl.pallas_call(prep_kernel, in_specs=[anywhere] * 4 + [VM] * 2, out_specs...  4.9 us
  transfers between devices with their start and end apart: 15, of which 5 were waited for; matrix products, arithmetic and copies ran while one was open for 0% of the time, Pallas kernels for 35%

profile of v7, /device:TPU:14, one launch (start us, length us, event | category | flops | bytes accessed | tf_op | source)
XLA Modules:
  0.0 82.4 jit_solution(17403691505458976971)
XLA Ops:
  0.0 0.0 copy-start.6
  0.0 4.9 %prep.1 = (bf16[8,128,512]{2,1,0:T(8,128)(2,1)}, bf16[1088,256]{1,0:T(8,128)(2,1)}, bf16[528,256]{1,0:T(8,128)(2,1)}) custom-call(bf16[8,64,512]{2,1,0:T(8,128)(2,1)} %points.1, bf16[8,64,512]{2,1,0:T(8,128)(2,1)} %sides.2, bf16[8,512,256]{2,1,0:T(8,128)(2,1)} %basis.3, bf16[8,256,256]{2,1,0:T(8,128)(2,1)} %transfer.3, s32[8,256]{1,0:T(8,128)} %skeleton.1, ...), custom_call_target="tpu_custom_call" | custom-call | flops 4000000000 | bytes 1000000 | tf_op jit(solution)/shard_map/prep/pallas_call | solution.py:101
  4.9 2.0 %collective-permute-start = (bf16[528,256]{1,0:T(8,128)(2,1)}, bf16[528,256]{1,0:T(8,128)(2,1)S(1)}, u32[]{:S(2)}, u32[]{:S(2)}) collective-permute-start(bf16[528,256]{1,0:T(8,128)(2,1)} %get-tuple-element.47.t0), channel_id=1, source_target_pairs={{0,1},{1,2},{2,3},{3,0},{4,5},{5,6},{6,7},{7,4},{8,9},{9,10},{10,1... | collective-permute-start | bytes 811016 | tf_op jit(solution)/shard_map/ppermute | solution.py:456
  6.9 2.2 %collective-permute-start.1 = (bf16[528,256]{1,0:T(8,128)(2,1)}, bf16[528,256]{1,0:T(8,128)(2,1)S(1)}, u32[]{:S(2)}, u32[]{:S(2)}) collective-permute-start(bf16[528,256]{1,0:T(8,128)(2,1)} %get-tuple-element.47.t0), channel_id=1, source_target_pairs={{0,3},{1,0},{2,1},{3,2},{4,7},{5,4},{6,5},{7,6},{8,11},{9,8},{10,9... | collective-permute-start | bytes 811016 | tf_op jit(solution)/shard_map/ppermute | solution.py:456
  9.1 0.5 collective-permute-start.2
  9.6 1.5 %collective-permute-start.3 = (bf16[1088,256]{1,0:T(8,128)(2,1)}, bf16[1088,256]{1,0:T(8,128)(2,1)S(1)}, u32[]{:S(2)}, u32[]{:S(2)}) collective-permute-start(bf16[1088,256]{1,0:T(8,128)(2,1)} %get-tuple-element.42.s0), channel_id=1, source_target_pairs={{0,12},{1,13},{2,14},{3,15},{4,0},{5,1},{6,2},{7,3},{8,4},{9,5},{1... | collective-permute-start | bytes 1671176 | tf_op jit(solution)/shard_map/ppermute | solution.py:456
  11.1 0.0 copy-done.6
  11.1 0.0 copy-start.4
  11.1 1.2 %copy-done.4 = bf16[8,128,512]{2,1,0:T(8,128)(2,1)S(1)} copy-done((bf16[8,128,512]{2,1,0:T(8,128)(2,1)S(1)}, bf16[8,128,512]{2,1,0:T(8,128)(2,1)}, u32[]{:S(2)}) %copy-start.4) | copy-done | bytes 1048600
  12.3 0.0 copy-start.1
  12.3 0.0 copy-start
  12.4 7.8 %near_own.1.given = f32[8,64,512]{2,1,0:T(8,128)S(1)} custom-call(s32[8,8]{1,0:T(8,128)S(1)} %copy-done.6, s32[1]{0:T(128)} %bitcast.first, bf16[8,128,512]{2,1,0:T(8,128)(2,1)S(1)} %copy-done.4), custom_call_target="tpu_custom_call" | custom-call | flops 8999999488 | bytes 1000000 | tf_op jit(solution)/shard_map/near_own/pallas_call | solution.py:365
  20.2 0.0 copy-start.7
  20.2 0.9 %copy-done.7 = f32[8,64,512]{2,1,0:T(8,128)} copy-done((f32[8,64,512]{2,1,0:T(8,128)}, f32[8,64,512]{2,1,0:T(8,128)S(1)}, u32[]{:S(2)}) %copy-start.7) | copy-done | bytes 1048600
  21.1 0.0 collective-permute-done.t1
  21.1 0.0 collective-permute-done.1.t2
  21.1 2.3 %collective-permute-done.2.s1 = bf16[1088,256]{1,0:T(8,128)(2,1)S(1)} collective-permute-done((bf16[1088,256]{1,0:T(8,128)(2,1)}, bf16[1088,256]{1,0:T(8,128)(2,1)S(1)}, u32[]{:S(2)}, u32[]{:S(2)}) %collective-permute-start.2) | collective-permute-done | bytes 557088 | tf_op jit(solution)/shard_map/ppermute | solution.py:456
  23.4 1.4 %collective-permute-done.3.s2 = bf16[1088,256]{1,0:T(8,128)(2,1)S(1)} collective-permute-done((bf16[1088,256]{1,0:T(8,128)(2,1)}, bf16[1088,256]{1,0:T(8,128)(2,1)S(1)}, u32[]{:S(2)}, u32[]{:S(2)}) %collective-permute-start.3) | collective-permute-done | bytes 557088 | tf_op jit(solution)/shard_map/ppermute | solution.py:456
  24.8 0.3 collective-permute-start.6
  25.1 0.0 copy-done.1
  25.1 1.5 %collective-permute-start.7 = (bf16[528,256]{1,0:T(8,128)(2,1)S(1)}, bf16[528,256]{1,0:T(8,128)(2,1)S(1)}, u32[]{:S(2)}, u32[]{:S(2)}) collective-permute-start(bf16[528,256]{1,0:T(8,128)(2,1)S(1)} %copy-done.1), channel_id=1, source_target_pairs={{0,2},{1,3},{2,0},{3,1},{4,6},{5,7},{6,4},{7,5},{8,10},{9,11},{10,... | collective-permute-start | bytes 811016 | tf_op jit(solution)/shard_map/ppermute | solution.py:456
  26.6 0.0 copy-start.5
  26.6 0.1 pad_add_fusion.place
  26.7 0.0 copy-done
  26.7 0.5 sides.3.side
  27.2 0.6 copy-done.5
  27.8 2.9 %collective-permute-start.4 = (bf16[8,128,512]{2,1,0:T(8,128)(2,1)S(1)}, bf16[8,128,512]{2,1,0:T(8,128)(2,1)S(1)}, u32[]{:S(2)}, u32[]{:S(2)}) collective-permute-start(bf16[8,128,512]{2,1,0:T(8,128)(2,1)S(1)} %copy-done.5), channel_id=1, source_target_pairs={{0,1},{1,2},{2,3},{3,4},{4,5},{5,6},{6,7},{7,8},{8,9},{9,10},{10,1... | collective-permute-start | bytes 3145736 | tf_op jit(solution)/shard_map/ppermute | solution.py:487
  30.7 5.0 %collective-permute-start.5 = (bf16[8,128,512]{2,1,0:T(8,128)(2,1)S(1)}, bf16[8,128,512]{2,1,0:T(8,128)(2,1)S(1)}, u32[]{:S(2)}, u32[]{:S(2)}) collective-permute-start(bf16[8,128,512]{2,1,0:T(8,128)(2,1)S(1)} %copy-done.5), channel_id=1, source_target_pairs={{1,0},{2,1},{3,2},{4,3},{5,4},{6,5},{7,6},{8,7},{9,8},{10,9},{11,1... | collective-permute-start | bytes 3145736 | tf_op jit(solution)/shard_map/ppermute | solution.py:488
  35.8 0.0 copy-start.9
  35.8 5.0 %far_a.1 = (f32[512,256]{1,0:T(8,128)S(1)}, f32[512,256]{1,0:T(8,128)S(1)}, f32[512,256]{1,0:T(8,128)S(1)}) custom-call(s32[24,16]{1,0:T(8,128)S(1)} %maximum_convert_fusion.1.ids, s32[2]{0:T(128)S(1)} %pad_add_fusion.place, bf16[24,256,128]{2,1,0:T(8,128)(2,1)S(1)} %sides.3.side, bf16[1088,256]{1,0:T(8,128)(2,1)S(1)} %copy-done, ...), custom_call_target="tpu_custom_call" | custom-call | flops 10000000 | bytes 1000000 | tf_op jit(solution)/shard_map/far_a/pallas_call | solution.py:218
  40.8 0.0 collective-permute-done.7.t3
  40.8 0.0 collective-permute-done.6.s3
  40.9 0.0 copy-done.9
  40.9 0.3 collective-permute-start.8
  41.2 2.9 %far_b.1 = (bf16[512,256]{1,0:T(8,128)(2,1)S(1)}, bf16[8,256,128]{2,1,0:T(8,128)(2,1)S(1)}) custom-call(s32[32,16]{1,0:T(8,128)S(1)} %maximum_convert_fusion.ids, s32[2]{0:T(128)S(1)} %pad_add_fusion.place, bf16[24,256,128]{2,1,0:T(8,128)(2,1)S(1)} %sides.3.side, bf16[1088,256]{1,0:T(8,128)(2,1)S(1)} %copy-done, ...), custom_call_target="tpu_custom_call" | custom-call | flops 3000000000 | bytes 1000000 | tf_op jit(solution)/shard_map/far_b/pallas_call | solution.py:243
  44.1 0.0 collective-permute-done.8.pair
  44.2 1.7 %collective-permute-start.9 = (bf16[256,256]{1,0:T(8,128)(2,1)S(1)}, bf16[256,256]{1,0:T(8,128)(2,1)S(1)}, u32[]{:S(2)}, u32[]{:S(2)}) collective-permute-start(bf16[256,256]{1,0:T(8,128)(2,1)S(1)} %pad_maximum_fusion), channel_id=1, source_target_pairs={{0,32},{16,48},{32,64},{48,80},{64,96},{80,112},{96,0},{112,16},{1... | collective-permute-start | bytes 393224 | tf_op jit(solution)/shard_map/ppermute | solution.py:463
  45.8 0.4 collective-permute-start.10
  46.2 2.3 %collective-permute-start.11 = (bf16[256,256]{1,0:T(8,128)(2,1)S(1)}, bf16[256,256]{1,0:T(8,128)(2,1)S(1)}, u32[]{:S(2)}, u32[]{:S(2)}) collective-permute-start(bf16[256,256]{1,0:T(8,128)(2,1)S(1)} %pad_maximum_fusion), channel_id=1, source_target_pairs={{0,64},{16,80},{32,96},{48,112},{64,0},{80,16},{96,32},{112,48},{1... | collective-permute-start | bytes 393224 | tf_op jit(solution)/shard_map/ppermute | solution.py:463
  48.6 2.5 %far_c.1 = (f32[512,256]{1,0:T(8,128)S(1)}, bf16[512,256]{1,0:T(8,128)(2,1)S(1)}, bf16[512,256]{1,0:T(8,128)(2,1)S(1)}) custom-call(s32[32,16]{1,0:T(8,128)S(1)} %maximum_convert_fusion.ids, s32[2]{0:T(128)S(1)} %pad_add_fusion.place, bf16[8,256,128]{2,1,0:T(8,128)(2,1)S(1)} %get-tuple-element.58.side, bf16[1088,256]{1,0:T(8,128)(2,1)S(1)} %collective-permute-done.6.s3, ...), custom_call_target="tpu_custom_call" | custom-call | flops 4000000000 | bytes 1000000 | tf_op jit(solution)/shard_map/far_c/pallas_call | solution.py:269
  51.0 0.0 collective-permute-done.9.n1
  51.0 3.2 %collective-permute-done.10.n2 = bf16[256,256]{1,0:T(8,128)(2,1)S(1)} collective-permute-done((bf16[256,256]{1,0:T(8,128)(2,1)S(1)}, bf16[256,256]{1,0:T(8,128)(2,1)S(1)}, u32[]{:S(2)}, u32[]{:S(2)}) %collective-permute-start.10) | collective-permute-done | bytes 131104 | tf_op jit(solution)/shard_map/ppermute | solution.py:463
  54.2 8.5 %collective-permute-done.11.n3 = bf16[256,256]{1,0:T(8,128)(2,1)S(1)} collective-permute-done((bf16[256,256]{1,0:T(8,128)(2,1)S(1)}, bf16[256,256]{1,0:T(8,128)(2,1)S(1)}, u32[]{:S(2)}, u32[]{:S(2)}) %collective-permute-start.11) | collective-permute-done | bytes 131104 | tf_op jit(solution)/shard_map/ppermute | solution.py:463
  62.7 0.0 copy-start.8
  62.7 0.8 %top_sum.1 = (f32[64,256]{1,0:T(8,128)S(1)}, bf16[576,256]{1,0:T(8,128)(2,1)S(1)}, bf16[576,256]{1,0:T(8,128)(2,1)S(1)}, bf16[576,256]{1,0:T(8,128)(2,1)S(1)}) custom-call(bf16[128,256]{1,0:T(8,128)(2,1)S(1)} %pad_maximum_fusion.1.mine, bf16[128,256]{1,0:T(8,128)(2,1)S(1)} %collective-permute-done.8.pair, bf16[256,256]{1,0:T(8,128)(2,1)S(1)} %collective-permute-done.9.n1, ...), custom_call_target="tpu_custom_call" | custom-call | flops 2000000000 | bytes 1000000 | tf_op jit(solution)/shard_map/top_sum/pallas_call | solution.py:299
  63.6 0.1 collective-permute-start.12
  63.6 2.0 %collective-permute-start.13 = (bf16[576,256]{1,0:T(8,128)(2,1)S(1)}, bf16[576,256]{1,0:T(8,128)(2,1)S(1)}, u32[]{:S(2)}, u32[]{:S(2)}) collective-permute-start(bf16[576,256]{1,0:T(8,128)(2,1)S(1)} %get-tuple-element.68), channel_id=1, source_target_pairs={{0,1},{1,2},{2,3},{3,0},{4,5},{5,6},{6,7},{7,4},{8,9},{9,10},{10,1... | collective-permute-start | bytes 884744 | tf_op jit(solution)/shard_map/ppermute | solution.py:456
  65.7 0.0 copy-start.2
  65.7 0.0 copy-start.3
  65.7 0.0 collective-permute-start.14
  65.7 0.0 collective-permute-done.4.before
  65.7 0.0 collective-permute-done.5.after
  65.7 0.0 copy-done.8
  65.7 9.2 %near_rest.1.near_sum = f32[8,64,512]{2,1,0:T(8,128)S(1)} custom-call(s32[8,8]{1,0:T(8,128)S(1)} %copy-done.6, s32[1]{0:T(128)} %bitcast.first, bf16[8,128,512]{2,1,0:T(8,128)(2,1)S(1)} %copy-done.5, bf16[8,128,512]{2,1,0:T(8,128)(2,1)S(1)} %collective-permute-done.4.before, bf16[8,128,512]{2,1,0:T(8,128)(2,1)S(1)} %collective-permute-done.5.after, ...), custom_call_target="tpu_custom_call" | custom-call | flops 11000000512 | bytes 1000000 | tf_op jit(solution)/shard_map/near_rest/pallas_call | solution.py:401
  74.9 0.0 collective-permute-done.12.r1
  74.9 5.0 %collective-permute-done.13.r2 = bf16[576,256]{1,0:T(8,128)(2,1)S(1)} collective-permute-done((bf16[576,256]{1,0:T(8,128)(2,1)S(1)}, bf16[576,256]{1,0:T(8,128)(2,1)S(1)}, u32[]{:S(2)}, u32[]{:S(2)}) %collective-permute-start.13) | collective-permute-done | bytes 294944 | tf_op jit(solution)/shard_map/ppermute | solution.py:456
  79.9 0.0 collective-permute-done.14.r3
  79.9 0.0 copy-done.2
  79.9 0.0 copy-done.3
  79.9 2.5 %final.1 = bf16[8,64,512]{2,1,0:T(8,128)(2,1)} custom-call(f32[8,64,512]{2,1,0:T(8,128)S(1)} %near_rest.1.near_sum, bf16[8,512,256]{2,1,0:T(8,128)(2,1)S(1)} %copy-done.2, bf16[8,256,256]{2,1,0:T(8,128)(2,1)S(1)} %copy-done.3, f32[512,256]{1,0:T(8,128)S(1)} %get-tuple-element.62.own, bf16[576,256]{1,0:T(8,128)(2,1)S(1)} %collective-permute-done.12.r1, ...), custom_call_target="tpu_custom_call" | custom-call | flops 3000000000 | bytes 1000000 | tf_op jit(solution)/shard_map/final/pallas_call | solution.py:439
  (9 shorter events, 0.1 us)
Async XLA Ops:
  0.0 11.1 %copy-start.6 = (s32[8,8]{1,0:T(8,128)S(1)}, s32[8,8]{1,0:T(8,128)}, u32[]{:S(2)}) copy-start(s32[8,8]{1,0:T(8,128)} %ids.3) | copy-start | bytes 772
  4.9 16.2 %collective-permute-start = (bf16[528,256]{1,0:T(8,128)(2,1)}, bf16[528,256]{1,0:T(8,128)(2,1)S(1)}, u32[]{:S(2)}, u32[]{:S(2)}) collective-permute-start(bf16[528,256]{1,0:T(8,128)(2,1)} %get-tuple-element.47.t0), channel_id=1, source_target_pairs={{0,1},{1,2},{2,3},{3,0},{4,5},{5,6},{6,7},{7,4},{8,9},{9,10},{10,1... | collective-permute-start | bytes 811016 | tf_op jit(solution)/shard_map/ppermute | solution.py:456
  6.9 14.2 %collective-permute-start.1 = (bf16[528,256]{1,0:T(8,128)(2,1)}, bf16[528,256]{1,0:T(8,128)(2,1)S(1)}, u32[]{:S(2)}, u32[]{:S(2)}) collective-permute-start(bf16[528,256]{1,0:T(8,128)(2,1)} %get-tuple-element.47.t0), channel_id=1, source_target_pairs={{0,3},{1,0},{2,1},{3,2},{4,7},{5,4},{6,5},{7,6},{8,11},{9,8},{10,9... | collective-permute-start | bytes 811016 | tf_op jit(solution)/shard_map/ppermute | solution.py:456
  9.1 14.3 %collective-permute-start.2 = (bf16[1088,256]{1,0:T(8,128)(2,1)}, bf16[1088,256]{1,0:T(8,128)(2,1)S(1)}, u32[]{:S(2)}, u32[]{:S(2)}) collective-permute-start(bf16[1088,256]{1,0:T(8,128)(2,1)} %get-tuple-element.42.s0), channel_id=1, source_target_pairs={{0,4},{1,5},{2,6},{3,7},{4,8},{5,9},{6,10},{7,11},{8,12},{9,13},{1... | collective-permute-start | bytes 1671176 | tf_op jit(solution)/shard_map/ppermute | solution.py:456
  9.6 15.2 %collective-permute-start.3 = (bf16[1088,256]{1,0:T(8,128)(2,1)}, bf16[1088,256]{1,0:T(8,128)(2,1)S(1)}, u32[]{:S(2)}, u32[]{:S(2)}) collective-permute-start(bf16[1088,256]{1,0:T(8,128)(2,1)} %get-tuple-element.42.s0), channel_id=1, source_target_pairs={{0,12},{1,13},{2,14},{3,15},{4,0},{5,1},{6,2},{7,3},{8,4},{9,5},{1... | collective-permute-start | bytes 1671176 | tf_op jit(solution)/shard_map/ppermute | solution.py:456
  11.1 1.2 %copy-start.4 = (bf16[8,128,512]{2,1,0:T(8,128)(2,1)S(1)}, bf16[8,128,512]{2,1,0:T(8,128)(2,1)}, u32[]{:S(2)}) copy-start(bf16[8,128,512]{2,1,0:T(8,128)(2,1)} %get-tuple-element.45.own) | copy-start | bytes 3145732
  12.3 12.7 %copy-start.1 = (bf16[528,256]{1,0:T(8,128)(2,1)S(1)}, bf16[528,256]{1,0:T(8,128)(2,1)}, u32[]{:S(2)}) copy-start(bf16[528,256]{1,0:T(8,128)(2,1)} %get-tuple-element.47.t0) | copy-start | bytes 811012
  12.3 14.3 %copy-start = (bf16[1088,256]{1,0:T(8,128)(2,1)S(1)}, bf16[1088,256]{1,0:T(8,128)(2,1)}, u32[]{:S(2)}) copy-start(bf16[1088,256]{1,0:T(8,128)(2,1)} %get-tuple-element.42.s0) | copy-start | bytes 1671172
  20.2 1.0 %copy-start.7 = (f32[8,64,512]{2,1,0:T(8,128)}, f32[8,64,512]{2,1,0:T(8,128)S(1)}, u32[]{:S(2)}) copy-start(f32[8,64,512]{2,1,0:T(8,128)S(1)} %near_own.1.given) | copy-start | bytes 3145732
  24.8 16.0 %collective-permute-start.6 = (bf16[1088,256]{1,0:T(8,128)(2,1)S(1)}, bf16[1088,256]{1,0:T(8,128)(2,1)S(1)}, u32[]{:S(2)}, u32[]{:S(2)}) collective-permute-start(bf16[1088,256]{1,0:T(8,128)(2,1)S(1)} %collective-permute-done.2.s1), channel_id=1, source_target_pairs={{0,4},{1,5},{2,6},{3,7},{4,8},{5,9},{6,10},{7,11},{8,12},{9,13},{1... | collective-permute-start | bytes 1671176 | tf_op jit(solution)/shard_map/ppermute | solution.py:456
  25.1 15.7 %collective-permute-start.7 = (bf16[528,256]{1,0:T(8,128)(2,1)S(1)}, bf16[528,256]{1,0:T(8,128)(2,1)S(1)}, u32[]{:S(2)}, u32[]{:S(2)}) collective-permute-start(bf16[528,256]{1,0:T(8,128)(2,1)S(1)} %copy-done.1), channel_id=1, source_target_pairs={{0,2},{1,3},{2,0},{3,1},{4,6},{5,7},{6,4},{7,5},{8,10},{9,11},{10,... | collective-permute-start | bytes 811016 | tf_op jit(solution)/shard_map/ppermute | solution.py:456
  26.6 1.2 %copy-start.5 = (bf16[8,128,512]{2,1,0:T(8,128)(2,1)S(1)}, bf16[8,128,512]{2,1,0:T(8,128)(2,1)}, u32[]{:S(2)}) copy-start(bf16[8,128,512]{2,1,0:T(8,128)(2,1)} %get-tuple-element.45.own) | copy-start | bytes 3145732
  27.8 37.9 %collective-permute-start.4 = (bf16[8,128,512]{2,1,0:T(8,128)(2,1)S(1)}, bf16[8,128,512]{2,1,0:T(8,128)(2,1)S(1)}, u32[]{:S(2)}, u32[]{:S(2)}) collective-permute-start(bf16[8,128,512]{2,1,0:T(8,128)(2,1)S(1)} %copy-done.5), channel_id=1, source_target_pairs={{0,1},{1,2},{2,3},{3,4},{4,5},{5,6},{6,7},{7,8},{8,9},{9,10},{10,1... | collective-permute-start | bytes 3145736 | tf_op jit(solution)/shard_map/ppermute | solution.py:487
  30.7 34.9 %collective-permute-start.5 = (bf16[8,128,512]{2,1,0:T(8,128)(2,1)S(1)}, bf16[8,128,512]{2,1,0:T(8,128)(2,1)S(1)}, u32[]{:S(2)}, u32[]{:S(2)}) collective-permute-start(bf16[8,128,512]{2,1,0:T(8,128)(2,1)S(1)} %copy-done.5), channel_id=1, source_target_pairs={{1,0},{2,1},{3,2},{4,3},{5,4},{6,5},{7,6},{8,7},{9,8},{10,9},{11,1... | collective-permute-start | bytes 3145736 | tf_op jit(solution)/shard_map/ppermute | solution.py:488
  35.8 5.0 %copy-start.9 = (bf16[1,64,256]{2,1,0:T(8,128)(2,1)S(1)}, bf16[1,64,256]{2,1,0:T(8,128)(2,1)}, u32[]{:S(2)}) copy-start(bf16[1,64,256]{2,1,0:T(8,128)(2,1)} %param.12) | copy-start | bytes 98308
  40.9 3.2 %collective-permute-start.8 = (bf16[128,256]{1,0:T(8,128)(2,1)S(1)}, bf16[128,256]{1,0:T(8,128)(2,1)S(1)}, u32[]{:S(2)}, u32[]{:S(2)}) collective-permute-start(bf16[128,256]{1,0:T(8,128)(2,1)S(1)} %pad_maximum_fusion.1.mine), channel_id=1, source_target_pairs={{0,16},{16,0},{32,48},{48,32},{64,80},{80,64},{96,112},{112,96},{1... | collective-permute-start | bytes 196616 | tf_op jit(solution)/shard_map/ppermute | solution.py:462
  44.2 6.9 %collective-permute-start.9 = (bf16[256,256]{1,0:T(8,128)(2,1)S(1)}, bf16[256,256]{1,0:T(8,128)(2,1)S(1)}, u32[]{:S(2)}, u32[]{:S(2)}) collective-permute-start(bf16[256,256]{1,0:T(8,128)(2,1)S(1)} %pad_maximum_fusion), channel_id=1, source_target_pairs={{0,32},{16,48},{32,64},{48,80},{64,96},{80,112},{96,0},{112,16},{1... | collective-permute-start | bytes 393224 | tf_op jit(solution)/shard_map/ppermute | solution.py:463
  45.8 8.4 %collective-permute-start.10 = (bf16[256,256]{1,0:T(8,128)(2,1)S(1)}, bf16[256,256]{1,0:T(8,128)(2,1)S(1)}, u32[]{:S(2)}, u32[]{:S(2)}) collective-permute-start(bf16[256,256]{1,0:T(8,128)(2,1)S(1)} %pad_maximum_fusion), channel_id=1, source_target_pairs={{0,96},{16,112},{32,0},{48,16},{64,32},{80,48},{96,64},{112,80},{1... | collective-permute-start | bytes 393224 | tf_op jit(solution)/shard_map/ppermute | solution.py:463
  46.2 16.5 %collective-permute-start.11 = (bf16[256,256]{1,0:T(8,128)(2,1)S(1)}, bf16[256,256]{1,0:T(8,128)(2,1)S(1)}, u32[]{:S(2)}, u32[]{:S(2)}) collective-permute-start(bf16[256,256]{1,0:T(8,128)(2,1)S(1)} %pad_maximum_fusion), channel_id=1, source_target_pairs={{0,64},{16,80},{32,96},{48,112},{64,0},{80,16},{96,32},{112,48},{1... | collective-permute-start | bytes 393224 | tf_op jit(solution)/shard_map/ppermute | solution.py:463
  62.7 3.0 %copy-start.8 = (f32[8,64,512]{2,1,0:T(8,128)S(1)}, f32[8,64,512]{2,1,0:T(8,128)}, u32[]{:S(2)}) copy-start(f32[8,64,512]{2,1,0:T(8,128)} %copy-done.7) | copy-start | bytes 3145732
  63.6 11.3 %collective-permute-start.12 = (bf16[576,256]{1,0:T(8,128)(2,1)S(1)}, bf16[576,256]{1,0:T(8,128)(2,1)S(1)}, u32[]{:S(2)}, u32[]{:S(2)}) collective-permute-start(bf16[576,256]{1,0:T(8,128)(2,1)S(1)} %get-tuple-element.67), channel_id=1, source_target_pairs={{0,3},{1,0},{2,1},{3,2},{4,7},{5,4},{6,5},{7,6},{8,11},{9,8},{10,9... | collective-permute-start | bytes 884744 | tf_op jit(solution)/shard_map/ppermute | solution.py:456
  63.6 16.3 %collective-permute-start.13 = (bf16[576,256]{1,0:T(8,128)(2,1)S(1)}, bf16[576,256]{1,0:T(8,128)(2,1)S(1)}, u32[]{:S(2)}, u32[]{:S(2)}) collective-permute-start(bf16[576,256]{1,0:T(8,128)(2,1)S(1)} %get-tuple-element.68), channel_id=1, source_target_pairs={{0,1},{1,2},{2,3},{3,0},{4,5},{5,6},{6,7},{7,4},{8,9},{9,10},{10,1... | collective-permute-start | bytes 884744 | tf_op jit(solution)/shard_map/ppermute | solution.py:456
  65.7 14.3 %copy-start.2 = (bf16[8,512,256]{2,1,0:T(8,128)(2,1)S(1)}, bf16[8,512,256]{2,1,0:T(8,128)(2,1)}, u32[]{:S(2)}) copy-start(bf16[8,512,256]{2,1,0:T(8,128)(2,1)} %basis.3) | copy-start | bytes 6291460
  65.7 14.3 %copy-start.3 = (bf16[8,256,256]{2,1,0:T(8,128)(2,1)S(1)}, bf16[8,256,256]{2,1,0:T(8,128)(2,1)}, u32[]{:S(2)}) copy-start(bf16[8,256,256]{2,1,0:T(8,128)(2,1)} %transfer.3) | copy-start | bytes 3145732
  65.7 14.3 %collective-permute-start.14 = (bf16[576,256]{1,0:T(8,128)(2,1)S(1)}, bf16[576,256]{1,0:T(8,128)(2,1)S(1)}, u32[]{:S(2)}, u32[]{:S(2)}) collective-permute-start(bf16[576,256]{1,0:T(8,128)(2,1)S(1)} %get-tuple-element.69), channel_id=1, source_target_pairs={{0,2},{1,3},{2,0},{3,1},{4,6},{5,7},{6,4},{7,5},{8,10},{9,11},{10,... | collective-permute-start | bytes 884744 | tf_op jit(solution)/shard_map/ppermute | solution.py:456

commit v8 on v7

--- a/solution.py
+++ b/solution.py
@@ -279,7 +279,7 @@
     )(ids, place, side, source, *targets, *given)
 
 
-def top_kernel(mine, pair, n1, n2, n3, a1, a2, a3, top, r1, r2, r3):
+def top_kernel(mine, pair, n1, n2, n3, top, sent):
     points = target_side(mine[RHS:, :])
     total = jnp.zeros((RHS, SK), F32)
     rows = 2 * RHS
@@ -290,22 +290,22 @@
         ).astype(BF)
         total += jnp.dot(other[:RHS, :], kernel, preferred_element_type=F32)
     top[...] = total
-    for given, out in ((a1, r1), (a2, r2), (a3, r3)):
-        out[: LD * F, :] = given[...]
-        out[LD * F :, :] = total.astype(BF)
-
-
-def top_sum(mine, pair, others, parts):
+    sent[...] = total.astype(BF)
+
+
+def top_sum(mine, pair, others):
     return pl.pallas_call(
         top_kernel,
-        in_specs=[VM] * 8,
-        out_specs=[VM] * 4,
-        out_shape=[jax.ShapeDtypeStruct((RHS, SK), F32)]
-        + [jax.ShapeDtypeStruct((LD * F + RHS, SK), BF)] * 3,
-        compiler_params=params(16),
-        cost_estimate=cost(2),
+        in_specs=[VM] * 5,
+        out_specs=[VM] * 2,
+        out_shape=[
+            jax.ShapeDtypeStruct((RHS, SK), F32),
+            jax.ShapeDtypeStruct((RHS, SK), BF),
+        ],
+        compiler_params=params(16),
+        cost_estimate=cost(0.01),
         name="top_sum",
-    )(mine, pair, *others, *parts)
+    )(mine, pair, *others)
 
 
 def near_groups(ids, leaf, place_of, points, side, rights, slots, out, given=None):
@@ -374,77 +374,101 @@
     )(ids, first, own)
 
 
-def near_rest_kernel(ids, first, own, before, after, given, out, side, rights, slots):
-    for d, block in enumerate((before, after)):
-
-        @pl.loop(0, LD, unroll=4)
-        def _(leaf, d=d, block=block):
-            side[d * LD + leaf] = source_side(block[leaf, :F, :])
-            rights[d * LD + leaf] = block[leaf, F:, :]
-
+def near_rest_leaves(ids, first, own, given, out, side, rights, slots, begin):
     def place_of(named):
         at = named - first[0]
         below = (at >= -LD) & (at < 0)
         above = (at >= LD) & (at < 2 * LD)
         return (named >= 0) & (below | above), jnp.where(below, at + LD, at)
 
-    @pl.loop(0, LD)
-    def _(leaf):
+    @pl.loop(0, out.shape[0])
+    def _(k):
+        leaf = k + begin
         points = target_side(own[leaf, :F, :])
         near_groups(
-            ids, leaf, place_of, points, side, lambda at: rights[at], slots, out.at[leaf],
+            ids, leaf, place_of, points, side, lambda at: rights[at], slots, out.at[k],
             given.at[leaf],
         )
 
 
-def near_rest(ids, first, own, before, after, given):
-    return pl.pallas_call(
-        near_rest_kernel,
+def near_rest_a_kernel(ids, first, own, before, after, given, out, side, rights, slots):
+    for d, block in enumerate((before, after)):
+
+        @pl.loop(0, LD, unroll=4)
+        def _(leaf, d=d, block=block):
+            side[d * LD + leaf] = source_side(block[leaf, :F, :])
+            rights[d * LD + leaf] = block[leaf, F:, :]
+
+    near_rest_leaves(ids, first, own, given, out, side, rights, slots, 0)
+
+
+def near_rest_b_kernel(ids, first, own, side, rights, given, out, slots):
+    near_rest_leaves(ids, first, own, given, out, side, rights, slots, LD // 2)
+
+
+def near_rest_a(ids, first, own, before, after, given):
+    return pl.pallas_call(
+        near_rest_a_kernel,
+        in_specs=[SM, SM, VM, VM, VM, VM],
+        out_specs=[VM] * 3,
+        out_shape=[
+            jax.ShapeDtypeStruct((LD // 2, RHS, LP), F32),
+            jax.ShapeDtypeStruct((2 * LD, LP, AUG), BF),
+            jax.ShapeDtypeStruct((2 * LD, RHS, LP), BF),
+        ],
+        scratch_shapes=[pltpu.SMEM((16,), jnp.int32)],
+        compiler_params=params(16),
+        cost_estimate=cost(0.01),
+        name="near_rest_a",
+    )(ids, first, own, before, after, given)
+
+
+def near_rest_b(ids, first, own, side, rights, given):
+    return pl.pallas_call(
+        near_rest_b_kernel,
         in_specs=[SM, SM, VM, VM, VM, VM],
         out_specs=VM,
-        out_shape=jax.ShapeDtypeStruct((LD, RHS, LP), F32),
-        scratch_shapes=[
-            pltpu.VMEM((2 * LD, LP, AUG), BF),
-            pltpu.VMEM((2 * LD, RHS, LP), BF),
-            pltpu.SMEM((16,), jnp.int32),
-        ],
-        compiler_params=params(24),
-        cost_estimate=cost(11),
-        name="near_rest",
-    )(ids, first, own, before, after, given)
-
-
-def final_kernel(near_sum, basis, transfer, own, r1, r2, r3, top, out):
+        out_shape=jax.ShapeDtypeStruct((LD // 2, RHS, LP), F32),
+        scratch_shapes=[pltpu.SMEM((16,), jnp.int32)],
+        compiler_params=params(16),
+        cost_estimate=cost(0.01),
+        name="near_rest_b",
+    )(ids, first, own, side, rights, given)
+
+
+def final_kernel(near_a, near_b, basis, transfer, own, r1, r2, r3, top, q1, q2, q3, out):
     nt = (((1,), (1,)), ((), ()))
-    last = LD * F
     total = top[...]
-    for r in (r1, r2, r3):
-        total += r[last:, :].astype(F32)
+    for q in (q1, q2, q3):
+        total += q[...].astype(F32)
     total = total.astype(BF)
-
-    @pl.loop(0, LD, unroll=UNROLL)
-    def _(leaf):
-        rows = pl.ds(pl.multiple_of(leaf * F, F), F)
-        potential = own[rows, :]
-        for r in (r1, r2, r3):
-            potential += r[rows, :].astype(F32)
-        potential += lax.dot_general(total, transfer[leaf], nt, preferred_element_type=F32)
-        far_out = lax.dot_general(
-            potential.astype(BF), basis[leaf], nt, preferred_element_type=F32
-        )
-        out[leaf] = (near_sum[leaf] + far_out).astype(BF)
-
-
-def final(near_sum, basis, transfer, own, returned, top):
+    half = LD // 2
+    for h, near_sum in enumerate((near_a, near_b)):
+
+        @pl.loop(0, half, unroll=half)
+        def _(k, h=h, near_sum=near_sum):
+            leaf = h * half + k
+            rows = rows_of(leaf)
+            potential = own[rows, :]
+            for r in (r1, r2, r3):
+                potential += r[rows, :].astype(F32)
+            potential += lax.dot_general(total, transfer[leaf], nt, preferred_element_type=F32)
+            far_out = lax.dot_general(
+                potential.astype(BF), basis[leaf], nt, preferred_element_type=F32
+            )
+            out[leaf] = (near_sum[k] + far_out).astype(BF)
+
+
+def final(near_sums, basis, transfer, own, returned, top, others):
     return pl.pallas_call(
         final_kernel,
-        in_specs=[VM] * 8,
+        in_specs=[VM] * 12,
         out_specs=VM,
         out_shape=jax.ShapeDtypeStruct((LD, RHS, LP), BF),
         compiler_params=params(16),
         cost_estimate=cost(3),
         name="final",
-    )(near_sum, basis, transfer, own, *returned, top)
+    )(*near_sums, basis, transfer, own, *returned, top, *others)
 
 
 def shifted(value, dx, dz):
@@ -504,10 +528,17 @@
     both = jnp.concatenate([mine, pair], axis=0)
     others = [leaf_shifted(both, dy) for dy in (1, -1, 2)]
     own, r1, r2 = far_c(ids, place, last, opposite, targets[:3], given)
-    top, *parts = top_sum(mine, pair, others, (r1, r2, r3))
-    returned = [shifted(r, 0, dz) for r, dz in zip(parts, (-1, 1, 2))]
-    near_sum = near_rest(neighbours, first, near_msg, before, after, near_sum)
-    return final(near_sum, leaf_basis, transfer, own, returned, top)
+    before, after, r1, r2, r3 = lax.optimization_barrier((before, after, r1, r2, r3))
+    returned = [shifted(r, 0, dz) for r, dz in zip((r1, r2, r3), (-1, 1, 2))]
+    near_a, near_side, near_rights = near_rest_a(
+        neighbours, first, near_msg, before, after, near_sum
+    )
+    others, near_side = lax.optimization_barrier((others, near_side))
+    top, sent = top_sum(mine, pair, others)
+    tops = [shifted(sent, 0, dz) for dz in (1, -1, 2)]
+    top, near_side, returned[2] = lax.optimization_barrier((top, near_side, returned[2]))
+    near_b = near_rest_b(neighbours, first, near_msg, near_side, near_rights, near_sum)
+    return final((near_a, near_b), leaf_basis, transfer, own, returned, top, tops)
 
 
 def solution(mesh):

time: 82.7 us -> 88.2 us (1.067)
  the two profiles are of different devices: /device:TPU:14 before, /device:TPU:0 now
where the time goes in v8:
time: 88.2 us; the launch traced here: 88.1 us
  starting transfers between devices  40.1 us (45%)
  Pallas kernels  37.8 us (43%)
  waiting for transfers between devices  5.76 us (7%)
  local copies, waits for them, and re-layouts  3.28 us (4%)
  other arithmetic  0.9 us (1%)
    ppermute x12, starting transfers between devices, shifted(): return lax.ppermute(value, 'top', pairs)  21.7 us
    ppermute x3, starting transfers between devices, leaf_shifted(): lax.ppermute(value, 'leaf', [(i, (i + 2 * dy) % count) for i in range(cou...  11.7 us
    pallas_call x1, Pallas kernels, near_own(): pl.pallas_call(near_own_kernel, in_specs=[SM, SM, VM], out_specs=VM, out_...  7.87 us
    pallas_call x1, Pallas kernels, far_a(): pl.pallas_call(far_a_kernel, in_specs=[SM, SM] + [VM] * 7, out_specs=[VM]...  5.44 us
    pallas_call x1, Pallas kernels, near_rest_b(): pl.pallas_call(near_rest_b_kernel, in_specs=[SM, SM, VM, VM, VM, VM], out...  5.07 us
    pallas_call x1, Pallas kernels, prep(): pl.pallas_call(prep_kernel, in_specs=[anywhere] * 4 + [VM] * 2, out_specs...  4.89 us
    pallas_call x1, Pallas kernels, far_b(): pl.pallas_call(far_b_kernel, in_specs=[SM, SM] + [VM] * 6, out_specs=[VM]...  3.43 us
    pallas_call x1, Pallas kernels, near_rest_a(): pl.pallas_call(near_rest_a_kernel, in_specs=[SM, SM, VM, VM, VM, VM], out...  3.27 us
  transfers between devices with their start and end apart: 18, of which 3 were waited for; matrix products, arithmetic and copies ran while one was open for 3% of the time, Pallas kernels for 34%

profile of v8, /device:TPU:0, one launch (start us, length us, event | category | flops | bytes accessed | tf_op | source)
XLA Modules:
  0.0 88.1 jit_solution(4795542939983688498)
XLA Ops:
  0.0 0.0 copy-start.4
  0.0 4.9 %prep.1 = (bf16[8,128,512]{2,1,0:T(8,128)(2,1)}, bf16[1088,256]{1,0:T(8,128)(2,1)}, bf16[528,256]{1,0:T(8,128)(2,1)}) custom-call(bf16[8,64,512]{2,1,0:T(8,128)(2,1)} %points.1, bf16[8,64,512]{2,1,0:T(8,128)(2,1)} %sides.2, bf16[8,512,256]{2,1,0:T(8,128)(2,1)} %basis.3, bf16[8,256,256]{2,1,0:T(8,128)(2,1)} %transfer.3, s32[8,256]{1,0:T(8,128)} %skeleton.1, ...), custom_call_target="tpu_custom_call" | custom-call | flops 4000000000 | bytes 1000000 | tf_op jit(solution)/shard_map/prep/pallas_call | solution.py:101
  4.9 2.1 %collective-permute-start = (bf16[528,256]{1,0:T(8,128)(2,1)}, bf16[528,256]{1,0:T(8,128)(2,1)}, u32[]{:S(2)}, u32[]{:S(2)}) collective-permute-start(bf16[528,256]{1,0:T(8,128)(2,1)} %get-tuple-element.59.t0), channel_id=1, source_target_pairs={{0,1},{1,2},{2,3},{3,0},{4,5},{5,6},{6,7},{7,4},{8,9},{9,10},{10,1... | collective-permute-start | bytes 811016 | tf_op jit(solution)/shard_map/ppermute | solution.py:480
  7.0 2.2 %collective-permute-start.1 = (bf16[528,256]{1,0:T(8,128)(2,1)}, bf16[528,256]{1,0:T(8,128)(2,1)}, u32[]{:S(2)}, u32[]{:S(2)}) collective-permute-start(bf16[528,256]{1,0:T(8,128)(2,1)} %get-tuple-element.59.t0), channel_id=1, source_target_pairs={{0,3},{1,0},{2,1},{3,2},{4,7},{5,4},{6,5},{7,6},{8,11},{9,8},{10,9... | collective-permute-start | bytes 811016 | tf_op jit(solution)/shard_map/ppermute | solution.py:480
  9.2 1.5 %collective-permute-start.2 = (bf16[1088,256]{1,0:T(8,128)(2,1)}, bf16[1088,256]{1,0:T(8,128)(2,1)S(1)}, u32[]{:S(2)}, u32[]{:S(2)}) collective-permute-start(bf16[1088,256]{1,0:T(8,128)(2,1)} %get-tuple-element.55.s0), channel_id=1, source_target_pairs={{0,4},{1,5},{2,6},{3,7},{4,8},{5,9},{6,10},{7,11},{8,12},{9,13},{1... | collective-permute-start | bytes 1671176 | tf_op jit(solution)/shard_map/ppermute | solution.py:480
  10.7 1.7 %collective-permute-start.3 = (bf16[1088,256]{1,0:T(8,128)(2,1)}, bf16[1088,256]{1,0:T(8,128)(2,1)}, u32[]{:S(2)}, u32[]{:S(2)}) collective-permute-start(bf16[1088,256]{1,0:T(8,128)(2,1)} %get-tuple-element.55.s0), channel_id=1, source_target_pairs={{0,12},{1,13},{2,14},{3,15},{4,0},{5,1},{6,2},{7,3},{8,4},{9,5},{1... | collective-permute-start | bytes 1671176 | tf_op jit(solution)/shard_map/ppermute | solution.py:480
  12.4 0.0 copy-done.4
  12.4 0.0 copy-start
  12.4 1.2 %copy-done = bf16[8,128,512]{2,1,0:T(8,128)(2,1)S(1)} copy-done((bf16[8,128,512]{2,1,0:T(8,128)(2,1)S(1)}, bf16[8,128,512]{2,1,0:T(8,128)(2,1)}, u32[]{:S(2)}) %copy-start) | copy-done | bytes 1048600
  13.6 0.0 copy-start.3
  13.6 0.0 copy-start.2
  13.6 7.9 %near_own.1.given = f32[8,64,512]{2,1,0:T(8,128)S(1)} custom-call(s32[8,8]{1,0:T(8,128)S(1)} %copy-done.4, s32[1]{0:T(128)} %bitcast.first, bf16[8,128,512]{2,1,0:T(8,128)(2,1)S(1)} %copy-done), custom_call_target="tpu_custom_call" | custom-call | flops 8999999488 | bytes 1000000 | tf_op jit(solution)/shard_map/near_own/pallas_call | solution.py:365
  21.5 0.0 copy-start.1
  21.5 0.0 collective-permute-done.t1
  21.5 0.0 collective-permute-done.1.t2
  21.6 3.1 %collective-permute-done.2.s1 = bf16[1088,256]{1,0:T(8,128)(2,1)S(1)} collective-permute-done((bf16[1088,256]{1,0:T(8,128)(2,1)}, bf16[1088,256]{1,0:T(8,128)(2,1)S(1)}, u32[]{:S(2)}, u32[]{:S(2)}) %collective-permute-start.2) | collective-permute-done | bytes 557088 | tf_op jit(solution)/shard_map/ppermute | solution.py:480
  24.7 0.1 collective-permute-done.3.s2
  24.8 1.5 %collective-permute-start.6 = (bf16[1088,256]{1,0:T(8,128)(2,1)S(1)}, bf16[1088,256]{1,0:T(8,128)(2,1)}, u32[]{:S(2)}, u32[]{:S(2)}) collective-permute-start(bf16[1088,256]{1,0:T(8,128)(2,1)S(1)} %collective-permute-done.2.s1), channel_id=1, source_target_pairs={{0,4},{1,5},{2,6},{3,7},{4,8},{5,9},{6,10},{7,11},{8,12},{9,13},{1... | collective-permute-start | bytes 1671176 | tf_op jit(solution)/shard_map/ppermute | solution.py:480
  26.3 0.0 copy-done.3
  26.3 1.5 %collective-permute-start.7 = (bf16[528,256]{1,0:T(8,128)(2,1)S(1)}, bf16[528,256]{1,0:T(8,128)(2,1)}, u32[]{:S(2)}, u32[]{:S(2)}) collective-permute-start(bf16[528,256]{1,0:T(8,128)(2,1)S(1)} %copy-done.3), channel_id=1, source_target_pairs={{0,2},{1,3},{2,0},{3,1},{4,6},{5,7},{6,4},{7,5},{8,10},{9,11},{10,... | collective-permute-start | bytes 811016 | tf_op jit(solution)/shard_map/ppermute | solution.py:480
  27.8 0.1 pad_add_fusion.place
  27.9 0.0 copy-done.2
  27.9 1.6 %sides.3.side = bf16[24,256,128]{2,1,0:T(8,128)(2,1)S(1)} custom-call(bf16[1088,256]{1,0:T(8,128)(2,1)S(1)} %copy-done.2, bf16[1088,256]{1,0:T(8,128)(2,1)S(1)} %collective-permute-done.2.s1, bf16[1088,256]{1,0:T(8,128)(2,1)} %collective-permute-done.3.s2), custom_call_target="tpu_custom_call" | custom-call | flops 10000000 | bytes 1000000 | tf_op jit(solution)/shard_map/sides/pallas_call | solution.py:196
  29.4 0.0 copy-done.1
  29.4 3.0 %collective-permute-start.4 = (bf16[8,128,512]{2,1,0:T(8,128)(2,1)S(1)}, bf16[8,128,512]{2,1,0:T(8,128)(2,1)S(1)}, u32[]{:S(2)}, u32[]{:S(2)}) collective-permute-start(bf16[8,128,512]{2,1,0:T(8,128)(2,1)S(1)} %copy-done.1), channel_id=1, source_target_pairs={{0,1},{1,2},{2,3},{3,4},{4,5},{5,6},{6,7},{7,8},{8,9},{9,10},{10,1... | collective-permute-start | bytes 3145736 | tf_op jit(solution)/shard_map/ppermute | solution.py:511
  32.4 1.3 %collective-permute-start.5 = (bf16[8,128,512]{2,1,0:T(8,128)(2,1)S(1)}, bf16[8,128,512]{2,1,0:T(8,128)(2,1)S(1)}, u32[]{:S(2)}, u32[]{:S(2)}) collective-permute-start(bf16[8,128,512]{2,1,0:T(8,128)(2,1)S(1)} %copy-done.1), channel_id=1, source_target_pairs={{1,0},{2,1},{3,2},{4,3},{5,4},{6,5},{7,6},{8,7},{9,8},{10,9},{11,1... | collective-permute-start | bytes 3145736 | tf_op jit(solution)/shard_map/ppermute | solution.py:512
  33.8 0.7 slice.28
  34.4 0.7 slice.29
  35.1 5.4 %far_a.1 = (f32[512,256]{1,0:T(8,128)S(1)}, f32[512,256]{1,0:T(8,128)S(1)}, f32[512,256]{1,0:T(8,128)S(1)}) custom-call(s32[24,16]{1,0:T(8,128)S(1)} %maximum_convert_fusion.1.ids, s32[2]{0:T(128)S(1)} %pad_add_fusion.place, bf16[24,256,128]{2,1,0:T(8,128)(2,1)S(1)} %sides.3.side, bf16[1088,256]{1,0:T(8,128)(2,1)S(1)} %copy-done.2, ...), custom_call_target="tpu_custom_call" | custom-call | flops 10000000 | bytes 1000000 | tf_op jit(solution)/shard_map/far_a/pallas_call | solution.py:218
  40.6 0.0 collective-permute-done.7.t3
  40.6 0.0 collective-permute-done.6.s3
  40.6 0.8 add_convert_fusion
  41.4 0.7 slice.30
  42.1 0.0 copy-done.7
  42.1 2.4 %collective-permute-start.8 = (bf16[128,256]{1,0:T(8,128)(2,1)S(1)}, bf16[128,256]{1,0:T(8,128)(2,1)S(1)}, u32[]{:S(2)}, u32[]{:S(2)}) collective-permute-start(bf16[128,256]{1,0:T(8,128)(2,1)S(1)} %pad_maximum_fusion.1.mine), channel_id=1, source_target_pairs={{0,16},{16,0},{32,48},{48,32},{64,80},{80,64},{96,112},{112,96},{1... | collective-permute-start | bytes 196616 | tf_op jit(solution)/shard_map/ppermute | solution.py:486
  44.5 3.4 %far_b.1 = (bf16[512,256]{1,0:T(8,128)(2,1)S(1)}, bf16[8,256,128]{2,1,0:T(8,128)(2,1)S(1)}) custom-call(s32[32,16]{1,0:T(8,128)S(1)} %maximum_convert_fusion.ids, s32[2]{0:T(128)S(1)} %pad_add_fusion.place, bf16[24,256,128]{2,1,0:T(8,128)(2,1)S(1)} %sides.3.side, bf16[1088,256]{1,0:T(8,128)(2,1)S(1)} %copy-done.2, ...), custom_call_target="tpu_custom_call" | custom-call | flops 3000000000 | bytes 1000000 | tf_op jit(solution)/shard_map/far_b/pallas_call | solution.py:243
  47.9 0.0 collective-permute-done.8.pair
  47.9 6.5 %collective-permute-start.10 = (bf16[256,256]{1,0:T(8,128)(2,1)S(1)}, bf16[256,256]{1,0:T(8,128)(2,1)S(1)}, u32[]{:S(2)}, u32[]{:S(2)}) collective-permute-start(bf16[256,256]{1,0:T(8,128)(2,1)S(1)} %pad_maximum_fusion), channel_id=1, source_target_pairs={{0,96},{16,112},{32,0},{48,16},{64,32},{80,48},{96,64},{112,80},{1... | collective-permute-start | bytes 393224 | tf_op jit(solution)/shard_map/ppermute | solution.py:487
  54.4 2.9 %far_c.1 = (f32[512,256]{1,0:T(8,128)S(1)}, bf16[512,256]{1,0:T(8,128)(2,1)S(1)}, bf16[512,256]{1,0:T(8,128)(2,1)S(1)}) custom-call(s32[32,16]{1,0:T(8,128)S(1)} %maximum_convert_fusion.ids, s32[2]{0:T(128)S(1)} %pad_add_fusion.place, bf16[8,256,128]{2,1,0:T(8,128)(2,1)S(1)} %get-tuple-element.70.side, bf16[1088,256]{1,0:T(8,128)(2,1)} %collective-permute-done.6.s3, ...), custom_call_target="tpu_custom_call" | custom-call | flops 4000000000 | bytes 1000000 | tf_op jit(solution)/shard_map/far_c/pallas_call | solution.py:269
  57.3 0.0 collective-permute-done.4.before
  57.3 0.0 collective-permute-done.5.after
  57.3 1.8 %collective-permute-start.12 = (bf16[512,256]{1,0:T(8,128)(2,1)S(1)}, bf16[512,256]{1,0:T(8,128)(2,1)S(1)}, u32[]{:S(2)}, u32[]{:S(2)}) collective-permute-start(bf16[512,256]{1,0:T(8,128)(2,1)S(1)} %get-tuple-element.88), channel_id=1, source_target_pairs={{0,2},{1,3},{2,0},{3,1},{4,6},{5,7},{6,4},{7,5},{8,10},{9,11},{10,... | collective-permute-start | bytes 786440 | tf_op jit(solution)/shard_map/ppermute | solution.py:480
  59.1 2.4 %collective-permute-start.13 = (bf16[512,256]{1,0:T(8,128)(2,1)S(1)}, bf16[512,256]{1,0:T(8,128)(2,1)S(1)}, u32[]{:S(2)}, u32[]{:S(2)}) collective-permute-start(bf16[512,256]{1,0:T(8,128)(2,1)S(1)} %get-tuple-element.92), channel_id=1, source_target_pairs={{0,3},{1,0},{2,1},{3,2},{4,7},{5,4},{6,5},{7,6},{8,11},{9,8},{10,9... | collective-permute-start | bytes 786440 | tf_op jit(solution)/shard_map/ppermute | solution.py:480
  61.5 0.9 collective-permute-start.14
  62.4 4.0 %collective-permute-start.11 = (bf16[256,256]{1,0:T(8,128)(2,1)S(1)}, bf16[256,256]{1,0:T(8,128)(2,1)S(1)}, u32[]{:S(2)}, u32[]{:S(2)}) collective-permute-start(bf16[256,256]{1,0:T(8,128)(2,1)S(1)} %pad_maximum_fusion), channel_id=1, source_target_pairs={{0,64},{16,80},{32,96},{48,112},{64,0},{80,16},{96,32},{112,48},{1... | collective-permute-start | bytes 393224 | tf_op jit(solution)/shard_map/ppermute | solution.py:487
  66.4 0.0 collective-permute-done.10.n2
  66.4 1.2 %collective-permute-start.9 = (bf16[256,256]{1,0:T(8,128)(2,1)S(1)}, bf16[256,256]{1,0:T(8,128)(2,1)S(1)}, u32[]{:S(2)}, u32[]{:S(2)}) collective-permute-start(bf16[256,256]{1,0:T(8,128)(2,1)S(1)} %pad_maximum_fusion), channel_id=1, source_target_pairs={{0,32},{16,48},{32,64},{48,80},{64,96},{80,112},{96,0},{112,16},{1... | collective-permute-start | bytes 393224 | tf_op jit(solution)/shard_map/ppermute | solution.py:487
  67.6 3.3 %near_rest_a.1 = (f32[4,64,512]{2,1,0:T(8,128)S(1)}, bf16[16,512,128]{2,1,0:T(8,128)(2,1)S(1)}, bf16[16,64,512]{2,1,0:T(8,128)(2,1)S(1)}) custom-call(s32[8,8]{1,0:T(8,128)S(1)} %copy-done.4, s32[1]{0:T(128)} %bitcast.first, bf16[8,128,512]{2,1,0:T(8,128)(2,1)S(1)} %copy-done.1, bf16[8,128,512]{2,1,0:T(8,128)(2,1)S(1)} %collective-permute-done.4.before, ...), custom_call_target="tpu_custom_call" | custom-call | flops 10000000 | bytes 1000000 | tf_op jit(solution)/shard_map/near_rest_a/pallas_call | solution.py:410
  70.9 0.0 collective-permute-done.11.n3
  70.9 2.5 %collective-permute-done.9.n1 = bf16[256,256]{1,0:T(8,128)(2,1)S(1)} collective-permute-done((bf16[256,256]{1,0:T(8,128)(2,1)S(1)}, bf16[256,256]{1,0:T(8,128)(2,1)S(1)}, u32[]{:S(2)}, u32[]{:S(2)}) %collective-permute-start.9) | collective-permute-done | bytes 131104 | tf_op jit(solution)/shard_map/ppermute | solution.py:487
  73.4 0.8 top_sum.1
  74.3 1.6 %collective-permute-start.15 = (bf16[64,256]{1,0:T(8,128)(2,1)S(1)}, bf16[64,256]{1,0:T(8,128)(2,1)S(1)}, u32[]{:S(2)}, u32[]{:S(2)}) collective-permute-start(bf16[64,256]{1,0:T(8,128)(2,1)S(1)} %get-tuple-element.96), channel_id=1, source_target_pairs={{0,1},{1,2},{2,3},{3,0},{4,5},{5,6},{6,7},{7,4},{8,9},{9,10},{10,1... | collective-permute-start | bytes 98312 | tf_op jit(solution)/shard_map/ppermute | solution.py:480
  75.8 1.7 %collective-permute-start.16 = (bf16[64,256]{1,0:T(8,128)(2,1)S(1)}, bf16[64,256]{1,0:T(8,128)(2,1)S(1)}, u32[]{:S(2)}, u32[]{:S(2)}) collective-permute-start(bf16[64,256]{1,0:T(8,128)(2,1)S(1)} %get-tuple-element.96), channel_id=1, source_target_pairs={{0,3},{1,0},{2,1},{3,2},{4,7},{5,4},{6,5},{7,6},{8,11},{9,8},{10,9... | collective-permute-start | bytes 98312 | tf_op jit(solution)/shard_map/ppermute | solution.py:480
  77.6 0.0 collective-permute-done.12.r3
  77.6 2.8 %collective-permute-start.17 = (bf16[64,256]{1,0:T(8,128)(2,1)S(1)}, bf16[64,256]{1,0:T(8,128)(2,1)S(1)}, u32[]{:S(2)}, u32[]{:S(2)}) collective-permute-start(bf16[64,256]{1,0:T(8,128)(2,1)S(1)} %get-tuple-element.96), channel_id=1, source_target_pairs={{0,2},{1,3},{2,0},{3,1},{4,6},{5,7},{6,4},{7,5},{8,10},{9,11},{10,... | collective-permute-start | bytes 98312 | tf_op jit(solution)/shard_map/ppermute | solution.py:480
  80.4 5.1 %near_rest_b.1.near_b = f32[4,64,512]{2,1,0:T(8,128)S(1)} custom-call(s32[8,8]{1,0:T(8,128)S(1)} %copy-done.4, s32[1]{0:T(128)} %bitcast.first, bf16[8,128,512]{2,1,0:T(8,128)(2,1)S(1)} %copy-done.1, bf16[16,512,128]{2,1,0:T(8,128)(2,1)S(1)} %get-tuple-element.89.side, bf16[16,64,512]{2,1,0:T(8,128)(2,1)S(1)} %get-tuple-element.90.rights, ...), custom_call_target="tpu_custom_call" | custom-call | flops 10000000 | bytes 1000000 | tf_op jit(solution)/shard_map/near_rest_b/pallas_call | solution.py:427
  85.5 0.0 collective-permute-done.15.q1
  85.5 0.0 collective-permute-done.16.q2
  85.5 0.0 collective-permute-done.17.q3
  85.5 0.0 collective-permute-done.13.r1
  85.5 0.0 collective-permute-done.14.r2
  85.5 0.0 copy-done.5
  85.6 0.0 copy-done.6
  85.6 2.5 %final.1 = bf16[8,64,512]{2,1,0:T(8,128)(2,1)} custom-call(f32[4,64,512]{2,1,0:T(8,128)S(1)} %get-tuple-element.80.near_a, f32[4,64,512]{2,1,0:T(8,128)S(1)} %near_rest_b.1.near_b, bf16[8,512,256]{2,1,0:T(8,128)(2,1)S(1)} %copy-done.5, bf16[8,256,256]{2,1,0:T(8,128)(2,1)S(1)} %copy-done.6, f32[512,256]{1,0:T(8,128)S(1)} %get-tuple-element.91.own, ...), custom_call_target="tpu_custom_call" | custom-call | flops 3000000000 | bytes 1000000 | tf_op jit(solution)/shard_map/final/pallas_call | solution.py:463
  (8 shorter events, 0.0 us)
Async XLA Ops:
  0.0 12.4 %copy-start.4 = (s32[8,8]{1,0:T(8,128)S(1)}, s32[8,8]{1,0:T(8,128)}, u32[]{:S(2)}) copy-start(s32[8,8]{1,0:T(8,128)} %ids.5) | copy-start | bytes 772
  4.9 16.6 %collective-permute-start = (bf16[528,256]{1,0:T(8,128)(2,1)}, bf16[528,256]{1,0:T(8,128)(2,1)}, u32[]{:S(2)}, u32[]{:S(2)}) collective-permute-start(bf16[528,256]{1,0:T(8,128)(2,1)} %get-tuple-element.59.t0), channel_id=1, source_target_pairs={{0,1},{1,2},{2,3},{3,0},{4,5},{5,6},{6,7},{7,4},{8,9},{9,10},{10,1... | collective-permute-start | bytes 811016 | tf_op jit(solution)/shard_map/ppermute | solution.py:480
  7.0 14.6 %collective-permute-start.1 = (bf16[528,256]{1,0:T(8,128)(2,1)}, bf16[528,256]{1,0:T(8,128)(2,1)}, u32[]{:S(2)}, u32[]{:S(2)}) collective-permute-start(bf16[528,256]{1,0:T(8,128)(2,1)} %get-tuple-element.59.t0), channel_id=1, source_target_pairs={{0,3},{1,0},{2,1},{3,2},{4,7},{5,4},{6,5},{7,6},{8,11},{9,8},{10,9... | collective-permute-start | bytes 811016 | tf_op jit(solution)/shard_map/ppermute | solution.py:480
  9.2 15.5 %collective-permute-start.2 = (bf16[1088,256]{1,0:T(8,128)(2,1)}, bf16[1088,256]{1,0:T(8,128)(2,1)S(1)}, u32[]{:S(2)}, u32[]{:S(2)}) collective-permute-start(bf16[1088,256]{1,0:T(8,128)(2,1)} %get-tuple-element.55.s0), channel_id=1, source_target_pairs={{0,4},{1,5},{2,6},{3,7},{4,8},{5,9},{6,10},{7,11},{8,12},{9,13},{1... | collective-permute-start | bytes 1671176 | tf_op jit(solution)/shard_map/ppermute | solution.py:480
  10.7 14.1 %collective-permute-start.3 = (bf16[1088,256]{1,0:T(8,128)(2,1)}, bf16[1088,256]{1,0:T(8,128)(2,1)}, u32[]{:S(2)}, u32[]{:S(2)}) collective-permute-start(bf16[1088,256]{1,0:T(8,128)(2,1)} %get-tuple-element.55.s0), channel_id=1, source_target_pairs={{0,12},{1,13},{2,14},{3,15},{4,0},{5,1},{6,2},{7,3},{8,4},{9,5},{1... | collective-permute-start | bytes 1671176 | tf_op jit(solution)/shard_map/ppermute | solution.py:480
  12.4 1.2 %copy-start = (bf16[8,128,512]{2,1,0:T(8,128)(2,1)S(1)}, bf16[8,128,512]{2,1,0:T(8,128)(2,1)}, u32[]{:S(2)}) copy-start(bf16[8,128,512]{2,1,0:T(8,128)(2,1)} %get-tuple-element.58.own) | copy-start | bytes 3145732
  13.6 12.6 %copy-start.3 = (bf16[528,256]{1,0:T(8,128)(2,1)S(1)}, bf16[528,256]{1,0:T(8,128)(2,1)}, u32[]{:S(2)}) copy-start(bf16[528,256]{1,0:T(8,128)(2,1)} %get-tuple-element.59.t0) | copy-start | bytes 811012
  13.6 14.2 %copy-start.2 = (bf16[1088,256]{1,0:T(8,128)(2,1)S(1)}, bf16[1088,256]{1,0:T(8,128)(2,1)}, u32[]{:S(2)}) copy-start(bf16[1088,256]{1,0:T(8,128)(2,1)} %get-tuple-element.55.s0) | copy-start | bytes 1671172
  21.5 7.9 %copy-start.1 = (bf16[8,128,512]{2,1,0:T(8,128)(2,1)S(1)}, bf16[8,128,512]{2,1,0:T(8,128)(2,1)}, u32[]{:S(2)}) copy-start(bf16[8,128,512]{2,1,0:T(8,128)(2,1)} %get-tuple-element.58.own) | copy-start | bytes 3145732
  24.8 15.8 %collective-permute-start.6 = (bf16[1088,256]{1,0:T(8,128)(2,1)S(1)}, bf16[1088,256]{1,0:T(8,128)(2,1)}, u32[]{:S(2)}, u32[]{:S(2)}) collective-permute-start(bf16[1088,256]{1,0:T(8,128)(2,1)S(1)} %collective-permute-done.2.s1), channel_id=1, source_target_pairs={{0,4},{1,5},{2,6},{3,7},{4,8},{5,9},{6,10},{7,11},{8,12},{9,13},{1... | collective-permute-start | bytes 1671176 | tf_op jit(solution)/shard_map/ppermute | solution.py:480
  26.3 14.3 %collective-permute-start.7 = (bf16[528,256]{1,0:T(8,128)(2,1)S(1)}, bf16[528,256]{1,0:T(8,128)(2,1)}, u32[]{:S(2)}, u32[]{:S(2)}) collective-permute-start(bf16[528,256]{1,0:T(8,128)(2,1)S(1)} %copy-done.3), channel_id=1, source_target_pairs={{0,2},{1,3},{2,0},{3,1},{4,6},{5,7},{6,4},{7,5},{8,10},{9,11},{10,... | collective-permute-start | bytes 811016 | tf_op jit(solution)/shard_map/ppermute | solution.py:480
  29.4 27.9 %collective-permute-start.4 = (bf16[8,128,512]{2,1,0:T(8,128)(2,1)S(1)}, bf16[8,128,512]{2,1,0:T(8,128)(2,1)S(1)}, u32[]{:S(2)}, u32[]{:S(2)}) collective-permute-start(bf16[8,128,512]{2,1,0:T(8,128)(2,1)S(1)} %copy-done.1), channel_id=1, source_target_pairs={{0,1},{1,2},{2,3},{3,4},{4,5},{5,6},{6,7},{7,8},{8,9},{9,10},{10,1... | collective-permute-start | bytes 3145736 | tf_op jit(solution)/shard_map/ppermute | solution.py:511
  32.4 24.9 %collective-permute-start.5 = (bf16[8,128,512]{2,1,0:T(8,128)(2,1)S(1)}, bf16[8,128,512]{2,1,0:T(8,128)(2,1)S(1)}, u32[]{:S(2)}, u32[]{:S(2)}) collective-permute-start(bf16[8,128,512]{2,1,0:T(8,128)(2,1)S(1)} %copy-done.1), channel_id=1, source_target_pairs={{1,0},{2,1},{3,2},{4,3},{5,4},{6,5},{7,6},{8,7},{9,8},{10,9},{11,1... | collective-permute-start | bytes 3145736 | tf_op jit(solution)/shard_map/ppermute | solution.py:512
  35.1 7.0 %copy-start.7 = (bf16[1,64,256]{2,1,0:T(8,128)(2,1)S(1)}, bf16[1,64,256]{2,1,0:T(8,128)(2,1)}, u32[]{:S(2)}) copy-start(bf16[1,64,256]{2,1,0:T(8,128)(2,1)} %param.12) | copy-start | bytes 98308
  42.1 5.8 %collective-permute-start.8 = (bf16[128,256]{1,0:T(8,128)(2,1)S(1)}, bf16[128,256]{1,0:T(8,128)(2,1)S(1)}, u32[]{:S(2)}, u32[]{:S(2)}) collective-permute-start(bf16[128,256]{1,0:T(8,128)(2,1)S(1)} %pad_maximum_fusion.1.mine), channel_id=1, source_target_pairs={{0,16},{16,0},{32,48},{48,32},{64,80},{80,64},{96,112},{112,96},{1... | collective-permute-start | bytes 196616 | tf_op jit(solution)/shard_map/ppermute | solution.py:486
  47.9 18.5 %collective-permute-start.10 = (bf16[256,256]{1,0:T(8,128)(2,1)S(1)}, bf16[256,256]{1,0:T(8,128)(2,1)S(1)}, u32[]{:S(2)}, u32[]{:S(2)}) collective-permute-start(bf16[256,256]{1,0:T(8,128)(2,1)S(1)} %pad_maximum_fusion), channel_id=1, source_target_pairs={{0,96},{16,112},{32,0},{48,16},{64,32},{80,48},{96,64},{112,80},{1... | collective-permute-start | bytes 393224 | tf_op jit(solution)/shard_map/ppermute | solution.py:487
  57.3 20.2 %collective-permute-start.12 = (bf16[512,256]{1,0:T(8,128)(2,1)S(1)}, bf16[512,256]{1,0:T(8,128)(2,1)S(1)}, u32[]{:S(2)}, u32[]{:S(2)}) collective-permute-start(bf16[512,256]{1,0:T(8,128)(2,1)S(1)} %get-tuple-element.88), channel_id=1, source_target_pairs={{0,2},{1,3},{2,0},{3,1},{4,6},{5,7},{6,4},{7,5},{8,10},{9,11},{10,... | collective-permute-start | bytes 786440 | tf_op jit(solution)/shard_map/ppermute | solution.py:480
  59.1 26.4 %collective-permute-start.13 = (bf16[512,256]{1,0:T(8,128)(2,1)S(1)}, bf16[512,256]{1,0:T(8,128)(2,1)S(1)}, u32[]{:S(2)}, u32[]{:S(2)}) collective-permute-start(bf16[512,256]{1,0:T(8,128)(2,1)S(1)} %get-tuple-element.92), channel_id=1, source_target_pairs={{0,3},{1,0},{2,1},{3,2},{4,7},{5,4},{6,5},{7,6},{8,11},{9,8},{10,9... | collective-permute-start | bytes 786440 | tf_op jit(solution)/shard_map/ppermute | solution.py:480
  61.5 24.0 %collective-permute-start.14 = (bf16[512,256]{1,0:T(8,128)(2,1)S(1)}, bf16[512,256]{1,0:T(8,128)(2,1)S(1)}, u32[]{:S(2)}, u32[]{:S(2)}) collective-permute-start(bf16[512,256]{1,0:T(8,128)(2,1)S(1)} %get-tuple-element.93), channel_id=1, source_target_pairs={{0,1},{1,2},{2,3},{3,0},{4,5},{5,6},{6,7},{7,4},{8,9},{9,10},{10,1... | collective-permute-start | bytes 786440 | tf_op jit(solution)/shard_map/ppermute | solution.py:480
  62.4 8.5 %collective-permute-start.11 = (bf16[256,256]{1,0:T(8,128)(2,1)S(1)}, bf16[256,256]{1,0:T(8,128)(2,1)S(1)}, u32[]{:S(2)}, u32[]{:S(2)}) collective-permute-start(bf16[256,256]{1,0:T(8,128)(2,1)S(1)} %pad_maximum_fusion), channel_id=1, source_target_pairs={{0,64},{16,80},{32,96},{48,112},{64,0},{80,16},{96,32},{112,48},{1... | collective-permute-start | bytes 393224 | tf_op jit(solution)/shard_map/ppermute | solution.py:487
  66.4 7.0 %collective-permute-start.9 = (bf16[256,256]{1,0:T(8,128)(2,1)S(1)}, bf16[256,256]{1,0:T(8,128)(2,1)S(1)}, u32[]{:S(2)}, u32[]{:S(2)}) collective-permute-start(bf16[256,256]{1,0:T(8,128)(2,1)S(1)} %pad_maximum_fusion), channel_id=1, source_target_pairs={{0,32},{16,48},{32,64},{48,80},{64,96},{80,112},{96,0},{112,16},{1... | collective-permute-start | bytes 393224 | tf_op jit(solution)/shard_map/ppermute | solution.py:487
  74.3 11.2 %collective-permute-start.15 = (bf16[64,256]{1,0:T(8,128)(2,1)S(1)}, bf16[64,256]{1,0:T(8,128)(2,1)S(1)}, u32[]{:S(2)}, u32[]{:S(2)}) collective-permute-start(bf16[64,256]{1,0:T(8,128)(2,1)S(1)} %get-tuple-element.96), channel_id=1, source_target_pairs={{0,1},{1,2},{2,3},{3,0},{4,5},{5,6},{6,7},{7,4},{8,9},{9,10},{10,1... | collective-permute-start | bytes 98312 | tf_op jit(solution)/shard_map/ppermute | solution.py:480
  75.8 9.7 %collective-permute-start.16 = (bf16[64,256]{1,0:T(8,128)(2,1)S(1)}, bf16[64,256]{1,0:T(8,128)(2,1)S(1)}, u32[]{:S(2)}, u32[]{:S(2)}) collective-permute-start(bf16[64,256]{1,0:T(8,128)(2,1)S(1)} %get-tuple-element.96), channel_id=1, source_target_pairs={{0,3},{1,0},{2,1},{3,2},{4,7},{5,4},{6,5},{7,6},{8,11},{9,8},{10,9... | collective-permute-start | bytes 98312 | tf_op jit(solution)/shard_map/ppermute | solution.py:480
  77.6 8.0 %collective-permute-start.17 = (bf16[64,256]{1,0:T(8,128)(2,1)S(1)}, bf16[64,256]{1,0:T(8,128)(2,1)S(1)}, u32[]{:S(2)}, u32[]{:S(2)}) collective-permute-start(bf16[64,256]{1,0:T(8,128)(2,1)S(1)} %get-tuple-element.96), channel_id=1, source_target_pairs={{0,2},{1,3},{2,0},{3,1},{4,6},{5,7},{6,4},{7,5},{8,10},{9,11},{10,... | collective-permute-start | bytes 98312 | tf_op jit(solution)/shard_map/ppermute | solution.py:480
  80.4 5.1 %copy-start.5 = (bf16[8,512,256]{2,1,0:T(8,128)(2,1)S(1)}, bf16[8,512,256]{2,1,0:T(8,128)(2,1)}, u32[]{:S(2)}) copy-start(bf16[8,512,256]{2,1,0:T(8,128)(2,1)} %basis.3) | copy-start | bytes 6291460
  80.4 5.1 %copy-start.6 = (bf16[8,256,256]{2,1,0:T(8,128)(2,1)S(1)}, bf16[8,256,256]{2,1,0:T(8,128)(2,1)}, u32[]{:S(2)}) copy-start(bf16[8,256,256]{2,1,0:T(8,128)(2,1)} %transfer.3) | copy-start | bytes 3145732

commit v9 on v7

--- a/solution.py
+++ b/solution.py
@@ -14,6 +14,8 @@
 LP = 512
 SK = 256
 LD = 8
+HALF = 4
+ABSENT = -32
 SIDE = 4
 AUG = 128
 UNROLL = 8
@@ -56,14 +58,29 @@
     return full.astype(BF)
 
 
+def half_of(low, high, leaf):
+    return (low, leaf) if leaf < HALF else (high, leaf - HALF)
+
+
+def points_at(pair):
+    block, leaf = pair
+    return block.at[leaf * 2 * F : leaf * 2 * F + F, :]
+
+
+def sides_at(pair):
+    block, leaf = pair
+    return block.at[leaf * 2 * F + F : (leaf + 1) * 2 * F, :]
+
+
 def prep_kernel(
-    points, sides, basis, transfer, skeleton, far, near_msg, source_msg, target_msg,
-    own_basis, own_transfer, node, ids, sems,
+    first, points, sides, basis, transfer, skeleton, far, near, low, high, source_msg,
+    target_msg, own_basis, own_transfer, node, ids, near_ids, sems,
 ):
     def fetch(leaf):
+        place = half_of(low, high, leaf)
         pairs = (
-            (points, near_msg.at[leaf, :F, :]),
-            (sides, near_msg.at[leaf, F:, :]),
+            (points, points_at(place)),
+            (sides, sides_at(place)),
             (basis, own_basis.at[leaf]),
             (transfer, own_transfer.at[leaf]),
         )
@@ -79,16 +96,23 @@
     named = far[...]
     ids[:LD, : SIDE * SIDE] = jnp.where(named >= 0, named & (LD - 1), -1).astype(F32)
     target_msg[LD * F :, :] = ids[...].astype(BF)
+    near_ids[...] = jnp.zeros_like(near_ids)
+    named = near[...]
+    own_leaf = first[0] + lax.broadcasted_iota(jnp.int32, named.shape, 0)
+    near_ids[:LD, : named.shape[1]] = jnp.where(named >= 0, named - own_leaf, ABSENT).astype(F32)
+    for block in (low, high):
+        block[HALF * 2 * F :, :] = near_ids[...].astype(BF)
     position = lax.broadcasted_iota(jnp.int32, (LP, SK), 0)
     node[...] = jnp.zeros_like(node)
     for leaf in range(LD):
+        place = half_of(low, high, leaf)
         for copy in fetch(leaf):
             copy.wait()
         charge = jnp.dot(
-            near_msg[leaf, F:, :], own_basis[leaf], preferred_element_type=F32
+            sides_at(place)[...], own_basis[leaf], preferred_element_type=F32
         ).astype(BF)
         chosen = jnp.where(position == skeleton[leaf : leaf + 1, :], 1.0, 0.0).astype(BF)
-        skel = jnp.dot(near_msg[leaf, :F, :], chosen, preferred_element_type=F32).astype(BF)
+        skel = jnp.dot(points_at(place)[...], chosen, preferred_element_type=F32).astype(BF)
         source_msg[leaf * 2 * F : leaf * 2 * F + F, :] = charge
         source_msg[leaf * 2 * F + F : (leaf + 1) * 2 * F, :] = skel
         target_msg[leaf * F : (leaf + 1) * F, :] = skel
@@ -96,14 +120,14 @@
     source_msg[LD * 2 * F :, :] = node[...].astype(BF)
 
 
-def prep(points, sides, basis, transfer, skeleton, far):
+def prep(first, points, sides, basis, transfer, skeleton, far, near):
     anywhere = pl.BlockSpec(memory_space=pl.ANY)
     return pl.pallas_call(
         prep_kernel,
-        in_specs=[anywhere] * 4 + [VM] * 2,
-        out_specs=[VM] * 3,
-        out_shape=[
-            jax.ShapeDtypeStruct((LD, 2 * F, LP), BF),
+        in_specs=[SM] + [anywhere] * 4 + [VM] * 3,
+        out_specs=[VM] * 4,
+        out_shape=[jax.ShapeDtypeStruct((HALF * 2 * F + 16, LP), BF)] * 2
+        + [
             jax.ShapeDtypeStruct((LD * 2 * F + RHS, SK), BF),
             jax.ShapeDtypeStruct((LD * F + 16, SK), BF),
         ],
@@ -112,12 +136,13 @@
             pltpu.VMEM((LD, SK, SK), BF),
             pltpu.VMEM((RHS, SK), F32),
             pltpu.VMEM((16, SK), F32),
+            pltpu.VMEM((16, LP), F32),
             pltpu.SemaphoreType.DMA((4, LD)),
         ],
         compiler_params=params(56),
         cost_estimate=cost(4),
         name="prep",
-    )(points, sides, basis, transfer, skeleton, far)
+    )(first, points, sides, basis, transfer, skeleton, far, near)
 
 
 def far_run(ids, columns, jobs, side_of, weight_of, tile):
@@ -344,77 +369,125 @@
             out[...] = group(full * size, used, out[...])
 
 
-def near_own_kernel(ids, first, own, out, side, slots):
-    @pl.loop(0, LD, unroll=4)
-    def _(leaf):
-        side[leaf] = source_side(own[leaf, :F, :])
+def near_own_kernel(ids, first, low, high, out, side, rights, slots):
+    for leaf in range(LD):
+        place = half_of(low, high, leaf)
+        side[leaf] = source_side(points_at(place)[...])
+        rights[leaf] = sides_at(place)[...]
 
     def place_of(named):
         at = named - first[0]
         return (named >= 0) & (at >= 0) & (at < LD), at
 
-    @pl.loop(0, LD)
-    def _(leaf):
-        points = target_side(own[leaf, :F, :])
-        near_groups(
-            ids, leaf, place_of, points, side, lambda at: own[at, F:, :], slots, out.at[leaf]
-        )
-
-
-def near_own(ids, first, own):
+    for h, block in enumerate((low, high)):
+
+        @pl.loop(0, HALF)
+        def _(k, h=h, block=block):
+            leaf = h * HALF + k
+            near_groups(
+                ids, leaf, place_of, target_side(block_points(block, k)), side,
+                lambda at: rights[at], slots, out.at[leaf],
+            )
+
+
+def block_points(block, k):
+    return block[pl.ds(pl.multiple_of(k * 2 * F, 2 * F), F), :]
+
+
+def near_own(ids, first, low, high):
     return pl.pallas_call(
         near_own_kernel,
-        in_specs=[SM, SM, VM],
-        out_specs=VM,
-        out_shape=jax.ShapeDtypeStruct((LD, RHS, LP), F32),
-        scratch_shapes=[pltpu.VMEM((LD, LP, AUG), BF), pltpu.SMEM((16,), jnp.int32)],
+        in_specs=[SM, SM, VM, VM],
+        out_specs=[VM] * 3,
+        out_shape=[
+            jax.ShapeDtypeStruct((LD, RHS, LP), F32),
+            jax.ShapeDtypeStruct((LD, LP, AUG), BF),
+            jax.ShapeDtypeStruct((LD, RHS, LP), BF),
+        ],
+        scratch_shapes=[pltpu.SMEM((16,), jnp.int32)],
         compiler_params=params(16),
         cost_estimate=cost(9),
         name="near_own",
-    )(ids, first, own)
-
-
-def near_rest_kernel(ids, first, own, before, after, given, out, side, rights, slots):
+    )(ids, first, low, high)
+
+
+def near_lent_kernel(offsets, side, rights, before, after, to_prev, to_next, sums, slots):
+    for block, out, row, shift, least in (
+        (before, to_prev, HALF, HALF - LD, HALF),
+        (after, to_next, LD, LD, 0),
+    ):
+
+        @pl.loop(0, HALF)
+        def _(k, block=block, row=row, shift=shift, least=least):
+            def place_of(offset):
+                at = k + shift + offset
+                return (offset > ABSENT) & (at >= least) & (at < least + HALF), at
+
+            near_groups(
+                offsets, row + k, place_of, target_side(block_points(block, k)), side,
+                lambda at: rights[at], slots, sums.at[k],
+            )
+
+        out[...] = sums[...].astype(BF)
+
+
+def near_lent(offsets, side, rights, before, after):
+    return pl.pallas_call(
+        near_lent_kernel,
+        in_specs=[SM] + [VM] * 4,
+        out_specs=[VM] * 2,
+        out_shape=[jax.ShapeDtypeStruct((HALF, RHS, LP), BF)] * 2,
+        scratch_shapes=[
+            pltpu.VMEM((HALF, RHS, LP), F32),
+            pltpu.SMEM((16,), jnp.int32),
+        ],
+        compiler_params=params(16),
+        cost_estimate=cost(4),
+        name="near_lent",
+    )(offsets, side, rights, before, after)
+
+
+def near_rest_kernel(ids, first, low, high, before, after, given, out, side, rights, slots):
     for d, block in enumerate((before, after)):
-
-        @pl.loop(0, LD, unroll=4)
-        def _(leaf, d=d, block=block):
-            side[d * LD + leaf] = source_side(block[leaf, :F, :])
-            rights[d * LD + leaf] = block[leaf, F:, :]
+        for leaf in range(HALF):
+            side[d * HALF + leaf] = source_side(points_at((block, leaf))[...])
+            rights[d * HALF + leaf] = sides_at((block, leaf))[...]
 
     def place_of(named):
         at = named - first[0]
-        below = (at >= -LD) & (at < 0)
-        above = (at >= LD) & (at < 2 * LD)
-        return (named >= 0) & (below | above), jnp.where(below, at + LD, at)
-
-    @pl.loop(0, LD)
-    def _(leaf):
-        points = target_side(own[leaf, :F, :])
-        near_groups(
-            ids, leaf, place_of, points, side, lambda at: rights[at], slots, out.at[leaf],
-            given.at[leaf],
-        )
-
-
-def near_rest(ids, first, own, before, after, given):
+        below = (at >= -HALF) & (at < 0)
+        above = (at >= LD) & (at < LD + HALF)
+        return (named >= 0) & (below | above), jnp.where(below, at + HALF, at - HALF)
+
+    for h, block in enumerate((low, high)):
+
+        @pl.loop(0, HALF)
+        def _(k, h=h, block=block):
+            leaf = h * HALF + k
+            near_groups(
+                ids, leaf, place_of, target_side(block_points(block, k)), side,
+                lambda at: rights[at], slots, out.at[leaf], given.at[leaf],
+            )
+
+
+def near_rest(ids, first, low, high, before, after, given):
     return pl.pallas_call(
         near_rest_kernel,
-        in_specs=[SM, SM, VM, VM, VM, VM],
+        in_specs=[SM, SM] + [VM] * 5,
         out_specs=VM,
         out_shape=jax.ShapeDtypeStruct((LD, RHS, LP), F32),
         scratch_shapes=[
-            pltpu.VMEM((2 * LD, LP, AUG), BF),
-            pltpu.VMEM((2 * LD, RHS, LP), BF),
+            pltpu.VMEM((LD, LP, AUG), BF),
+            pltpu.VMEM((LD, RHS, LP), BF),
             pltpu.SMEM((16,), jnp.int32),
         ],
-        compiler_params=params(24),
-        cost_estimate=cost(11),
+        compiler_params=params(16),
+        cost_estimate=cost(7),
         name="near_rest",
-    )(ids, first, own, before, after, given)
-
-
-def final_kernel(near_sum, basis, transfer, own, r1, r2, r3, top, out):
+    )(ids, first, low, high, before, after, given)
+
+
+def final_kernel(near_sum, lent_low, lent_high, basis, transfer, own, r1, r2, r3, top, out):
     nt = (((1,), (1,)), ((), ()))
     last = LD * F
     total = top[...]
@@ -422,9 +495,8 @@
         total += r[last:, :].astype(F32)
     total = total.astype(BF)
 
-    @pl.loop(0, LD, unroll=UNROLL)
-    def _(leaf):
-        rows = pl.ds(pl.multiple_of(leaf * F, F), F)
+    for leaf in range(LD):
+        rows = slice(leaf * F, leaf * F + F)
         potential = own[rows, :]
         for r in (r1, r2, r3):
             potential += r[rows, :].astype(F32)
@@ -432,19 +504,20 @@
         far_out = lax.dot_general(
             potential.astype(BF), basis[leaf], nt, preferred_element_type=F32
         )
-        out[leaf] = (near_sum[leaf] + far_out).astype(BF)
-
-
-def final(near_sum, basis, transfer, own, returned, top):
+        lent, k = half_of(lent_low, lent_high, leaf)
+        out[leaf] = (near_sum[leaf] + lent[k].astype(F32) + far_out).astype(BF)
+
+
+def final(near_sum, lent, basis, transfer, own, returned, top):
     return pl.pallas_call(
         final_kernel,
-        in_specs=[VM] * 8,
+        in_specs=[VM] * 10,
         out_specs=VM,
         out_shape=jax.ShapeDtypeStruct((LD, RHS, LP), BF),
         compiler_params=params(16),
         cost_estimate=cost(3),
         name="final",
-    )(near_sum, basis, transfer, own, *returned, top)
+    )(near_sum, *lent, basis, transfer, own, *returned, top)
 
 
 def shifted(value, dx, dz):
@@ -468,24 +541,25 @@
 ):
     node, at = lax.axis_index("leaf"), lax.axis_index("top")
     position = node * SIDE * SIDE + at
-    near_msg, source_msg, target_msg = prep(
-        points, right_sides, leaf_basis, transfer, skeleton, far_sources
+    first = (position * LD).astype(jnp.int32).reshape(1)
+    near_low, near_high, source_msg, target_msg = prep(
+        first, points, right_sides, leaf_basis, transfer, skeleton, far_sources, neighbours
     )
     sources = [source_msg] + [shifted(source_msg, dx, 0) for dx in (1, -1)]
     targets = [target_msg] + [shifted(target_msg, 0, dz) for dz in (1, -1, 2)]
-    first = (position * LD).astype(jnp.int32).reshape(1)
-    near_sum = near_own(neighbours, first, near_msg)
-
-    targets[:3], sources, near_msg, near_sum = lax.optimization_barrier(
-        (targets[:3], sources, near_msg, near_sum)
+    near_sum, near_side, near_rights = near_own(neighbours, first, near_low, near_high)
+
+    targets[:3], sources, near_low, near_high, near_sum = lax.optimization_barrier(
+        (targets[:3], sources, near_low, near_high, near_sum)
     )
     opposite = shifted(sources[1], 1, 0)
     side = sides_of(sources)
-    near_msg, side = lax.optimization_barrier((near_msg, side))
+    near_low, near_high, side = lax.optimization_barrier((near_low, near_high, side))
     count = lax.axis_size("leaf") * lax.axis_size("top")
     up = [(i, i + 1) for i in range(count - 1)]
-    before = lax.ppermute(near_msg, ("leaf", "top"), up)
-    after = lax.ppermute(near_msg, ("leaf", "top"), [(j, i) for i, j in up])
+    down = [(j, i) for i, j in up]
+    before = lax.ppermute(near_high, ("leaf", "top"), up)
+    after = lax.ppermute(near_low, ("leaf", "top"), down)
 
     def ids_of(which):
         ids = jnp.concatenate([t[LD * F : LD * F + LD, : SIDE * SIDE] for t in which])
@@ -504,10 +578,21 @@
     both = jnp.concatenate([mine, pair], axis=0)
     others = [leaf_shifted(both, dy) for dy in (1, -1, 2)]
     own, r1, r2 = far_c(ids, place, last, opposite, targets[:3], given)
+    width = neighbours.shape[1]
+    before, after, own = lax.optimization_barrier((before, after, own))
+    offsets = jnp.concatenate(
+        [block[HALF * 2 * F : HALF * 2 * F + LD, :width] for block in (before, after)]
+    ).astype(jnp.int32)
+    to_prev, to_next = near_lent(offsets, near_side, near_rights, before, after)
+    others, to_prev, to_next = lax.optimization_barrier((others, to_prev, to_next))
+    lent = (
+        lax.ppermute(to_next, ("leaf", "top"), up),
+        lax.ppermute(to_prev, ("leaf", "top"), down),
+    )
     top, *parts = top_sum(mine, pair, others, (r1, r2, r3))
     returned = [shifted(r, 0, dz) for r, dz in zip(parts, (-1, 1, 2))]
-    near_sum = near_rest(neighbours, first, near_msg, before, after, near_sum)
-    return final(near_sum, leaf_basis, transfer, own, returned, top)
+    near_sum = near_rest(neighbours, first, near_low, near_high, before, after, near_sum)
+    return final(near_sum, lent, leaf_basis, transfer, own, returned, top)
 
 
 def solution(mesh):

time: 82.7 us -> 87.6 us (1.059)
  the two profiles are of different devices: /device:TPU:14 before, /device:TPU:0 now
where the time goes in v9:
time: 87.6 us; the launch traced here: 87.4 us
  Pallas kernels  36.8 us (42%)
  starting transfers between devices  28.5 us (33%)
  waiting for transfers between devices  16.2 us (18%)
  local copies, waits for them, and re-layouts  5.33 us (6%)
    ppermute x9, starting transfers between devices, shifted(): return lax.ppermute(value, 'top', pairs)  10.5 us
    pallas_call x1, Pallas kernels, near_own(): pl.pallas_call(near_own_kernel, in_specs=[SM, SM, VM, VM], out_specs=[VM]...  9.43 us
    ppermute x1, waiting for transfers between devices, on_device(): lax.ppermute(to_next, ('leaf', 'top'), up)  6.65 us
    ppermute x3, starting transfers between devices, leaf_shifted(): lax.ppermute(value, 'leaf', [(i, (i + 2 * dy) % count) for i in range(cou...  6.2 us
    pallas_call x1, Pallas kernels, near_rest(): pl.pallas_call(near_rest_kernel, in_specs=[SM, SM] + [VM] * 5, out_specs=...  5.69 us
    unnamed x32, local copies, waits for them, and re-layouts  5.32 us
    pallas_call x1, Pallas kernels, far_a(): pl.pallas_call(far_a_kernel, in_specs=[SM, SM] + [VM] * 7, out_specs=[VM]...  4.97 us
    pallas_call x1, Pallas kernels, prep(): pl.pallas_call(prep_kernel, in_specs=[SM] + [anywhere] * 4 + [VM] * 3, ou...  4.97 us
  transfers between devices with their start and end apart: 17, of which 5 were waited for; matrix products, arithmetic and copies ran while one was open for 0% of the time, Pallas kernels for 33%

profile of v9, /device:TPU:0, one launch (start us, length us, event | category | flops | bytes accessed | tf_op | source)
XLA Modules:
  0.0 87.4 jit_solution(9731611344491565443)
XLA Ops:
  0.0 5.0 %prep.1 = (bf16[528,512]{1,0:T(8,128)(2,1)}, bf16[528,512]{1,0:T(8,128)(2,1)}, bf16[1088,256]{1,0:T(8,128)(2,1)}, bf16[528,256]{1,0:T(8,128)(2,1)}) custom-call(s32[1]{0:T(128)} %bitcast.first, bf16[8,64,512]{2,1,0:T(8,128)(2,1)} %points.1, bf16[8,64,512]{2,1,0:T(8,128)(2,1)} %sides.2, bf16[8,512,256]{2,1,0:T(8,128)(2,1)} %basis.3, ...), custom_call_target="tpu_custom_call" | custom-call | flops 4000000000 | bytes 1000000 | tf_op jit(solution)/shard_map/prep/pallas_call | solution.py:125
  5.0 2.1 %collective-permute-start = (bf16[528,256]{1,0:T(8,128)(2,1)}, bf16[528,256]{1,0:T(8,128)(2,1)S(1)}, u32[]{:S(2)}, u32[]{:S(2)}) collective-permute-start(bf16[528,256]{1,0:T(8,128)(2,1)} %get-tuple-element.66.t0), channel_id=1, source_target_pairs={{0,1},{1,2},{2,3},{3,0},{4,5},{5,6},{6,7},{7,4},{8,9},{9,10},{10,1... | collective-permute-start | bytes 811016 | tf_op jit(solution)/shard_map/ppermute | solution.py:529
  7.0 2.2 %collective-permute-start.1 = (bf16[528,256]{1,0:T(8,128)(2,1)}, bf16[528,256]{1,0:T(8,128)(2,1)S(1)}, u32[]{:S(2)}, u32[]{:S(2)}) collective-permute-start(bf16[528,256]{1,0:T(8,128)(2,1)} %get-tuple-element.66.t0), channel_id=1, source_target_pairs={{0,3},{1,0},{2,1},{3,2},{4,7},{5,4},{6,5},{7,6},{8,11},{9,8},{10,9... | collective-permute-start | bytes 811016 | tf_op jit(solution)/shard_map/ppermute | solution.py:529
  9.2 1.5 %collective-permute-start.2 = (bf16[1088,256]{1,0:T(8,128)(2,1)}, bf16[1088,256]{1,0:T(8,128)(2,1)S(1)}, u32[]{:S(2)}, u32[]{:S(2)}) collective-permute-start(bf16[1088,256]{1,0:T(8,128)(2,1)} %get-tuple-element.61.s0), channel_id=1, source_target_pairs={{0,4},{1,5},{2,6},{3,7},{4,8},{5,9},{6,10},{7,11},{8,12},{9,13},{1... | collective-permute-start | bytes 1671176 | tf_op jit(solution)/shard_map/ppermute | solution.py:529
  10.7 1.7 %collective-permute-start.3 = (bf16[1088,256]{1,0:T(8,128)(2,1)}, bf16[1088,256]{1,0:T(8,128)(2,1)S(1)}, u32[]{:S(2)}, u32[]{:S(2)}) collective-permute-start(bf16[1088,256]{1,0:T(8,128)(2,1)} %get-tuple-element.61.s0), channel_id=1, source_target_pairs={{0,12},{1,13},{2,14},{3,15},{4,0},{5,1},{6,2},{7,3},{8,4},{9,5},{1... | collective-permute-start | bytes 1671176 | tf_op jit(solution)/shard_map/ppermute | solution.py:529
  12.5 0.0 copy-done.8
  12.5 1.0 %copy-done.4 = bf16[528,512]{1,0:T(8,128)(2,1)S(1)} copy-done((bf16[528,512]{1,0:T(8,128)(2,1)S(1)}, bf16[528,512]{1,0:T(8,128)(2,1)}, u32[]{:S(2)}) %copy-start.4) | copy-done | bytes 540696
  13.5 1.0 %copy-done.6 = bf16[528,512]{1,0:T(8,128)(2,1)S(1)} copy-done((bf16[528,512]{1,0:T(8,128)(2,1)S(1)}, bf16[528,512]{1,0:T(8,128)(2,1)}, u32[]{:S(2)}) %copy-start.6) | copy-done | bytes 540696
  14.6 9.4 %near_own.1 = (f32[8,64,512]{2,1,0:T(8,128)S(1)}, bf16[8,512,128]{2,1,0:T(8,128)(2,1)S(1)}, bf16[8,64,512]{2,1,0:T(8,128)(2,1)S(1)}) custom-call(s32[8,8]{1,0:T(8,128)S(1)} %copy-done.8, s32[1]{0:T(128)} %bitcast.first, bf16[528,512]{1,0:T(8,128)(2,1)S(1)} %copy-done.4, bf16[528,512]{1,0:T(8,128)(2,1)S(1)} %copy-done.6), custom_call_target="tpu_custom_call" | custom-call | flops 8999999488 | bytes 1000000 | tf_op jit(solution)/shard_map/near_own/pallas_call | solution.py:398
  24.0 0.0 copy-start.9
  24.0 1.0 %copy-done.9 = bf16[8,512,128]{2,1,0:T(8,128)(2,1)} copy-done((bf16[8,512,128]{2,1,0:T(8,128)(2,1)}, bf16[8,512,128]{2,1,0:T(8,128)(2,1)S(1)}, u32[]{:S(2)}) %copy-start.9) | copy-done | bytes 1048600
  25.0 0.8 copy-done.11
  25.8 1.0 %copy-done.13 = f32[8,64,512]{2,1,0:T(8,128)} copy-done((f32[8,64,512]{2,1,0:T(8,128)}, f32[8,64,512]{2,1,0:T(8,128)S(1)}, u32[]{:S(2)}) %copy-start.13) | copy-done | bytes 1048600
  26.8 0.0 collective-permute-done.t1
  26.8 0.0 collective-permute-done.1.t2
  26.8 0.0 collective-permute-done.2.s1
  26.8 0.0 collective-permute-done.3.s2
  26.8 0.1 collective-permute-start.6
  26.9 0.0 copy-done.1
  26.9 0.9 collective-permute-start.7
  27.8 0.1 pad_add_fusion.place
  27.8 0.0 copy-done
  27.8 0.5 sides.3.side
  28.4 0.4 copy-done.7
  28.8 2.9 %collective-permute-start.4 = (bf16[528,512]{1,0:T(8,128)(2,1)S(1)}, bf16[528,512]{1,0:T(8,128)(2,1)S(1)}, u32[]{:S(2)}, u32[]{:S(2)}) collective-permute-start(bf16[528,512]{1,0:T(8,128)(2,1)S(1)} %copy-done.7), channel_id=1, source_target_pairs={{0,1},{1,2},{2,3},{3,4},{4,5},{5,6},{6,7},{7,8},{8,9},{9,10},{10,1... | collective-permute-start | bytes 1622024 | tf_op jit(solution)/shard_map/ppermute | solution.py:561
  31.8 0.0 copy-done.5
  31.8 1.5 %collective-permute-start.5 = (bf16[528,512]{1,0:T(8,128)(2,1)S(1)}, bf16[528,512]{1,0:T(8,128)(2,1)S(1)}, u32[]{:S(2)}, u32[]{:S(2)}) collective-permute-start(bf16[528,512]{1,0:T(8,128)(2,1)S(1)} %copy-done.5), channel_id=1, source_target_pairs={{1,0},{2,1},{3,2},{4,3},{5,4},{6,5},{7,6},{8,7},{9,8},{10,9},{11,1... | collective-permute-start | bytes 1622024 | tf_op jit(solution)/shard_map/ppermute | solution.py:562
  33.3 0.0 copy-start.15
  33.3 5.0 %far_a.1 = (f32[512,256]{1,0:T(8,128)S(1)}, f32[512,256]{1,0:T(8,128)S(1)}, f32[512,256]{1,0:T(8,128)S(1)}) custom-call(s32[24,16]{1,0:T(8,128)S(1)} %maximum_convert_fusion.1.ids, s32[2]{0:T(128)S(1)} %pad_add_fusion.place, bf16[24,256,128]{2,1,0:T(8,128)(2,1)S(1)} %sides.3.side, bf16[1088,256]{1,0:T(8,128)(2,1)S(1)} %copy-done, ...), custom_call_target="tpu_custom_call" | custom-call | flops 10000000 | bytes 1000000 | tf_op jit(solution)/shard_map/far_a/pallas_call | solution.py:243
  38.3 0.0 collective-permute-done.7.t3
  38.3 2.4 %collective-permute-done.6.s3 = bf16[1088,256]{1,0:T(8,128)(2,1)S(1)} collective-permute-done((bf16[1088,256]{1,0:T(8,128)(2,1)S(1)}, bf16[1088,256]{1,0:T(8,128)(2,1)S(1)}, u32[]{:S(2)}, u32[]{:S(2)}) %collective-permute-start.6) | collective-permute-done | bytes 557088 | tf_op jit(solution)/shard_map/ppermute | solution.py:529
  40.7 0.0 copy-done.15
  40.7 1.7 %collective-permute-start.8 = (bf16[128,256]{1,0:T(8,128)(2,1)S(1)}, bf16[128,256]{1,0:T(8,128)(2,1)S(1)}, u32[]{:S(2)}, u32[]{:S(2)}) collective-permute-start(bf16[128,256]{1,0:T(8,128)(2,1)S(1)} %pad_maximum_fusion.1.mine), channel_id=1, source_target_pairs={{0,16},{16,0},{32,48},{48,32},{64,80},{80,64},{96,112},{112,96},{1... | collective-permute-start | bytes 196616 | tf_op jit(solution)/shard_map/ppermute | solution.py:535
  42.4 2.9 %far_b.1 = (bf16[512,256]{1,0:T(8,128)(2,1)S(1)}, bf16[8,256,128]{2,1,0:T(8,128)(2,1)S(1)}) custom-call(s32[32,16]{1,0:T(8,128)S(1)} %maximum_convert_fusion.ids, s32[2]{0:T(128)S(1)} %pad_add_fusion.place, bf16[24,256,128]{2,1,0:T(8,128)(2,1)S(1)} %sides.3.side, bf16[1088,256]{1,0:T(8,128)(2,1)S(1)} %copy-done, ...), custom_call_target="tpu_custom_call" | custom-call | flops 3000000000 | bytes 1000000 | tf_op jit(solution)/shard_map/far_b/pallas_call | solution.py:268
  45.4 0.0 collective-permute-done.8.pair
  45.4 0.0 copy-start.10
  45.4 0.0 copy-start.12
  45.4 4.9 %collective-permute-start.10 = (bf16[256,256]{1,0:T(8,128)(2,1)S(1)}, bf16[256,256]{1,0:T(8,128)(2,1)S(1)}, u32[]{:S(2)}, u32[]{:S(2)}) collective-permute-start(bf16[256,256]{1,0:T(8,128)(2,1)S(1)} %pad_maximum_fusion), channel_id=1, source_target_pairs={{0,96},{16,112},{32,0},{48,16},{64,32},{80,48},{96,64},{112,80},{1... | collective-permute-start | bytes 393224 | tf_op jit(solution)/shard_map/ppermute | solution.py:536
  50.3 0.4 collective-permute-start.11
  50.8 0.9 %collective-permute-start.9 = (bf16[256,256]{1,0:T(8,128)(2,1)S(1)}, bf16[256,256]{1,0:T(8,128)(2,1)S(1)}, u32[]{:S(2)}, u32[]{:S(2)}) collective-permute-start(bf16[256,256]{1,0:T(8,128)(2,1)S(1)} %pad_maximum_fusion), channel_id=1, source_target_pairs={{0,32},{16,48},{32,64},{48,80},{64,96},{80,112},{96,0},{112,16},{1... | collective-permute-start | bytes 393224 | tf_op jit(solution)/shard_map/ppermute | solution.py:536
  51.6 2.5 %far_c.1 = (f32[512,256]{1,0:T(8,128)S(1)}, bf16[512,256]{1,0:T(8,128)(2,1)S(1)}, bf16[512,256]{1,0:T(8,128)(2,1)S(1)}) custom-call(s32[32,16]{1,0:T(8,128)S(1)} %maximum_convert_fusion.ids, s32[2]{0:T(128)S(1)} %pad_add_fusion.place, bf16[8,256,128]{2,1,0:T(8,128)(2,1)S(1)} %get-tuple-element.77.side, bf16[1088,256]{1,0:T(8,128)(2,1)S(1)} %collective-permute-done.6.s3, ...), custom_call_target="tpu_custom_call" | custom-call | flops 4000000000 | bytes 1000000 | tf_op jit(solution)/shard_map/far_c/pallas_call | solution.py:294
  54.1 0.0 collective-permute-done.4.before
  54.1 0.0 collective-permute-done.5.after
  54.2 0.0 copy-done.10
  54.2 0.0 copy-done.12
  54.2 2.5 %near_lent.1 = (bf16[4,64,512]{2,1,0:T(8,128)(2,1)S(1)}, bf16[4,64,512]{2,1,0:T(8,128)(2,1)S(1)}) custom-call(s32[16,8]{1,0:T(8,128)S(1)} %maximum_convert_fusion.2.offsets, bf16[8,512,128]{2,1,0:T(8,128)(2,1)S(1)} %copy-done.10, bf16[8,64,512]{2,1,0:T(8,128)(2,1)S(1)} %copy-done.12, bf16[528,512]{1,0:T(8,128)(2,1)S(1)} %collective-permute-done.4.before, ...), custom_call_target="tpu_custom_call" | custom-call | flops 4000000000 | bytes 1000000 | tf_op jit(solution)/shard_map/near_lent/pallas_call | solution.py:435
  56.7 0.0 collective-permute-done.10.n2
  56.7 1.5 %collective-permute-done.11.n3 = bf16[256,256]{1,0:T(8,128)(2,1)S(1)} collective-permute-done((bf16[256,256]{1,0:T(8,128)(2,1)S(1)}, bf16[256,256]{1,0:T(8,128)(2,1)S(1)}, u32[]{:S(2)}, u32[]{:S(2)}) %collective-permute-start.11) | collective-permute-done | bytes 131104 | tf_op jit(solution)/shard_map/ppermute | solution.py:536
  58.2 1.9 %collective-permute-done.9.n1 = bf16[256,256]{1,0:T(8,128)(2,1)S(1)} collective-permute-done((bf16[256,256]{1,0:T(8,128)(2,1)S(1)}, bf16[256,256]{1,0:T(8,128)(2,1)S(1)}, u32[]{:S(2)}, u32[]{:S(2)}) %collective-permute-start.9) | collective-permute-done | bytes 131104 | tf_op jit(solution)/shard_map/ppermute | solution.py:536
  60.1 0.8 top_sum.1
  61.0 0.1 collective-permute-start.14
  61.0 2.0 %collective-permute-start.15 = (bf16[576,256]{1,0:T(8,128)(2,1)S(1)}, bf16[576,256]{1,0:T(8,128)(2,1)S(1)}, u32[]{:S(2)}, u32[]{:S(2)}) collective-permute-start(bf16[576,256]{1,0:T(8,128)(2,1)S(1)} %get-tuple-element.100), channel_id=1, source_target_pairs={{0,1},{1,2},{2,3},{3,0},{4,5},{5,6},{6,7},{7,4},{8,9},{9,10},{10,1... | collective-permute-start | bytes 884744 | tf_op jit(solution)/shard_map/ppermute | solution.py:529
  63.1 0.0 collective-permute-start.16
  63.1 4.1 %collective-permute-start.12 = (bf16[4,64,512]{2,1,0:T(8,128)(2,1)S(1)}, bf16[4,64,512]{2,1,0:T(8,128)(2,1)S(1)}, u32[]{:S(2)}, u32[]{:S(2)}) collective-permute-start(bf16[4,64,512]{2,1,0:T(8,128)(2,1)S(1)} %get-tuple-element.90), channel_id=1, source_target_pairs={{0,1},{1,2},{2,3},{3,4},{4,5},{5,6},{6,7},{7,8},{8,9},{9,10},{10,1... | collective-permute-start | bytes 786440 | tf_op jit(solution)/shard_map/ppermute | solution.py:589
  67.1 1.6 %collective-permute-start.13 = (bf16[4,64,512]{2,1,0:T(8,128)(2,1)S(1)}, bf16[4,64,512]{2,1,0:T(8,128)(2,1)S(1)}, u32[]{:S(2)}, u32[]{:S(2)}) collective-permute-start(bf16[4,64,512]{2,1,0:T(8,128)(2,1)S(1)} %get-tuple-element.91), channel_id=1, source_target_pairs={{1,0},{2,1},{3,2},{4,3},{5,4},{6,5},{7,6},{8,7},{9,8},{10,9},{11,1... | collective-permute-start | bytes 786440 | tf_op jit(solution)/shard_map/ppermute | solution.py:590
  68.7 0.0 copy-done.14
  68.7 5.7 %near_rest.1.near_sum = f32[8,64,512]{2,1,0:T(8,128)S(1)} custom-call(s32[8,8]{1,0:T(8,128)S(1)} %copy-done.8, s32[1]{0:T(128)} %bitcast.first, bf16[528,512]{1,0:T(8,128)(2,1)S(1)} %copy-done.5, bf16[528,512]{1,0:T(8,128)(2,1)S(1)} %copy-done.7, bf16[528,512]{1,0:T(8,128)(2,1)S(1)} %collective-permute-done.4.before, ...), custom_call_target="tpu_custom_call" | custom-call | flops 7000000000 | bytes 1000000 | tf_op jit(solution)/shard_map/near_rest/pallas_call | solution.py:474
  74.4 6.6 %collective-permute-done.12.lent_low = bf16[4,64,512]{2,1,0:T(8,128)(2,1)S(1)} collective-permute-done((bf16[4,64,512]{2,1,0:T(8,128)(2,1)S(1)}, bf16[4,64,512]{2,1,0:T(8,128)(2,1)S(1)}, u32[]{:S(2)}, u32[]{:S(2)}) %collective-permute-start.12) | collective-permute-done | bytes 262176 | tf_op jit(solution)/shard_map/ppermute | solution.py:589
  81.1 3.8 %collective-permute-done.13.lent_high = bf16[4,64,512]{2,1,0:T(8,128)(2,1)S(1)} collective-permute-done((bf16[4,64,512]{2,1,0:T(8,128)(2,1)S(1)}, bf16[4,64,512]{2,1,0:T(8,128)(2,1)S(1)}, u32[]{:S(2)}, u32[]{:S(2)}) %collective-permute-start.13) | collective-permute-done | bytes 262176 | tf_op jit(solution)/shard_map/ppermute | solution.py:590
  84.8 0.0 collective-permute-done.14.r1
  84.8 0.0 collective-permute-done.15.r2
  84.8 0.0 collective-permute-done.16.r3
  84.8 0.0 copy-done.2
  84.9 2.5 %final.1 = bf16[8,64,512]{2,1,0:T(8,128)(2,1)} custom-call(f32[8,64,512]{2,1,0:T(8,128)S(1)} %near_rest.1.near_sum, bf16[4,64,512]{2,1,0:T(8,128)(2,1)S(1)} %collective-permute-done.12.lent_low, bf16[4,64,512]{2,1,0:T(8,128)(2,1)S(1)} %collective-permute-done.13.lent_high, bf16[8,512,256]{2,1,0:T(8,128)(2,1)S(1)} %copy-done.2, ...), custom_call_target="tpu_custom_call" | custom-call | flops 3000000000 | bytes 1000000 | tf_op jit(solution)/shard_map/final/pallas_call | solution.py:512
  (25 shorter events, 0.1 us)
Async XLA Ops:
  0.0 12.5 %copy-start.8 = (s32[8,8]{1,0:T(8,128)S(1)}, s32[8,8]{1,0:T(8,128)}, u32[]{:S(2)}) copy-start(s32[8,8]{1,0:T(8,128)} %ids.3) | copy-start | bytes 772
  5.0 21.8 %collective-permute-start = (bf16[528,256]{1,0:T(8,128)(2,1)}, bf16[528,256]{1,0:T(8,128)(2,1)S(1)}, u32[]{:S(2)}, u32[]{:S(2)}) collective-permute-start(bf16[528,256]{1,0:T(8,128)(2,1)} %get-tuple-element.66.t0), channel_id=1, source_target_pairs={{0,1},{1,2},{2,3},{3,0},{4,5},{5,6},{6,7},{7,4},{8,9},{9,10},{10,1... | collective-permute-start | bytes 811016 | tf_op jit(solution)/shard_map/ppermute | solution.py:529
  7.0 19.7 %collective-permute-start.1 = (bf16[528,256]{1,0:T(8,128)(2,1)}, bf16[528,256]{1,0:T(8,128)(2,1)S(1)}, u32[]{:S(2)}, u32[]{:S(2)}) collective-permute-start(bf16[528,256]{1,0:T(8,128)(2,1)} %get-tuple-element.66.t0), channel_id=1, source_target_pairs={{0,3},{1,0},{2,1},{3,2},{4,7},{5,4},{6,5},{7,6},{8,11},{9,8},{10,9... | collective-permute-start | bytes 811016 | tf_op jit(solution)/shard_map/ppermute | solution.py:529
  9.2 17.5 %collective-permute-start.2 = (bf16[1088,256]{1,0:T(8,128)(2,1)}, bf16[1088,256]{1,0:T(8,128)(2,1)S(1)}, u32[]{:S(2)}, u32[]{:S(2)}) collective-permute-start(bf16[1088,256]{1,0:T(8,128)(2,1)} %get-tuple-element.61.s0), channel_id=1, source_target_pairs={{0,4},{1,5},{2,6},{3,7},{4,8},{5,9},{6,10},{7,11},{8,12},{9,13},{1... | collective-permute-start | bytes 1671176 | tf_op jit(solution)/shard_map/ppermute | solution.py:529
  10.7 16.0 %collective-permute-start.3 = (bf16[1088,256]{1,0:T(8,128)(2,1)}, bf16[1088,256]{1,0:T(8,128)(2,1)S(1)}, u32[]{:S(2)}, u32[]{:S(2)}) collective-permute-start(bf16[1088,256]{1,0:T(8,128)(2,1)} %get-tuple-element.61.s0), channel_id=1, source_target_pairs={{0,12},{1,13},{2,14},{3,15},{4,0},{5,1},{6,2},{7,3},{8,4},{9,5},{1... | collective-permute-start | bytes 1671176 | tf_op jit(solution)/shard_map/ppermute | solution.py:529
  12.5 1.0 %copy-start.4 = (bf16[528,512]{1,0:T(8,128)(2,1)S(1)}, bf16[528,512]{1,0:T(8,128)(2,1)}, u32[]{:S(2)}) copy-start(bf16[528,512]{1,0:T(8,128)(2,1)} %get-tuple-element.64.low) | copy-start | bytes 1622020
  13.5 1.0 %copy-start.6 = (bf16[528,512]{1,0:T(8,128)(2,1)S(1)}, bf16[528,512]{1,0:T(8,128)(2,1)}, u32[]{:S(2)}) copy-start(bf16[528,512]{1,0:T(8,128)(2,1)} %get-tuple-element.65.high) | copy-start | bytes 1622020
  14.6 12.3 %copy-start.1 = (bf16[528,256]{1,0:T(8,128)(2,1)S(1)}, bf16[528,256]{1,0:T(8,128)(2,1)}, u32[]{:S(2)}) copy-start(bf16[528,256]{1,0:T(8,128)(2,1)} %get-tuple-element.66.t0) | copy-start | bytes 811012
  14.6 13.3 %copy-start = (bf16[1088,256]{1,0:T(8,128)(2,1)S(1)}, bf16[1088,256]{1,0:T(8,128)(2,1)}, u32[]{:S(2)}) copy-start(bf16[1088,256]{1,0:T(8,128)(2,1)} %get-tuple-element.61.s0) | copy-start | bytes 1671172
  24.0 1.0 %copy-start.9 = (bf16[8,512,128]{2,1,0:T(8,128)(2,1)}, bf16[8,512,128]{2,1,0:T(8,128)(2,1)S(1)}, u32[]{:S(2)}) copy-start(bf16[8,512,128]{2,1,0:T(8,128)(2,1)S(1)} %get-tuple-element.86.side) | copy-start | bytes 3145732
  25.0 0.8 copy-start.11
  25.8 1.0 %copy-start.13 = (f32[8,64,512]{2,1,0:T(8,128)}, f32[8,64,512]{2,1,0:T(8,128)S(1)}, u32[]{:S(2)}) copy-start(f32[8,64,512]{2,1,0:T(8,128)S(1)} %get-tuple-element.84.given) | copy-start | bytes 3145732
  26.8 13.9 %collective-permute-start.6 = (bf16[1088,256]{1,0:T(8,128)(2,1)S(1)}, bf16[1088,256]{1,0:T(8,128)(2,1)S(1)}, u32[]{:S(2)}, u32[]{:S(2)}) collective-permute-start(bf16[1088,256]{1,0:T(8,128)(2,1)S(1)} %collective-permute-done.2.s1), channel_id=1, source_target_pairs={{0,4},{1,5},{2,6},{3,7},{4,8},{5,9},{6,10},{7,11},{8,12},{9,13},{1... | collective-permute-start | bytes 1671176 | tf_op jit(solution)/shard_map/ppermute | solution.py:529
  26.9 11.4 %collective-permute-start.7 = (bf16[528,256]{1,0:T(8,128)(2,1)S(1)}, bf16[528,256]{1,0:T(8,128)(2,1)S(1)}, u32[]{:S(2)}, u32[]{:S(2)}) collective-permute-start(bf16[528,256]{1,0:T(8,128)(2,1)S(1)} %copy-done.1), channel_id=1, source_target_pairs={{0,2},{1,3},{2,0},{3,1},{4,6},{5,7},{6,4},{7,5},{8,10},{9,11},{10,... | collective-permute-start | bytes 811016 | tf_op jit(solution)/shard_map/ppermute | solution.py:529
  27.8 1.0 %copy-start.7 = (bf16[528,512]{1,0:T(8,128)(2,1)S(1)}, bf16[528,512]{1,0:T(8,128)(2,1)}, u32[]{:S(2)}) copy-start(bf16[528,512]{1,0:T(8,128)(2,1)} %get-tuple-element.65.high) | copy-start | bytes 1622020
  27.8 4.0 %copy-start.5 = (bf16[528,512]{1,0:T(8,128)(2,1)S(1)}, bf16[528,512]{1,0:T(8,128)(2,1)}, u32[]{:S(2)}) copy-start(bf16[528,512]{1,0:T(8,128)(2,1)} %get-tuple-element.64.low) | copy-start | bytes 1622020
  28.8 25.3 %collective-permute-start.4 = (bf16[528,512]{1,0:T(8,128)(2,1)S(1)}, bf16[528,512]{1,0:T(8,128)(2,1)S(1)}, u32[]{:S(2)}, u32[]{:S(2)}) collective-permute-start(bf16[528,512]{1,0:T(8,128)(2,1)S(1)} %copy-done.7), channel_id=1, source_target_pairs={{0,1},{1,2},{2,3},{3,4},{4,5},{5,6},{6,7},{7,8},{8,9},{9,10},{10,1... | collective-permute-start | bytes 1622024 | tf_op jit(solution)/shard_map/ppermute | solution.py:561
  31.8 22.4 %collective-permute-start.5 = (bf16[528,512]{1,0:T(8,128)(2,1)S(1)}, bf16[528,512]{1,0:T(8,128)(2,1)S(1)}, u32[]{:S(2)}, u32[]{:S(2)}) collective-permute-start(bf16[528,512]{1,0:T(8,128)(2,1)S(1)} %copy-done.5), channel_id=1, source_target_pairs={{1,0},{2,1},{3,2},{4,3},{5,4},{6,5},{7,6},{8,7},{9,8},{10,9},{11,1... | collective-permute-start | bytes 1622024 | tf_op jit(solution)/shard_map/ppermute | solution.py:562
  33.3 7.5 %copy-start.15 = (bf16[1,64,256]{2,1,0:T(8,128)(2,1)S(1)}, bf16[1,64,256]{2,1,0:T(8,128)(2,1)}, u32[]{:S(2)}) copy-start(bf16[1,64,256]{2,1,0:T(8,128)(2,1)} %param.12) | copy-start | bytes 98308
  40.7 4.6 %collective-permute-start.8 = (bf16[128,256]{1,0:T(8,128)(2,1)S(1)}, bf16[128,256]{1,0:T(8,128)(2,1)S(1)}, u32[]{:S(2)}, u32[]{:S(2)}) collective-permute-start(bf16[128,256]{1,0:T(8,128)(2,1)S(1)} %pad_maximum_fusion.1.mine), channel_id=1, source_target_pairs={{0,16},{16,0},{32,48},{48,32},{64,80},{80,64},{96,112},{112,96},{1... | collective-permute-start | bytes 196616 | tf_op jit(solution)/shard_map/ppermute | solution.py:535
  45.4 8.8 %copy-start.10 = (bf16[8,512,128]{2,1,0:T(8,128)(2,1)S(1)}, bf16[8,512,128]{2,1,0:T(8,128)(2,1)}, u32[]{:S(2)}) copy-start(bf16[8,512,128]{2,1,0:T(8,128)(2,1)} %copy-done.9) | copy-start | bytes 3145732
  45.4 8.8 %copy-start.12 = (bf16[8,64,512]{2,1,0:T(8,128)(2,1)S(1)}, bf16[8,64,512]{2,1,0:T(8,128)(2,1)}, u32[]{:S(2)}) copy-start(bf16[8,64,512]{2,1,0:T(8,128)(2,1)} %copy-done.11) | copy-start | bytes 1572868
  45.4 11.3 %collective-permute-start.10 = (bf16[256,256]{1,0:T(8,128)(2,1)S(1)}, bf16[256,256]{1,0:T(8,128)(2,1)S(1)}, u32[]{:S(2)}, u32[]{:S(2)}) collective-permute-start(bf16[256,256]{1,0:T(8,128)(2,1)S(1)} %pad_maximum_fusion), channel_id=1, source_target_pairs={{0,96},{16,112},{32,0},{48,16},{64,32},{80,48},{96,64},{112,80},{1... | collective-permute-start | bytes 393224 | tf_op jit(solution)/shard_map/ppermute | solution.py:536
  50.3 7.9 %collective-permute-start.11 = (bf16[256,256]{1,0:T(8,128)(2,1)S(1)}, bf16[256,256]{1,0:T(8,128)(2,1)S(1)}, u32[]{:S(2)}, u32[]{:S(2)}) collective-permute-start(bf16[256,256]{1,0:T(8,128)(2,1)S(1)} %pad_maximum_fusion), channel_id=1, source_target_pairs={{0,64},{16,80},{32,96},{48,112},{64,0},{80,16},{96,32},{112,48},{1... | collective-permute-start | bytes 393224 | tf_op jit(solution)/shard_map/ppermute | solution.py:536
  50.8 9.3 %collective-permute-start.9 = (bf16[256,256]{1,0:T(8,128)(2,1)S(1)}, bf16[256,256]{1,0:T(8,128)(2,1)S(1)}, u32[]{:S(2)}, u32[]{:S(2)}) collective-permute-start(bf16[256,256]{1,0:T(8,128)(2,1)S(1)} %pad_maximum_fusion), channel_id=1, source_target_pairs={{0,32},{16,48},{32,64},{48,80},{64,96},{80,112},{96,0},{112,16},{1... | collective-permute-start | bytes 393224 | tf_op jit(solution)/shard_map/ppermute | solution.py:536
  60.1 8.6 %copy-start.14 = (f32[8,64,512]{2,1,0:T(8,128)S(1)}, f32[8,64,512]{2,1,0:T(8,128)}, u32[]{:S(2)}) copy-start(f32[8,64,512]{2,1,0:T(8,128)} %copy-done.13) | copy-start | bytes 3145732
  61.0 23.9 %collective-permute-start.14 = (bf16[576,256]{1,0:T(8,128)(2,1)S(1)}, bf16[576,256]{1,0:T(8,128)(2,1)S(1)}, u32[]{:S(2)}, u32[]{:S(2)}) collective-permute-start(bf16[576,256]{1,0:T(8,128)(2,1)S(1)} %get-tuple-element.99), channel_id=1, source_target_pairs={{0,3},{1,0},{2,1},{3,2},{4,7},{5,4},{6,5},{7,6},{8,11},{9,8},{10,9... | collective-permute-start | bytes 884744 | tf_op jit(solution)/shard_map/ppermute | solution.py:529
  61.0 23.8 %collective-permute-start.15 = (bf16[576,256]{1,0:T(8,128)(2,1)S(1)}, bf16[576,256]{1,0:T(8,128)(2,1)S(1)}, u32[]{:S(2)}, u32[]{:S(2)}) collective-permute-start(bf16[576,256]{1,0:T(8,128)(2,1)S(1)} %get-tuple-element.100), channel_id=1, source_target_pairs={{0,1},{1,2},{2,3},{3,0},{4,5},{5,6},{6,7},{7,4},{8,9},{9,10},{10,1... | collective-permute-start | bytes 884744 | tf_op jit(solution)/shard_map/ppermute | solution.py:529
  63.1 21.8 %copy-start.2 = (bf16[8,512,256]{2,1,0:T(8,128)(2,1)S(1)}, bf16[8,512,256]{2,1,0:T(8,128)(2,1)}, u32[]{:S(2)}) copy-start(bf16[8,512,256]{2,1,0:T(8,128)(2,1)} %basis.3) | copy-start | bytes 6291460
  63.1 21.8 %copy-start.3 = (bf16[8,256,256]{2,1,0:T(8,128)(2,1)S(1)}, bf16[8,256,256]{2,1,0:T(8,128)(2,1)}, u32[]{:S(2)}) copy-start(bf16[8,256,256]{2,1,0:T(8,128)(2,1)} %transfer.3) | copy-start | bytes 3145732
  63.1 21.8 %collective-permute-start.16 = (bf16[576,256]{1,0:T(8,128)(2,1)S(1)}, bf16[576,256]{1,0:T(8,128)(2,1)S(1)}, u32[]{:S(2)}, u32[]{:S(2)}) collective-permute-start(bf16[576,256]{1,0:T(8,128)(2,1)S(1)} %get-tuple-element.101), channel_id=1, source_target_pairs={{0,2},{1,3},{2,0},{3,1},{4,6},{5,7},{6,4},{7,5},{8,10},{9,11},{10,... | collective-permute-start | bytes 884744 | tf_op jit(solution)/shard_map/ppermute | solution.py:529
  63.1 18.0 %collective-permute-start.12 = (bf16[4,64,512]{2,1,0:T(8,128)(2,1)S(1)}, bf16[4,64,512]{2,1,0:T(8,128)(2,1)S(1)}, u32[]{:S(2)}, u32[]{:S(2)}) collective-permute-start(bf16[4,64,512]{2,1,0:T(8,128)(2,1)S(1)} %get-tuple-element.90), channel_id=1, source_target_pairs={{0,1},{1,2},{2,3},{3,4},{4,5},{5,6},{6,7},{7,8},{8,9},{9,10},{10,1... | collective-permute-start | bytes 786440 | tf_op jit(solution)/shard_map/ppermute | solution.py:589
  67.1 17.7 %collective-permute-start.13 = (bf16[4,64,512]{2,1,0:T(8,128)(2,1)S(1)}, bf16[4,64,512]{2,1,0:T(8,128)(2,1)S(1)}, u32[]{:S(2)}, u32[]{:S(2)}) collective-permute-start(bf16[4,64,512]{2,1,0:T(8,128)(2,1)S(1)} %get-tuple-element.91), channel_id=1, source_target_pairs={{1,0},{2,1},{3,2},{4,3},{5,4},{6,5},{7,6},{8,7},{9,8},{10,9},{11,1... | collective-permute-start | bytes 786440 | tf_op jit(solution)/shard_map/ppermute | solution.py:590

commit v10 on v7

--- a/solution.py
+++ b/solution.py
@@ -204,22 +204,19 @@
     )(*sources)
 
 
-def far_a_kernel(ids, place, side, s0, s1, s2, t0, t1, t2, o0, o1, o2, tile):
-    jobs = []
-    for b, (target, out) in enumerate(((t0, o0), (t1, o1), (t2, o2))):
-        jobs += target_jobs(b, target, out)
+def far_a_kernel(ids, place, side, s0, s1, s2, t0, t1, o0, o1, tile):
     far_run(
-        ids, columns_of(place)[:3], jobs, lambda d, at: side[d * LD + at],
-        lambda d, at: charges_at((s0, s1, s2)[d], at), tile,
+        ids, columns_of(place)[:3], target_jobs(0, t0, o0) + target_jobs(1, t1, o1),
+        lambda d, at: side[d * LD + at], lambda d, at: charges_at((s0, s1, s2)[d], at), tile,
     )
 
 
 def far_a(ids, place, side, sources, targets):
     return pl.pallas_call(
         far_a_kernel,
-        in_specs=[SM, SM] + [VM] * 7,
-        out_specs=[VM] * 3,
-        out_shape=[jax.ShapeDtypeStruct((LD * F, SK), F32)] * 3,
+        in_specs=[SM, SM] + [VM] * 6,
+        out_specs=[VM] * 2,
+        out_shape=[jax.ShapeDtypeStruct((LD * F, SK), F32)] * 2,
         scratch_shapes=[pltpu.VMEM((2 * BATCH, 3 * SK, SK), BF)],
         compiler_params=params(16),
         cost_estimate=cost(0.01),
@@ -255,28 +252,33 @@
     )(ids, place, side, *sources, target)
 
 
-def far_c_kernel(ids, place, side, s3, t0, t1, t2, a0, a1, a2, own, r1, r2, tile):
-    jobs = []
-    for b, (target, given, out) in enumerate(((t0, a0, own), (t1, a1, r1), (t2, a2, r2))):
-        jobs += target_jobs(b, target, out, given)
+def far_c_kernel(
+    ids, place, side, last, s0, s1, s2, s3, t0, t1, t2, a0, a1, own, r1, r2, tile
+):
+    columns = columns_of(place)
     far_run(
-        ids, columns_of(place)[3:], jobs, lambda d, at: side[at],
-        lambda d, at: charges_at(s3, at), tile,
-    )
-
-
-def far_c(ids, place, side, source, targets, given):
+        ids, columns, target_jobs(2, t2, r2),
+        lambda d, at: last[at] if d == 3 else side[d * LD + at],
+        lambda d, at: charges_at((s0, s1, s2, s3)[d], at), tile,
+    )
+    far_run(
+        ids, columns[3:], target_jobs(0, t0, own, a0) + target_jobs(1, t1, r1, a1),
+        lambda d, at: last[at], lambda d, at: charges_at(s3, at), tile,
+    )
+
+
+def far_c(ids, place, side, last, sources, targets, given):
     return pl.pallas_call(
         far_c_kernel,
-        in_specs=[SM, SM] + [VM] * 8,
+        in_specs=[SM, SM] + [VM] * 11,
         out_specs=[VM] * 3,
         out_shape=[jax.ShapeDtypeStruct((LD * F, SK), F32)]
         + [jax.ShapeDtypeStruct((LD * F, SK), BF)] * 2,
-        scratch_shapes=[pltpu.VMEM((2 * BATCH, SK, SK), BF)],
+        scratch_shapes=[pltpu.VMEM((2 * BATCH, SIDE * SK, SK), BF)],
         compiler_params=params(16),
         cost_estimate=cost(4),
         name="far_c",
-    )(ids, place, side, source, *targets, *given)
+    )(ids, place, side, last, *sources, *targets, *given)
 
 
 def top_kernel(mine, pair, n1, n2, n3, a1, a2, a3, top, r1, r2, r3):
@@ -476,8 +478,8 @@
     first = (position * LD).astype(jnp.int32).reshape(1)
     near_sum = near_own(neighbours, first, near_msg)
 
-    targets[:3], sources, near_msg, near_sum = lax.optimization_barrier(
-        (targets[:3], sources, near_msg, near_sum)
+    targets, sources, near_msg, near_sum = lax.optimization_barrier(
+        (targets, sources, near_msg, near_sum)
     )
     opposite = shifted(sources[1], 1, 0)
     side = sides_of(sources)
@@ -492,8 +494,8 @@
         return ids.astype(jnp.int32)
 
     place = jnp.stack([at // SIDE, at % SIDE]).astype(jnp.int32)
-    given = far_a(ids_of(targets[:3]), place, side, sources, targets[:3])
-    opposite, given, targets[3] = lax.optimization_barrier((opposite, given, targets[3]))
+    given = far_a(ids_of(targets[:2]), place, side, sources, targets[:2])
+    opposite, given, targets[2:] = lax.optimization_barrier((opposite, given, targets[2:]))
     sources.append(opposite)
     line_charge = sum(s[2 * LD * F :].astype(F32) for s in sources)
     mine = jnp.concatenate([line_charge.astype(BF), node_points[0]], axis=0)
@@ -503,7 +505,7 @@
     pair, r3, last = lax.optimization_barrier((pair, r3, last))
     both = jnp.concatenate([mine, pair], axis=0)
     others = [leaf_shifted(both, dy) for dy in (1, -1, 2)]
-    own, r1, r2 = far_c(ids, place, last, opposite, targets[:3], given)
+    own, r1, r2 = far_c(ids, place, side, last, sources, targets[:3], given)
     top, *parts = top_sum(mine, pair, others, (r1, r2, r3))
     returned = [shifted(r, 0, dz) for r, dz in zip(parts, (-1, 1, 2))]
     near_sum = near_rest(neighbours, first, near_msg, before, after, near_sum)

time: 82.7 us -> 81.8 us (0.989)
  the two profiles are of different devices: /device:TPU:14 before, /device:TPU:0 now
where the time goes in v10:
time: 81.8 us; the launch traced here: 80.7 us
  Pallas kernels  31.6 us (39%)
  starting transfers between devices  29.3 us (36%)
  waiting for transfers between devices  16.6 us (20%)
  local copies, waits for them, and re-layouts  2.84 us (3%)
    ppermute x9, starting transfers between devices, shifted(): return lax.ppermute(value, 'top', pairs)  17.1 us
    ppermute x9, waiting for transfers between devices, shifted(): return lax.ppermute(value, 'top', pairs)  14.5 us
    ppermute x3, starting transfers between devices, leaf_shifted(): lax.ppermute(value, 'leaf', [(i, (i + 2 * dy) % count) for i in range(cou...  7.73 us
    pallas_call x1, Pallas kernels, near_own(): pl.pallas_call(near_own_kernel, in_specs=[SM, SM, VM], out_specs=VM, out_...  6.51 us
    pallas_call x1, Pallas kernels, near_rest(): pl.pallas_call(near_rest_kernel, in_specs=[SM, SM, VM, VM, VM, VM], out_s...  6.11 us
    pallas_call x1, Pallas kernels, prep(): pl.pallas_call(prep_kernel, in_specs=[anywhere] * 4 + [VM] * 2, out_specs...  4.89 us
    pallas_call x1, Pallas kernels, far_c(): pl.pallas_call(far_c_kernel, in_specs=[SM, SM] + [VM] * 11, out_specs=[VM...  3.8 us
    pallas_call x1, Pallas kernels, far_a(): pl.pallas_call(far_a_kernel, in_specs=[SM, SM] + [VM] * 6, out_specs=[VM]...  3.55 us
  transfers between devices with their start and end apart: 15, of which 6 were waited for; matrix products, arithmetic and copies ran while one was open for 0% of the time, Pallas kernels for 30%

profile of v10, /device:TPU:0, one launch (start us, length us, event | category | flops | bytes accessed | tf_op | source)
XLA Modules:
  0.0 80.7 jit_solution(9084481854571962488)
XLA Ops:
  0.0 0.0 copy-start.6
  0.0 4.9 %prep.1 = (bf16[8,128,512]{2,1,0:T(8,128)(2,1)}, bf16[1088,256]{1,0:T(8,128)(2,1)}, bf16[528,256]{1,0:T(8,128)(2,1)}) custom-call(bf16[8,64,512]{2,1,0:T(8,128)(2,1)} %points.1, bf16[8,64,512]{2,1,0:T(8,128)(2,1)} %sides.2, bf16[8,512,256]{2,1,0:T(8,128)(2,1)} %basis.3, bf16[8,256,256]{2,1,0:T(8,128)(2,1)} %transfer.3, s32[8,256]{1,0:T(8,128)} %skeleton.1, ...), custom_call_target="tpu_custom_call" | custom-call | flops 4000000000 | bytes 1000000 | tf_op jit(solution)/shard_map/prep/pallas_call | solution.py:101
  4.9 2.1 %collective-permute-start = (bf16[528,256]{1,0:T(8,128)(2,1)}, bf16[528,256]{1,0:T(8,128)(2,1)S(1)}, u32[]{:S(2)}, u32[]{:S(2)}) collective-permute-start(bf16[528,256]{1,0:T(8,128)(2,1)} %get-tuple-element.47.t0), channel_id=1, source_target_pairs={{0,1},{1,2},{2,3},{3,0},{4,5},{5,6},{6,7},{7,4},{8,9},{9,10},{10,1... | collective-permute-start | bytes 811016 | tf_op jit(solution)/shard_map/ppermute | solution.py:458
  7.0 2.2 %collective-permute-start.1 = (bf16[528,256]{1,0:T(8,128)(2,1)}, bf16[528,256]{1,0:T(8,128)(2,1)S(1)}, u32[]{:S(2)}, u32[]{:S(2)}) collective-permute-start(bf16[528,256]{1,0:T(8,128)(2,1)} %get-tuple-element.47.t0), channel_id=1, source_target_pairs={{0,3},{1,0},{2,1},{3,2},{4,7},{5,4},{6,5},{7,6},{8,11},{9,8},{10,9... | collective-permute-start | bytes 811016 | tf_op jit(solution)/shard_map/ppermute | solution.py:458
  9.2 1.8 %collective-permute-start.2 = (bf16[528,256]{1,0:T(8,128)(2,1)}, bf16[528,256]{1,0:T(8,128)(2,1)S(1)}, u32[]{:S(2)}, u32[]{:S(2)}) collective-permute-start(bf16[528,256]{1,0:T(8,128)(2,1)} %get-tuple-element.47.t0), channel_id=1, source_target_pairs={{0,2},{1,3},{2,0},{3,1},{4,6},{5,7},{6,4},{7,5},{8,10},{9,11},{10,... | collective-permute-start | bytes 811016 | tf_op jit(solution)/shard_map/ppermute | solution.py:458
  11.0 1.5 %collective-permute-start.3 = (bf16[1088,256]{1,0:T(8,128)(2,1)}, bf16[1088,256]{1,0:T(8,128)(2,1)S(1)}, u32[]{:S(2)}, u32[]{:S(2)}) collective-permute-start(bf16[1088,256]{1,0:T(8,128)(2,1)} %get-tuple-element.42.s0), channel_id=1, source_target_pairs={{0,4},{1,5},{2,6},{3,7},{4,8},{5,9},{6,10},{7,11},{8,12},{9,13},{1... | collective-permute-start | bytes 1671176 | tf_op jit(solution)/shard_map/ppermute | solution.py:458
  12.5 1.7 %collective-permute-start.4 = (bf16[1088,256]{1,0:T(8,128)(2,1)}, bf16[1088,256]{1,0:T(8,128)(2,1)S(1)}, u32[]{:S(2)}, u32[]{:S(2)}) collective-permute-start(bf16[1088,256]{1,0:T(8,128)(2,1)} %get-tuple-element.42.s0), channel_id=1, source_target_pairs={{0,12},{1,13},{2,14},{3,15},{4,0},{5,1},{6,2},{7,3},{8,4},{9,5},{1... | collective-permute-start | bytes 1671176 | tf_op jit(solution)/shard_map/ppermute | solution.py:458
  14.2 0.0 copy-done.6
  14.2 0.0 copy-start.4
  14.2 1.2 %copy-done.4 = bf16[8,128,512]{2,1,0:T(8,128)(2,1)S(1)} copy-done((bf16[8,128,512]{2,1,0:T(8,128)(2,1)S(1)}, bf16[8,128,512]{2,1,0:T(8,128)(2,1)}, u32[]{:S(2)}) %copy-start.4) | copy-done | bytes 1048600
  15.4 0.0 copy-start
  15.4 6.5 %near_own.1.given = f32[8,64,512]{2,1,0:T(8,128)S(1)} custom-call(s32[8,8]{1,0:T(8,128)S(1)} %copy-done.6, s32[1]{0:T(128)} %bitcast.first, bf16[8,128,512]{2,1,0:T(8,128)(2,1)S(1)} %copy-done.4), custom_call_target="tpu_custom_call" | custom-call | flops 8999999488 | bytes 1000000 | tf_op jit(solution)/shard_map/near_own/pallas_call | solution.py:367
  21.9 0.0 copy-start.7
  22.0 0.9 %copy-done.7 = f32[8,64,512]{2,1,0:T(8,128)} copy-done((f32[8,64,512]{2,1,0:T(8,128)}, f32[8,64,512]{2,1,0:T(8,128)S(1)}, u32[]{:S(2)}) %copy-start.7) | copy-done | bytes 1048600
  22.9 0.0 copy-start.1
  22.9 0.0 collective-permute-done.t1
  22.9 0.0 collective-permute-done.1.t2
  22.9 0.0 collective-permute-done.2.t3
  22.9 3.0 %collective-permute-done.3.s1 = bf16[1088,256]{1,0:T(8,128)(2,1)S(1)} collective-permute-done((bf16[1088,256]{1,0:T(8,128)(2,1)}, bf16[1088,256]{1,0:T(8,128)(2,1)S(1)}, u32[]{:S(2)}, u32[]{:S(2)}) %collective-permute-start.3) | collective-permute-done | bytes 557088 | tf_op jit(solution)/shard_map/ppermute | solution.py:458
  25.9 0.0 collective-permute-done.4.s2
  25.9 1.5 %collective-permute-start.7 = (bf16[1088,256]{1,0:T(8,128)(2,1)S(1)}, bf16[1088,256]{1,0:T(8,128)(2,1)S(1)}, u32[]{:S(2)}, u32[]{:S(2)}) collective-permute-start(bf16[1088,256]{1,0:T(8,128)(2,1)S(1)} %collective-permute-done.3.s1), channel_id=1, source_target_pairs={{0,4},{1,5},{2,6},{3,7},{4,8},{5,9},{6,10},{7,11},{8,12},{9,13},{1... | collective-permute-start | bytes 1671176 | tf_op jit(solution)/shard_map/ppermute | solution.py:458
  27.4 0.0 copy-start.5
  27.4 0.1 pad_add_fusion.place
  27.5 0.0 copy-done
  27.5 0.5 sides.3.side
  28.0 0.6 copy-done.5
  28.6 0.0 copy-start.9
  28.6 3.1 %collective-permute-start.5 = (bf16[8,128,512]{2,1,0:T(8,128)(2,1)S(1)}, bf16[8,128,512]{2,1,0:T(8,128)(2,1)S(1)}, u32[]{:S(2)}, u32[]{:S(2)}) collective-permute-start(bf16[8,128,512]{2,1,0:T(8,128)(2,1)S(1)} %copy-done.5), channel_id=1, source_target_pairs={{0,1},{1,2},{2,3},{3,4},{4,5},{5,6},{6,7},{7,8},{8,9},{9,10},{10,1... | collective-permute-start | bytes 3145736 | tf_op jit(solution)/shard_map/ppermute | solution.py:489
  31.7 1.3 %collective-permute-start.6 = (bf16[8,128,512]{2,1,0:T(8,128)(2,1)S(1)}, bf16[8,128,512]{2,1,0:T(8,128)(2,1)S(1)}, u32[]{:S(2)}, u32[]{:S(2)}) collective-permute-start(bf16[8,128,512]{2,1,0:T(8,128)(2,1)S(1)} %copy-done.5), channel_id=1, source_target_pairs={{1,0},{2,1},{3,2},{4,3},{5,4},{6,5},{7,6},{8,7},{9,8},{10,9},{11,1... | collective-permute-start | bytes 3145736 | tf_op jit(solution)/shard_map/ppermute | solution.py:490
  33.1 0.0 copy-done.1
  33.1 3.5 %far_a.1 = (f32[512,256]{1,0:T(8,128)S(1)}, f32[512,256]{1,0:T(8,128)S(1)}) custom-call(s32[16,16]{1,0:T(8,128)S(1)} %maximum_convert_fusion.1.ids, s32[2]{0:T(128)S(1)} %pad_add_fusion.place, bf16[24,256,128]{2,1,0:T(8,128)(2,1)S(1)} %sides.3.side, bf16[1088,256]{1,0:T(8,128)(2,1)S(1)} %copy-done, bf16[1088,256]{1,0:T(8,128)(2,1)S(1)} %collective-permute-done.3.s1, ...), custom_call_target="tpu_custom_call" | custom-call | flops 10000000 | bytes 1000000 | tf_op jit(solution)/shard_map/far_a/pallas_call | solution.py:215
  36.6 3.1 %collective-permute-done.7.s3 = bf16[1088,256]{1,0:T(8,128)(2,1)S(1)} collective-permute-done((bf16[1088,256]{1,0:T(8,128)(2,1)S(1)}, bf16[1088,256]{1,0:T(8,128)(2,1)S(1)}, u32[]{:S(2)}, u32[]{:S(2)}) %collective-permute-start.7) | collective-permute-done | bytes 557088 | tf_op jit(solution)/shard_map/ppermute | solution.py:458
  39.8 0.0 copy-done.9
  39.8 0.1 collective-permute-start.8
  39.9 2.9 %far_b.1 = (bf16[512,256]{1,0:T(8,128)(2,1)S(1)}, bf16[8,256,128]{2,1,0:T(8,128)(2,1)S(1)}) custom-call(s32[32,16]{1,0:T(8,128)S(1)} %maximum_convert_fusion.ids, s32[2]{0:T(128)S(1)} %pad_add_fusion.place, bf16[24,256,128]{2,1,0:T(8,128)(2,1)S(1)} %sides.3.side, bf16[1088,256]{1,0:T(8,128)(2,1)S(1)} %copy-done, ...), custom_call_target="tpu_custom_call" | custom-call | flops 3000000000 | bytes 1000000 | tf_op jit(solution)/shard_map/far_b/pallas_call | solution.py:240
  42.8 0.0 collective-permute-done.8.pair
  42.9 4.1 %collective-permute-start.9 = (bf16[256,256]{1,0:T(8,128)(2,1)S(1)}, bf16[256,256]{1,0:T(8,128)(2,1)S(1)}, u32[]{:S(2)}, u32[]{:S(2)}) collective-permute-start(bf16[256,256]{1,0:T(8,128)(2,1)S(1)} %pad_maximum_fusion), channel_id=1, source_target_pairs={{0,32},{16,48},{32,64},{48,80},{64,96},{80,112},{96,0},{112,16},{1... | collective-permute-start | bytes 393224 | tf_op jit(solution)/shard_map/ppermute | solution.py:465
  46.9 1.7 %collective-permute-start.10 = (bf16[256,256]{1,0:T(8,128)(2,1)S(1)}, bf16[256,256]{1,0:T(8,128)(2,1)S(1)}, u32[]{:S(2)}, u32[]{:S(2)}) collective-permute-start(bf16[256,256]{1,0:T(8,128)(2,1)S(1)} %pad_maximum_fusion), channel_id=1, source_target_pairs={{0,96},{16,112},{32,0},{48,16},{64,32},{80,48},{96,64},{112,80},{1... | collective-permute-start | bytes 393224 | tf_op jit(solution)/shard_map/ppermute | solution.py:465
  48.6 1.9 %collective-permute-start.11 = (bf16[256,256]{1,0:T(8,128)(2,1)S(1)}, bf16[256,256]{1,0:T(8,128)(2,1)S(1)}, u32[]{:S(2)}, u32[]{:S(2)}) collective-permute-start(bf16[256,256]{1,0:T(8,128)(2,1)S(1)} %pad_maximum_fusion), channel_id=1, source_target_pairs={{0,64},{16,80},{32,96},{48,112},{64,0},{80,16},{96,32},{112,48},{1... | collective-permute-start | bytes 393224 | tf_op jit(solution)/shard_map/ppermute | solution.py:465
  50.6 3.8 %far_c.1 = (f32[512,256]{1,0:T(8,128)S(1)}, bf16[512,256]{1,0:T(8,128)(2,1)S(1)}, bf16[512,256]{1,0:T(8,128)(2,1)S(1)}) custom-call(s32[32,16]{1,0:T(8,128)S(1)} %maximum_convert_fusion.ids, s32[2]{0:T(128)S(1)} %pad_add_fusion.place, bf16[24,256,128]{2,1,0:T(8,128)(2,1)S(1)} %sides.3.side, bf16[8,256,128]{2,1,0:T(8,128)(2,1)S(1)} %get-tuple-element.59.last, ...), custom_call_target="tpu_custom_call" | custom-call | flops 4000000000 | bytes 1000000 | tf_op jit(solution)/shard_map/far_c/pallas_call | solution.py:271
  54.4 0.0 collective-permute-done.9.n1
  54.4 0.5 collective-permute-done.10.n2
  54.9 1.6 %collective-permute-done.11.n3 = bf16[256,256]{1,0:T(8,128)(2,1)S(1)} collective-permute-done((bf16[256,256]{1,0:T(8,128)(2,1)S(1)}, bf16[256,256]{1,0:T(8,128)(2,1)S(1)}, u32[]{:S(2)}, u32[]{:S(2)}) %collective-permute-start.11) | collective-permute-done | bytes 131104 | tf_op jit(solution)/shard_map/ppermute | solution.py:465
  56.5 0.0 copy-start.8
  56.5 0.8 %top_sum.1 = (f32[64,256]{1,0:T(8,128)S(1)}, bf16[576,256]{1,0:T(8,128)(2,1)S(1)}, bf16[576,256]{1,0:T(8,128)(2,1)S(1)}, bf16[576,256]{1,0:T(8,128)(2,1)S(1)}) custom-call(bf16[128,256]{1,0:T(8,128)(2,1)S(1)} %pad_maximum_fusion.1.mine, bf16[128,256]{1,0:T(8,128)(2,1)S(1)} %collective-permute-done.8.pair, bf16[256,256]{1,0:T(8,128)(2,1)S(1)} %collective-permute-done.9.n1, ...), custom_call_target="tpu_custom_call" | custom-call | flops 2000000000 | bytes 1000000 | tf_op jit(solution)/shard_map/top_sum/pallas_call | solution.py:301
  57.4 4.8 %collective-permute-start.12 = (bf16[576,256]{1,0:T(8,128)(2,1)S(1)}, bf16[576,256]{1,0:T(8,128)(2,1)S(1)}, u32[]{:S(2)}, u32[]{:S(2)}) collective-permute-start(bf16[576,256]{1,0:T(8,128)(2,1)S(1)} %get-tuple-element.67), channel_id=1, source_target_pairs={{0,3},{1,0},{2,1},{3,2},{4,7},{5,4},{6,5},{7,6},{8,11},{9,8},{10,9... | collective-permute-start | bytes 884744 | tf_op jit(solution)/shard_map/ppermute | solution.py:458
  62.1 0.0 collective-permute-start.13
  62.1 0.0 copy-start.2
  62.1 0.0 copy-start.3
  62.1 1.5 %collective-permute-start.14 = (bf16[576,256]{1,0:T(8,128)(2,1)S(1)}, bf16[576,256]{1,0:T(8,128)(2,1)S(1)}, u32[]{:S(2)}, u32[]{:S(2)}) collective-permute-start(bf16[576,256]{1,0:T(8,128)(2,1)S(1)} %get-tuple-element.69), channel_id=1, source_target_pairs={{0,2},{1,3},{2,0},{3,1},{4,6},{5,7},{6,4},{7,5},{8,10},{9,11},{10,... | collective-permute-start | bytes 884744 | tf_op jit(solution)/shard_map/ppermute | solution.py:458
  63.7 0.0 collective-permute-done.5.before
  63.7 0.0 collective-permute-done.6.after
  63.7 0.0 copy-done.8
  63.7 6.1 %near_rest.1.near_sum = f32[8,64,512]{2,1,0:T(8,128)S(1)} custom-call(s32[8,8]{1,0:T(8,128)S(1)} %copy-done.6, s32[1]{0:T(128)} %bitcast.first, bf16[8,128,512]{2,1,0:T(8,128)(2,1)S(1)} %copy-done.5, bf16[8,128,512]{2,1,0:T(8,128)(2,1)S(1)} %collective-permute-done.5.before, bf16[8,128,512]{2,1,0:T(8,128)(2,1)S(1)} %collective-permute-done.6.after, ...), custom_call_target="tpu_custom_call" | custom-call | flops 11000000512 | bytes 1000000 | tf_op jit(solution)/shard_map/near_rest/pallas_call | solution.py:403
  69.8 5.0 %collective-permute-done.12.r1 = bf16[576,256]{1,0:T(8,128)(2,1)S(1)} collective-permute-done((bf16[576,256]{1,0:T(8,128)(2,1)S(1)}, bf16[576,256]{1,0:T(8,128)(2,1)S(1)}, u32[]{:S(2)}, u32[]{:S(2)}) %collective-permute-start.12) | collective-permute-done | bytes 294944 | tf_op jit(solution)/shard_map/ppermute | solution.py:458
  74.8 3.4 %collective-permute-done.13.r2 = bf16[576,256]{1,0:T(8,128)(2,1)S(1)} collective-permute-done((bf16[576,256]{1,0:T(8,128)(2,1)S(1)}, bf16[576,256]{1,0:T(8,128)(2,1)S(1)}, u32[]{:S(2)}, u32[]{:S(2)}) %collective-permute-start.13) | collective-permute-done | bytes 294944 | tf_op jit(solution)/shard_map/ppermute | solution.py:458
  78.2 0.0 collective-permute-done.14.r3
  78.2 0.0 copy-done.2
  78.2 0.0 copy-done.3
  78.2 2.5 %final.1 = bf16[8,64,512]{2,1,0:T(8,128)(2,1)} custom-call(f32[8,64,512]{2,1,0:T(8,128)S(1)} %near_rest.1.near_sum, bf16[8,512,256]{2,1,0:T(8,128)(2,1)S(1)} %copy-done.2, bf16[8,256,256]{2,1,0:T(8,128)(2,1)S(1)} %copy-done.3, f32[512,256]{1,0:T(8,128)S(1)} %get-tuple-element.62.own, bf16[576,256]{1,0:T(8,128)(2,1)S(1)} %collective-permute-done.12.r1, ...), custom_call_target="tpu_custom_call" | custom-call | flops 3000000000 | bytes 1000000 | tf_op jit(solution)/shard_map/final/pallas_call | solution.py:441
  (9 shorter events, 0.1 us)
Async XLA Ops:
  0.0 14.2 %copy-start.6 = (s32[8,8]{1,0:T(8,128)S(1)}, s32[8,8]{1,0:T(8,128)}, u32[]{:S(2)}) copy-start(s32[8,8]{1,0:T(8,128)} %ids.3) | copy-start | bytes 772
  4.9 18.0 %collective-permute-start = (bf16[528,256]{1,0:T(8,128)(2,1)}, bf16[528,256]{1,0:T(8,128)(2,1)S(1)}, u32[]{:S(2)}, u32[]{:S(2)}) collective-permute-start(bf16[528,256]{1,0:T(8,128)(2,1)} %get-tuple-element.47.t0), channel_id=1, source_target_pairs={{0,1},{1,2},{2,3},{3,0},{4,5},{5,6},{6,7},{7,4},{8,9},{9,10},{10,1... | collective-permute-start | bytes 811016 | tf_op jit(solution)/shard_map/ppermute | solution.py:458
  7.0 15.9 %collective-permute-start.1 = (bf16[528,256]{1,0:T(8,128)(2,1)}, bf16[528,256]{1,0:T(8,128)(2,1)S(1)}, u32[]{:S(2)}, u32[]{:S(2)}) collective-permute-start(bf16[528,256]{1,0:T(8,128)(2,1)} %get-tuple-element.47.t0), channel_id=1, source_target_pairs={{0,3},{1,0},{2,1},{3,2},{4,7},{5,4},{6,5},{7,6},{8,11},{9,8},{10,9... | collective-permute-start | bytes 811016 | tf_op jit(solution)/shard_map/ppermute | solution.py:458
  9.2 13.7 %collective-permute-start.2 = (bf16[528,256]{1,0:T(8,128)(2,1)}, bf16[528,256]{1,0:T(8,128)(2,1)S(1)}, u32[]{:S(2)}, u32[]{:S(2)}) collective-permute-start(bf16[528,256]{1,0:T(8,128)(2,1)} %get-tuple-element.47.t0), channel_id=1, source_target_pairs={{0,2},{1,3},{2,0},{3,1},{4,6},{5,7},{6,4},{7,5},{8,10},{9,11},{10,... | collective-permute-start | bytes 811016 | tf_op jit(solution)/shard_map/ppermute | solution.py:458
  11.0 14.9 %collective-permute-start.3 = (bf16[1088,256]{1,0:T(8,128)(2,1)}, bf16[1088,256]{1,0:T(8,128)(2,1)S(1)}, u32[]{:S(2)}, u32[]{:S(2)}) collective-permute-start(bf16[1088,256]{1,0:T(8,128)(2,1)} %get-tuple-element.42.s0), channel_id=1, source_target_pairs={{0,4},{1,5},{2,6},{3,7},{4,8},{5,9},{6,10},{7,11},{8,12},{9,13},{1... | collective-permute-start | bytes 1671176 | tf_op jit(solution)/shard_map/ppermute | solution.py:458
  12.5 13.5 %collective-permute-start.4 = (bf16[1088,256]{1,0:T(8,128)(2,1)}, bf16[1088,256]{1,0:T(8,128)(2,1)S(1)}, u32[]{:S(2)}, u32[]{:S(2)}) collective-permute-start(bf16[1088,256]{1,0:T(8,128)(2,1)} %get-tuple-element.42.s0), channel_id=1, source_target_pairs={{0,12},{1,13},{2,14},{3,15},{4,0},{5,1},{6,2},{7,3},{8,4},{9,5},{1... | collective-permute-start | bytes 1671176 | tf_op jit(solution)/shard_map/ppermute | solution.py:458
  14.2 1.2 %copy-start.4 = (bf16[8,128,512]{2,1,0:T(8,128)(2,1)S(1)}, bf16[8,128,512]{2,1,0:T(8,128)(2,1)}, u32[]{:S(2)}) copy-start(bf16[8,128,512]{2,1,0:T(8,128)(2,1)} %get-tuple-element.45.own) | copy-start | bytes 3145732
  15.4 12.1 %copy-start = (bf16[1088,256]{1,0:T(8,128)(2,1)S(1)}, bf16[1088,256]{1,0:T(8,128)(2,1)}, u32[]{:S(2)}) copy-start(bf16[1088,256]{1,0:T(8,128)(2,1)} %get-tuple-element.42.s0) | copy-start | bytes 1671172
  21.9 1.0 %copy-start.7 = (f32[8,64,512]{2,1,0:T(8,128)}, f32[8,64,512]{2,1,0:T(8,128)S(1)}, u32[]{:S(2)}) copy-start(f32[8,64,512]{2,1,0:T(8,128)S(1)} %near_own.1.given) | copy-start | bytes 3145732
  22.9 10.2 %copy-start.1 = (bf16[528,256]{1,0:T(8,128)(2,1)S(1)}, bf16[528,256]{1,0:T(8,128)(2,1)}, u32[]{:S(2)}) copy-start(bf16[528,256]{1,0:T(8,128)(2,1)} %get-tuple-element.47.t0) | copy-start | bytes 811012
  25.9 13.8 %collective-permute-start.7 = (bf16[1088,256]{1,0:T(8,128)(2,1)S(1)}, bf16[1088,256]{1,0:T(8,128)(2,1)S(1)}, u32[]{:S(2)}, u32[]{:S(2)}) collective-permute-start(bf16[1088,256]{1,0:T(8,128)(2,1)S(1)} %collective-permute-done.3.s1), channel_id=1, source_target_pairs={{0,4},{1,5},{2,6},{3,7},{4,8},{5,9},{6,10},{7,11},{8,12},{9,13},{1... | collective-permute-start | bytes 1671176 | tf_op jit(solution)/shard_map/ppermute | solution.py:458
  27.4 1.2 %copy-start.5 = (bf16[8,128,512]{2,1,0:T(8,128)(2,1)S(1)}, bf16[8,128,512]{2,1,0:T(8,128)(2,1)}, u32[]{:S(2)}) copy-start(bf16[8,128,512]{2,1,0:T(8,128)(2,1)} %get-tuple-element.45.own) | copy-start | bytes 3145732
  28.6 11.1 %copy-start.9 = (bf16[1,64,256]{2,1,0:T(8,128)(2,1)S(1)}, bf16[1,64,256]{2,1,0:T(8,128)(2,1)}, u32[]{:S(2)}) copy-start(bf16[1,64,256]{2,1,0:T(8,128)(2,1)} %param.12) | copy-start | bytes 98308
  28.6 35.0 %collective-permute-start.5 = (bf16[8,128,512]{2,1,0:T(8,128)(2,1)S(1)}, bf16[8,128,512]{2,1,0:T(8,128)(2,1)S(1)}, u32[]{:S(2)}, u32[]{:S(2)}) collective-permute-start(bf16[8,128,512]{2,1,0:T(8,128)(2,1)S(1)} %copy-done.5), channel_id=1, source_target_pairs={{0,1},{1,2},{2,3},{3,4},{4,5},{5,6},{6,7},{7,8},{8,9},{9,10},{10,1... | collective-permute-start | bytes 3145736 | tf_op jit(solution)/shard_map/ppermute | solution.py:489
  31.7 31.9 %collective-permute-start.6 = (bf16[8,128,512]{2,1,0:T(8,128)(2,1)S(1)}, bf16[8,128,512]{2,1,0:T(8,128)(2,1)S(1)}, u32[]{:S(2)}, u32[]{:S(2)}) collective-permute-start(bf16[8,128,512]{2,1,0:T(8,128)(2,1)S(1)} %copy-done.5), channel_id=1, source_target_pairs={{1,0},{2,1},{3,2},{4,3},{5,4},{6,5},{7,6},{8,7},{9,8},{10,9},{11,1... | collective-permute-start | bytes 3145736 | tf_op jit(solution)/shard_map/ppermute | solution.py:490
  39.8 3.0 %collective-permute-start.8 = (bf16[128,256]{1,0:T(8,128)(2,1)S(1)}, bf16[128,256]{1,0:T(8,128)(2,1)S(1)}, u32[]{:S(2)}, u32[]{:S(2)}) collective-permute-start(bf16[128,256]{1,0:T(8,128)(2,1)S(1)} %pad_maximum_fusion.1.mine), channel_id=1, source_target_pairs={{0,16},{16,0},{32,48},{48,32},{64,80},{80,64},{96,112},{112,96},{1... | collective-permute-start | bytes 196616 | tf_op jit(solution)/shard_map/ppermute | solution.py:464
  42.9 11.5 %collective-permute-start.9 = (bf16[256,256]{1,0:T(8,128)(2,1)S(1)}, bf16[256,256]{1,0:T(8,128)(2,1)S(1)}, u32[]{:S(2)}, u32[]{:S(2)}) collective-permute-start(bf16[256,256]{1,0:T(8,128)(2,1)S(1)} %pad_maximum_fusion), channel_id=1, source_target_pairs={{0,32},{16,48},{32,64},{48,80},{64,96},{80,112},{96,0},{112,16},{1... | collective-permute-start | bytes 393224 | tf_op jit(solution)/shard_map/ppermute | solution.py:465
  46.9 7.9 %collective-permute-start.10 = (bf16[256,256]{1,0:T(8,128)(2,1)S(1)}, bf16[256,256]{1,0:T(8,128)(2,1)S(1)}, u32[]{:S(2)}, u32[]{:S(2)}) collective-permute-start(bf16[256,256]{1,0:T(8,128)(2,1)S(1)} %pad_maximum_fusion), channel_id=1, source_target_pairs={{0,96},{16,112},{32,0},{48,16},{64,32},{80,48},{96,64},{112,80},{1... | collective-permute-start | bytes 393224 | tf_op jit(solution)/shard_map/ppermute | solution.py:465
  48.6 7.9 %collective-permute-start.11 = (bf16[256,256]{1,0:T(8,128)(2,1)S(1)}, bf16[256,256]{1,0:T(8,128)(2,1)S(1)}, u32[]{:S(2)}, u32[]{:S(2)}) collective-permute-start(bf16[256,256]{1,0:T(8,128)(2,1)S(1)} %pad_maximum_fusion), channel_id=1, source_target_pairs={{0,64},{16,80},{32,96},{48,112},{64,0},{80,16},{96,32},{112,48},{1... | collective-permute-start | bytes 393224 | tf_op jit(solution)/shard_map/ppermute | solution.py:465
  56.5 7.2 %copy-start.8 = (f32[8,64,512]{2,1,0:T(8,128)S(1)}, f32[8,64,512]{2,1,0:T(8,128)}, u32[]{:S(2)}) copy-start(f32[8,64,512]{2,1,0:T(8,128)} %copy-done.7) | copy-start | bytes 3145732
  57.4 17.4 %collective-permute-start.12 = (bf16[576,256]{1,0:T(8,128)(2,1)S(1)}, bf16[576,256]{1,0:T(8,128)(2,1)S(1)}, u32[]{:S(2)}, u32[]{:S(2)}) collective-permute-start(bf16[576,256]{1,0:T(8,128)(2,1)S(1)} %get-tuple-element.67), channel_id=1, source_target_pairs={{0,3},{1,0},{2,1},{3,2},{4,7},{5,4},{6,5},{7,6},{8,11},{9,8},{10,9... | collective-permute-start | bytes 884744 | tf_op jit(solution)/shard_map/ppermute | solution.py:458
  62.1 16.1 %collective-permute-start.13 = (bf16[576,256]{1,0:T(8,128)(2,1)S(1)}, bf16[576,256]{1,0:T(8,128)(2,1)S(1)}, u32[]{:S(2)}, u32[]{:S(2)}) collective-permute-start(bf16[576,256]{1,0:T(8,128)(2,1)S(1)} %get-tuple-element.68), channel_id=1, source_target_pairs={{0,1},{1,2},{2,3},{3,0},{4,5},{5,6},{6,7},{7,4},{8,9},{9,10},{10,1... | collective-permute-start | bytes 884744 | tf_op jit(solution)/shard_map/ppermute | solution.py:458
  62.1 16.1 %copy-start.2 = (bf16[8,512,256]{2,1,0:T(8,128)(2,1)S(1)}, bf16[8,512,256]{2,1,0:T(8,128)(2,1)}, u32[]{:S(2)}) copy-start(bf16[8,512,256]{2,1,0:T(8,128)(2,1)} %basis.3) | copy-start | bytes 6291460
  62.1 16.1 %copy-start.3 = (bf16[8,256,256]{2,1,0:T(8,128)(2,1)S(1)}, bf16[8,256,256]{2,1,0:T(8,128)(2,1)}, u32[]{:S(2)}) copy-start(bf16[8,256,256]{2,1,0:T(8,128)(2,1)} %transfer.3) | copy-start | bytes 3145732
  62.1 16.1 %collective-permute-start.14 = (bf16[576,256]{1,0:T(8,128)(2,1)S(1)}, bf16[576,256]{1,0:T(8,128)(2,1)S(1)}, u32[]{:S(2)}, u32[]{:S(2)}) collective-permute-start(bf16[576,256]{1,0:T(8,128)(2,1)S(1)} %get-tuple-element.69), channel_id=1, source_target_pairs={{0,2},{1,3},{2,0},{3,1},{4,6},{5,7},{6,4},{7,5},{8,10},{9,11},{10,... | collective-permute-start | bytes 884744 | tf_op jit(solution)/shard_map/ppermute | solution.py:458

commit v11 on v10

--- a/solution.py
+++ b/solution.py
@@ -482,12 +482,12 @@
         (targets, sources, near_msg, near_sum)
     )
     opposite = shifted(sources[1], 1, 0)
+    count = lax.axis_size("leaf") * lax.axis_size("top")
+    up = [(i, i + 1) for i in range(count - 1)]
+    after = lax.ppermute(near_msg, ("leaf", "top"), [(j, i) for i, j in up])
     side = sides_of(sources)
     near_msg, side = lax.optimization_barrier((near_msg, side))
-    count = lax.axis_size("leaf") * lax.axis_size("top")
-    up = [(i, i + 1) for i in range(count - 1)]
     before = lax.ppermute(near_msg, ("leaf", "top"), up)
-    after = lax.ppermute(near_msg, ("leaf", "top"), [(j, i) for i, j in up])
 
     def ids_of(which):
         ids = jnp.concatenate([t[LD * F : LD * F + LD, : SIDE * SIDE] for t in which])

time: 81.8 us -> 79.7 us (0.974)
  waiting for transfers between devices: 16.6 us -> 13.3 us
  Pallas kernels: 31.6 us -> 33.4 us
    ppermute x9, waiting for transfers between devices: 14.5 us -> 11.4 us  [shifted(): return lax.ppermute(value, 'top', pairs)]
    ppermute x3, starting transfers between devices: 7.73 us -> 5.49 us  [leaf_shifted(): lax.ppermute(value, 'leaf', [(i, (i + 2 * dy) % count) for i in range(cou...]
    pallas_call x1, Pallas kernels: 6.51 us -> 8.33 us  [near_own(): pl.pallas_call(near_own_kernel, in_specs=[SM, SM, VM], out_specs=VM, out_...]
    ppermute x1, starting transfers between devices: 3.11 us -> 4.61 us  [on_device(): before = lax.ppermute(near_msg, ('leaf', 'top'), up)]
    ppermute x9, starting transfers between devices: 17.1 us -> 18.5 us  [shifted(): return lax.ppermute(value, 'top', pairs)]
  transfers between devices with their start and end apart: 15 -> 15, of which waited for: 6 -> 6; matrix products, arithmetic and copies ran while one was open for 0% -> 0% of each run, Pallas kernels for 30% -> 33%
where the time goes in v11:
time: 79.7 us; the launch traced here: 79.4 us
  Pallas kernels  33.4 us (42%)
  starting transfers between devices  30.1 us (38%)
  waiting for transfers between devices  13.3 us (17%)
  local copies, waits for them, and re-layouts  2.21 us (3%)
    ppermute x9, starting transfers between devices, shifted(): return lax.ppermute(value, 'top', pairs)  18.5 us
    ppermute x9, waiting for transfers between devices, shifted(): return lax.ppermute(value, 'top', pairs)  11.4 us
    pallas_call x1, Pallas kernels, near_own(): pl.pallas_call(near_own_kernel, in_specs=[SM, SM, VM], out_specs=VM, out_...  8.33 us
    pallas_call x1, Pallas kernels, near_rest(): pl.pallas_call(near_rest_kernel, in_specs=[SM, SM, VM, VM, VM, VM], out_s...  6 us
    ppermute x3, starting transfers between devices, leaf_shifted(): lax.ppermute(value, 'leaf', [(i, (i + 2 * dy) % count) for i in range(cou...  5.49 us
    pallas_call x1, Pallas kernels, prep(): pl.pallas_call(prep_kernel, in_specs=[anywhere] * 4 + [VM] * 2, out_specs...  4.89 us
    ppermute x1, starting transfers between devices, on_device(): before = lax.ppermute(near_msg, ('leaf', 'top'), up)  4.61 us
    pallas_call x1, Pallas kernels, far_c(): pl.pallas_call(far_c_kernel, in_specs=[SM, SM] + [VM] * 11, out_specs=[VM...  3.8 us
  transfers between devices with their start and end apart: 15, of which 6 were waited for; matrix products, arithmetic and copies ran while one was open for 0% of the time, Pallas kernels for 33%

profile of v11, /device:TPU:0, one launch (start us, length us, event | category | flops | bytes accessed | tf_op | source)
XLA Modules:
  0.0 79.4 jit_solution(11703812383277741618)
XLA Ops:
  0.0 0.0 copy-start.6
  0.0 4.9 %prep.1 = (bf16[8,128,512]{2,1,0:T(8,128)(2,1)}, bf16[1088,256]{1,0:T(8,128)(2,1)}, bf16[528,256]{1,0:T(8,128)(2,1)}) custom-call(bf16[8,64,512]{2,1,0:T(8,128)(2,1)} %points.1, bf16[8,64,512]{2,1,0:T(8,128)(2,1)} %sides.2, bf16[8,512,256]{2,1,0:T(8,128)(2,1)} %basis.3, bf16[8,256,256]{2,1,0:T(8,128)(2,1)} %transfer.3, s32[8,256]{1,0:T(8,128)} %skeleton.1, ...), custom_call_target="tpu_custom_call" | custom-call | flops 4000000000 | bytes 1000000 | tf_op jit(solution)/shard_map/prep/pallas_call | solution.py:101
  4.9 2.1 %collective-permute-start = (bf16[528,256]{1,0:T(8,128)(2,1)}, bf16[528,256]{1,0:T(8,128)(2,1)S(1)}, u32[]{:S(2)}, u32[]{:S(2)}) collective-permute-start(bf16[528,256]{1,0:T(8,128)(2,1)} %get-tuple-element.47.t0), channel_id=1, source_target_pairs={{0,1},{1,2},{2,3},{3,0},{4,5},{5,6},{6,7},{7,4},{8,9},{9,10},{10,1... | collective-permute-start | bytes 811016 | tf_op jit(solution)/shard_map/ppermute | solution.py:458
  7.0 2.2 %collective-permute-start.1 = (bf16[528,256]{1,0:T(8,128)(2,1)}, bf16[528,256]{1,0:T(8,128)(2,1)S(1)}, u32[]{:S(2)}, u32[]{:S(2)}) collective-permute-start(bf16[528,256]{1,0:T(8,128)(2,1)} %get-tuple-element.47.t0), channel_id=1, source_target_pairs={{0,3},{1,0},{2,1},{3,2},{4,7},{5,4},{6,5},{7,6},{8,11},{9,8},{10,9... | collective-permute-start | bytes 811016 | tf_op jit(solution)/shard_map/ppermute | solution.py:458
  9.2 1.8 %collective-permute-start.2 = (bf16[528,256]{1,0:T(8,128)(2,1)}, bf16[528,256]{1,0:T(8,128)(2,1)S(1)}, u32[]{:S(2)}, u32[]{:S(2)}) collective-permute-start(bf16[528,256]{1,0:T(8,128)(2,1)} %get-tuple-element.47.t0), channel_id=1, source_target_pairs={{0,2},{1,3},{2,0},{3,1},{4,6},{5,7},{6,4},{7,5},{8,10},{9,11},{10,... | collective-permute-start | bytes 811016 | tf_op jit(solution)/shard_map/ppermute | solution.py:458
  11.0 1.5 %collective-permute-start.3 = (bf16[1088,256]{1,0:T(8,128)(2,1)}, bf16[1088,256]{1,0:T(8,128)(2,1)S(1)}, u32[]{:S(2)}, u32[]{:S(2)}) collective-permute-start(bf16[1088,256]{1,0:T(8,128)(2,1)} %get-tuple-element.42.s0), channel_id=1, source_target_pairs={{0,4},{1,5},{2,6},{3,7},{4,8},{5,9},{6,10},{7,11},{8,12},{9,13},{1... | collective-permute-start | bytes 1671176 | tf_op jit(solution)/shard_map/ppermute | solution.py:458
  12.5 1.7 %collective-permute-start.4 = (bf16[1088,256]{1,0:T(8,128)(2,1)}, bf16[1088,256]{1,0:T(8,128)(2,1)S(1)}, u32[]{:S(2)}, u32[]{:S(2)}) collective-permute-start(bf16[1088,256]{1,0:T(8,128)(2,1)} %get-tuple-element.42.s0), channel_id=1, source_target_pairs={{0,12},{1,13},{2,14},{3,15},{4,0},{5,1},{6,2},{7,3},{8,4},{9,5},{1... | collective-permute-start | bytes 1671176 | tf_op jit(solution)/shard_map/ppermute | solution.py:458
  14.2 0.0 copy-done.6
  14.2 0.0 copy-start.4
  14.2 1.2 %copy-done.4 = bf16[8,128,512]{2,1,0:T(8,128)(2,1)S(1)} copy-done((bf16[8,128,512]{2,1,0:T(8,128)(2,1)S(1)}, bf16[8,128,512]{2,1,0:T(8,128)(2,1)}, u32[]{:S(2)}) %copy-start.4) | copy-done | bytes 1048600
  15.4 0.0 copy-start
  15.4 8.3 %near_own.1.given = f32[8,64,512]{2,1,0:T(8,128)S(1)} custom-call(s32[8,8]{1,0:T(8,128)S(1)} %copy-done.6, s32[1]{0:T(128)} %bitcast.first, bf16[8,128,512]{2,1,0:T(8,128)(2,1)S(1)} %copy-done.4), custom_call_target="tpu_custom_call" | custom-call | flops 8999999488 | bytes 1000000 | tf_op jit(solution)/shard_map/near_own/pallas_call | solution.py:367
  23.8 0.0 copy-start.7
  23.8 0.9 %copy-done.7 = f32[8,64,512]{2,1,0:T(8,128)} copy-done((f32[8,64,512]{2,1,0:T(8,128)}, f32[8,64,512]{2,1,0:T(8,128)S(1)}, u32[]{:S(2)}) %copy-start.7) | copy-done | bytes 1048600
  24.7 0.0 copy-start.1
  24.7 0.0 collective-permute-done.t1
  24.7 0.0 collective-permute-done.1.t2
  24.7 0.0 collective-permute-done.2.t3
  24.7 1.2 %collective-permute-done.3.s1 = bf16[1088,256]{1,0:T(8,128)(2,1)S(1)} collective-permute-done((bf16[1088,256]{1,0:T(8,128)(2,1)}, bf16[1088,256]{1,0:T(8,128)(2,1)S(1)}, u32[]{:S(2)}, u32[]{:S(2)}) %collective-permute-start.3) | collective-permute-done | bytes 557088 | tf_op jit(solution)/shard_map/ppermute | solution.py:458
  25.9 0.0 collective-permute-done.4.s2
  25.9 1.5 %collective-permute-start.7 = (bf16[1088,256]{1,0:T(8,128)(2,1)S(1)}, bf16[1088,256]{1,0:T(8,128)(2,1)S(1)}, u32[]{:S(2)}, u32[]{:S(2)}) collective-permute-start(bf16[1088,256]{1,0:T(8,128)(2,1)S(1)} %collective-permute-done.3.s1), channel_id=1, source_target_pairs={{0,4},{1,5},{2,6},{3,7},{4,8},{5,9},{6,10},{7,11},{8,12},{9,13},{1... | collective-permute-start | bytes 1671176 | tf_op jit(solution)/shard_map/ppermute | solution.py:458
  27.4 0.0 copy-start.5
  27.4 0.1 pad_add_fusion.place
  27.5 1.4 %collective-permute-start.6 = (bf16[8,128,512]{2,1,0:T(8,128)(2,1)}, bf16[8,128,512]{2,1,0:T(8,128)(2,1)S(1)}, u32[]{:S(2)}, u32[]{:S(2)}) collective-permute-start(bf16[8,128,512]{2,1,0:T(8,128)(2,1)} %get-tuple-element.45.own), channel_id=1, source_target_pairs={{1,0},{2,1},{3,2},{4,3},{5,4},{6,5},{7,6},{8,7},{9,8},{10,9},{11,1... | collective-permute-start | bytes 3145736 | tf_op jit(solution)/shard_map/ppermute | solution.py:487
  28.9 0.0 copy-done
  28.9 0.5 sides.3.side
  29.4 0.0 copy-done.5
  29.4 0.0 copy-start.9
  29.4 4.6 %collective-permute-start.5 = (bf16[8,128,512]{2,1,0:T(8,128)(2,1)S(1)}, bf16[8,128,512]{2,1,0:T(8,128)(2,1)S(1)}, u32[]{:S(2)}, u32[]{:S(2)}) collective-permute-start(bf16[8,128,512]{2,1,0:T(8,128)(2,1)S(1)} %copy-done.5), channel_id=1, source_target_pairs={{0,1},{1,2},{2,3},{3,4},{4,5},{5,6},{6,7},{7,8},{8,9},{9,10},{10,1... | collective-permute-start | bytes 3145736 | tf_op jit(solution)/shard_map/ppermute | solution.py:490
  34.1 0.0 copy-done.1
  34.1 3.6 %far_a.1 = (f32[512,256]{1,0:T(8,128)S(1)}, f32[512,256]{1,0:T(8,128)S(1)}) custom-call(s32[16,16]{1,0:T(8,128)S(1)} %maximum_convert_fusion.1.ids, s32[2]{0:T(128)S(1)} %pad_add_fusion.place, bf16[24,256,128]{2,1,0:T(8,128)(2,1)S(1)} %sides.3.side, bf16[1088,256]{1,0:T(8,128)(2,1)S(1)} %copy-done, bf16[1088,256]{1,0:T(8,128)(2,1)S(1)} %collective-permute-done.3.s1, ...), custom_call_target="tpu_custom_call" | custom-call | flops 10000000 | bytes 1000000 | tf_op jit(solution)/shard_map/far_a/pallas_call | solution.py:215
  37.7 2.0 %collective-permute-done.7.s3 = bf16[1088,256]{1,0:T(8,128)(2,1)S(1)} collective-permute-done((bf16[1088,256]{1,0:T(8,128)(2,1)S(1)}, bf16[1088,256]{1,0:T(8,128)(2,1)S(1)}, u32[]{:S(2)}, u32[]{:S(2)}) %collective-permute-start.7) | collective-permute-done | bytes 557088 | tf_op jit(solution)/shard_map/ppermute | solution.py:458
  39.8 0.0 copy-done.9
  39.8 0.1 collective-permute-start.8
  39.9 3.0 %far_b.1 = (bf16[512,256]{1,0:T(8,128)(2,1)S(1)}, bf16[8,256,128]{2,1,0:T(8,128)(2,1)S(1)}) custom-call(s32[32,16]{1,0:T(8,128)S(1)} %maximum_convert_fusion.ids, s32[2]{0:T(128)S(1)} %pad_add_fusion.place, bf16[24,256,128]{2,1,0:T(8,128)(2,1)S(1)} %sides.3.side, bf16[1088,256]{1,0:T(8,128)(2,1)S(1)} %copy-done, ...), custom_call_target="tpu_custom_call" | custom-call | flops 3000000000 | bytes 1000000 | tf_op jit(solution)/shard_map/far_b/pallas_call | solution.py:240
  42.9 0.0 collective-permute-done.8.pair
  42.9 1.6 %collective-permute-start.9 = (bf16[256,256]{1,0:T(8,128)(2,1)S(1)}, bf16[256,256]{1,0:T(8,128)(2,1)S(1)}, u32[]{:S(2)}, u32[]{:S(2)}) collective-permute-start(bf16[256,256]{1,0:T(8,128)(2,1)S(1)} %pad_maximum_fusion), channel_id=1, source_target_pairs={{0,32},{16,48},{32,64},{48,80},{64,96},{80,112},{96,0},{112,16},{1... | collective-permute-start | bytes 393224 | tf_op jit(solution)/shard_map/ppermute | solution.py:465
  44.5 1.7 %collective-permute-start.10 = (bf16[256,256]{1,0:T(8,128)(2,1)S(1)}, bf16[256,256]{1,0:T(8,128)(2,1)S(1)}, u32[]{:S(2)}, u32[]{:S(2)}) collective-permute-start(bf16[256,256]{1,0:T(8,128)(2,1)S(1)} %pad_maximum_fusion), channel_id=1, source_target_pairs={{0,96},{16,112},{32,0},{48,16},{64,32},{80,48},{96,64},{112,80},{1... | collective-permute-start | bytes 393224 | tf_op jit(solution)/shard_map/ppermute | solution.py:465
  46.2 2.2 %collective-permute-start.11 = (bf16[256,256]{1,0:T(8,128)(2,1)S(1)}, bf16[256,256]{1,0:T(8,128)(2,1)S(1)}, u32[]{:S(2)}, u32[]{:S(2)}) collective-permute-start(bf16[256,256]{1,0:T(8,128)(2,1)S(1)} %pad_maximum_fusion), channel_id=1, source_target_pairs={{0,64},{16,80},{32,96},{48,112},{64,0},{80,16},{96,32},{112,48},{1... | collective-permute-start | bytes 393224 | tf_op jit(solution)/shard_map/ppermute | solution.py:465
  48.4 3.8 %far_c.1 = (f32[512,256]{1,0:T(8,128)S(1)}, bf16[512,256]{1,0:T(8,128)(2,1)S(1)}, bf16[512,256]{1,0:T(8,128)(2,1)S(1)}) custom-call(s32[32,16]{1,0:T(8,128)S(1)} %maximum_convert_fusion.ids, s32[2]{0:T(128)S(1)} %pad_add_fusion.place, bf16[24,256,128]{2,1,0:T(8,128)(2,1)S(1)} %sides.3.side, bf16[8,256,128]{2,1,0:T(8,128)(2,1)S(1)} %get-tuple-element.59.last, ...), custom_call_target="tpu_custom_call" | custom-call | flops 4000000000 | bytes 1000000 | tf_op jit(solution)/shard_map/far_c/pallas_call | solution.py:271
  52.2 0.0 collective-permute-done.9.n1
  52.2 0.1 collective-permute-done.10.n2
  52.3 1.8 %collective-permute-done.11.n3 = bf16[256,256]{1,0:T(8,128)(2,1)S(1)} collective-permute-done((bf16[256,256]{1,0:T(8,128)(2,1)S(1)}, bf16[256,256]{1,0:T(8,128)(2,1)S(1)}, u32[]{:S(2)}, u32[]{:S(2)}) %collective-permute-start.11) | collective-permute-done | bytes 131104 | tf_op jit(solution)/shard_map/ppermute | solution.py:465
  54.1 0.0 copy-start.8
  54.1 0.8 %top_sum.1 = (f32[64,256]{1,0:T(8,128)S(1)}, bf16[576,256]{1,0:T(8,128)(2,1)S(1)}, bf16[576,256]{1,0:T(8,128)(2,1)S(1)}, bf16[576,256]{1,0:T(8,128)(2,1)S(1)}) custom-call(bf16[128,256]{1,0:T(8,128)(2,1)S(1)} %pad_maximum_fusion.1.mine, bf16[128,256]{1,0:T(8,128)(2,1)S(1)} %collective-permute-done.8.pair, bf16[256,256]{1,0:T(8,128)(2,1)S(1)} %collective-permute-done.9.n1, ...), custom_call_target="tpu_custom_call" | custom-call | flops 2000000000 | bytes 1000000 | tf_op jit(solution)/shard_map/top_sum/pallas_call | solution.py:301
  54.9 6.2 %collective-permute-start.12 = (bf16[576,256]{1,0:T(8,128)(2,1)S(1)}, bf16[576,256]{1,0:T(8,128)(2,1)S(1)}, u32[]{:S(2)}, u32[]{:S(2)}) collective-permute-start(bf16[576,256]{1,0:T(8,128)(2,1)S(1)} %get-tuple-element.67), channel_id=1, source_target_pairs={{0,3},{1,0},{2,1},{3,2},{4,7},{5,4},{6,5},{7,6},{8,11},{9,8},{10,9... | collective-permute-start | bytes 884744 | tf_op jit(solution)/shard_map/ppermute | solution.py:458
  61.1 0.0 collective-permute-start.13
  61.1 0.0 copy-start.2
  61.1 0.0 copy-start.3
  61.1 1.5 %collective-permute-start.14 = (bf16[576,256]{1,0:T(8,128)(2,1)S(1)}, bf16[576,256]{1,0:T(8,128)(2,1)S(1)}, u32[]{:S(2)}, u32[]{:S(2)}) collective-permute-start(bf16[576,256]{1,0:T(8,128)(2,1)S(1)} %get-tuple-element.69), channel_id=1, source_target_pairs={{0,2},{1,3},{2,0},{3,1},{4,6},{5,7},{6,4},{7,5},{8,10},{9,11},{10,... | collective-permute-start | bytes 884744 | tf_op jit(solution)/shard_map/ppermute | solution.py:458
  62.7 0.0 collective-permute-done.5.before
  62.7 0.0 collective-permute-done.6.after
  62.7 0.0 copy-done.8
  62.7 6.0 %near_rest.1.near_sum = f32[8,64,512]{2,1,0:T(8,128)S(1)} custom-call(s32[8,8]{1,0:T(8,128)S(1)} %copy-done.6, s32[1]{0:T(128)} %bitcast.first, bf16[8,128,512]{2,1,0:T(8,128)(2,1)S(1)} %copy-done.5, bf16[8,128,512]{2,1,0:T(8,128)(2,1)S(1)} %collective-permute-done.5.before, bf16[8,128,512]{2,1,0:T(8,128)(2,1)S(1)} %collective-permute-done.6.after, ...), custom_call_target="tpu_custom_call" | custom-call | flops 11000000512 | bytes 1000000 | tf_op jit(solution)/shard_map/near_rest/pallas_call | solution.py:403
  68.7 4.8 %collective-permute-done.12.r1 = bf16[576,256]{1,0:T(8,128)(2,1)S(1)} collective-permute-done((bf16[576,256]{1,0:T(8,128)(2,1)S(1)}, bf16[576,256]{1,0:T(8,128)(2,1)S(1)}, u32[]{:S(2)}, u32[]{:S(2)}) %collective-permute-start.12) | collective-permute-done | bytes 294944 | tf_op jit(solution)/shard_map/ppermute | solution.py:458
  73.4 3.4 %collective-permute-done.13.r2 = bf16[576,256]{1,0:T(8,128)(2,1)S(1)} collective-permute-done((bf16[576,256]{1,0:T(8,128)(2,1)S(1)}, bf16[576,256]{1,0:T(8,128)(2,1)S(1)}, u32[]{:S(2)}, u32[]{:S(2)}) %collective-permute-start.13) | collective-permute-done | bytes 294944 | tf_op jit(solution)/shard_map/ppermute | solution.py:458
  76.9 0.0 collective-permute-done.14.r3
  76.9 0.0 copy-done.2
  76.9 0.0 copy-done.3
  76.9 2.5 %final.1 = bf16[8,64,512]{2,1,0:T(8,128)(2,1)} custom-call(f32[8,64,512]{2,1,0:T(8,128)S(1)} %near_rest.1.near_sum, bf16[8,512,256]{2,1,0:T(8,128)(2,1)S(1)} %copy-done.2, bf16[8,256,256]{2,1,0:T(8,128)(2,1)S(1)} %copy-done.3, f32[512,256]{1,0:T(8,128)S(1)} %get-tuple-element.62.own, bf16[576,256]{1,0:T(8,128)(2,1)S(1)} %collective-permute-done.12.r1, ...), custom_call_target="tpu_custom_call" | custom-call | flops 3000000000 | bytes 1000000 | tf_op jit(solution)/shard_map/final/pallas_call | solution.py:441
  (9 shorter events, 0.1 us)
Async XLA Ops:
  0.0 14.2 %copy-start.6 = (s32[8,8]{1,0:T(8,128)S(1)}, s32[8,8]{1,0:T(8,128)}, u32[]{:S(2)}) copy-start(s32[8,8]{1,0:T(8,128)} %ids.3) | copy-start | bytes 772
  4.9 19.8 %collective-permute-start = (bf16[528,256]{1,0:T(8,128)(2,1)}, bf16[528,256]{1,0:T(8,128)(2,1)S(1)}, u32[]{:S(2)}, u32[]{:S(2)}) collective-permute-start(bf16[528,256]{1,0:T(8,128)(2,1)} %get-tuple-element.47.t0), channel_id=1, source_target_pairs={{0,1},{1,2},{2,3},{3,0},{4,5},{5,6},{6,7},{7,4},{8,9},{9,10},{10,1... | collective-permute-start | bytes 811016 | tf_op jit(solution)/shard_map/ppermute | solution.py:458
  7.0 17.8 %collective-permute-start.1 = (bf16[528,256]{1,0:T(8,128)(2,1)}, bf16[528,256]{1,0:T(8,128)(2,1)S(1)}, u32[]{:S(2)}, u32[]{:S(2)}) collective-permute-start(bf16[528,256]{1,0:T(8,128)(2,1)} %get-tuple-element.47.t0), channel_id=1, source_target_pairs={{0,3},{1,0},{2,1},{3,2},{4,7},{5,4},{6,5},{7,6},{8,11},{9,8},{10,9... | collective-permute-start | bytes 811016 | tf_op jit(solution)/shard_map/ppermute | solution.py:458
  9.2 15.6 %collective-permute-start.2 = (bf16[528,256]{1,0:T(8,128)(2,1)}, bf16[528,256]{1,0:T(8,128)(2,1)S(1)}, u32[]{:S(2)}, u32[]{:S(2)}) collective-permute-start(bf16[528,256]{1,0:T(8,128)(2,1)} %get-tuple-element.47.t0), channel_id=1, source_target_pairs={{0,2},{1,3},{2,0},{3,1},{4,6},{5,7},{6,4},{7,5},{8,10},{9,11},{10,... | collective-permute-start | bytes 811016 | tf_op jit(solution)/shard_map/ppermute | solution.py:458
  11.0 14.9 %collective-permute-start.3 = (bf16[1088,256]{1,0:T(8,128)(2,1)}, bf16[1088,256]{1,0:T(8,128)(2,1)S(1)}, u32[]{:S(2)}, u32[]{:S(2)}) collective-permute-start(bf16[1088,256]{1,0:T(8,128)(2,1)} %get-tuple-element.42.s0), channel_id=1, source_target_pairs={{0,4},{1,5},{2,6},{3,7},{4,8},{5,9},{6,10},{7,11},{8,12},{9,13},{1... | collective-permute-start | bytes 1671176 | tf_op jit(solution)/shard_map/ppermute | solution.py:458
  12.5 13.5 %collective-permute-start.4 = (bf16[1088,256]{1,0:T(8,128)(2,1)}, bf16[1088,256]{1,0:T(8,128)(2,1)S(1)}, u32[]{:S(2)}, u32[]{:S(2)}) collective-permute-start(bf16[1088,256]{1,0:T(8,128)(2,1)} %get-tuple-element.42.s0), channel_id=1, source_target_pairs={{0,12},{1,13},{2,14},{3,15},{4,0},{5,1},{6,2},{7,3},{8,4},{9,5},{1... | collective-permute-start | bytes 1671176 | tf_op jit(solution)/shard_map/ppermute | solution.py:458
  14.2 1.2 %copy-start.4 = (bf16[8,128,512]{2,1,0:T(8,128)(2,1)S(1)}, bf16[8,128,512]{2,1,0:T(8,128)(2,1)}, u32[]{:S(2)}) copy-start(bf16[8,128,512]{2,1,0:T(8,128)(2,1)} %get-tuple-element.45.own) | copy-start | bytes 3145732
  15.4 13.5 %copy-start = (bf16[1088,256]{1,0:T(8,128)(2,1)S(1)}, bf16[1088,256]{1,0:T(8,128)(2,1)}, u32[]{:S(2)}) copy-start(bf16[1088,256]{1,0:T(8,128)(2,1)} %get-tuple-element.42.s0) | copy-start | bytes 1671172
  23.8 1.0 %copy-start.7 = (f32[8,64,512]{2,1,0:T(8,128)}, f32[8,64,512]{2,1,0:T(8,128)S(1)}, u32[]{:S(2)}) copy-start(f32[8,64,512]{2,1,0:T(8,128)S(1)} %near_own.1.given) | copy-start | bytes 3145732
  24.7 9.4 %copy-start.1 = (bf16[528,256]{1,0:T(8,128)(2,1)S(1)}, bf16[528,256]{1,0:T(8,128)(2,1)}, u32[]{:S(2)}) copy-start(bf16[528,256]{1,0:T(8,128)(2,1)} %get-tuple-element.47.t0) | copy-start | bytes 811012
  25.9 13.8 %collective-permute-start.7 = (bf16[1088,256]{1,0:T(8,128)(2,1)S(1)}, bf16[1088,256]{1,0:T(8,128)(2,1)S(1)}, u32[]{:S(2)}, u32[]{:S(2)}) collective-permute-start(bf16[1088,256]{1,0:T(8,128)(2,1)S(1)} %collective-permute-done.3.s1), channel_id=1, source_target_pairs={{0,4},{1,5},{2,6},{3,7},{4,8},{5,9},{6,10},{7,11},{8,12},{9,13},{1... | collective-permute-start | bytes 1671176 | tf_op jit(solution)/shard_map/ppermute | solution.py:458
  27.4 2.0 %copy-start.5 = (bf16[8,128,512]{2,1,0:T(8,128)(2,1)S(1)}, bf16[8,128,512]{2,1,0:T(8,128)(2,1)}, u32[]{:S(2)}) copy-start(bf16[8,128,512]{2,1,0:T(8,128)(2,1)} %get-tuple-element.45.own) | copy-start | bytes 3145732
  27.5 35.2 %collective-permute-start.6 = (bf16[8,128,512]{2,1,0:T(8,128)(2,1)}, bf16[8,128,512]{2,1,0:T(8,128)(2,1)S(1)}, u32[]{:S(2)}, u32[]{:S(2)}) collective-permute-start(bf16[8,128,512]{2,1,0:T(8,128)(2,1)} %get-tuple-element.45.own), channel_id=1, source_target_pairs={{1,0},{2,1},{3,2},{4,3},{5,4},{6,5},{7,6},{8,7},{9,8},{10,9},{11,1... | collective-permute-start | bytes 3145736 | tf_op jit(solution)/shard_map/ppermute | solution.py:487
  29.4 10.3 %copy-start.9 = (bf16[1,64,256]{2,1,0:T(8,128)(2,1)S(1)}, bf16[1,64,256]{2,1,0:T(8,128)(2,1)}, u32[]{:S(2)}) copy-start(bf16[1,64,256]{2,1,0:T(8,128)(2,1)} %param.12) | copy-start | bytes 98308
  29.4 33.2 %collective-permute-start.5 = (bf16[8,128,512]{2,1,0:T(8,128)(2,1)S(1)}, bf16[8,128,512]{2,1,0:T(8,128)(2,1)S(1)}, u32[]{:S(2)}, u32[]{:S(2)}) collective-permute-start(bf16[8,128,512]{2,1,0:T(8,128)(2,1)S(1)} %copy-done.5), channel_id=1, source_target_pairs={{0,1},{1,2},{2,3},{3,4},{4,5},{5,6},{6,7},{7,8},{8,9},{9,10},{10,1... | collective-permute-start | bytes 3145736 | tf_op jit(solution)/shard_map/ppermute | solution.py:490
  39.8 3.1 %collective-permute-start.8 = (bf16[128,256]{1,0:T(8,128)(2,1)S(1)}, bf16[128,256]{1,0:T(8,128)(2,1)S(1)}, u32[]{:S(2)}, u32[]{:S(2)}) collective-permute-start(bf16[128,256]{1,0:T(8,128)(2,1)S(1)} %pad_maximum_fusion.1.mine), channel_id=1, source_target_pairs={{0,16},{16,0},{32,48},{48,32},{64,80},{80,64},{96,112},{112,96},{1... | collective-permute-start | bytes 196616 | tf_op jit(solution)/shard_map/ppermute | solution.py:464
  42.9 9.3 %collective-permute-start.9 = (bf16[256,256]{1,0:T(8,128)(2,1)S(1)}, bf16[256,256]{1,0:T(8,128)(2,1)S(1)}, u32[]{:S(2)}, u32[]{:S(2)}) collective-permute-start(bf16[256,256]{1,0:T(8,128)(2,1)S(1)} %pad_maximum_fusion), channel_id=1, source_target_pairs={{0,32},{16,48},{32,64},{48,80},{64,96},{80,112},{96,0},{112,16},{1... | collective-permute-start | bytes 393224 | tf_op jit(solution)/shard_map/ppermute | solution.py:465
  44.5 7.8 %collective-permute-start.10 = (bf16[256,256]{1,0:T(8,128)(2,1)S(1)}, bf16[256,256]{1,0:T(8,128)(2,1)S(1)}, u32[]{:S(2)}, u32[]{:S(2)}) collective-permute-start(bf16[256,256]{1,0:T(8,128)(2,1)S(1)} %pad_maximum_fusion), channel_id=1, source_target_pairs={{0,96},{16,112},{32,0},{48,16},{64,32},{80,48},{96,64},{112,80},{1... | collective-permute-start | bytes 393224 | tf_op jit(solution)/shard_map/ppermute | solution.py:465
  46.2 7.9 %collective-permute-start.11 = (bf16[256,256]{1,0:T(8,128)(2,1)S(1)}, bf16[256,256]{1,0:T(8,128)(2,1)S(1)}, u32[]{:S(2)}, u32[]{:S(2)}) collective-permute-start(bf16[256,256]{1,0:T(8,128)(2,1)S(1)} %pad_maximum_fusion), channel_id=1, source_target_pairs={{0,64},{16,80},{32,96},{48,112},{64,0},{80,16},{96,32},{112,48},{1... | collective-permute-start | bytes 393224 | tf_op jit(solution)/shard_map/ppermute | solution.py:465
  54.1 8.6 %copy-start.8 = (f32[8,64,512]{2,1,0:T(8,128)S(1)}, f32[8,64,512]{2,1,0:T(8,128)}, u32[]{:S(2)}) copy-start(f32[8,64,512]{2,1,0:T(8,128)} %copy-done.7) | copy-start | bytes 3145732
  54.9 18.5 %collective-permute-start.12 = (bf16[576,256]{1,0:T(8,128)(2,1)S(1)}, bf16[576,256]{1,0:T(8,128)(2,1)S(1)}, u32[]{:S(2)}, u32[]{:S(2)}) collective-permute-start(bf16[576,256]{1,0:T(8,128)(2,1)S(1)} %get-tuple-element.67), channel_id=1, source_target_pairs={{0,3},{1,0},{2,1},{3,2},{4,7},{5,4},{6,5},{7,6},{8,11},{9,8},{10,9... | collective-permute-start | bytes 884744 | tf_op jit(solution)/shard_map/ppermute | solution.py:458
  61.1 15.7 %collective-permute-start.13 = (bf16[576,256]{1,0:T(8,128)(2,1)S(1)}, bf16[576,256]{1,0:T(8,128)(2,1)S(1)}, u32[]{:S(2)}, u32[]{:S(2)}) collective-permute-start(bf16[576,256]{1,0:T(8,128)(2,1)S(1)} %get-tuple-element.68), channel_id=1, source_target_pairs={{0,1},{1,2},{2,3},{3,0},{4,5},{5,6},{6,7},{7,4},{8,9},{9,10},{10,1... | collective-permute-start | bytes 884744 | tf_op jit(solution)/shard_map/ppermute | solution.py:458
  61.1 15.7 %copy-start.2 = (bf16[8,512,256]{2,1,0:T(8,128)(2,1)S(1)}, bf16[8,512,256]{2,1,0:T(8,128)(2,1)}, u32[]{:S(2)}) copy-start(bf16[8,512,256]{2,1,0:T(8,128)(2,1)} %basis.3) | copy-start | bytes 6291460
  61.1 15.7 %copy-start.3 = (bf16[8,256,256]{2,1,0:T(8,128)(2,1)S(1)}, bf16[8,256,256]{2,1,0:T(8,128)(2,1)}, u32[]{:S(2)}) copy-start(bf16[8,256,256]{2,1,0:T(8,128)(2,1)} %transfer.3) | copy-start | bytes 3145732
  61.1 15.7 %collective-permute-start.14 = (bf16[576,256]{1,0:T(8,128)(2,1)S(1)}, bf16[576,256]{1,0:T(8,128)(2,1)S(1)}, u32[]{:S(2)}, u32[]{:S(2)}) collective-permute-start(bf16[576,256]{1,0:T(8,128)(2,1)S(1)} %get-tuple-element.69), channel_id=1, source_target_pairs={{0,2},{1,3},{2,0},{3,1},{4,6},{5,7},{6,4},{7,5},{8,10},{9,11},{10,... | collective-permute-start | bytes 884744 | tf_op jit(solution)/shard_map/ppermute | solution.py:458
